TPU v7x, 32 devices: a whole 2x2x4 slice. The times are simulated.
32 devices in a mesh: seq: 8 (over z, x), doc: 4 (over y, core).
Axes of the slice: x: 2, y: 2, z: 4, core: 2. Of those that a mesh axis runs over, the one named last changes fastest.
Arguments:
- tokens: bfloat16 [4, 3072, 1024], P('doc', 'seq'), may hold values from -7 to 7
- doc_lengths: int32 [4, 4], P('doc'), may hold values from 1 to 2752, as said below
- out_grad: bfloat16 [4, 3072, 1024], P('doc', 'seq'), may hold values from -6 to 6
- first_gain: float32 [1024], replicated, may hold values from 0.5 to 1.5
- query_weight: bfloat16 [1024, 1024], replicated, may hold values from -0.1875 to 0.1875
- key_weight: bfloat16 [1024, 1024], replicated, may hold values from -0.1875 to 0.1875
- value_weight: bfloat16 [1024, 1024], replicated, may hold values from -0.1875 to 0.1875
- gate_weight: bfloat16 [1024, 1024], replicated, may hold values from -0.1875 to 0.1875
- beta_weight: bfloat16 [1024, 8], replicated, may hold values from -1 to 1
- conv_weight: float32 [3, 4, 1024], replicated, may hold values from -3 to 3
- head_gain: float32 [128], replicated, may hold values from 0.5 to 1.5
- out_weight: bfloat16 [1024, 1024], replicated, may hold values from -0.1875 to 0.1875
- second_gain: float32 [1024], replicated, may hold values from 0.5 to 1.5
- hidden_gate: bfloat16 [1024, 2816], replicated, may hold values from -0.1875 to 0.1875
- hidden_up: bfloat16 [1024, 2816], replicated, may hold values from -0.1875 to 0.1875
- hidden_down: bfloat16 [2816, 1024], replicated, may hold values from -0.109375 to 0.109375
Outputs:
- block_out: bfloat16 [4, 3072, 1024], P('doc', 'seq')
- input_grad: bfloat16 [4, 3072, 1024], P('doc', 'seq')
- first_gain_grad: float32 [1024], P('seq')
- query_grad: float32 [1024, 1024], P('seq')
- key_grad: float32 [1024, 1024], P('seq')
- value_grad: float32 [1024, 1024], P('seq')
- gate_grad: float32 [1024, 1024], P('seq')
- beta_grad: float32 [1024, 8], P('seq')
- conv_grad: float32 [3, 4, 1024], P(None, None, 'seq')
- head_gain_grad: float32 [128], P('seq')
- out_grad_weight: float32 [1024, 1024], P('seq')
- second_gain_grad: float32 [1024], P('seq')
- hidden_gate_grad: float32 [1024, 2816], P('seq')
- hidden_up_grad: float32 [1024, 2816], P('seq')
- hidden_down_grad: float32 [2816, 1024], P('seq')
Inputs may be any that keep to these rules, and one draw needn't show every extreme that they name: `doc_lengths`: in each group the lengths rounded up to multiples of 64 add up to 3072; one document of each group, at a place drawn from the seed, has exactly 2752 tokens and the others fill the remaining 384 - 64 slots; some document of each group has a single token.
All inputs are finite; a program needn't handle non-finite values.
Results may differ from a plain program's by a relative error of at most 0.011.
Values sent between devices are 32-bit elements; how exact they have to be, the bound alone decides.
No kernel may reach another device: no remote copies, remote signals or barrier semaphores. Data moves between devices by JAX's collectives and lax.ppermute only.
A program may use at most 384 MiB of HBM per device.

v0:
```python
import jax
import jax.numpy as jnp
from jax import lax
from jax.sharding import PartitionSpec as P

CK = 64


EPS = 1e-05
KEY_EPS = 1e-06
HIGH = lax.Precision.HIGHEST


def passed_along(value, axis, by):
    devices = lax.axis_size(axis)
    pairs = [(i, i + by) for i in range(devices) if 0 <= i + by < devices]
    return lax.ppermute(value, axis, pairs)


def carried_in(part, axis, combine, identity, reverse):
    count = lax.axis_size(axis)
    place = lax.axis_index(axis)
    ahead = count - 1 - place if reverse else place
    gathered = jax.tree.map(lambda a: lax.all_gather(a, axis), part)
    state = jax.tree.map(lambda a, e: jnp.zeros_like(a) + jnp.asarray(e, a.dtype), part, identity)

    def one(lap, state):
        source = count - 1 - lap if reverse else lap
        return combine(
            state, jax.tree.map(lambda a: lax.dynamic_index_in_dim(a, source, 0, False), gathered)
        )

    return lax.fori_loop(0, ahead, one, state)


def linear_map_result(form, left, right):
    return jnp.einsum(form, left, right, precision=HIGH)


def outer_sum(left, right):
    return lax.dot_general(
        left, right, (((0,), (0,)), ((), ())), preferred_element_type=jnp.float32
    )


def across(left, right):
    return lax.dot_general(
        left, right, (((1,), (1,)), ((), ())), preferred_element_type=jnp.float32
    )


def forward_dot(left, right):
    return jnp.dot(left, right, preferred_element_type=jnp.float32)


def root_norm(value, gain):
    return value * lax.rsqrt(jnp.mean(value * value, -1, keepdims=True) + EPS) * gain


def unit_norm(value):
    return value * lax.rsqrt(jnp.sum(value * value, -1, keepdims=True) + KEY_EPS)


def doc_info(lengths, first, count):
    padded = (lengths + CK - 1) // CK * CK
    ends = jnp.cumsum(padded)
    starts = ends - padded
    place = first + jnp.arange(count, dtype=jnp.int32)
    inside = ((place[:, None] >= starts[None, :]) & (place[:, None] < ends[None, :])).astype(
        jnp.int32
    )
    position = place - jnp.sum(inside * starts[None, :], 1)
    length = jnp.sum(inside * lengths[None, :], 1)
    live = (position < length).astype(jnp.float32)
    return (position, live)


def short_conv(extended, weight, position):
    count = position.shape[0]
    width = weight.shape[0]
    running_total = jnp.zeros((count, extended.shape[1]), jnp.float32)
    for tap in range(width):
        valid = (position >= width - 1 - tap).astype(jnp.float32)[:, None]
        running_total = running_total + weight[tap][None, :] * extended[tap : tap + count] * valid
    return jax.nn.silu(running_total)


def features(extended, conv_weight, beta_pre, position, live, head_count):
    weight = conv_weight.transpose(1, 0, 2).reshape(conv_weight.shape[1], -1)
    mixed = short_conv(extended, weight, position)
    count = mixed.shape[0]
    width = mixed.shape[1] // 3
    query = unit_norm(mixed[:, :width].reshape(count, head_count, -1)).reshape(count, width)
    key_rows = (
        unit_norm(mixed[:, width : 2 * width].reshape(count, head_count, -1)) * live[:, None, None]
    ).reshape(count, width)
    values = mixed[:, 2 * width :]
    betas = jax.nn.sigmoid(beta_pre) * live[:, None]
    return (query, key_rows, values, betas)


def to_spans(flat, head_count, size):
    count, width = flat.shape
    return flat.reshape(count // size, size, head_count, width // head_count).transpose(0, 2, 1, 3)


def beta_spans(betas, size):
    count, head_count = betas.shape
    return betas.reshape(count // size, size, head_count).transpose(0, 2, 1)


def from_spans(blocks):
    number, head_count, size, layer_count = blocks.shape
    return blocks.transpose(0, 2, 1, 3).reshape(number * size, head_count * layer_count)


def lower_inverse(strict):
    size = strict.shape[-1]
    identity_matrix = jnp.eye(size, dtype=jnp.float32)
    result = identity_matrix - strict
    power = strict
    for level in range(1, size.bit_length() - 1):
        power = linear_map_result("...ij,...jk->...ik", power, power)
        result = linear_map_result("...ij,...jk->...ik", result, identity_matrix + power)
    return result


def span_prep(query, key_rows, values, betas):
    size = key_rows.shape[2]
    lower = jnp.tril(jnp.ones((size, size), jnp.float32), -1)
    inclusive = jnp.tril(jnp.ones((size, size), jnp.float32))
    scores = linear_map_result("bhid,bhjd->bhij", key_rows, key_rows)
    solved = lower_inverse(betas[..., :, None] * scores * lower)
    erase_terms = linear_map_result("bhij,bhjd->bhid", solved, betas[..., None] * key_rows)
    updates = linear_map_result("bhij,bhjd->bhid", solved, betas[..., None] * values)
    attend = linear_map_result("bhid,bhjd->bhij", query, key_rows) * inclusive
    state_loader = query - linear_map_result("bhij,bhjd->bhid", attend, erase_terms)
    local_state = linear_map_result("bhij,bhjd->bhid", attend, updates)
    identity_matrix = jnp.eye(key_rows.shape[3], dtype=jnp.float32)
    recurrent_memory_slot = identity_matrix - linear_map_result(
        "pfxt,pfxa->pfta", key_rows, erase_terms
    )
    feature_supplier = linear_map_result("pfxt,pfxa->pfta", key_rows, updates)
    return (state_loader, local_state, recurrent_memory_slot, feature_supplier)


def span_run(data, keep_mask, state):

    def span_scan_step(carried_state, batch_entry):
        state_loader, local_state, recurrent_memory_slot, feature_supplier, genuine_token_flag = (
            batch_entry
        )
        interval_first_place = carried_state * genuine_token_flag
        residual_unit_result = (
            linear_map_result("hid,hde->hie", state_loader, interval_first_place) + local_state
        )
        return (
            linear_map_result("jlr,jrd->jld", recurrent_memory_slot, interval_first_place)
            + feature_supplier,
            residual_unit_result,
        )

    final, outputs = lax.scan(span_scan_step, state, data + (keep_mask,))
    return (outputs, final)


def document_span_table(recurrent_memory_slot, feature_supplier, keep_mask):
    head_count, layer_count = (recurrent_memory_slot.shape[1], recurrent_memory_slot.shape[2])
    identity_matrix = jnp.broadcast_to(
        jnp.eye(layer_count, dtype=jnp.float32), (head_count, layer_count, layer_count)
    )

    def document_scan_step(carried_state, batch_entry):
        learned_coefficients, leading_shift = carried_state
        residual_unit_slot, block_provider, genuine_token_flag = batch_entry
        learned_coefficients = linear_map_result(
            "jlr,jrd->jld", residual_unit_slot, learned_coefficients * genuine_token_flag
        )
        leading_shift = (
            linear_map_result(
                "jlr,jrd->jld", residual_unit_slot, leading_shift * genuine_token_flag
            )
            + block_provider
        )
        return ((learned_coefficients, leading_shift), None)

    (learned_coefficients, leading_shift), ignored_value = lax.scan(
        document_scan_step,
        (identity_matrix, jnp.zeros_like(identity_matrix)),
        (recurrent_memory_slot, feature_supplier, keep_mask),
    )
    return (learned_coefficients, leading_shift)


def state_gather(state_loader, recurrent_memory_slot, keep_mask, gradient_list):
    head_count, layer_count = (recurrent_memory_slot.shape[1], recurrent_memory_slot.shape[2])

    def state_scan_step(carried_state, batch_entry):
        block_loader, residual_unit_slot, genuine_token_flag, block_gradient = batch_entry
        running_total = linear_map_result(
            "auc,auj->acj", residual_unit_slot, carried_state
        ) + linear_map_result("hid,hie->hde", block_loader, block_gradient)
        return (running_total * genuine_token_flag, None)

    result, ignored_value = lax.scan(
        state_scan_step,
        jnp.zeros((head_count, layer_count, layer_count), jnp.float32),
        (state_loader, recurrent_memory_slot, keep_mask, gradient_list),
        reverse=True,
    )
    return result


def compose(preceding_part, following_part):
    return (
        linear_map_result("jlr,jrd->jld", following_part[0], preceding_part[0]),
        linear_map_result("jlr,jrd->jld", following_part[0], preceding_part[1]) + following_part[1],
    )


def head_norm(mixed, gate_pre, gain, head_count):
    count, width = mixed.shape
    shaped = root_norm(mixed.reshape(count, head_count, -1), gain)
    return (shaped * jax.nn.silu(gate_pre.reshape(count, head_count, -1))).reshape(count, width)


def local(
    tokens,
    doc_lengths,
    out_grad,
    first_gain,
    query_weight,
    key_weight,
    value_weight,
    gate_weight,
    beta_weight,
    conv_weight,
    head_gain,
    out_weight,
    second_gain,
    hidden_gate,
    hidden_up,
    hidden_down,
):
    count, width = (tokens.shape[1], tokens.shape[2])
    head_count = beta_weight.shape[1]
    layer_count = width // head_count
    reach = conv_weight.shape[1] - 1
    first = lax.axis_index("seq") * count
    position, live = doc_info(doc_lengths[0], first, count)
    keep_mask = 1.0 - (position[::CK] == 0).astype(jnp.float32)
    inputs = tokens[0].astype(jnp.float32)
    grad_top = out_grad[0]
    norm_one_out, norm_one_pull = jax.vjp(root_norm, inputs, first_gain)
    normed_one = norm_one_out.astype(jnp.bfloat16)
    query_pre = forward_dot(normed_one, query_weight)
    key_pre = forward_dot(normed_one, key_weight)
    value_pre = forward_dot(normed_one, value_weight)
    gate_pre = forward_dot(normed_one, gate_weight)
    beta_pre = forward_dot(normed_one, beta_weight)
    mixed_pre = jnp.concatenate([query_pre, key_pre, value_pre], 1)
    previous = passed_along(mixed_pre[count - reach :], "seq", 1)
    extended = jnp.concatenate([previous, mixed_pre], 0)

    def make_features(extended, conv_weight, beta_pre):
        return features(extended, conv_weight, beta_pre, position, live, head_count)

    (query, key_rows, values, betas), feature_pull = jax.vjp(
        make_features, extended, conv_weight, beta_pre
    )

    def prepare(query, key_rows, values, betas):
        return span_prep(
            to_spans(query, head_count, CK),
            to_spans(key_rows, head_count, CK),
            to_spans(values, head_count, CK),
            beta_spans(betas, CK),
        )

    def run(data, state):
        return span_run(data, keep_mask, state)

    data, prepare_pull = jax.vjp(prepare, query, key_rows, values, betas)
    learned_coefficients, leading_shift = document_span_table(data[2], data[3], keep_mask)
    identity_matrix = jnp.broadcast_to(
        jnp.eye(layer_count, dtype=jnp.float32), learned_coefficients.shape
    )
    identity = (identity_matrix, jnp.zeros_like(identity_matrix))
    state_in = carried_in((learned_coefficients, leading_shift), "seq", compose, identity, False)[1]
    (outputs, final), run_pull = jax.vjp(run, data, state_in)
    mixed = from_spans(outputs)

    def gated(mixed, gate_pre, head_gain):
        return head_norm(mixed, gate_pre, head_gain, head_count)

    head_out, head_pull = jax.vjp(gated, mixed, gate_pre, head_gain)
    normed_head = head_out.astype(jnp.bfloat16)
    hidden_state = inputs + forward_dot(normed_head, out_weight)
    norm_two_out, norm_two_pull = jax.vjp(root_norm, hidden_state, second_gain)
    normed_two = norm_two_out.astype(jnp.bfloat16)
    gate = forward_dot(normed_two, hidden_gate)
    up = forward_dot(normed_two, hidden_up)
    inner = (jax.nn.silu(gate) * up).astype(jnp.bfloat16)
    block_out = (hidden_state + forward_dot(inner, hidden_down)).astype(jnp.bfloat16)
    grad_down_w = outer_sum(inner, grad_top)
    grad_inner = across(grad_top, hidden_down)
    sigma = jax.nn.sigmoid(gate)
    grad_gate = (grad_inner * up * sigma * (1.0 + gate * (1.0 - sigma))).astype(jnp.bfloat16)
    grad_up = (grad_inner * gate * sigma).astype(jnp.bfloat16)
    grad_gate_w = outer_sum(normed_two, grad_gate)
    grad_up_w = outer_sum(normed_two, grad_up)
    grad_normed_two = across(grad_gate, hidden_gate) + across(grad_up, hidden_up)
    grad_hidden_part, grad_second_gain = norm_two_pull(grad_normed_two)
    grad_hidden = grad_top.astype(jnp.float32) + grad_hidden_part
    grad_branch = grad_hidden.astype(jnp.bfloat16)
    grad_out_w = outer_sum(normed_head, grad_branch)
    grad_head = across(grad_branch, out_weight)
    grad_mixed, grad_gate_part, grad_head_gain = head_pull(grad_head)
    grad_blocks = to_spans(grad_mixed, head_count, CK)
    local_grad = state_gather(data[0], data[2], keep_mask, grad_blocks)
    transposed = jnp.swapaxes(learned_coefficients, 1, 2)
    state_grad = carried_in((transposed, local_grad), "seq", compose, identity, True)[1]
    grad_data = run_pull((grad_blocks, state_grad))[0]
    grad_query, grad_keys, grad_values, grad_betas = prepare_pull(grad_data)
    grad_extended, grad_conv, grad_beta_pre = feature_pull(
        (grad_query, grad_keys, grad_values, grad_betas)
    )
    returned = passed_along(grad_extended[:reach], "seq", -1)
    grad_mixed_pre = grad_extended[reach:] + jnp.concatenate(
        [jnp.zeros((count - reach, 3 * width), jnp.float32), returned], 0
    )
    grad_query_pre = grad_mixed_pre[:, :width].astype(jnp.bfloat16)
    grad_key_pre = grad_mixed_pre[:, width : 2 * width].astype(jnp.bfloat16)
    grad_value_pre = grad_mixed_pre[:, 2 * width :].astype(jnp.bfloat16)
    grad_gate_pre = grad_gate_part.astype(jnp.bfloat16)
    grad_beta_low = grad_beta_pre.astype(jnp.bfloat16)
    grad_query_w = outer_sum(normed_one, grad_query_pre)
    grad_key_w = outer_sum(normed_one, grad_key_pre)
    grad_value_w = outer_sum(normed_one, grad_value_pre)
    grad_gate_pre_w = outer_sum(normed_one, grad_gate_pre)
    grad_beta_w = outer_sum(normed_one, grad_beta_low)
    grad_normed_one = (
        across(grad_query_pre, query_weight)
        + across(grad_key_pre, key_weight)
        + across(grad_value_pre, value_weight)
        + across(grad_gate_pre, gate_weight)
        + across(grad_beta_low, beta_weight)
    )
    grad_input_part, grad_first_gain = norm_one_pull(grad_normed_one)
    input_grad = (grad_hidden + grad_input_part).astype(jnp.bfloat16)
    parts = (
        lax.psum_scatter(grad_first_gain, "seq", scatter_dimension=0, tiled=True),
        lax.psum_scatter(grad_query_w, "seq", scatter_dimension=0, tiled=True),
        lax.psum_scatter(grad_key_w, "seq", scatter_dimension=0, tiled=True),
        lax.psum_scatter(grad_value_w, "seq", scatter_dimension=0, tiled=True),
        lax.psum_scatter(grad_gate_pre_w, "seq", scatter_dimension=0, tiled=True),
        lax.psum_scatter(grad_beta_w, "seq", scatter_dimension=0, tiled=True),
        lax.psum_scatter(grad_conv, "seq", scatter_dimension=2, tiled=True),
        lax.psum_scatter(grad_head_gain, "seq", scatter_dimension=0, tiled=True),
        lax.psum_scatter(grad_out_w, "seq", scatter_dimension=0, tiled=True),
        lax.psum_scatter(grad_second_gain, "seq", scatter_dimension=0, tiled=True),
        lax.psum_scatter(grad_gate_w, "seq", scatter_dimension=0, tiled=True),
        lax.psum_scatter(grad_up_w, "seq", scatter_dimension=0, tiled=True),
        lax.psum_scatter(grad_down_w, "seq", scatter_dimension=0, tiled=True),
    )
    summed = lax.psum(
        (
            parts[0],
            parts[1],
            parts[2],
            parts[3],
            parts[4],
            parts[5],
            parts[6],
            parts[7],
            parts[8],
            parts[9],
            parts[10],
            parts[11],
            parts[12],
        ),
        "doc",
    )
    return (
        block_out[None],
        input_grad[None],
        summed[0],
        summed[1],
        summed[2],
        summed[3],
        summed[4],
        summed[5],
        summed[6],
        summed[7],
        summed[8],
        summed[9],
        summed[10],
        summed[11],
        summed[12],
    )


def solution(mesh):
    in_specs = (
        P("doc", "seq", None),
        P("doc", None),
        P("doc", "seq", None),
        P(),
        P(),
        P(),
        P(),
        P(),
        P(),
        P(),
        P(),
        P(),
        P(),
        P(),
        P(),
        P(),
    )
    out_specs = (
        P("doc", "seq", None),
        P("doc", "seq", None),
        P("seq"),
        P("seq", None),
        P("seq", None),
        P("seq", None),
        P("seq", None),
        P("seq", None),
        P(None, None, "seq"),
        P("seq"),
        P("seq", None),
        P("seq"),
        P("seq", None),
        P("seq", None),
        P("seq", None),
    )
    return jax.shard_map(local, mesh=mesh, in_specs=in_specs, out_specs=out_specs, check_vma=False)
```

profile of v0, /device:TPU:0, one launch (start us, length us, event | category | flops | bytes accessed | tf_op | source)
XLA Modules:
  0.0 1961.0 jit_solution(1448625091050630713)
XLA Ops:
  16.2 4.8 collective-permute-start
  26.8 5.3 fusion.67
  38.5 5.1 fusion.111
  44.8 4.0 fusion.166
  51.9 4.8 fusion.260
  59.7 4.8 fusion.261
  67.5 5.0 fusion.262
  75.5 4.7 convolution_add_fusion.8
  102.0 7.3 fusion.108
  109.3 7.5 convolution_subtract_fusion
  117.6 49.1 %while.94 = (s32[]{:T(128)}, f32[8,128,128]{2,1,0:T(8,128)}, f32[8,128,128]{2,1,0:T(8,128)}, f32[6,8,128,128]{3,2,1,0:T(8,128)}, f32[6]{0:T(128)S(1)}, /*index=5*/f32[6,8,128,128]{3,2,1,0:T(8,128)}, s32[]{:T(128)}, s32[]{:T(128)}) while((s32[]{:T(128)}, f32[8,128,128]{2,1,0:T(8,128)}, f32[8,128,128]{2,1,0:T(8,128)}, ...), condition=%wide.region_6.7_spmd.clone, body=%wide.region_5.6_spmd.clone.sunk | while | flops 403177472 | bytes 7867026 | solution.py:187
  122.5 3.3 convolution_add_fusion.17
  138.8 3.3 convolution_add_fusion.17
  155.2 3.3 convolution_add_fusion.17
  167.6 3.9 copy.499
  173.6 3.7 copy.422
  182.1 5.4 fusion.128
  190.5 3.4 bitcast_subtract_fusion
  193.9 47.6 %all-gather.9.cloned.1.call-done = f32[64,128,128]{2,1,0:T(8,128)} async-done(((f32[8,128,128]{2,1,0:T(8,128)}), f32[64,128,128]{2,1,0:T(8,128)}) %all-gather.9.cloned.1.call-update) | async-done | bytes 4194320 | tf_op jit(solution)/shard_map/all_gather | solution.py:24
  241.5 74.4 %all-gather.11.cloned.1.call-done = f32[64,128,128]{2,1,0:T(8,128)} async-done(((f32[8,128,128]{2,1,0:T(8,128)}), f32[64,128,128]{2,1,0:T(8,128)}) %all-gather.11.cloned.1.call-update) | async-done | bytes 4194320 | tf_op jit(solution)/shard_map/all_gather | solution.py:24
  318.6 50.4 %while.91 = (s32[]{:T(128)}, f32[8,128,128]{2,1,0:T(8,128)S(1)}, f32[6,8,64,128]{3,1,2,0:T(8,128)}, f32[6,8,128,128]{3,2,1,0:T(8,128)}, f32[6,8,128,128]{3,2,1,0...) while((s32[]{:T(128)}, f32[8,128,128]{2,1,0:T(8,128)S(1)}, ...), condition=%wide.region_11.12_spmd, body=%wide.region_10.11_spmd.sunk | while | flops 302579712 | bytes 6033025 | solution.py:163
  374.2 3.8 multiply_convert_fusion.4
  379.4 8.1 fusion.265
  387.5 4.5 fusion.266
  392.0 10.4 multiply_convert_fusion
  402.4 6.6 fusion.267
  409.0 5.9 multiply_reduce_fusion.4
  428.2 46.5 %while.95 = (s32[]{:T(128)}, f32[8,128,128]{2,1,0:T(8,128)}, f32[6,8,128,128]{2,3,1,0:T(8,128)}, f32[6,8,64,128]{3,2,1,0:T(8,128)}, f32[6,8,64,128]{3,2,1,0:T(8,...) while((s32[]{:T(128)}, f32[8,128,128]{2,1,0:T(8,128)}, ...), condition=%wide.region_17.18_spmd.clone, body=%wide.region_16.17_spmd.clone.sunk | while | flops 302383104 | bytes 4196103 | solution.py:205
  474.8 4.6 fusion.174
  482.4 4.8 fusion.214
  487.3 79.0 %all-gather.15.cloned.1.call-done = f32[64,128,128]{2,1,0:T(8,128)} async-done(((f32[8,128,128]{2,1,0:T(8,128)}), f32[64,128,128]{2,1,0:T(8,128)}) %all-gather.15.cloned.1.call-update) | async-done | bytes 4194320 | tf_op jit(solution)/shard_map/all_gather | solution.py:24
  566.3 19.7 %while.92 = (s32[]{:T(128)}, f32[8,128,128]{2,1,0:T(8,128)S(1)}, s32[]{:T(128)}, f32[8,8,128,128]{3,2,1,0:T(8,128)}, f32[8,8,128,128]{3,2,1,0:T(8,128)}, /*index=5*/s32[]{:T(128)}, s32[]{:T(128)}, s32[]{:T(128)}, s32[]{:T(128)}) while((s32[]{:T(128)}, f32[8,128,128]{2,1,0:T(8,128)S(1)}, s32[]{:T(128)}, f32[8,8,128,128]{3,2,1,0:T(8,128)}, ...), condition=%wide.region_19.20_spmd, body=%wide.region_18.19_spmd.sunk | while | flops 201457664 | bytes 3146899 | solution.py:33
  592.9 75.0 %while.93 = (s32[]{:T(128)}, f32[8,128,128]{2,1,0:T(8,128)S(1)}, f32[6,8,64,128]{3,2,1,0:T(8,128)}, f32[6,8,64,128]{3,2,1,0:T(8,128)}, f32[6,8,128,128]{2,3,1,0:...) while((s32[]{:T(128)}, f32[8,128,128]{2,1,0:T(8,128)S(1)}, ...), condition=%wide.region_21.22_spmd, body=%wide.region_20.21_spmd.sunk | while | flops 604241920 | bytes 14684481 | solution.py:163
  667.9 4.7 fusion.268
  672.6 3.4 fusion.116
  681.8 6.6 fusion.121
  688.4 3.8 convolution_add_fusion.7
  741.1 4.8 fusion.113
  748.5 6.2 fusion.269
  757.9 3.8 multiply_reduce_fusion.6
  777.1 4.3 add_bitcast_fusion
  785.1 5.5 fusion.97
  800.1 7.9 add_add_fusion.2
  808.2 7.4 multiply_reduce_fusion.2
  815.6 4.4 multiply_multiply_fusion.3
  828.0 3.3 fusion.210
  831.4 4.6 fusion.206
  836.1 4.5 fusion.203
  840.9 9.4 fusion.283
  850.3 9.3 fusion.284
  859.7 9.3 fusion.168
  871.6 3.4 reshape.451
  876.4 40.6 %reduce-scatter.13.cloned.1.call-done = f32[128,1024]{1,0:T(8,128)} async-done(((f32[1024,1024]{1,0:T(8,128)}), f32[128,1024]{1,0:T(8,128)}) %reduce-scatter.13.cloned.1.call-update) | async-done | bytes 524304 | tf_op jit(solution)/shard_map/reduce_scatter | solution.py:353
  917.0 91.8 %reduce-scatter.15.cloned.1.call-done = f32[128,1024]{1,0:T(8,128)} async-done(((f32[1024,1024]{1,0:T(8,128)}), f32[128,1024]{1,0:T(8,128)}) %reduce-scatter.15.cloned.1.call-update) | async-done | bytes 524304 | tf_op jit(solution)/shard_map/reduce_scatter | solution.py:354
  1008.8 91.5 %reduce-scatter.17.cloned.1.call-done = f32[128,1024]{1,0:T(8,128)} async-done(((f32[1024,1024]{1,0:T(8,128)}), f32[128,1024]{1,0:T(8,128)}) %reduce-scatter.17.cloned.1.call-update) | async-done | bytes 524304 | tf_op jit(solution)/shard_map/reduce_scatter | solution.py:355
  1100.3 196.3 %reduce-scatter.25.cloned.1.call-done = f32[128,2816]{1,0:T(8,128)} async-done(((f32[1024,2816]{1,0:T(8,128)}), f32[128,2816]{1,0:T(8,128)}) %reduce-scatter.25.cloned.1.call-update) | async-done | bytes 1441808 | tf_op jit(solution)/shard_map/reduce_scatter | solution.py:362
  1296.6 195.9 %reduce-scatter.27.cloned.1.call-done = f32[128,2816]{1,0:T(8,128)} async-done(((f32[1024,2816]{1,0:T(8,128)}), f32[128,2816]{1,0:T(8,128)}) %reduce-scatter.27.cloned.1.call-update) | async-done | bytes 1441808 | tf_op jit(solution)/shard_map/reduce_scatter | solution.py:363
  1492.5 195.7 %reduce-scatter.29.cloned.1.call-done = f32[352,1024]{1,0:T(8,128)} async-done(((f32[2816,1024]{1,0:T(8,128)}), f32[352,1024]{1,0:T(8,128)}) %reduce-scatter.29.cloned.1.call-update) | async-done | bytes 1441808 | tf_op jit(solution)/shard_map/reduce_scatter | solution.py:364
  1693.8 6.1 fusion.160
  1705.6 20.2 %all-reduce.15 = (f32[1024]{0:T(1024)S(1)}, f32[128]{0:T(128)S(1)}, f32[1024]{0:T(1024)S(1)}) all-reduce(f32[1024]{0:T(1024)S(1)} %get-tuple-element.793, f32[128]{0:T(128)S(1)} %copy-done.138, f32[1024]{0:T(1024)S(1)} %copy-done.136), channel_id=6, replica_groups=mesh['seq'=8,'doc'=4] {'seq'}, use_global_device_ids=true, to_apply=%region_29.30.clone | all-reduce | flops 2176 | bytes 17408
  1729.3 24.3 %reduce-scatter.31.cloned.1.call-done = f32[128,12]{1,0:T(8,128)} async-done(((f32[1024,12]{1,0:T(8,128)}), f32[128,12]{1,0:T(8,128)}) %reduce-scatter.31.cloned.1.call-update) | async-done | bytes 6160
  1754.7 55.1 %reduce-scatter.21.cloned.1.call-done = f32[128,8]{0,1:T(8,128)} async-done(((f32[1024,8]{0,1:T(8,128)}), f32[128,8]{0,1:T(8,128)}) %reduce-scatter.21.cloned.1.call-update) | async-done | bytes 4112 | tf_op jit(solution)/shard_map/reduce_scatter | solution.py:357
  1809.8 11.6 all-reduce.16
  1821.4 121.7 %all-reduce.20.cloned.1.call-done = (f32[128,1024]{1,0:T(8,128)}, f32[128,1024]{1,0:T(8,128)}, f32[128,1024]{1,0:T(8,128)}, f32[128,1024]{1,0:T(8,128)}, f32[128...) async-done(((f32[128,1024]{1,0:T(8,128)}, f32[128,1024]{1,0:T(8,128)}, f32[128,1024]{1,0:T(8,128)}, f32[128,1024]{1,0:T(8,128)}, ...) | async-done | bytes 6946832 | tf_op jit(solution)/shard_map/psum | solution.py:366
  (707 shorter events, 455.7 us)
Async XLA Ops:
  7.2 234.3 %all-gather.9.cloned.1.call-start = ((), (), s32[]{:S(2)}) async-start(), calls=%async_computation.19 | async-start | bytes 4718592 | tf_op jit(solution)/shard_map/all_gather | solution.py:24
  9.3 12.5 copy-start.97
  15.0 6.1 copy-start.139
  15.0 6.7 copy-start.119
  15.0 6.9 copy-start.132
  16.2 6.8 collective-permute-start
  21.8 58.4 %copy-start.83 = (f32[64,64]{0,1:T(8,128)}, f32[64,64]{0,1:T(8,128)S(1)}, u32[]{:S(2)}) copy-start(f32[64,64]{0,1:T(8,128)S(1)} %fusion.223) | copy-start | bytes 49156
  26.0 6.1 copy-start.4
  80.3 11.5 copy-start.59
  98.4 10.9 copy-start.19
  102.0 7.3 copy-start.22
  117.6 4.8 copy-start.44
  125.8 4.8 copy-start.44
  166.7 4.9 copy-start.145
  166.7 149.2 %all-gather.11.cloned.1.call-start = ((), (), s32[]{:S(2)}) async-start(), calls=%async_computation.20 | async-start | bytes 4718592 | tf_op jit(solution)/shard_map/all_gather | solution.py:24
  167.5 319.8 %all-gather.13.cloned.1.call-start = ((), (), s32[]{:S(2)}) async-start(), calls=%async_computation.21 | async-start | bytes 4718592 | tf_op jit(solution)/shard_map/all_gather | solution.py:24
  182.1 5.4 copy-start.23
  193.9 372.4 %all-gather.15.cloned.1.call-start = ((), (), s32[]{:S(2)}) async-start(), calls=%async_computation.22 | async-start | bytes 4718592 | tf_op jit(solution)/shard_map/all_gather | solution.py:24
  378.0 9.5 slice-start.6
  379.1 35.9 %copy-start.57 = (f32[384,1024]{1,0:T(8,128)}, f32[384,1024]{1,0:T(8,128)S(1)}, u32[]{:S(2)}) copy-start(f32[384,1024]{1,0:T(8,128)S(1)} %get-tuple-element.928) | copy-start | bytes 4718596
  379.3 8.1 copy-start.76
  379.3 8.1 slice-start.7
  402.4 6.6 copy-start.82
  402.4 6.6 copy-start.81
  474.8 401.6 %reduce-scatter.19.cloned.1.call-start = ((), (), s32[]{:S(2)}) async-start(), calls=%async_computation.13 | async-start | bytes 4718592 | tf_op jit(solution)/shard_map/reduce_scatter | solution.py:356
  479.4 397.0 %reduce-scatter.23.cloned.1.call-start = ((), (), s32[]{:S(2)}) async-start(), calls=%async_computation.15 | async-start | bytes 4718592 | tf_op jit(solution)/shard_map/reduce_scatter | solution.py:360
  487.2 429.8 %reduce-scatter.13.cloned.1.call-start = ((), (), s32[]{:S(2)}) async-start(), calls=%async_computation.10 | async-start | bytes 4718592 | tf_op jit(solution)/shard_map/reduce_scatter | solution.py:353
  593.8 5.0 copy-start.147
  606.3 5.0 copy-start.147
  618.7 5.0 copy-start.147
  631.2 5.0 copy-start.147
  643.6 5.0 copy-start.147
  656.0 5.0 copy-start.147
  748.5 6.3 copy-start.21
  785.1 14.8 slice-start.2
  785.1 22.9 %slice-start.4 = ((s8[4718592]{0:T(1024)(128)(4,1)}), s8[4194304]{0:T(1024)(128)(4,1)S(1)}, s32[]{:S(2)}) async-start(s8[4718592]{0:T(1024)(128)(4,1)} %bitcast.527), calls=%async_computation.29 | async-start | bytes 8388608
  791.1 8.9 slice-start.3
  795.1 12.9 slice-start.5
  800.0 8.1 slice-start
  800.0 8.0 slice-start.1
  800.0 8.0 copy-start.33
  800.0 8.0 copy-start.36
  800.0 8.0 copy-start.39
  800.0 8.0 copy-start.121
  800.0 8.0 copy-start.123
  800.0 8.0 copy-start.125
  800.1 8.0 copy-start.127
  808.1 7.5 copy-start.102
  808.1 7.5 copy-start.104
  808.1 7.5 copy-start.106
  808.1 7.5 copy-start.108
  820.0 6.0 collective-permute-start.1
  831.4 177.4 %reduce-scatter.15.cloned.1.call-start = ((), (), s32[]{:S(2)}) async-start(), calls=%async_computation.11 | async-start | bytes 4718592 | tf_op jit(solution)/shard_map/reduce_scatter | solution.py:354
  836.0 264.3 %reduce-scatter.17.cloned.1.call-start = ((), (), s32[]{:S(2)}) async-start(), calls=%async_computation.12 | async-start | bytes 4718592 | tf_op jit(solution)/shard_map/reduce_scatter | solution.py:355
  840.6 456.0 %reduce-scatter.25.cloned.1.call-start = ((), (), s32[]{:S(2)}) async-start(), calls=%async_computation.16 | async-start | bytes 12976128 | tf_op jit(solution)/shard_map/reduce_scatter | solution.py:362
  850.3 642.2 %reduce-scatter.27.cloned.1.call-start = ((), (), s32[]{:S(2)}) async-start(), calls=%async_computation.17 | async-start | bytes 12976128 | tf_op jit(solution)/shard_map/reduce_scatter | solution.py:363
  859.6 828.5 %reduce-scatter.29.cloned.1.call-start = ((), (), s32[]{:S(2)}) async-start(), calls=%async_computation.18 | async-start | bytes 12976128 | tf_op jit(solution)/shard_map/reduce_scatter | solution.py:364
  869.0 884.6 %reduce-scatter.31.cloned.1.call-start = ((), (), s32[]{:S(2)}) async-start(), calls=%async_computation.23 | async-start | bytes 589824
  875.1 934.7 %reduce-scatter.21.cloned.1.call-start = ((), (), s32[]{:S(2)}) async-start(), calls=%async_computation.14 | async-start | bytes 36864 | tf_op jit(solution)/shard_map/reduce_scatter | solution.py:357
  876.1 1067.0 %all-reduce.20.cloned.1.call-start = ((), (), s32[]{:S(2)}) async-start(), calls=%async_computation.24 | async-start | bytes 13893632 | tf_op jit(solution)/shard_map/psum | solution.py:366
  1693.8 6.1 copy-start.133
  1693.8 6.5 copy-start.74
  1693.8 6.5 copy-start.141
  1703.0 23.1 %copy-start.131 = (f32[384]{0:T(512)S(1)}, f32[384]{0:T(512)}, u32[]{:S(2)}) copy-start(f32[384]{0:T(512)} %copy-done.130) | copy-start | bytes 4612
  (129 other events, 367.2 us)
Sparse Core Ops, SparseCore 0:
  166.8 74.6 all-gather.8
  244.2 71.6 all-gather.10
  318.6 71.6 all-gather.12
  474.9 91.3 all-gather.14
  569.8 86.1 reduce-scatter.18
  659.9 87.6 reduce-scatter.22
  831.5 85.4 reduce-scatter.12
  921.1 87.6 reduce-scatter.14
  1012.4 87.8 reduce-scatter.16
  1104.2 192.4 reduce-scatter.24
  1300.6 191.7 reduce-scatter.26
  1496.4 191.7 reduce-scatter.28
  1692.5 61.0 reduce-scatter.30
  1757.2 52.5 reduce-scatter.20
  1812.5 130.5 all-reduce.19
where the time goes:
time: 1970 us; the launch traced here: 1960 us
  waiting for transfers between devices  1220 us (62%)
  matrix products  474 us (24%)
  local copies, waits for them, and re-layouts  155 us (8%)
  other arithmetic  56.4 us (3%)
  blocking collectives  31.8 us (2%)
    dot_general x121, matrix products, linear_map_result(): return jnp.einsum(form, left, right, precision=HIGH)  363 us
    all_gather x4, waiting for transfers between devices, carried_in(): gathered = jax.tree.map(lambda a: lax.all_gather(a, axis), part)  201 us
    reduce_scatter x1, waiting for transfers between devices, local(): lax.psum_scatter(grad_gate_w, 'seq', scatter_dimension=0, tiled=True)  196 us
    reduce_scatter x1, waiting for transfers between devices, local(): lax.psum_scatter(grad_up_w, 'seq', scatter_dimension=0, tiled=True)  196 us
    reduce_scatter x1, waiting for transfers between devices, local(): lax.psum_scatter(grad_down_w, 'seq', scatter_dimension=0, tiled=True)  196 us
    psum x1, waiting for transfers between devices, local(): lax.psum((parts[0], parts[1], parts[2], parts[3], parts[4], parts[5], par...  122 us
    reduce_scatter x1, waiting for transfers between devices, local(): lax.psum_scatter(grad_key_w, 'seq', scatter_dimension=0, tiled=True)  91.8 us
    reduce_scatter x1, waiting for transfers between devices, local(): lax.psum_scatter(grad_value_w, 'seq', scatter_dimension=0, tiled=True)  91.5 us
  transfers between devices with their start and end apart: 17, of which 13 were waited for; matrix products, arithmetic and copies ran while one was open for 26% of the time, Pallas kernels for 0%

commit v1 on v0

v1 whole, which is shorter than its diff:
```python
import jax
import jax.numpy as jnp
from jax import lax
from jax.experimental import pallas as pl
from jax.experimental.pallas import tpu as pltpu
from jax.sharding import PartitionSpec as P

CK = 64


EPS = 1e-05
KEY_EPS = 1e-06
HIGH = lax.Precision.HIGHEST


def doc_info(lengths, first, count):
    padded = (lengths + CK - 1) // CK * CK
    ends = jnp.cumsum(padded)
    starts = ends - padded
    place = first + jnp.arange(count, dtype=jnp.int32)
    inside = ((place[:, None] >= starts[None, :]) & (place[:, None] < ends[None, :])).astype(
        jnp.int32
    )
    position = place - jnp.sum(inside * starts[None, :], 1)
    length = jnp.sum(inside * lengths[None, :], 1)
    live = (position < length).astype(jnp.float32)
    return (position, live)


SPAN = CK
LANES = 128
LOW = jnp.bfloat16
NN = (((1,), (0,)), ((), ()))
NT = (((1,), (1,)), ((), ()))
TN = (((0,), (0,)), ((), ()))


def params(mib=48):
    return pltpu.CompilerParams(vmem_limit_bytes=mib * 2**20)


def cost(flops, moved):
    return pl.CostEstimate(flops=int(flops), bytes_accessed=int(moved), transcendentals=0)


def mxu(left, right, dims):
    return lax.dot_general(left, right, dims, preferred_element_type=jnp.float32)


def halves(value):
    high = value.astype(LOW)
    return high, (value - high.astype(jnp.float32)).astype(LOW)


def fold(value):
    half = value.shape[1] // 2
    return value[:, :half] + value[:, half:]


def product(left, right):
    left_high, left_low = halves(left)
    right_high, right_low = halves(right)
    both = jnp.concatenate([left_high, left_low], 1)
    if right.shape[1] <= LANES:
        wide = jnp.concatenate([right_high, right_low], 1)
        return fold(mxu(both, jnp.concatenate([wide, wide], 0), NN))
    return mxu(both, jnp.concatenate([right_high, right_high], 0), NN) + mxu(
        left_high, right_low, NN
    )


def product_t(left, right):
    left_high, left_low = halves(left)
    right_high, right_low = halves(right)
    both = jnp.concatenate([left_high, left_low], 1)
    if right.shape[0] <= LANES:
        rows = jnp.concatenate(
            [
                jnp.concatenate([right_high, right_high], 1),
                jnp.concatenate([right_low, right_low], 1),
            ],
            0,
        )
        return fold(mxu(both, rows, NT))
    return mxu(both, jnp.concatenate([right_high, right_high], 1), NT) + mxu(
        left_high, right_low, NT
    )


def t_product(left, right):
    left_high, left_low = halves(left)
    right_high, right_low = halves(right)
    both = jnp.concatenate([left_high, left_low], 0)
    if right.shape[1] <= LANES:
        wide = jnp.concatenate([right_high, right_low], 1)
        return fold(mxu(both, jnp.concatenate([wide, wide], 0), TN))
    return mxu(both, jnp.concatenate([right_high, right_high], 0), TN) + mxu(
        left_high, right_low, TN
    )


def head(value, h):
    return value[:, h * LANES : (h + 1) * LANES]


def pair(value, p):
    return jnp.concatenate([head(value, 2 * p), head(value, 2 * p + 1)], 0)


def pair_column(value, p):
    return jnp.concatenate([value[:, 2 * p : 2 * p + 1], value[:, 2 * p + 1 : 2 * p + 2]], 0)


def masks(rows):
    i = lax.broadcasted_iota(jnp.int32, (rows, rows), 0)
    j = lax.broadcasted_iota(jnp.int32, (rows, rows), 1)
    same = (i >= SPAN) == (j >= SPAN)
    strict = jnp.where(same & (j < i), 1.0, 0.0)
    inclusive = jnp.where(same & (j <= i), 1.0, 0.0)
    upper = jnp.where(same & (j >= i), 1.0, 0.0)
    return strict, inclusive, upper, jnp.where(i == j, 1.0, 0.0)


def inverse(strict_part, identity):
    rows = strict_part.shape[0]
    result = identity - strict_part
    power = product(strict_part, strict_part)
    for level in range(SPAN.bit_length() - 3):
        both = product(jnp.concatenate([result, power], 0), power)
        result = result + both[:rows]
        power = both[rows:]
    return result + product(result, power)


def sigmoid(value):
    return 1.0 / (1.0 + jnp.exp(-value))


HALO = 16


def project_kernel(
    tokens, halo, gain, position, live, query_w, key_w, value_w, gate_w, beta_w, conv,
    normed_out, pre_out, feature_out, gate_out, beta_pre_out, beta_out, normed,
):
    count = tokens.shape[0]

    @pl.when(pl.program_id(0) == 0)
    def _():
        def norm(rows):
            return (
                rows * lax.rsqrt(jnp.mean(rows * rows, -1, keepdims=True) + EPS) * gain[...]
            ).astype(LOW)

        normed[:HALO, :] = norm(halo[...])
        rounded = norm(tokens[...].astype(jnp.float32))
        normed[HALO:, :] = rounded
        normed_out[...] = rounded.astype(jnp.float32).T
        beta_pre = mxu(rounded, beta_w[...], NN)
        beta_pre_out[...] = beta_pre
        beta_out[...] = sigmoid(beta_pre) * live[...]

    gate_out[...] = mxu(normed[HALO:, :], gate_w[...], NN)
    valid = [
        jnp.where(position[...] >= conv.shape[1] - 1 - tap, 1.0, 0.0)
        for tap in range(conv.shape[1])
    ]
    for which, weight in enumerate((query_w, key_w, value_w)):
        pre_out[which] = mxu(normed[...], weight[...], NN)
        for part in range(pre_out.shape[2] // LANES):
            lanes = slice(part * LANES, (part + 1) * LANES)
            total = conv_total(pre_out, which, HALO, count, lanes, conv, valid)
            value = total * sigmoid(total)
            if which < 2:
                value = value * lax.rsqrt(jnp.sum(value * value, -1, keepdims=True) + KEY_EPS)
            if which == 1:
                value = value * live[...]
            feature_out[which, :, lanes] = value


def conv_total(pre, which, first, count, lanes, conv, valid):
    taps = conv.shape[1]
    total = None
    for tap in range(taps):
        start = first - (taps - 1) + tap
        term = conv[which, tap : tap + 1, lanes] * pre[which, start : start + count, lanes] * valid[tap]
        total = term if total is None else total + term
    return total


def project(tokens, halo, gain, position, live, query_w, key_w, value_w, gate_w, beta_w, conv):
    count, width = tokens.shape
    heads = beta_w.shape[1]
    block = 2 * LANES
    whole = lambda shape: pl.BlockSpec(shape, lambda j: (0,) * len(shape))
    weight = pl.BlockSpec((width, block), lambda j: (0, j))
    f32 = lambda shape: jax.ShapeDtypeStruct(shape, jnp.float32)
    return pl.pallas_call(
        project_kernel,
        grid=(width // block,),
        in_specs=[
            whole((count, width)), whole((HALO, width)), whole((1, width)), whole((count, 1)),
            whole((count, 1)), weight, weight, weight, weight, whole((width, heads)),
            pl.BlockSpec((3, conv.shape[1], block), lambda j: (0, 0, j)),
        ],
        out_specs=[
            whole((width, count)),
            pl.BlockSpec((3, HALO + count, block), lambda j: (0, 0, j)),
            pl.BlockSpec((3, count, block), lambda j: (0, 0, j)),
            pl.BlockSpec((count, block), lambda j: (0, j)),
            whole((count, heads)), whole((count, heads)),
        ],
        out_shape=[
            f32((width, count)), f32((3, HALO + count, width)), f32((3, count, width)),
            f32((count, width)), f32((count, heads)), f32((count, heads)),
        ],
        scratch_shapes=[pltpu.VMEM((HALO + count, width), LOW)],
        compiler_params=params(),
        cost_estimate=cost(8 * count * width * width, 8 * width * width + 40 * count * width),
        name="project",
    )(tokens, halo, gain, position, live, query_w, key_w, value_w, gate_w, beta_w, conv)


def prepare_kernel(keep, features, beta, solved_out, inverse_out, attend_out, state):
    span = pl.program_id(0)
    heads = state.shape[0]
    size = state.shape[1]
    strict, inclusive, upper, identity = masks(2 * SPAN)

    @pl.when(span == 0)
    def _():
        i = lax.broadcasted_iota(jnp.int32, (size, 2 * size), 0)
        j = lax.broadcasted_iota(jnp.int32, (size, 2 * size), 1)
        for h in range(heads):
            state[h] = jnp.where(j == i + size, 1.0, 0.0)

    query, key, value = features[0], features[1], features[2]
    betas = beta[...]
    flag = keep[span]
    for p in range(heads // 2):
        q, k, v, b = pair(query, p), pair(key, p), pair(value, p), pair_column(betas, p)
        scores = product_t(jnp.concatenate([k, q], 0), k)
        solved = inverse(b * scores[: 2 * SPAN] * strict, identity)
        both = product(solved, jnp.concatenate([b * k, b * v], 1))
        inverse_out[0, p] = solved
        attend_out[0, p] = scores[2 * SPAN :] * inclusive
        for i in range(2):
            h = 2 * p + i
            erase = both[i * SPAN : (i + 1) * SPAN, :size]
            update = both[i * SPAN : (i + 1) * SPAN, size:]
            solved_out[0, :, h * size : (h + 1) * size] = erase
            solved_out[1, :, h * size : (h + 1) * size] = update
            start = state[h] * flag
            new = jnp.concatenate([update, jnp.zeros_like(update)], 1) - product(erase, start)
            state[h] = start + t_product(head(key, h), new)


def prepare(keep, features, beta):
    _, count, width = features.shape
    heads = beta.shape[1]
    size = width // heads
    spans = count // SPAN
    f32 = lambda shape: jax.ShapeDtypeStruct(shape, jnp.float32)
    matrix = pl.BlockSpec((1, heads // 2, 2 * SPAN, 2 * SPAN), lambda c: (c, 0, 0, 0))
    return pl.pallas_call(
        prepare_kernel,
        grid=(spans,),
        in_specs=[
            pl.BlockSpec(memory_space=pltpu.SMEM),
            pl.BlockSpec((3, SPAN, width), lambda c: (0, c, 0)),
            pl.BlockSpec((SPAN, heads), lambda c: (c, 0)),
        ],
        out_specs=[
            pl.BlockSpec((2, SPAN, width), lambda c: (0, c, 0)), matrix, matrix,
            pl.BlockSpec((heads, size, 2 * size), lambda c: (0, 0, 0)),
        ],
        out_shape=[
            f32((2, count, width)), f32((spans, heads // 2, 2 * SPAN, 2 * SPAN)),
            f32((spans, heads // 2, 2 * SPAN, 2 * SPAN)), f32((heads, size, 2 * size)),
        ],
        compiler_params=params(),
        cost_estimate=cost(40 * count * width * size * 4, 60 * count * width),
        name="prepare",
    )(keep, features, beta)


def mix_kernel(
    keep, features, solved, attend, gate, gain, state_in, starts_out, new_out, mixed_out, normed_out,
    state,
):
    span = pl.program_id(0)
    heads = state.shape[0]

    @pl.when(span == 0)
    def _():
        state[...] = state_in[...]

    query, key = features[0], features[1]
    erase, update = solved[0], solved[1]
    flag = keep[span]
    for p in range(heads // 2):
        reads, news = [], []
        for h in (2 * p, 2 * p + 1):
            start = state[h] * flag
            starts_out[0, h] = start
            both = product(jnp.concatenate([head(erase, h), head(query, h)], 0), start)
            new = head(update, h) - both[:SPAN]
            state[h] = start + t_product(head(key, h), new)
            new_out[:, h * LANES : (h + 1) * LANES] = new
            reads.append(both[SPAN:])
            news.append(new)
        mixed = jnp.concatenate(reads, 0) + product(attend[0, p], jnp.concatenate(news, 0))
        for i in range(2):
            lanes = slice((2 * p + i) * LANES, (2 * p + i + 1) * LANES)
            rows = mixed[i * SPAN : (i + 1) * SPAN]
            mixed_out[:, lanes] = rows
            shaped = rows * lax.rsqrt(jnp.mean(rows * rows, -1, keepdims=True) + EPS) * gain[...]
            gates = gate[:, lanes]
            normed = (shaped * (gates * sigmoid(gates))).astype(LOW)
            normed_out[:, lanes] = normed


def mix(keep, features, solved, attend, gate, gain, state_in):
    _, count, width = features.shape
    heads, size, _ = state_in.shape
    spans = count // SPAN
    f32 = lambda shape: jax.ShapeDtypeStruct(shape, jnp.float32)
    rows = pl.BlockSpec((SPAN, width), lambda c: (c, 0))
    pairs = pl.BlockSpec((2, SPAN, width), lambda c: (0, c, 0))
    return pl.pallas_call(
        mix_kernel,
        grid=(spans,),
        in_specs=[
            pl.BlockSpec(memory_space=pltpu.SMEM), pairs, pairs,
            pl.BlockSpec((1, heads // 2, 2 * SPAN, 2 * SPAN), lambda c: (c, 0, 0, 0)),
            rows, pl.BlockSpec((1, size), lambda c: (0, 0)),
            pl.BlockSpec((heads, size, size), lambda c: (0, 0, 0)),
        ],
        out_specs=[
            pl.BlockSpec((1, heads, size, size), lambda c: (c, 0, 0, 0)), rows, rows, rows,
        ],
        out_shape=[
            f32((spans, heads, size, size)), f32((count, width)), f32((count, width)),
            jax.ShapeDtypeStruct((count, width), LOW),
        ],
        scratch_shapes=[pltpu.VMEM((heads, size, size), jnp.float32)],
        compiler_params=params(),
        cost_estimate=cost(8 * count * width * size * 4, 40 * count * width),
        name="mix",
    )(keep, features, solved, attend, gate, gain, state_in)


def feed_kernel(
    core, tokens, normed_head, grad_top, second_gain, out_w, gate_w, up_w, down_w,
    block_out, normed_out, inner_out, kept_out, sent_out, grad_hidden_out, branch_out, grad_head_out,
    gain_grad_out, hidden, normed, total, grad_total,
):
    step = pl.program_id(0)

    @pl.when(step == 0)
    def _():
        state = tokens[...].astype(jnp.float32) + mxu(normed_head[...], out_w[...], NN)
        hidden[...] = state
        rounded = (
            state * lax.rsqrt(jnp.mean(state * state, -1, keepdims=True) + EPS) * second_gain[...]
        ).astype(LOW)
        normed[...] = rounded
        normed_out[...] = rounded.astype(jnp.float32).T

    gate = mxu(normed[...], gate_w[...], NN)
    up = mxu(normed[...], up_w[...], NN)
    grad_inner = mxu(grad_top[...], down_w[...], NT)
    sigma = sigmoid(gate)
    inner = (gate * sigma * up).astype(LOW)
    inner_out[...] = inner.astype(jnp.float32).T
    grad_gate = (grad_inner * up * sigma * (1.0 + gate * (1.0 - sigma))).astype(LOW)
    grad_up = (grad_inner * gate * sigma).astype(LOW)
    first = core[0] == 0
    wide_gate, wide_up = grad_gate.astype(jnp.float32), grad_up.astype(jnp.float32)
    kept_out[...] = jnp.where(first, wide_gate, wide_up).astype(LOW)
    sent_out[...] = jnp.where(first, wide_up, wide_gate)
    out_term = mxu(inner, down_w[...], NN)
    grad_term = mxu(grad_gate, gate_w[...], NT) + mxu(grad_up, up_w[...], NT)

    @pl.when(step == 0)
    def _():
        total[...] = out_term
        grad_total[...] = grad_term

    @pl.when(step > 0)
    def _():
        total[...] += out_term
        grad_total[...] += grad_term

    @pl.when(step == pl.num_programs(0) - 1)
    def _():
        state = hidden[...]
        block_out[...] = (state + total[...]).astype(LOW)
        part, gain_part = norm_back(state, second_gain[...], grad_total[...])
        gain_grad_out[...] = gain_part
        grad_hidden = grad_top[...].astype(jnp.float32) + part
        grad_hidden_out[...] = grad_hidden
        branch = grad_hidden.astype(LOW)
        branch_out[...] = branch.astype(jnp.float32)
        grad_head_out[...] = mxu(branch, out_w[...], NT)


def norm_back(value, gain, grad):
    scale = lax.rsqrt(jnp.mean(value * value, -1, keepdims=True) + EPS)
    unit = value * scale
    gain_grad = jnp.sum(grad * unit, 0, keepdims=True)
    inward = grad * gain
    return scale * (inward - unit * jnp.mean(inward * unit, -1, keepdims=True)), gain_grad


def feed(core, tokens, normed_head, grad_top, second_gain, out_w, gate_w, up_w, down_w):
    count, width = tokens.shape
    hidden = gate_w.shape[1]
    block = 2 * LANES
    whole = lambda shape: pl.BlockSpec(shape, lambda j: (0,) * len(shape))
    f32 = lambda shape: jax.ShapeDtypeStruct(shape, jnp.float32)
    low = lambda shape: jax.ShapeDtypeStruct(shape, LOW)
    rows = whole((count, width))
    columns = pl.BlockSpec((count, block), lambda j: (0, j))
    return pl.pallas_call(
        feed_kernel,
        grid=(hidden // block,),
        in_specs=[
            pl.BlockSpec(memory_space=pltpu.SMEM), rows, rows, rows, whole((1, width)),
            whole((width, width)), pl.BlockSpec((width, block), lambda j: (0, j)),
            pl.BlockSpec((width, block), lambda j: (0, j)),
            pl.BlockSpec((block, width), lambda j: (j, 0)),
        ],
        out_specs=[
            rows, whole((width, count)), pl.BlockSpec((block, count), lambda j: (j, 0)), columns,
            columns, rows, rows, rows, whole((1, width)),
        ],
        out_shape=[
            low((count, width)), f32((width, count)), f32((hidden, count)), low((count, hidden)),
            f32((count, hidden)), f32((count, width)), f32((count, width)), f32((count, width)),
            f32((1, width)),
        ],
        scratch_shapes=[
            pltpu.VMEM((count, width), jnp.float32), pltpu.VMEM((count, width), LOW),
            pltpu.VMEM((count, width), jnp.float32), pltpu.VMEM((count, width), jnp.float32),
        ],
        compiler_params=params(),
        cost_estimate=cost(
            12 * count * width * hidden + 4 * count * width * width,
            6 * width * hidden + 10 * count * hidden + 30 * count * width,
        ),
        name="feed",
    )(core, tokens, normed_head, grad_top, second_gain, out_w, gate_w, up_w, down_w)


def gather_kernel(
    keep, grad_head, mixed, gate, gain, features, solved, grad_mixed_out, grad_gate_out, gain_out,
    state,
):
    step = pl.program_id(0)
    span = pl.num_programs(0) - 1 - step
    heads = state.shape[0]
    strict, inclusive, upper, identity = masks(2 * SPAN)

    @pl.when(step == 0)
    def _():
        state[...] = jnp.zeros_like(state)
        gain_out[...] = jnp.zeros_like(gain_out)

    query, key = features[0], features[1]
    erase = solved[0]
    flag = keep[span]
    gain_total = jnp.zeros_like(gain_out[...])
    for p in range(heads // 2):
        grads = []
        for h in (2 * p, 2 * p + 1):
            lanes = slice(h * LANES, (h + 1) * LANES)
            gates = gate[:, lanes]
            sigma = sigmoid(gates)
            rows = mixed[:, lanes]
            grad = grad_head[:, lanes]
            scale = lax.rsqrt(jnp.mean(rows * rows, -1, keepdims=True) + EPS)
            unit = rows * scale
            grad_gate = grad * unit * gain[...] * sigma * (1.0 + gates * (1.0 - sigma))
            grad_gate_out[:, lanes] = grad_gate.astype(LOW).astype(jnp.float32)
            shaped = grad * gates * sigma
            gain_total = gain_total + jnp.sum(shaped * unit, 0, keepdims=True)
            inward = shaped * gain[...]
            grad_rows = scale * (inward - unit * jnp.mean(inward * unit, -1, keepdims=True))
            grad_mixed_out[:, lanes] = grad_rows
            grads.append(grad_rows)
        q, k = pair(query, p), pair(key, p)
        passed = product(product_t(k, q) * upper, jnp.concatenate(grads, 0))
        for i in range(2):
            h = 2 * p + i
            end = state[h]
            grad_new = passed[i * SPAN : (i + 1) * SPAN] + product(head(key, h), end)
            state[h] = flag * (
                end
                + t_product(
                    jnp.concatenate([head(query, h), -head(erase, h)], 0),
                    jnp.concatenate([grads[i], grad_new], 0),
                )
            )
    gain_out[...] += gain_total


def gather_states(keep, grad_head, mixed, gate, gain, features, solved, heads):
    _, count, width = features.shape
    size = width // heads
    spans = count // SPAN
    f32 = lambda shape: jax.ShapeDtypeStruct(shape, jnp.float32)
    rows = pl.BlockSpec((SPAN, width), lambda c: (spans - 1 - c, 0))
    pairs = pl.BlockSpec((2, SPAN, width), lambda c: (0, spans - 1 - c, 0))
    one = pl.BlockSpec((1, SPAN, width), lambda c: (0, spans - 1 - c, 0))
    return pl.pallas_call(
        gather_kernel,
        grid=(spans,),
        in_specs=[
            pl.BlockSpec(memory_space=pltpu.SMEM), rows, rows, rows,
            pl.BlockSpec((1, size), lambda c: (0, 0)), pairs, one,
        ],
        out_specs=[
            rows, rows, pl.BlockSpec((1, size), lambda c: (0, 0)),
            pl.BlockSpec((heads, size, size), lambda c: (0, 0, 0)),
        ],
        out_shape=[
            f32((count, width)), f32((count, width)), f32((1, size)), f32((heads, size, size)),
        ],
        compiler_params=params(),
        cost_estimate=cost(8 * count * width * size * 4, 32 * count * width),
        name="gather_states",
    )(keep, grad_head, mixed, gate, gain, features, solved)


def back_kernel(
    keep, features, beta, beta_pre, solved, inverses, starts, news, grad_mixed, state_in, pre, conv,
    position, live, grad_pre_out, borrowed_out, conv_out, grad_beta_out, state, later,
):
    step = pl.program_id(0)
    span = pl.num_programs(0) - 1 - step
    heads = state.shape[0]
    taps = conv.shape[1]
    strict, inclusive, upper, identity = masks(2 * SPAN)

    @pl.when(step == 0)
    def _():
        state[...] = state_in[...]
        conv_out[...] = jnp.zeros_like(conv_out)
        later[...] = jnp.zeros_like(later)

    @pl.when(step > 0)
    def _():
        later[:, 8 + SPAN :, :] = later[:, 8:16, :]

    query, key, value = features[0], features[1], features[2]
    erase, update = solved[0], solved[1]
    betas = beta[...]
    flag = keep[span]
    base = pl.multiple_of(span * SPAN, SPAN)
    places = position[pl.ds(base, SPAN + 16), :]
    lives = live[pl.ds(base, SPAN), :]
    valid = [jnp.where(places >= taps - 1 - tap, 1.0, 0.0) for tap in range(taps)]
    beta_columns = []
    for p in range(heads // 2):
        q, k, v, b = pair(query, p), pair(key, p), pair(value, p), pair_column(betas, p)
        grad_out = pair(grad_mixed, p)
        new = pair(news, p)
        scores = product_t(k, jnp.concatenate([k, q], 0))
        passed = product(scores[:, 2 * SPAN :] * upper, grad_out)
        grad_query, grad_key, grad_new, grad_erase = [], [], [], []
        for i in range(2):
            h = 2 * p + i
            rows = slice(i * SPAN, (i + 1) * SPAN)
            end = state[h]
            grad_new_h = passed[rows] + product(k[rows], end)
            both = product_t(jnp.concatenate([grad_out[rows], grad_new_h], 0), starts[0, h])
            grad_query.append(both[:SPAN])
            grad_erase.append(-both[SPAN:])
            grad_key.append(product_t(new[rows], end))
            grad_new.append(grad_new_h)
            state[h] = flag * (
                end
                + t_product(
                    jnp.concatenate([q[rows], -head(erase, h)], 0),
                    jnp.concatenate([grad_out[rows], grad_new_h], 0),
                )
            )
        grad_new = jnp.concatenate(grad_new, 0)
        grad_erase = jnp.concatenate(grad_erase, 0)
        grad_attend = product_t(grad_out, new) * inclusive
        grad_q = jnp.concatenate(grad_query, 0) + product(grad_attend, k)
        grad_k = jnp.concatenate(grad_key, 0) + product(grad_attend.T, q)
        turned = product(inverses[0, p].T, jnp.concatenate([grad_new, grad_erase], 1))
        grad_bv, grad_bk = turned[:, :LANES], turned[:, LANES:]
        grad_lower = -strict * (
            product_t(grad_bv, pair(update, p)) + product_t(grad_bk, pair(erase, p))
        )
        grad_b = (
            jnp.sum(grad_lower * scores[:, : 2 * SPAN], -1, keepdims=True)
            + jnp.sum(grad_bv * v, -1, keepdims=True)
            + jnp.sum(grad_bk * k, -1, keepdims=True)
        )
        inner = b * grad_lower
        grad_k = grad_k + product(inner + inner.T, k) + b * grad_bk
        grad_v = b * grad_bv
        beta_columns += [grad_b[:SPAN], grad_b[SPAN:]]
        for i in range(2):
            h = 2 * p + i
            rows = slice(i * SPAN, (i + 1) * SPAN)
            lanes = slice(h * LANES, (h + 1) * LANES)
            for which, grad in enumerate((grad_q[rows], grad_k[rows] * lives, grad_v[rows])):
                window = pre[which, pl.ds(base + HALO - 8, SPAN + 8), lanes]
                shifted = [window[8 - (taps - 1) + tap :][:SPAN] for tap in range(taps)]
                total = None
                for tap in range(taps):
                    term = conv[which, tap : tap + 1, lanes] * shifted[tap] * valid[tap][8 : 8 + SPAN]
                    total = term if total is None else total + term
                sigma = sigmoid(total)
                if which < 2:
                    act = total * sigma
                    scale = lax.rsqrt(jnp.sum(act * act, -1, keepdims=True) + KEY_EPS)
                    unit = act * scale
                    grad = scale * (grad - unit * jnp.sum(grad * unit, -1, keepdims=True))
                grad = grad * sigma * (1.0 + total * (1.0 - sigma))
                for tap in range(taps):
                    conv_out[which, tap : tap + 1, lanes] += jnp.sum(
                        grad * valid[tap][8 : 8 + SPAN] * shifted[tap], 0, keepdims=True
                    )
                later[which, 8 : 8 + SPAN, lanes] = grad
                result = None
                for tap in range(taps):
                    ahead = 8 + taps - 1 - tap
                    term = (
                        conv[which, tap : tap + 1, lanes]
                        * later[which, ahead : ahead + SPAN, lanes]
                        * valid[tap][ahead : ahead + SPAN]
                    )
                    result = term if result is None else result + term
                grad_pre_out[which, :, lanes] = result
    columns = lax.broadcasted_iota(jnp.int32, (SPAN, heads), 1)
    grad_beta = jnp.zeros((SPAN, heads), jnp.float32)
    for h in range(heads):
        grad_beta = jnp.where(columns == h, beta_columns[h], grad_beta)
    sigma = sigmoid(beta_pre[...])
    grad_beta_out[...] = (
        (grad_beta * lives * sigma * (1.0 - sigma)).astype(LOW).astype(jnp.float32)
    )

    @pl.when(span == 0)
    def _():
        for which in range(3):
            result = None
            for tap in range(taps):
                ahead = taps - 1 - tap
                term = (
                    conv[which, tap : tap + 1, :]
                    * later[which, ahead : ahead + 8, :]
                    * valid[tap][ahead : ahead + 8]
                )
                result = term if result is None else result + term
            borrowed_out[which] = result


def back(
    keep, features, beta, beta_pre, solved, inverses, starts, news, grad_mixed, state_in, pre, conv,
    position, live,
):
    _, count, width = features.shape
    heads, size, _ = state_in.shape
    spans = count // SPAN
    taps = conv.shape[1]
    f32 = lambda shape: jax.ShapeDtypeStruct(shape, jnp.float32)
    whole = lambda shape: pl.BlockSpec(shape, lambda c: (0,) * len(shape))
    rows = pl.BlockSpec((SPAN, width), lambda c: (spans - 1 - c, 0))
    triple = pl.BlockSpec((3, SPAN, width), lambda c: (0, spans - 1 - c, 0))
    column = pl.BlockSpec((SPAN, heads), lambda c: (spans - 1 - c, 0))
    position = jnp.pad(position, ((8, 8), (0, 0)))
    return pl.pallas_call(
        back_kernel,
        grid=(spans,),
        in_specs=[
            pl.BlockSpec(memory_space=pltpu.SMEM), triple, column, column,
            pl.BlockSpec((2, SPAN, width), lambda c: (0, spans - 1 - c, 0)),
            pl.BlockSpec((1, heads // 2, 2 * SPAN, 2 * SPAN), lambda c: (spans - 1 - c, 0, 0, 0)),
            pl.BlockSpec((1, heads, size, size), lambda c: (spans - 1 - c, 0, 0, 0)),
            rows, rows, whole((heads, size, size)), whole(pre.shape), whole(conv.shape),
            whole(position.shape), whole(live.shape),
        ],
        out_specs=[triple, whole((3, 8, width)), whole((3, taps, width)), column],
        out_shape=[
            f32((3, count, width)), f32((3, 8, width)), f32((3, taps, width)), f32((count, heads)),
        ],
        scratch_shapes=[
            pltpu.VMEM((heads, size, size), jnp.float32),
            pltpu.VMEM((3, SPAN + 16, width), jnp.float32),
        ],
        compiler_params=params(),
        cost_estimate=cost(30 * count * width * size * 4, 60 * count * width),
        name="back",
    )(
        keep, features, beta, beta_pre, solved, inverses, starts, news, grad_mixed, state_in, pre,
        conv, position, live,
    )


def enter_kernel(
    tokens, gain, grad_hidden, grads, grad_gate, grad_beta, query_w, key_w, value_w, gate_w, beta_w,
    input_grad_out, gain_out, total,
):
    step = pl.program_id(0)
    term = mxu(grad_gate[...].astype(LOW), gate_w[...], NT)
    for which, weight in enumerate((query_w, key_w, value_w)):
        term = term + mxu(grads[which], weight[...], NT)

    @pl.when(step == 0)
    def _():
        total[...] = term + mxu(grad_beta[...].astype(LOW), beta_w[...], NT)

    @pl.when(step > 0)
    def _():
        total[...] += term

    @pl.when(step == pl.num_programs(0) - 1)
    def _():
        part, gain_part = norm_back(tokens[...].astype(jnp.float32), gain[...], total[...])
        gain_out[...] = gain_part
        input_grad_out[...] = (grad_hidden[...] + part).astype(LOW)


def enter(
    tokens, gain, grad_hidden, grads, grad_gate, grad_beta, query_w, key_w, value_w, gate_w, beta_w
):
    count, width = tokens.shape
    heads = beta_w.shape[1]
    block = 2 * LANES
    whole = lambda shape: pl.BlockSpec(shape, lambda j: (0,) * len(shape))
    weight = pl.BlockSpec((width, block), lambda j: (0, j))
    return pl.pallas_call(
        enter_kernel,
        grid=(width // block,),
        in_specs=[
            whole((count, width)), whole((1, width)), whole((count, width)),
            pl.BlockSpec((3, count, block), lambda j: (0, 0, j)),
            pl.BlockSpec((count, block), lambda j: (0, j)), whole((count, heads)),
            weight, weight, weight, weight, whole((width, heads)),
        ],
        out_specs=[whole((count, width)), whole((1, width))],
        out_shape=[
            jax.ShapeDtypeStruct((count, width), LOW), jax.ShapeDtypeStruct((1, width), jnp.float32),
        ],
        scratch_shapes=[pltpu.VMEM((count, width), jnp.float32)],
        compiler_params=params(),
        cost_estimate=cost(8 * count * width * width, 8 * width * width + 20 * count * width),
        name="enter",
    )(
        tokens, gain, grad_hidden, grads, grad_gate, grad_beta, query_w, key_w, value_w, gate_w,
        beta_w,
    )


def passed_along(value, axis, by):
    devices = lax.axis_size(axis)
    pairs = [(i, i + by) for i in range(devices) if 0 <= i + by < devices]
    return lax.ppermute(value, axis, pairs)


def tuned():
    return (lax.axis_size("seq"), lax.axis_size("doc")) == (8, 4)


HOPS = {"core": ("doc", 1), "y": ("doc", 2), "x": ("seq", 1), "near": ("seq", 2), "far": ("seq", 4)}


def hop(value, way):
    axis, bit = HOPS[way]
    return lax.ppermute(value, axis, [(i, i ^ bit) for i in range(lax.axis_size(axis))])


def side(way):
    axis, bit = HOPS[way]
    return lax.axis_index(axis) // bit % 2


def apply_kernel(maps, state, out, *, turned):
    size = maps.shape[1]
    for h in range(maps.shape[0]):
        matrix = maps[h, :, size:]
        moved = (t_product if turned else product)(matrix, state[h])
        if state.shape[2] == size:
            out[h] = moved + maps[h, :, :size]
        else:
            out[h] = moved + jnp.concatenate([maps[h, :, :size], jnp.zeros_like(matrix)], 1)


def apply_map(maps, state, turned=False):
    return pl.pallas_call(
        lambda *refs: apply_kernel(*refs, turned=turned),
        out_shape=jax.ShapeDtypeStruct(state.shape, jnp.float32),
        compiler_params=params(),
        cost_estimate=cost(2 * maps.size * state.shape[2], 4 * (maps.size + 2 * state.size)),
        name="apply_map",
    )(maps, state)


def carried_forward(maps):
    heads, size, _ = maps.shape
    if not tuned():
        gathered = lax.all_gather(maps, "seq")

        def one(lap, state):
            return apply_map(lax.dynamic_index_in_dim(gathered, lap, 0, False), state)

        zeros = jnp.zeros((heads, size, size), jnp.float32)
        return lax.fori_loop(0, lax.axis_index("seq"), one, zeros), (maps,)
    half = heads // 2
    here, z = side("x") == 0, lax.axis_index("seq") // 2
    kept = jnp.where(here, maps[:half], maps[half:])
    other = hop(jnp.where(here, maps[half:], maps[:half]), "x")
    first, second = jnp.where(here, kept, other), jnp.where(here, other, kept)
    pair_map = apply_map(second, first)
    state = jnp.zeros((half, size, size), jnp.float32)
    for step in range(3):
        sent = pair_map[:, :, :size] if step == 0 else apply_map(pair_map, state)
        state = state + lax.ppermute(sent, "seq", [(2 * step + x, 2 * step + 2 + x) for x in range(2)])
    moved = apply_map(first, state)
    mine = jnp.where(here, state, moved)
    other = hop(jnp.where(here, moved, state), "x")
    low, high = jnp.where(here, mine, other), jnp.where(here, other, mine)
    return jnp.concatenate([low, high], 0), (first, second, pair_map)


def carried_back(shift, context):
    heads, size, _ = shift.shape
    if not tuned():
        gathered = lax.all_gather(
            jnp.concatenate([shift, context[0][:, :, size:]], 2), "seq"
        )
        count = lax.axis_size("seq")

        def one(lap, state):
            maps = lax.dynamic_index_in_dim(gathered, count - 1 - lap, 0, False)
            return apply_map(maps, state, True)

        zeros = jnp.zeros((heads, size, size), jnp.float32)
        return lax.fori_loop(0, count - 1 - lax.axis_index("seq"), one, zeros)
    first, second, pair_map = context
    half = heads // 2
    here = side("x") == 0
    kept = jnp.where(here, shift[:half], shift[half:])
    other = hop(jnp.where(here, shift[half:], shift[:half]), "x")
    first = jnp.concatenate([jnp.where(here, kept, other), first[:, :, size:]], 2)
    second = jnp.concatenate([jnp.where(here, other, kept), second[:, :, size:]], 2)
    pair_map = jnp.concatenate([apply_map(first, second[:, :, :size], True), pair_map[:, :, size:]], 2)
    state = jnp.zeros((half, size, size), jnp.float32)
    for step in range(3, 0, -1):
        sent = pair_map[:, :, :size] if step == 3 else apply_map(pair_map, state, True)
        state = state + lax.ppermute(sent, "seq", [(2 * step + x, 2 * step - 2 + x) for x in range(2)])
    moved = apply_map(second, state, True)
    mine = jnp.where(here, moved, state)
    other = hop(jnp.where(here, state, moved), "x")
    low, high = jnp.where(here, mine, other), jnp.where(here, other, mine)
    return jnp.concatenate([low, high], 0)


def outer_kernel(bit, *refs, blocks, post):
    count = len(blocks)
    lefts, rights = refs[: 2 * count], refs[2 * count : 4 * count]
    keep, send, stacked = refs[4 * count :]
    step = pl.program_id(0)
    tokens = lefts[0].shape[1]
    half = keep.shape[0]

    @pl.when(step == 0)
    def _():
        for piece in range(count):
            for which in range(2):
                for start in range(0, half, post):
                    for place, mine in ((start, bit[0]), (half + start, 1 - bit[0])):
                        rows = pl.ds(pl.multiple_of(2 * start + mine * post, 8), post)
                        stacked[
                            piece, place : place + post, which * tokens : (which + 1) * tokens
                        ] = lefts[2 * piece + which][rows, :].astype(LOW)

    for piece in range(count):
        low = sum(blocks[:piece])

        @pl.when((step >= low) & (step < low + blocks[piece]))
        def _(piece=piece):
            right = jnp.concatenate(
                [rights[2 * piece][...].astype(LOW), rights[2 * piece + 1][...].astype(LOW)], 0
            )
            keep[...] = mxu(stacked[piece, :half, :], right, NN)
            send[...] = mxu(stacked[piece, half:, :], right, NN)


def outer(pieces, way):
    rows, tokens = pieces[0][0].shape
    block = 2 * LANES
    post = rows // 8 * {"near": 2, "x": 1}.get(way, 0) or rows // 16
    counts = [piece[5] for piece in pieces]
    left = pl.BlockSpec((rows, tokens), lambda j: (0, 0), pipeline_mode=pl.Buffered(1))
    lefts, rights, specs = [], [], []
    for index, piece in enumerate(pieces):
        lefts += piece[:2]
        rights += piece[2:4]

        def place(j, low=sum(counts[:index]), first=piece[4], number=piece[5]):
            return 0, first + jnp.clip(j - low, 0, number - 1)

        specs += [pl.BlockSpec((tokens, block), place)] * 2
    total = sum(counts)
    out = pl.BlockSpec((rows // 2, block), lambda j: (0, j))
    shape = jax.ShapeDtypeStruct((rows // 2, total * block), jnp.float32)
    return pl.pallas_call(
        lambda *refs: outer_kernel(*refs, blocks=counts, post=post),
        grid=(total,),
        in_specs=[pl.BlockSpec(memory_space=pltpu.SMEM)] + [left] * len(lefts) + specs,
        out_specs=[out, out],
        out_shape=[shape, shape],
        scratch_shapes=[pltpu.VMEM((len(pieces), rows, 2 * tokens), LOW)],
        compiler_params=params(),
        cost_estimate=cost(
            4 * rows * tokens * total * block, 4 * rows * total * block + 8 * tokens * rows
        ),
        name="outer",
    )(side(way).astype(jnp.int32).reshape(1), *lefts, *rights)


def take(value, place, axis):
    return lax.dynamic_index_in_dim(value, place, axis, False)


def reduced(keep, send, order):
    names = ["far", "near", "x", "y"]
    names.remove(order[0])
    shape = (2, 2, 2, keep.shape[0] // 8, keep.shape[1])
    keep, come = keep.reshape(shape), hop(send, order[0]).reshape(shape)
    for way in order[1:]:
        at, bit = names.index(way), side(way)
        names.remove(way)
        send = take(keep, 1 - bit, at) + take(come, 1 - bit, at)
        keep = take(keep, bit, at) + take(come, bit, at)
        come = hop(send, way)
    keep = keep + come
    come = hop(keep, "y")
    first = side("y") == 0
    return jnp.concatenate([jnp.where(first, keep, come), jnp.where(first, come, keep)], 0)


XYZ, YZX, ZXY = ("x", "y", "near", "far"), ("y", "near", "x", "far"), ("near", "x", "y", "far")


def small_sums(small):
    first_gain, beta, conv, head_gain, second_gain = small
    seq = lax.axis_size("seq")
    flat = jnp.concatenate(
        [
            first_gain.reshape(seq, -1), beta.reshape(seq, -1),
            conv.reshape(conv.shape[0] * conv.shape[1], seq, -1).transpose(1, 0, 2).reshape(seq, -1),
            head_gain.reshape(seq, -1), second_gain.reshape(seq, -1),
        ],
        1,
    )
    size = flat.shape[1]
    rows = -(-size // 2048) * 16
    flat = jnp.pad(flat, ((0, 0), (0, rows * 128 - size))).reshape(seq * rows, 128)
    flat = flat + hop(flat, "core")
    split = flat.reshape(4, 2, rows, 128)
    here = side("x")
    halves_of = [take(split, place, 1).reshape(-1, 128) for place in (here, 1 - here)]
    flat = reduced(*halves_of, XYZ).reshape(-1)
    sizes = [a.size // seq for a in small]
    places = [sum(sizes[:i]) for i in range(len(sizes))]
    pieces = [flat[p : p + s] for p, s in zip(places, sizes)]
    return (
        pieces[0], pieces[1].reshape(-1, beta.shape[1]),
        pieces[2].reshape(conv.shape[0], conv.shape[1], -1), pieces[3], pieces[4],
    )


def outer_sum(left, right):
    return mxu(left.astype(LOW), right.astype(LOW), TN)


def local(
    tokens,
    doc_lengths,
    out_grad,
    first_gain,
    query_weight,
    key_weight,
    value_weight,
    gate_weight,
    beta_weight,
    conv_weight,
    head_gain,
    out_weight,
    second_gain,
    hidden_gate,
    hidden_up,
    hidden_down,
):
    count, width = (tokens.shape[1], tokens.shape[2])
    heads = beta_weight.shape[1]
    reach = conv_weight.shape[1] - 1
    first = lax.axis_index("seq") * count
    position, live = doc_info(doc_lengths[0], first, count)
    keep = 1.0 - (position[::CK] == 0).astype(jnp.float32)
    position, live = position[:, None], live[:, None]
    core = (lax.axis_index("doc") % 2).astype(jnp.int32).reshape(1)
    here = core[0] == 0
    rows, top = tokens[0], out_grad[0]
    halo = passed_along(rows[count - HALO :].astype(jnp.float32), "seq", 1)
    normed_one, pre, features, gate_pre, beta_pre, beta = project(
        rows, halo, first_gain[None], position, live, query_weight, key_weight, value_weight,
        gate_weight, beta_weight, conv_weight,
    )
    solved, inverses, attend, maps = prepare(keep, features, beta)
    state_in, context = carried_forward(maps)
    starts, news, mixed, normed_head = mix(
        keep, features, solved, attend, gate_pre, head_gain[None], state_in
    )
    head_turned = normed_head.T.astype(jnp.float32)
    (
        block_out, two_turned, inner_turned, kept, sent, grad_hidden, grad_branch, grad_head,
        grad_second_gain,
    ) = feed(
        core, rows, normed_head, top, second_gain[None], out_weight, hidden_gate, hidden_up,
        hidden_down,
    )
    grad_mixed, grad_gate_pre, grad_head_gain, shift = gather_states(
        keep, grad_head, mixed, gate_pre, head_gain[None], features, solved, heads
    )
    state_grad = carried_back(shift, context)
    grads, borrowed, grad_conv, grad_beta_pre = back(
        keep, features, beta, beta_pre, solved, inverses, starts, news, grad_mixed, state_grad, pre,
        conv_weight, position, live,
    )
    returned = passed_along(borrowed, "seq", -1)
    tail = grads[:, count - 8 :] + returned
    grads = lax.dynamic_update_slice(grads, tail, (0, count - 8, 0))
    grads = grads.astype(LOW)
    input_grad, grad_first_gain = enter(
        rows, first_gain[None], grad_hidden, grads, grad_gate_pre, grad_beta_pre, query_weight,
        key_weight, value_weight, gate_weight, beta_weight,
    )
    small = (
        grad_first_gain[0], outer_sum(normed_one.T, grad_beta_pre), grad_conv, grad_head_gain[0],
        grad_second_gain[0],
    )
    if tuned():
        half = width // 2

        def pick(zero, one):
            return jnp.where(here, zero, one)

        def both(value, send=None):
            return value, hop(value if send is None else send, "core")

        wide_top = top.astype(jnp.float32)
        tops = both(
            pick(top[:, :half], top[:, half:]), pick(wide_top[:, half:], wide_top[:, :half])
        )
        one = both(normed_one)
        two = both(two_turned)
        inners = both(inner_turned)
        heads_turned = both(head_turned)
        gate_up = both(kept, sent)
        out_left = pick(heads_turned[0], one[0]), pick(heads_turned[1], one[1])
        out_right = both(pick(grad_branch, grad_gate_pre), pick(grad_gate_pre, grad_branch))
        blocks = hidden_gate.shape[1] // 256
        low = blocks // 2
        some = width // 256 * 3 // 4
        early = (
            reduced(
                *outer([(*two, *gate_up, 0, low), (*out_left, *out_right, 0, some)], "x"), XYZ
            ),
            reduced(
                *outer(
                    [
                        (*two, *gate_up, low, blocks - low),
                        (*out_left, *out_right, some, width // 256 - some),
                    ],
                    "y",
                ),
                YZX,
            ),
            reduced(*outer([(*inners, *tops, 0, half // 256)], "near"), ZXY),
        )
        wide = grads.astype(jnp.float32)
        query_key = both(pick(grads[0], grads[1]), pick(wide[1], wide[0]))
        value = both(
            pick(grads[2, :, :half], grads[2, :, half:]), pick(wide[2, :, half:], wide[2, :, :half])
        )
        late = (
            reduced(*outer([(*one, *query_key, 0, half // 256)], "x"), XYZ),
            reduced(*outer([(*one, *query_key, half // 256, half // 256)], "y"), YZX),
            reduced(*outer([(*one, *value, 0, half // 256)], "near"), ZXY),
        )
        a, b = low * 256, (blocks - low) * 256
        own = (
            jnp.concatenate([early[0][:, :a], early[1][:, :b]], 1), early[2],
            jnp.concatenate([early[0][:, a:], early[1][:, b:]], 1),
            jnp.concatenate(late[:2], 1), late[2],
        )
        other = tuple(hop(v, "core") for v in own)
        zero = [pick(m, o) for m, o in zip(own, other)]
        one_ = [pick(o, m) for m, o in zip(own, other)]
        query_g, key_g = zero[3], one_[3]
        value_g = jnp.concatenate([zero[4], one_[4]], 1)
        gate_g, out_g, hidden_gate_g, hidden_up_g = one_[2], zero[2], zero[0], one_[0]
        hidden_down_g = jnp.concatenate([zero[1], one_[1]], 1)
        first_g, beta_g, conv_g, head_g, second_g = small_sums(small)
    else:

        def whole(term, dimension):
            part = lax.psum_scatter(term, "seq", scatter_dimension=dimension, tiled=True)
            return lax.psum(part, "doc")

        gate_grad, up_grad = jnp.where(here, kept, sent), jnp.where(here, sent, kept)
        terms = (
            outer_sum(normed_one.T, grads[0]), outer_sum(normed_one.T, grads[1]),
            outer_sum(normed_one.T, grads[2]), outer_sum(normed_one.T, grad_gate_pre),
            outer_sum(head_turned.T, grad_branch), outer_sum(two_turned.T, gate_grad),
            outer_sum(two_turned.T, up_grad), outer_sum(inner_turned.T, top),
        )
        query_g, key_g, value_g, gate_g, out_g, hidden_gate_g, hidden_up_g, hidden_down_g = (
            whole(term, 0) for term in terms
        )
        first_g, beta_g, conv_g, head_g, second_g = (
            whole(term, d) for term, d in zip(small, (0, 0, 2, 0, 0))
        )
    return (
        block_out[None], input_grad[None], first_g, query_g, key_g, value_g, gate_g, beta_g, conv_g,
        head_g, out_g, second_g, hidden_gate_g, hidden_up_g, hidden_down_g,
    )


def solution(mesh):
    in_specs = (
        P("doc", "seq", None),
        P("doc", None),
        P("doc", "seq", None),
        P(),
        P(),
        P(),
        P(),
        P(),
        P(),
        P(),
        P(),
        P(),
        P(),
        P(),
        P(),
        P(),
    )
    out_specs = (
        P("doc", "seq", None),
        P("doc", "seq", None),
        P("seq"),
        P("seq", None),
        P("seq", None),
        P("seq", None),
        P("seq", None),
        P("seq", None),
        P(None, None, "seq"),
        P("seq"),
        P("seq", None),
        P("seq"),
        P("seq", None),
        P("seq", None),
        P("seq", None),
    )
    return jax.shard_map(local, mesh=mesh, in_specs=in_specs, out_specs=out_specs, check_vma=False)
```

time: 1970 us -> 645 us (0.33)
  waiting for transfers between devices: 1220 us -> 296 us
  matrix products: 474 us -> 1.17 us
  Pallas kernels: 0 us -> 197 us
  local copies, waits for them, and re-layouts: 155 us -> 26.3 us
  starting transfers between devices: 7.14 us -> 64.5 us
  blocking collectives: 31.8 us -> 0 us
    reduce_scatter x9 -> x0, waiting for transfers between devices: 867 us -> none  [the longest x1 196 us: local(): lax.psum_scatter(grad_gate_w, 'seq', scatter_dimension=0, tiled=True)]
    dot_general x148 -> x1, matrix products: 474 us -> 1.17 us  [mxu(): lax.dot_general(left, right, dims, preferred_element_type=jnp.float32)]
    ppermute x0 -> x60, waiting for transfers between devices: none -> 294 us  [the longest x54 266 us: hop(): lax.ppermute(value, axis, [(i, i ^ bit) for i in range(lax.axis_size(axis...]
    all_gather x4 -> x0, waiting for transfers between devices: 201 us -> none  [carried_in(): gathered = jax.tree.map(lambda a: lax.all_gather(a, axis), part)]
    pallas_call x0 -> x21, Pallas kernels: none -> 197 us  [the longest x1 44.9 us: prepare(): pl.pallas_call(prepare_kernel, grid=(spans,), in_specs=[pl.BlockSpec(memo...]
    psum x1 -> x0, waiting for transfers between devices: 122 us -> none  [local(): lax.psum((parts[0], parts[1], parts[2], parts[3], parts[4], parts[5], par...]
    ppermute x0 -> x60, starting transfers between devices: none -> 58 us  [the longest x54 50.1 us: hop(): lax.ppermute(value, axis, [(i, i ^ bit) for i in range(lax.axis_size(axis...]
    unnamed x327 -> x118, local copies, waits for them, and re-layouts: 51 us -> 17.5 us
  transfers between devices with their start and end apart: 17 -> 62, of which waited for: 13 -> 25; matrix products, arithmetic and copies ran while one was open for 26% -> 9% of each run, Pallas kernels for 0% -> 14%
where the time goes in v1:
time: 645 us; the launch traced here: 638 us
  waiting for transfers between devices  296 us (46%)
  Pallas kernels  197 us (31%)
  starting transfers between devices  64.5 us (10%)
  other arithmetic  50.6 us (8%)
  local copies, waits for them, and re-layouts  26.3 us (4%)
    ppermute x54, waiting for transfers between devices, hop(): lax.ppermute(value, axis, [(i, i ^ bit) for i in range(lax.axis_size(axis...  266 us
    ppermute x54, starting transfers between devices, hop(): lax.ppermute(value, axis, [(i, i ^ bit) for i in range(lax.axis_size(axis...  50.1 us
    pallas_call x1, Pallas kernels, prepare(): pl.pallas_call(prepare_kernel, grid=(spans,), in_specs=[pl.BlockSpec(memo...  44.9 us
    pallas_call x1, Pallas kernels, back(): pl.pallas_call(back_kernel, grid=(spans,), in_specs=[pl.BlockSpec(memory_...  42 us
    pallas_call x6, Pallas kernels, outer(): pl.pallas_call(lambda *refs: outer_kernel(*refs, blocks=counts, post=post...  38.4 us
    pallas_call x1, Pallas kernels, feed(): pl.pallas_call(feed_kernel, grid=(hidden // block,), in_specs=[pl.BlockSp...  28.2 us
    ppermute x3, waiting for transfers between devices, carried_back(): lax.ppermute(sent, 'seq', [(2 * step + x, 2 * step - 2 + x) for x in rang...  23.4 us
    unnamed x118, local copies, waits for them, and re-layouts  17.5 us
  transfers between devices with their start and end apart: 62, of which 25 were waited for; matrix products, arithmetic and copies ran while one was open for 9% of the time, Pallas kernels for 14%

profile of v1, /device:TPU:0, one launch (start us, length us, event | category | flops | bytes accessed | tf_op | source)
XLA Modules:
  0.0 637.7 jit_solution(4595983402806250524)
XLA Ops:
  1.4 4.8 collective-permute-start
  12.6 12.1 %project.1 = (f32[1024,384]{1,0:T(8,128)S(1)}, f32[3,400,1024]{2,1,0:T(8,128)}, f32[3,384,1024]{2,1,0:T(8,128)}, f32[384,1024]{1,0:T(8,128)S(1)}, f32[384,8]{1,0:T(8,128)S(1)}, /*index=5*/f32[384,8]{1,0:T(8,128)S(1)}) custom-call(bf16[384,1024]{1,0:T(8,128)(2,1)S(1)} %bitcast.242, f32[16,1024]{1,0:T(8,128)S(1)} %collective-permute-done.halo, ...), custom_call_target="tpu_custom_call" | custom-call | flops 3221225472 | bytes 24117248 | tf_op jit(solution)/shard_map/project/pallas_call | solution.py:198
  25.8 44.9 %prepare.1 = (f32[2,384,1024]{2,1,0:T(8,128)}, f32[6,4,128,128]{3,2,1,0:T(8,128)S(1)}, f32[6,4,128,128]{3,2,1,0:T(8,128)S(1)}, f32[8,128,256]{2,1,0:T(8,128)S(1)}) custom-call(f32[6]{0:T(128)S(1)} %fusion.43.keep, f32[3,384,1024]{2,1,0:T(8,128)} %get-tuple-element.60.features, f32[384,8]{1,0:T(8,128)S(1)} %get-tuple-element.61.beta), custom_call_target="tpu_custom_call" | custom-call | flops 8053063680 | bytes 23592960 | tf_op jit(solution)/shard_map/prepare/pallas_call | solution.py:265
  70.8 1.6 collective-permute-start.1
  72.4 11.8 %collective-permute-done.1 = f32[4,128,256]{2,1,0:T(8,128)S(1)} collective-permute-done((f32[4,128,256]{2,1,0:T(8,128)S(1)}, f32[4,128,256]{2,1,0:T(8,128)S(1)}, u32[]{:S(2)}, u32[]{:S(2)}) %collective-permute-start.1) | collective-permute-done | bytes 524320 | tf_op jit(solution)/shard_map/ppermute | solution.py:777
  84.7 3.5 collective-permute-start.2
  88.2 4.3 collective-permute-done.2.refs_1_
  95.0 1.6 collective-permute-start.5
  96.6 4.9 collective-permute-done.5
  102.7 10.0 %mix.1 = (f32[6,8,128,128]{3,2,1,0:T(8,128)}, f32[384,1024]{1,0:T(8,128)S(1)}, f32[384,1024]{1,0:T(8,128)S(1)}, bf16[384,1024]{1,0:T(8,128)(2,1)S(1)}) custom-call(f32[6]{0:T(128)S(1)} %fusion.43.keep, f32[3,384,1024]{2,1,0:T(8,128)} %get-tuple-element.60.features, f32[2,384,1024]{2,1,0:T(8,128)} %get-tuple-element.62.solved, ...), custom_call_target="tpu_custom_call" | custom-call | flops 1610612736 | bytes 15728640 | tf_op jit(solution)/shard_map/mix/pallas_call | solution.py:330
  115.1 28.2 %feed.1 = (bf16[384,1024]{1,0:T(8,128)(2,1)}, f32[1024,384]{1,0:T(8,128)S(1)}, f32[2816,384]{1,0:T(8,128)}, bf16[384,2816]{1,0:T(8,128)(2,1)}, f32[384,2816]{1,0...) custom-call(s32[1]{0:T(128)} %bitcast.core, ...), custom_call_target="tpu_custom_call" | custom-call | flops 14898167808 | bytes 39911424 | tf_op jit(solution)/shard_map/feed/pallas_call | solution.py:425
  147.0 10.0 %gather_states.1 = (f32[384,1024]{1,0:T(8,128)S(1)}, f32[384,1024]{1,0:T(8,128)S(1)}, f32[1,128]{1,0:T(1,128)S(1)}, f32[8,128,128]{2,1,0:T(8,128)S(1)}) custom-call(f32[6]{0:T(128)S(1)} %fusion.43.keep, f32[384,1024]{1,0:T(8,128)S(1)} %copy-done.19, f32[384,1024]{1,0:T(8,128)} %copy-done.18, f32[384,1024]{1,0:T(8,128)} %copy-done.9, f32[1,128]{1,0:T(1,128)S(1)} %bitcast.250, ...), custom_call_target="tpu_custom_call" | custom-call | flops 1610612736 | bytes 12582912 | tf_op jit(solution)/shard_map/gather_states/pallas_call | solution.py:516
  157.1 1.6 collective-permute-start.6
  158.7 4.8 collective-permute-done.6
  168.2 1.5 collective-permute-start.9
  171.4 2.3 copy.115
  176.1 23.4 %collective-permute-done.9 = f32[4,128,128]{2,1,0:T(8,128)} collective-permute-done((f32[4,128,128]{2,1,0:T(8,128)}, f32[4,128,128]{2,1,0:T(8,128)}, u32[]{:S(2)}, u32[]{:S(2)}) %collective-permute-start.9) | collective-permute-done | bytes 262176 | tf_op jit(solution)/shard_map/ppermute | solution.py:858
  200.7 1.6 collective-permute-start.10
  204.3 2.9 collective-permute-done.10
  207.4 42.0 %back.1 = (f32[3,384,1024]{2,1,0:T(8,128)}, f32[3,8,1024]{2,1,0:T(8,128)S(1)}, f32[3,4,1024]{2,1,0:T(4,128)S(1)}, f32[384,8]{1,0:T(8,128)S(1)}) custom-call(f32[6]{0:T(128)S(1)} %fusion.43.keep, f32[3,384,1024]{2,1,0:T(8,128)} %get-tuple-element.60.features, f32[384,8]{1,0:T(8,128)S(1)} %copy-done.49, f32[384,8]{1,0:T(8,128)S(1)} %copy-done.47, ...), custom_call_target="tpu_custom_call" | custom-call | flops 6039797760 | bytes 23592960 | tf_op jit(solution)/shard_map/back/pallas_call | solution.py:679
  249.4 1.7 collective-permute-start.11
  252.2 1.9 reshape.299
  254.2 1.8 collective-permute-done.11
  256.0 1.6 add_dynamic-update-slice_fusion
  257.6 6.6 %fusion.46 = (f32[3,384,1024]{2,1,0:T(8,128)}, bf16[3,384,1024]{2,1,0:T(8,128)(2,1)}) fusion(f32[3,384,1024]{2,1,0:T(8,128)} %add_dynamic-update-slice_fusion), kind=kLoop, calls=%fused_computation.203 | loop fusion | flops 2359296 | bytes 11796480 | tf_op jit(solution)/shard_map/convert_element_type | solution.py:1091
  264.3 9.0 %enter.1 = (bf16[384,1024]{1,0:T(8,128)(2,1)}, f32[1,1024]{1,0:T(1,128)S(1)}) custom-call(bf16[384,1024]{1,0:T(8,128)(2,1)S(1)} %bitcast.244, f32[1,1024]{1,0:T(1,128)S(1)} %bitcast.246, f32[384,1024]{1,0:T(8,128)S(1)} %copy-done.17, bf16[3,384,1024]{2,1,0:T(8,128)(2,1)} %get-tuple-element.168.grads, f32[384,1024]{1,0:T(8,128)S(1)} %copy-done.7, ...), custom_call_target="tpu_custom_call" | custom-call | flops 3221225472 | bytes 16252928 | tf_op jit(solution)/shard_map/enter/pallas_call | solution.py:739
  274.9 4.7 collective-permute-start.13
  279.6 3.8 broadcast_select_fusion
  284.0 1.5 collective-permute-start.14
  285.7 2.2 collective-permute-done.14
  290.4 2.8 broadcast_select_fusion.2.refs_4_
  293.2 3.0 outer.8
  296.3 3.0 collective-permute-start.32
  299.3 9.8 %outer.10 = (f32[512,1792]{1,0:T(8,128)}, f32[512,1792]{1,0:T(8,128)}) custom-call(s32[1]{0:T(128)} %bitcast.44.refs_0_, f32[1024,384]{1,0:T(8,128)S(1)} %copy-done.5, f32[1024,384]{1,0:T(8,128)S(1)} %collective-permute-done.38.refs_2_, f32[1024,384]{1,0:T(8,128)S(1)} %broadcast_select_fusion.3.refs_3_, f32[1024,384]{1,0:T(8,128)} %broadcast_select_fusion.2.refs_4_, ...), custom_call_target="tpu_custom_call" | custom-call | flops 2818572288 | bytes 10485760 | tf_op jit(solution)/shard_map/outer/pallas_call | solution.py:915
  309.0 1.5 collective-permute-start.47
  310.5 10.9 %outer.9 = (f32[512,2048]{1,0:T(8,128)}, f32[512,2048]{1,0:T(8,128)}) custom-call(s32[1]{0:T(128)} %bitcast.31.refs_0_, f32[1024,384]{1,0:T(8,128)S(1)} %copy-done.5, f32[1024,384]{1,0:T(8,128)S(1)} %collective-permute-done.38.refs_2_, f32[1024,384]{1,0:T(8,128)S(1)} %broadcast_select_fusion.3.refs_3_, f32[1024,384]{1,0:T(8,128)} %broadcast_select_fusion.2.refs_4_, ...), custom_call_target="tpu_custom_call" | custom-call | flops 3221225472 | bytes 11534336 | tf_op jit(solution)/shard_map/outer/pallas_call | solution.py:915
  323.1 8.1 %outer.11 = (f32[1408,512]{1,0:T(8,128)S(1)}, f32[1408,512]{1,0:T(8,128)}) custom-call(s32[1]{0:T(128)} %bitcast.55.refs_0_, f32[2816,384]{1,0:T(8,128)} %get-tuple-element.102.refs_1_, f32[2816,384]{1,0:T(8,128)} %collective-permute-done.54.refs_2_, bf16[384,512]{1,0:T(8,128)(2,1)S(1)} %slice_select_fusion.6.refs_3_, ...), custom_call_target="tpu_custom_call" | custom-call | flops 2214592512 | bytes 14417920 | tf_op jit(solution)/shard_map/outer/pallas_call | solution.py:915
  331.2 1.5 copy-done.13
  337.2 58.1 %collective-permute-done.16 = f32[16,128]{1,0:T(8,128)S(1)} collective-permute-done((f32[16,128]{1,0:T(8,128)S(1)}, f32[16,128]{1,0:T(8,128)S(1)}, u32[]{:S(2)}, u32[]{:S(2)}) %collective-permute-start.16) | collective-permute-done | bytes 8224 | tf_op jit(solution)/shard_map/ppermute | solution.py:777
  395.3 1.5 collective-permute-start.33
  397.4 3.2 outer.7
  401.6 1.5 collective-permute-start.25
  404.2 3.4 outer.6
  408.6 18.0 %collective-permute-done.33 = f32[2,2,64,512]{3,2,0,1:T(8,128)} collective-permute-done((f32[2,2,64,512]{3,2,0,1:T(8,128)}, f32[2,2,64,512]{3,2,0,1:T(8,128)}, u32[]{:S(2)}, u32[]{:S(2)}) %collective-permute-start.33) | collective-permute-done | bytes 524320 | tf_op jit(solution)/shard_map/ppermute | solution.py:777
  433.4 17.5 %collective-permute-done.20 = f32[512,512]{1,0:T(8,128)S(1)} collective-permute-done((f32[512,512]{1,0:T(8,128)}, f32[512,512]{1,0:T(8,128)S(1)}, u32[]{:S(2)}, u32[]{:S(2)}) %collective-permute-start.20) | collective-permute-done | bytes 1048608 | tf_op jit(solution)/shard_map/ppermute | solution.py:777
  453.2 2.7 dynamic-slice_add_fusion.2
  456.2 2.5 dynamic-slice_add_fusion.1
  458.9 1.6 collective-permute-start.48
  460.9 3.4 dynamic-slice_add_fusion
  464.5 1.6 collective-permute-start.43
  466.4 1.6 collective-permute-start.57
  469.7 42.8 %collective-permute-done.36 = f32[64,512]{1,0:T(8,128)S(1)} collective-permute-done((f32[64,512]{1,0:T(8,128)S(1)}, f32[64,512]{1,0:T(8,128)S(1)}, u32[]{:S(2)}, u32[]{:S(2)}) %collective-permute-start.36) | collective-permute-done | bytes 131104 | tf_op jit(solution)/shard_map/ppermute | solution.py:777
  512.5 1.7 collective-permute-start.22
  514.4 1.6 collective-permute-start.28
  516.0 4.5 collective-permute-done.22
  523.2 6.9 %collective-permute-done.23 = f32[64,512]{1,0:T(8,128)S(1)} collective-permute-done((f32[64,512]{1,0:T(8,128)S(1)}, f32[64,512]{1,0:T(8,128)S(1)}, u32[]{:S(2)}, u32[]{:S(2)}) %collective-permute-start.23) | collective-permute-done | bytes 131104 | tf_op jit(solution)/shard_map/ppermute | solution.py:777
  536.5 17.3 %collective-permute-done.58 = f32[2,176,512]{2,1,0:T(8,128)S(1)} collective-permute-done((f32[2,176,512]{2,1,0:T(8,128)S(1)}, f32[2,176,512]{2,1,0:T(8,128)S(1)}, u32[]{:S(2)}, u32[]{:S(2)}) %collective-permute-start.58) | collective-permute-done | bytes 720928 | tf_op jit(solution)/shard_map/ppermute | solution.py:777
  554.1 17.9 %collective-permute-done.59 = f32[176,512]{1,0:T(8,128)S(1)} collective-permute-done((f32[176,512]{1,0:T(8,128)S(1)}, f32[176,512]{1,0:T(8,128)S(1)}, u32[]{:S(2)}, u32[]{:S(2)}) %collective-permute-start.59) | collective-permute-done | bytes 360480 | tf_op jit(solution)/shard_map/ppermute | solution.py:777
  573.0 3.0 collective-permute-start.45
  575.9 5.4 collective-permute-done.60
  581.4 24.6 %collective-permute-done.50 = f32[64,1792]{1,0:T(8,128)S(1)} collective-permute-done((f32[64,1792]{1,0:T(8,128)S(1)}, f32[64,1792]{1,0:T(8,128)S(1)}, u32[]{:S(2)}, u32[]{:S(2)}) %collective-permute-start.50) | collective-permute-done | bytes 458784 | tf_op jit(solution)/shard_map/ppermute | solution.py:777
  606.4 10.4 %collective-permute-done.45 = f32[64,2048]{1,0:T(8,128)S(1)} collective-permute-done((f32[64,2048]{1,0:T(8,128)S(1)}, f32[64,2048]{1,0:T(8,128)S(1)}, u32[]{:S(2)}, u32[]{:S(2)}) %collective-permute-start.45) | collective-permute-done | bytes 524320 | tf_op jit(solution)/shard_map/ppermute | solution.py:777
  617.9 12.5 %collective-permute-done.46 = f32[64,2048]{1,0:T(8,128)S(1)} collective-permute-done((f32[64,2048]{1,0:T(8,128)S(1)}, f32[64,2048]{1,0:T(8,128)S(1)}, u32[]{:S(2)}, u32[]{:S(2)}) %collective-permute-start.46) | collective-permute-done | bytes 524320 | tf_op jit(solution)/shard_map/ppermute | solution.py:777
  635.7 1.8 broadcast_select_fusion.4
  (317 shorter events, 75.2 us)
Async XLA Ops:
  1.4 8.5 %collective-permute-start = (f32[16,1024]{1,0:T(8,128)S(1)}, f32[16,1024]{1,0:T(8,128)S(1)}, u32[]{:S(2)}, u32[]{:S(2)}) collective-permute-start(f32[16,1024]{1,0:T(8,128)S(1)} %bitcast_convert_fusion), channel_id=1, source_target_pairs={{0,4},{4,8},{8,12},{12,16},{16,20},{20,24},{24,28},{1,5},{5,9},{9,... | collective-permute-start | bytes 196616 | tf_op jit(solution)/shard_map/ppermute | solution.py:765
  70.8 13.5 %collective-permute-start.1 = (f32[4,128,256]{2,1,0:T(8,128)S(1)}, f32[4,128,256]{2,1,0:T(8,128)S(1)}, u32[]{:S(2)}, u32[]{:S(2)}) collective-permute-start(f32[4,128,256]{2,1,0:T(8,128)S(1)} %slice_select_fusion.5), channel_id=1, source_target_pairs={{0,4},{4,0},{8,12},{12,8},{16,20},{20,16},{24,28},{28,24},{1,5},{5... | collective-permute-start | bytes 1572872 | tf_op jit(solution)/shard_map/ppermute | solution.py:777
  84.7 7.8 %collective-permute-start.2 = (f32[4,128,128]{2,1,0:T(8,128)S(1)}, f32[4,128,128]{2,1,0:T(8,128)S(1)}, u32[]{:S(2)}, u32[]{:S(2)}) collective-permute-start(f32[4,128,128]{2,1,0:T(8,128)S(1)} %get-tuple-element.226), channel_id=1, source_target_pairs={{0,8},{4,12},{1,9},{5,13},{2,10},{6,14},{3,11},{7,15}} | collective-permute-start | bytes 786440 | tf_op jit(solution)/shard_map/ppermute | solution.py:825
  92.8 0.7 collective-permute-start.3
  93.8 0.9 collective-permute-start.4
  95.0 6.5 %collective-permute-start.5 = (f32[4,128,128]{2,1,0:T(8,128)S(1)}, f32[4,128,128]{2,1,0:T(8,128)}, u32[]{:S(2)}, u32[]{:S(2)}) collective-permute-start(f32[4,128,128]{2,1,0:T(8,128)S(1)} %broadcast_select_fusion.30), channel_id=1, source_target_pairs={{0,4},{4,0},{8,12},{12,8},{16,20},{20,16},{24,28},{28,24},{1,5},{5... | collective-permute-start | bytes 786440 | tf_op jit(solution)/shard_map/ppermute | solution.py:777
  157.1 6.4 %collective-permute-start.6 = (f32[4,128,128]{2,1,0:T(8,128)S(1)}, f32[4,128,128]{2,1,0:T(8,128)S(1)}, u32[]{:S(2)}, u32[]{:S(2)}) collective-permute-start(f32[4,128,128]{2,1,0:T(8,128)S(1)} %slice_select_fusion.9), channel_id=1, source_target_pairs={{0,4},{4,0},{8,12},{12,8},{16,20},{20,16},{24,28},{28,24},{1,5},{5... | collective-permute-start | bytes 786440 | tf_op jit(solution)/shard_map/ppermute | solution.py:777
  164.6 1.4 collective-permute-start.7
  166.3 0.9 collective-permute-start.8
  168.2 31.3 %collective-permute-start.9 = (f32[4,128,128]{2,1,0:T(8,128)}, f32[4,128,128]{2,1,0:T(8,128)}, u32[]{:S(2)}, u32[]{:S(2)}) collective-permute-start(f32[4,128,128]{2,1,0:T(8,128)} %apply_map.14), channel_id=1, source_target_pairs={{8,0},{12,4},{9,1},{13,5},{10,2},{14,6},{11,3},{15,7}} | collective-permute-start | bytes 786440 | tf_op jit(solution)/shard_map/ppermute | solution.py:858
  170.7 112.8 %collective-permute-start.18 = (f32[1024,384]{1,0:T(8,128)S(1)}, f32[1024,384]{1,0:T(8,128)S(1)}, u32[]{:S(2)}, u32[]{:S(2)}) collective-permute-start(f32[1024,384]{1,0:T(8,128)S(1)} %get-tuple-element.84.refs_1_), channel_id=1, source_target_pairs={{0,1},{1,0},{2,3},{3,2},{4,5},{5,4},{6,7},{7,6},{8,9},{9,8},{10,11... | collective-permute-start | bytes 4718600 | tf_op jit(solution)/shard_map/ppermute | solution.py:777
  200.7 6.4 %collective-permute-start.10 = (f32[4,128,128]{2,1,0:T(8,128)S(1)}, f32[4,128,128]{2,1,0:T(8,128)S(1)}, u32[]{:S(2)}, u32[]{:S(2)}) collective-permute-start(f32[4,128,128]{2,1,0:T(8,128)S(1)} %broadcast_select_fusion.24), channel_id=1, source_target_pairs={{0,4},{4,0},{8,12},{12,8},{16,20},{20,16},{24,28},{28,24},{1,5},{5... | collective-permute-start | bytes 786440 | tf_op jit(solution)/shard_map/ppermute | solution.py:777
  203.6 80.4 %collective-permute-start.39 = (f32[1024,384]{1,0:T(8,128)}, f32[1024,384]{1,0:T(8,128)}, u32[]{:S(2)}, u32[]{:S(2)}) collective-permute-start(f32[1024,384]{1,0:T(8,128)} %convert_bitcast_fusion), channel_id=1, source_target_pairs={{0,1},{1,0},{2,3},{3,2},{4,5},{5,4},{6,7},{7,6},{8,9},{9,8},{10,11... | collective-permute-start | bytes 4718600 | tf_op jit(solution)/shard_map/ppermute | solution.py:777
  203.7 95.5 %collective-permute-start.40 = (f32[384,2816]{1,0:T(8,128)}, f32[384,2816]{1,0:T(8,128)}, u32[]{:S(2)}, u32[]{:S(2)}) collective-permute-start(f32[384,2816]{1,0:T(8,128)} %get-tuple-element.96), channel_id=1, source_target_pairs={{0,1},{1,0},{2,3},{3,2},{4,5},{5,4},{6,7},{7,6},{8,9},{9,8},{10,11... | collective-permute-start | bytes 12976136 | tf_op jit(solution)/shard_map/ppermute | solution.py:777
  204.2 118.4 %collective-permute-start.54 = (f32[2816,384]{1,0:T(8,128)}, f32[2816,384]{1,0:T(8,128)}, u32[]{:S(2)}, u32[]{:S(2)}) collective-permute-start(f32[2816,384]{1,0:T(8,128)} %get-tuple-element.102.refs_1_), channel_id=1, source_target_pairs={{0,1},{1,0},{2,3},{3,2},{4,5},{5,4},{6,7},{7,6},{8,9},{9,8},{10,11... | collective-permute-start | bytes 12976136 | tf_op jit(solution)/shard_map/ppermute | solution.py:777
  249.4 6.6 %collective-permute-start.11 = (f32[3,8,1024]{2,1,0:T(8,128)S(1)}, f32[3,8,1024]{2,1,0:T(8,128)}, u32[]{:S(2)}, u32[]{:S(2)}) collective-permute-start(f32[3,8,1024]{2,1,0:T(8,128)S(1)} %get-tuple-element.79), channel_id=1, source_target_pairs={{4,0},{8,4},{12,8},{16,12},{20,16},{24,20},{28,24},{5,1},{9,5},{13... | collective-permute-start | bytes 294920 | tf_op jit(solution)/shard_map/ppermute | solution.py:765
  273.5 1.4 collective-permute-start.12
  274.9 8.4 %collective-permute-start.13 = (f32[128,128]{1,0:T(8,128)S(1)}, f32[128,128]{1,0:T(8,128)S(1)}, u32[]{:S(2)}, u32[]{:S(2)}) collective-permute-start(f32[128,128]{1,0:T(8,128)S(1)} %bitcast.260), channel_id=1, source_target_pairs={{0,4},{4,0},{8,12},{12,8},{16,20},{20,16},{24,28},{28,24},{1,5},{5... | collective-permute-start | bytes 196616 | tf_op jit(solution)/shard_map/ppermute | solution.py:777
  283.4 12.8 %collective-permute-start.38 = (f32[1024,384]{1,0:T(8,128)S(1)}, f32[1024,384]{1,0:T(8,128)S(1)}, u32[]{:S(2)}, u32[]{:S(2)}) collective-permute-start(f32[1024,384]{1,0:T(8,128)S(1)} %copy-done.5), channel_id=1, source_target_pairs={{0,1},{1,0},{2,3},{3,2},{4,5},{5,4},{6,7},{7,6},{8,9},{9,8},{10,11... | collective-permute-start | bytes 4718600 | tf_op jit(solution)/shard_map/ppermute | solution.py:777
  283.5 12.8 %collective-permute-start.41 = (f32[384,1024]{1,0:T(8,128)}, f32[384,1024]{1,0:T(8,128)S(1)}, u32[]{:S(2)}, u32[]{:S(2)}) collective-permute-start(f32[384,1024]{1,0:T(8,128)} %get-tuple-element.179), channel_id=1, source_target_pairs={{0,1},{1,0},{2,3},{3,2},{4,5},{5,4},{6,7},{7,6},{8,9},{9,8},{10,11... | collective-permute-start | bytes 4718600 | tf_op jit(solution)/shard_map/ppermute | solution.py:777
  284.0 3.9 collective-permute-start.14
  287.9 2.3 collective-permute-start.31
  290.2 31.3 %collective-permute-start.55 = (f32[384,512]{1,0:T(8,128)}, f32[384,512]{1,0:T(8,128)S(1)}, u32[]{:S(2)}, u32[]{:S(2)}) collective-permute-start(f32[384,512]{1,0:T(8,128)} %slice_select_fusion.1), channel_id=1, source_target_pairs={{0,1},{1,0},{2,3},{3,2},{4,5},{5,4},{6,7},{7,6},{8,9},{9,8},{10,11... | collective-permute-start | bytes 2359304 | tf_op jit(solution)/shard_map/ppermute | solution.py:777
  296.2 100.7 %collective-permute-start.19 = (f32[384,1024]{1,0:T(8,128)}, f32[384,1024]{1,0:T(8,128)}, u32[]{:S(2)}, u32[]{:S(2)}) collective-permute-start(f32[384,1024]{1,0:T(8,128)} %fusion.2), channel_id=1, source_target_pairs={{0,1},{1,0},{2,3},{3,2},{4,5},{5,4},{6,7},{7,6},{8,9},{9,8},{10,11... | collective-permute-start | bytes 4718600 | tf_op jit(solution)/shard_map/ppermute | solution.py:777
  296.3 37.5 %collective-permute-start.32 = (f32[512,512]{1,0:T(8,128)S(1)}, f32[512,512]{1,0:T(8,128)S(1)}, u32[]{:S(2)}, u32[]{:S(2)}) collective-permute-start(f32[512,512]{1,0:T(8,128)S(1)} %get-tuple-element.93), channel_id=1, source_target_pairs={{0,8},{4,12},{8,0},{12,4},{16,24},{20,28},{24,16},{28,20},{1,9},{5... | collective-permute-start | bytes 3145736 | tf_op jit(solution)/shard_map/ppermute | solution.py:777
  309.0 146.9 %collective-permute-start.47 = (f32[512,1792]{1,0:T(8,128)}, f32[512,1792]{1,0:T(8,128)}, u32[]{:S(2)}, u32[]{:S(2)}) collective-permute-start(f32[512,1792]{1,0:T(8,128)} %get-tuple-element.101), channel_id=1, source_target_pairs={{0,2},{1,3},{2,0},{3,1},{4,6},{5,7},{6,4},{7,5},{8,10},{9,11},{10,... | collective-permute-start | bytes 11010056 | tf_op jit(solution)/shard_map/ppermute | solution.py:777
  321.5 11.2 %collective-permute-start.15 = (f32[2,16,128]{2,1,0:T(8,128)S(1)}, f32[2,16,128]{2,1,0:T(8,128)S(1)}, u32[]{:S(2)}, u32[]{:S(2)}) collective-permute-start(f32[2,16,128]{2,1,0:T(8,128)S(1)} %get-tuple-element.237), channel_id=1, source_target_pairs={{0,8},{4,12},{8,0},{12,4},{16,24},{20,28},{24,16},{28,20},{1,9},{5... | collective-permute-start | bytes 49160 | tf_op jit(solution)/shard_map/ppermute | solution.py:777
  322.6 137.9 %collective-permute-start.42 = (f32[512,2048]{1,0:T(8,128)}, f32[512,2048]{1,0:T(8,128)}, u32[]{:S(2)}, u32[]{:S(2)}) collective-permute-start(f32[512,2048]{1,0:T(8,128)} %get-tuple-element.99), channel_id=1, source_target_pairs={{0,4},{4,0},{8,12},{12,8},{16,20},{20,16},{24,28},{28,24},{1,5},{5... | collective-permute-start | bytes 12582920 | tf_op jit(solution)/shard_map/ppermute | solution.py:777
  332.7 119.4 %collective-permute-start.56 = (f32[1408,512]{1,0:T(8,128)}, f32[1408,512]{1,0:T(8,128)}, u32[]{:S(2)}, u32[]{:S(2)}) collective-permute-start(f32[1408,512]{1,0:T(8,128)} %get-tuple-element.104), channel_id=1, source_target_pairs={{0,8},{4,12},{8,0},{12,4},{16,24},{20,28},{24,16},{28,20},{1,9},{5... | collective-permute-start | bytes 8650760 | tf_op jit(solution)/shard_map/ppermute | solution.py:777
  333.8 63.6 %copy-start.2 = (bf16[384,1024]{1,0:T(8,128)(2,1)}, bf16[384,1024]{1,0:T(8,128)(2,1)S(1)}, u32[]{:S(2)}) copy-start(bf16[384,1024]{1,0:T(8,128)(2,1)S(1)} %fusion.8.refs_3_) | copy-start | bytes 2359300
  333.8 61.5 %collective-permute-start.16 = (f32[16,128]{1,0:T(8,128)S(1)}, f32[16,128]{1,0:T(8,128)S(1)}, u32[]{:S(2)}, u32[]{:S(2)}) collective-permute-start(f32[16,128]{1,0:T(8,128)S(1)} %fusion.41), channel_id=1, source_target_pairs={{0,16},{4,20},{8,24},{12,28},{16,0},{20,4},{24,8},{28,12},{1,17},{... | collective-permute-start | bytes 24584 | tf_op jit(solution)/shard_map/ppermute | solution.py:777
  336.3 61.1 %copy-start.1 = (f32[1024,384]{1,0:T(8,128)S(1)}, f32[1024,384]{1,0:T(8,128)}, u32[]{:S(2)}) copy-start(f32[1024,384]{1,0:T(8,128)} %copy-done) | copy-start | bytes 4718596
  395.3 31.3 %collective-permute-start.33 = (f32[2,2,64,512]{3,2,0,1:T(8,128)}, f32[2,2,64,512]{3,2,0,1:T(8,128)}, u32[]{:S(2)}, u32[]{:S(2)}) collective-permute-start(f32[2,2,64,512]{3,2,0,1:T(8,128)} %fusion.13), channel_id=1, source_target_pairs={{0,4},{4,0},{8,12},{12,8},{16,20},{20,16},{24,28},{28,24},{1,5},{5... | collective-permute-start | bytes 1572872 | tf_op jit(solution)/shard_map/ppermute | solution.py:777
  396.8 4.7 collective-permute-start.17
  401.6 29.7 %collective-permute-start.25 = (f32[512,512]{1,0:T(8,128)}, f32[512,512]{1,0:T(8,128)}, u32[]{:S(2)}, u32[]{:S(2)}) collective-permute-start(f32[512,512]{1,0:T(8,128)} %get-tuple-element.91), channel_id=1, source_target_pairs={{0,2},{1,3},{2,0},{3,1},{4,6},{5,7},{6,4},{7,5},{8,10},{9,11},{10,... | collective-permute-start | bytes 3145736 | tf_op jit(solution)/shard_map/ppermute | solution.py:777
  426.6 24.3 %collective-permute-start.20 = (f32[512,512]{1,0:T(8,128)}, f32[512,512]{1,0:T(8,128)S(1)}, u32[]{:S(2)}, u32[]{:S(2)}) collective-permute-start(f32[512,512]{1,0:T(8,128)} %get-tuple-element.89), channel_id=1, source_target_pairs={{0,4},{4,0},{8,12},{12,8},{16,20},{20,16},{24,28},{28,24},{1,5},{5... | collective-permute-start | bytes 3145736 | tf_op jit(solution)/shard_map/ppermute | solution.py:777
  431.3 20.1 %collective-permute-start.34 = (f32[2,64,512]{2,1,0:T(8,128)S(1)}, f32[2,64,512]{2,1,0:T(8,128)S(1)}, u32[]{:S(2)}, u32[]{:S(2)}) collective-permute-start(f32[2,64,512]{2,1,0:T(8,128)S(1)} %get-tuple-element.197), channel_id=1, source_target_pairs={{0,2},{1,3},{2,0},{3,1},{4,6},{5,7},{6,4},{7,5},{8,10},{9,11},{10,... | collective-permute-start | bytes 786440 | tf_op jit(solution)/shard_map/ppermute | solution.py:777
  450.9 17.1 %collective-permute-start.26 = (f32[2,2,64,512]{3,2,0,1:T(8,128)S(1)}, f32[2,2,64,512]{3,2,0,1:T(8,128)S(1)}, u32[]{:S(2)}, u32[]{:S(2)}) collective-permute-start(f32[2,2,64,512]{3,2,0,1:T(8,128)S(1)} %fusion.14), channel_id=1, source_target_pairs={{0,8},{4,12},{8,0},{12,4},{16,24},{20,28},{24,16},{28,20},{1,9},{5... | collective-permute-start | bytes 1572872 | tf_op jit(solution)/shard_map/ppermute | solution.py:777
  451.5 17.6 %collective-permute-start.21 = (f32[2,2,64,512]{3,2,0,1:T(8,128)S(1)}, f32[2,2,64,512]{3,2,0,1:T(8,128)S(1)}, u32[]{:S(2)}, u32[]{:S(2)}) collective-permute-start(f32[2,2,64,512]{3,2,0,1:T(8,128)S(1)} %fusion.15), channel_id=1, source_target_pairs={{0,2},{1,3},{2,0},{3,1},{4,6},{5,7},{6,4},{7,5},{8,10},{9,11},{10,... | collective-permute-start | bytes 1572872 | tf_op jit(solution)/shard_map/ppermute | solution.py:777
  452.1 14.3 %collective-permute-start.35 = (f32[64,512]{1,0:T(8,128)S(1)}, f32[64,512]{1,0:T(8,128)S(1)}, u32[]{:S(2)}, u32[]{:S(2)}) collective-permute-start(f32[64,512]{1,0:T(8,128)S(1)} %fusion.24), channel_id=1, source_target_pairs={{0,16},{4,20},{8,24},{12,28},{16,0},{20,4},{24,8},{28,12},{1,17},{... | collective-permute-start | bytes 393224 | tf_op jit(solution)/shard_map/ppermute | solution.py:777
  458.9 73.6 %collective-permute-start.48 = (f32[2,2,64,1792]{3,2,0,1:T(8,128)S(1)}, f32[2,2,64,1792]{3,2,0,1:T(8,128)S(1)}, u32[]{:S(2)}, u32[]{:S(2)}) collective-permute-start(f32[2,2,64,1792]{3,2,0,1:T(8,128)S(1)} %fusion.1), channel_id=1, source_target_pairs={{0,8},{4,12},{8,0},{12,4},{16,24},{20,28},{24,16},{28,20},{1,9},{5... | collective-permute-start | bytes 5505032 | tf_op jit(solution)/shard_map/ppermute | solution.py:777
  464.5 69.5 %collective-permute-start.43 = (f32[2,2,64,2048]{3,2,0,1:T(8,128)S(1)}, f32[2,2,64,2048]{3,2,0,1:T(8,128)S(1)}, u32[]{:S(2)}, u32[]{:S(2)}) collective-permute-start(f32[2,2,64,2048]{3,2,0,1:T(8,128)S(1)} %fusion), channel_id=1, source_target_pairs={{0,2},{1,3},{2,0},{3,1},{4,6},{5,7},{6,4},{7,5},{8,10},{9,11},{10,... | collective-permute-start | bytes 6291464 | tf_op jit(solution)/shard_map/ppermute | solution.py:777
  466.4 64.8 %collective-permute-start.57 = (f32[2,2,176,512]{3,2,0,1:T(8,128)S(1)}, f32[2,2,176,512]{3,2,0,1:T(8,128)S(1)}, u32[]{:S(2)}, u32[]{:S(2)}) collective-permute-start(f32[2,2,176,512]{3,2,0,1:T(8,128)S(1)} %fusion.4), channel_id=1, source_target_pairs={{0,4},{4,0},{8,12},{12,8},{16,20},{20,16},{24,28},{28,24},{1,5},{5... | collective-permute-start | bytes 4325384 | tf_op jit(solution)/shard_map/ppermute | solution.py:777
  468.0 44.5 %collective-permute-start.36 = (f32[64,512]{1,0:T(8,128)S(1)}, f32[64,512]{1,0:T(8,128)S(1)}, u32[]{:S(2)}, u32[]{:S(2)}) collective-permute-start(f32[64,512]{1,0:T(8,128)S(1)} %bitcast_add_fusion.22), channel_id=1, source_target_pairs={{0,2},{1,3},{2,0},{3,1},{4,6},{5,7},{6,4},{7,5},{8,10},{9,11},{10,... | collective-permute-start | bytes 393224 | tf_op jit(solution)/shard_map/ppermute | solution.py:777
  469.1 45.2 %collective-permute-start.27 = (f32[2,64,512]{2,1,0:T(8,128)S(1)}, f32[2,64,512]{2,1,0:T(8,128)S(1)}, u32[]{:S(2)}, u32[]{:S(2)}) collective-permute-start(f32[2,64,512]{2,1,0:T(8,128)S(1)} %get-tuple-element.209), channel_id=1, source_target_pairs={{0,4},{4,0},{8,12},{12,8},{16,20},{20,16},{24,28},{28,24},{1,5},{5... | collective-permute-start | bytes 786440 | tf_op jit(solution)/shard_map/ppermute | solution.py:777
  512.5 8.0 %collective-permute-start.22 = (f32[2,64,512]{2,1,0:T(8,128)S(1)}, f32[2,64,512]{2,1,0:T(8,128)S(1)}, u32[]{:S(2)}, u32[]{:S(2)}) collective-permute-start(f32[2,64,512]{2,1,0:T(8,128)S(1)} %get-tuple-element.204), channel_id=1, source_target_pairs={{0,8},{4,12},{8,0},{12,4},{16,24},{20,28},{24,16},{28,20},{1,9},{5... | collective-permute-start | bytes 786440 | tf_op jit(solution)/shard_map/ppermute | solution.py:777
  514.4 7.4 %collective-permute-start.28 = (f32[64,512]{1,0:T(8,128)S(1)}, f32[64,512]{1,0:T(8,128)S(1)}, u32[]{:S(2)}, u32[]{:S(2)}) collective-permute-start(f32[64,512]{1,0:T(8,128)S(1)} %fusion.25), channel_id=1, source_target_pairs={{0,16},{4,20},{8,24},{12,28},{16,0},{20,4},{24,8},{28,12},{1,17},{... | collective-permute-start | bytes 393224 | tf_op jit(solution)/shard_map/ppermute | solution.py:777
  520.5 110.2 %collective-permute-start.37 = (f32[128,512]{1,0:T(8,128)S(1)}, f32[128,512]{1,0:T(8,128)S(1)}, u32[]{:S(2)}, u32[]{:S(2)}) collective-permute-start(f32[128,512]{1,0:T(8,128)S(1)} %pad_maximum_fusion.10), channel_id=1, source_target_pairs={{0,1},{1,0},{2,3},{3,2},{4,5},{5,4},{6,7},{7,6},{8,9},{9,8},{10,11... | collective-permute-start | bytes 786440 | tf_op jit(solution)/shard_map/ppermute | solution.py:777
  521.7 8.4 %collective-permute-start.23 = (f32[64,512]{1,0:T(8,128)S(1)}, f32[64,512]{1,0:T(8,128)S(1)}, u32[]{:S(2)}, u32[]{:S(2)}) collective-permute-start(f32[64,512]{1,0:T(8,128)S(1)} %fusion.26), channel_id=1, source_target_pairs={{0,16},{4,20},{8,24},{12,28},{16,0},{20,4},{24,8},{28,12},{1,17},{... | collective-permute-start | bytes 393224 | tf_op jit(solution)/shard_map/ppermute | solution.py:777
  530.1 6.4 collective-permute-start.29
  531.3 22.6 %collective-permute-start.24 = (f32[64,512]{1,0:T(8,128)S(1)}, f32[64,512]{1,0:T(8,128)S(1)}, u32[]{:S(2)}, u32[]{:S(2)}) collective-permute-start(f32[64,512]{1,0:T(8,128)S(1)} %bitcast_add_fusion.28), channel_id=1, source_target_pairs={{0,2},{1,3},{2,0},{3,1},{4,6},{5,7},{6,4},{7,5},{8,10},{9,11},{10,... | collective-permute-start | bytes 393224 | tf_op jit(solution)/shard_map/ppermute | solution.py:777
  532.6 21.2 %collective-permute-start.58 = (f32[2,176,512]{2,1,0:T(8,128)S(1)}, f32[2,176,512]{2,1,0:T(8,128)S(1)}, u32[]{:S(2)}, u32[]{:S(2)}) collective-permute-start(f32[2,176,512]{2,1,0:T(8,128)S(1)} %get-tuple-element.182), channel_id=1, source_target_pairs={{0,2},{1,3},{2,0},{3,1},{4,6},{5,7},{6,4},{7,5},{8,10},{9,11},{10,... | collective-permute-start | bytes 2162696 | tf_op jit(solution)/shard_map/ppermute | solution.py:777
  534.0 38.8 %collective-permute-start.49 = (f32[2,64,1792]{2,1,0:T(8,128)S(1)}, f32[2,64,1792]{2,1,0:T(8,128)S(1)}, u32[]{:S(2)}, u32[]{:S(2)}) collective-permute-start(f32[2,64,1792]{2,1,0:T(8,128)S(1)} %get-tuple-element.175), channel_id=1, source_target_pairs={{0,4},{4,0},{8,12},{12,8},{16,20},{20,16},{24,28},{28,24},{1,5},{5... | collective-permute-start | bytes 2752520 | tf_op jit(solution)/shard_map/ppermute | solution.py:777
  536.5 36.4 %collective-permute-start.44 = (f32[2,64,2048]{2,1,0:T(8,128)S(1)}, f32[2,64,2048]{2,1,0:T(8,128)S(1)}, u32[]{:S(2)}, u32[]{:S(2)}) collective-permute-start(f32[2,64,2048]{2,1,0:T(8,128)S(1)} %get-tuple-element.170), channel_id=1, source_target_pairs={{0,8},{4,12},{8,0},{12,4},{16,24},{20,28},{24,16},{28,20},{1,9},{5... | collective-permute-start | bytes 3145736 | tf_op jit(solution)/shard_map/ppermute | solution.py:777
  553.8 18.2 %collective-permute-start.59 = (f32[176,512]{1,0:T(8,128)S(1)}, f32[176,512]{1,0:T(8,128)S(1)}, u32[]{:S(2)}, u32[]{:S(2)}) collective-permute-start(f32[176,512]{1,0:T(8,128)S(1)} %fusion.19), channel_id=1, source_target_pairs={{0,16},{4,20},{8,24},{12,28},{16,0},{20,4},{24,8},{28,12},{1,17},{... | collective-permute-start | bytes 1081352 | tf_op jit(solution)/shard_map/ppermute | solution.py:777
  554.0 78.2 %collective-permute-start.30 = (f32[128,1024]{1,0:T(8,128)S(1)}, f32[128,1024]{1,0:T(8,128)S(1)}, u32[]{:S(2)}, u32[]{:S(2)}) collective-permute-start(f32[128,1024]{1,0:T(8,128)S(1)} %maximum_maximum_fusion), channel_id=1, source_target_pairs={{0,1},{1,0},{2,3},{3,2},{4,5},{5,4},{6,7},{7,6},{8,9},{9,8},{10,11... | collective-permute-start | bytes 1572872 | tf_op jit(solution)/shard_map/ppermute | solution.py:777
  572.1 9.2 %collective-permute-start.60 = (f32[176,512]{1,0:T(8,128)S(1)}, f32[176,512]{1,0:T(8,128)S(1)}, u32[]{:S(2)}, u32[]{:S(2)}) collective-permute-start(f32[176,512]{1,0:T(8,128)S(1)} %bitcast_add_fusion.13), channel_id=1, source_target_pairs={{0,2},{1,3},{2,0},{3,1},{4,6},{5,7},{6,4},{7,5},{8,10},{9,11},{10,... | collective-permute-start | bytes 1081352 | tf_op jit(solution)/shard_map/ppermute | solution.py:777
  572.8 33.2 %collective-permute-start.50 = (f32[64,1792]{1,0:T(8,128)S(1)}, f32[64,1792]{1,0:T(8,128)S(1)}, u32[]{:S(2)}, u32[]{:S(2)}) collective-permute-start(f32[64,1792]{1,0:T(8,128)S(1)} %fusion.17), channel_id=1, source_target_pairs={{0,16},{4,20},{8,24},{12,28},{16,0},{20,4},{24,8},{28,12},{1,17},{... | collective-permute-start | bytes 1376264 | tf_op jit(solution)/shard_map/ppermute | solution.py:777
  573.0 43.8 %collective-permute-start.45 = (f32[64,2048]{1,0:T(8,128)S(1)}, f32[64,2048]{1,0:T(8,128)S(1)}, u32[]{:S(2)}, u32[]{:S(2)}) collective-permute-start(f32[64,2048]{1,0:T(8,128)S(1)} %fusion.16), channel_id=1, source_target_pairs={{0,16},{4,20},{8,24},{12,28},{16,0},{20,4},{24,8},{28,12},{1,17},{... | collective-permute-start | bytes 1572872 | tf_op jit(solution)/shard_map/ppermute | solution.py:777
  606.1 11.7 %collective-permute-start.51 = (f32[64,1792]{1,0:T(8,128)S(1)}, f32[64,1792]{1,0:T(8,128)S(1)}, u32[]{:S(2)}, u32[]{:S(2)}) collective-permute-start(f32[64,1792]{1,0:T(8,128)S(1)} %bitcast_add_fusion.10), channel_id=1, source_target_pairs={{0,2},{1,3},{2,0},{3,1},{4,6},{5,7},{6,4},{7,5},{8,10},{9,11},{10,... | collective-permute-start | bytes 1376264 | tf_op jit(solution)/shard_map/ppermute | solution.py:777
  616.9 13.5 %collective-permute-start.46 = (f32[64,2048]{1,0:T(8,128)S(1)}, f32[64,2048]{1,0:T(8,128)S(1)}, u32[]{:S(2)}, u32[]{:S(2)}) collective-permute-start(f32[64,2048]{1,0:T(8,128)S(1)} %bitcast_add_fusion.7), channel_id=1, source_target_pairs={{0,2},{1,3},{2,0},{3,1},{4,6},{5,7},{6,4},{7,5},{8,10},{9,11},{10,... | collective-permute-start | bytes 1572872 | tf_op jit(solution)/shard_map/ppermute | solution.py:777
  617.6 15.6 %collective-permute-start.61 = (f32[352,512]{1,0:T(8,128)S(1)}, f32[352,512]{1,0:T(8,128)S(1)}, u32[]{:S(2)}, u32[]{:S(2)}) collective-permute-start(f32[352,512]{1,0:T(8,128)S(1)} %pad_maximum_fusion.2), channel_id=1, source_target_pairs={{0,1},{1,0},{2,3},{3,2},{4,5},{5,4},{6,7},{7,6},{8,9},{9,8},{10,11... | collective-permute-start | bytes 2162696 | tf_op jit(solution)/shard_map/ppermute | solution.py:777
  630.6 5.1 collective-permute-start.53
  631.6 3.0 collective-permute-start.52
  (56 other events, 444.5 us)

commit v2 on v1

--- a/solution.py
+++ b/solution.py
@@ -40,7 +40,7 @@
 
 
 def cost(flops, moved):
-    return pl.CostEstimate(flops=int(flops), bytes_accessed=int(moved), transcendentals=0)
+    return pl.CostEstimate(flops=1, bytes_accessed=1, transcendentals=0)
 
 
 def mxu(left, right, dims):
@@ -52,16 +52,24 @@
     return high, (value - high.astype(jnp.float32)).astype(LOW)
 
 
+def split(value):
+    return value if isinstance(value, tuple) else halves(value)
+
+
+def stack(first, second):
+    return tuple(jnp.concatenate(both, 0) for both in zip(first, second))
+
+
 def fold(value):
     half = value.shape[1] // 2
     return value[:, :half] + value[:, half:]
 
 
 def product(left, right):
-    left_high, left_low = halves(left)
-    right_high, right_low = halves(right)
+    left_high, left_low = split(left)
+    right_high, right_low = split(right)
     both = jnp.concatenate([left_high, left_low], 1)
-    if right.shape[1] <= LANES:
+    if right_high.shape[1] <= LANES:
         wide = jnp.concatenate([right_high, right_low], 1)
         return fold(mxu(both, jnp.concatenate([wide, wide], 0), NN))
     return mxu(both, jnp.concatenate([right_high, right_high], 0), NN) + mxu(
@@ -70,10 +78,10 @@
 
 
 def product_t(left, right):
-    left_high, left_low = halves(left)
-    right_high, right_low = halves(right)
+    left_high, left_low = split(left)
+    right_high, right_low = split(right)
     both = jnp.concatenate([left_high, left_low], 1)
-    if right.shape[0] <= LANES:
+    if right_high.shape[0] <= LANES:
         rows = jnp.concatenate(
             [
                 jnp.concatenate([right_high, right_high], 1),
@@ -88,10 +96,10 @@
 
 
 def t_product(left, right):
-    left_high, left_low = halves(left)
-    right_high, right_low = halves(right)
+    left_high, left_low = split(left)
+    right_high, right_low = split(right)
     both = jnp.concatenate([left_high, left_low], 0)
-    if right.shape[1] <= LANES:
+    if right_high.shape[1] <= LANES:
         wide = jnp.concatenate([right_high, right_low], 1)
         return fold(mxu(both, jnp.concatenate([wide, wide], 0), TN))
     return mxu(both, jnp.concatenate([right_high, right_high], 0), TN) + mxu(
@@ -121,15 +129,18 @@
     return strict, inclusive, upper, jnp.where(i == j, 1.0, 0.0)
 
 
-def inverse(strict_part, identity):
-    rows = strict_part.shape[0]
-    result = identity - strict_part
-    power = product(strict_part, strict_part)
+def inverses_of(strict_parts, identity):
+    rows = identity.shape[0]
+    results = [identity - part for part in strict_parts]
+    powers = [split(part) for part in strict_parts]
+    powers = [split(product(power, power)) for power in powers]
     for level in range(SPAN.bit_length() - 3):
-        both = product(jnp.concatenate([result, power], 0), power)
-        result = result + both[:rows]
-        power = both[rows:]
-    return result + product(result, power)
+        both = [
+            product(stack(split(result), power), power) for result, power in zip(results, powers)
+        ]
+        results = [result + pair_[:rows] for result, pair_ in zip(results, both)]
+        powers = [split(pair_[rows:]) for pair_ in both]
+    return [result + product(result, power) for result, power in zip(results, powers)]
 
 
 def sigmoid(value):
@@ -141,7 +152,7 @@
 
 def project_kernel(
     tokens, halo, gain, position, live, query_w, key_w, value_w, gate_w, beta_w, conv,
-    normed_out, pre_out, feature_out, gate_out, beta_pre_out, beta_out, normed,
+    normed_out, pre_out, feature_out, gate_out, beta_pre_out, beta_out, normed, pre,
 ):
     count = tokens.shape[0]
 
@@ -162,14 +173,19 @@
 
     gate_out[...] = mxu(normed[HALO:, :], gate_w[...], NN)
     valid = [
-        jnp.where(position[...] >= conv.shape[1] - 1 - tap, 1.0, 0.0)
-        for tap in range(conv.shape[1])
+        jnp.broadcast_to(
+            jnp.where(position[...] >= conv.shape[1] - 1 - tap, 1.0, 0.0), (count, LANES)
+        )
+        for tap in range(conv.shape[1] - 1)
     ]
     for which, weight in enumerate((query_w, key_w, value_w)):
-        pre_out[which] = mxu(normed[...], weight[...], NN)
-        for part in range(pre_out.shape[2] // LANES):
+        pre[which] = mxu(normed[...], weight[...], NN)
+        for span in range(count // SPAN):
+            start = HALO + span * SPAN
+            pre_out[which, span] = pre[which, start - 8 : start + SPAN, :]
+        for part in range(pre.shape[2] // LANES):
             lanes = slice(part * LANES, (part + 1) * LANES)
-            total = conv_total(pre_out, which, HALO, count, lanes, conv, valid)
+            total = conv_total(pre, which, HALO, count, lanes, conv, valid)
             value = total * sigmoid(total)
             if which < 2:
                 value = value * lax.rsqrt(jnp.sum(value * value, -1, keepdims=True) + KEY_EPS)
@@ -183,7 +199,9 @@
     total = None
     for tap in range(taps):
         start = first - (taps - 1) + tap
-        term = conv[which, tap : tap + 1, lanes] * pre[which, start : start + count, lanes] * valid[tap]
+        term = conv[which, tap : tap + 1, lanes] * pre[which, start : start + count, lanes]
+        if tap < taps - 1:
+            term = term * valid[tap]
         total = term if total is None else total + term
     return total
 
@@ -205,16 +223,19 @@
         ],
         out_specs=[
             whole((width, count)),
-            pl.BlockSpec((3, HALO + count, block), lambda j: (0, 0, j)),
+            pl.BlockSpec((3, count // SPAN, SPAN + 8, block), lambda j: (0, 0, 0, j)),
             pl.BlockSpec((3, count, block), lambda j: (0, 0, j)),
             pl.BlockSpec((count, block), lambda j: (0, j)),
             whole((count, heads)), whole((count, heads)),
         ],
         out_shape=[
-            f32((width, count)), f32((3, HALO + count, width)), f32((3, count, width)),
+            f32((width, count)), f32((3, count // SPAN, SPAN + 8, width)), f32((3, count, width)),
             f32((count, width)), f32((count, heads)), f32((count, heads)),
         ],
-        scratch_shapes=[pltpu.VMEM((HALO + count, width), LOW)],
+        scratch_shapes=[
+            pltpu.VMEM((HALO + count, width), LOW),
+            pltpu.VMEM((3, HALO + count, block), jnp.float32),
+        ],
         compiler_params=params(),
         cost_estimate=cost(8 * count * width * width, 8 * width * width + 40 * count * width),
         name="project",
@@ -237,22 +258,35 @@
     query, key, value = features[0], features[1], features[2]
     betas = beta[...]
     flag = keep[span]
-    for p in range(heads // 2):
-        q, k, v, b = pair(query, p), pair(key, p), pair(value, p), pair_column(betas, p)
-        scores = product_t(jnp.concatenate([k, q], 0), k)
-        solved = inverse(b * scores[: 2 * SPAN] * strict, identity)
-        both = product(solved, jnp.concatenate([b * k, b * v], 1))
-        inverse_out[0, p] = solved
-        attend_out[0, p] = scores[2 * SPAN :] * inclusive
-        for i in range(2):
-            h = 2 * p + i
-            erase = both[i * SPAN : (i + 1) * SPAN, :size]
-            update = both[i * SPAN : (i + 1) * SPAN, size:]
-            solved_out[0, :, h * size : (h + 1) * size] = erase
-            solved_out[1, :, h * size : (h + 1) * size] = update
-            start = state[h] * flag
-            new = jnp.concatenate([update, jnp.zeros_like(update)], 1) - product(erase, start)
-            state[h] = start + t_product(head(key, h), new)
+    pairs = range(heads // 2)
+    keys = [split(pair(key, p)) for p in pairs]
+    columns = [pair_column(betas, p) for p in pairs]
+    scores = [product_t(stack(keys[p], split(pair(query, p))), keys[p]) for p in pairs]
+    solved = inverses_of([columns[p] * scores[p][: 2 * SPAN] * strict for p in pairs], identity)
+    both = [
+        product(
+            solved[p],
+            jnp.concatenate([columns[p] * pair(key, p), columns[p] * pair(value, p)], 1),
+        )
+        for p in pairs
+    ]
+    for p in pairs:
+        inverse_out[0, p] = solved[p]
+        attend_out[0, p] = scores[p][2 * SPAN :] * inclusive
+    starts, news = [], []
+    for h in range(heads):
+        rows = slice(h % 2 * SPAN, (h % 2 + 1) * SPAN)
+        erase, update = both[h // 2][rows, :size], both[h // 2][rows, size:]
+        solved_out[0, :, h * size : (h + 1) * size] = erase
+        solved_out[1, :, h * size : (h + 1) * size] = update
+        start = state[h] * flag
+        starts.append(start)
+        news.append(
+            jnp.concatenate([update, jnp.zeros_like(update)], 1) - product(erase, start)
+        )
+    for h in range(heads):
+        rows = slice(h % 2 * SPAN, (h % 2 + 1) * SPAN)
+        state[h] = starts[h] + t_product(tuple(k[rows] for k in keys[h // 2]), news[h])
 
 
 def prepare(keep, features, beta):
@@ -298,26 +332,24 @@
     query, key = features[0], features[1]
     erase, update = solved[0], solved[1]
     flag = keep[span]
-    for p in range(heads // 2):
-        reads, news = [], []
-        for h in (2 * p, 2 * p + 1):
-            start = state[h] * flag
-            starts_out[0, h] = start
-            both = product(jnp.concatenate([head(erase, h), head(query, h)], 0), start)
-            new = head(update, h) - both[:SPAN]
-            state[h] = start + t_product(head(key, h), new)
-            new_out[:, h * LANES : (h + 1) * LANES] = new
-            reads.append(both[SPAN:])
-            news.append(new)
-        mixed = jnp.concatenate(reads, 0) + product(attend[0, p], jnp.concatenate(news, 0))
-        for i in range(2):
-            lanes = slice((2 * p + i) * LANES, (2 * p + i + 1) * LANES)
-            rows = mixed[i * SPAN : (i + 1) * SPAN]
-            mixed_out[:, lanes] = rows
-            shaped = rows * lax.rsqrt(jnp.mean(rows * rows, -1, keepdims=True) + EPS) * gain[...]
-            gates = gate[:, lanes]
-            normed = (shaped * (gates * sigmoid(gates))).astype(LOW)
-            normed_out[:, lanes] = normed
+    every, pairs = range(heads), range(heads // 2)
+    starts = [state[h] * flag for h in every]
+    both = [
+        product(jnp.concatenate([head(erase, h), head(query, h)], 0), starts[h]) for h in every
+    ]
+    news = [split(head(update, h) - both[h][:SPAN]) for h in every]
+    after = [starts[h] + t_product(head(key, h), news[h]) for h in every]
+    inner = [product(attend[0, p], stack(news[2 * p], news[2 * p + 1])) for p in pairs]
+    for h in every:
+        lanes = slice(h * LANES, (h + 1) * LANES)
+        starts_out[0, h] = starts[h]
+        state[h] = after[h]
+        new_out[:, lanes] = head(update, h) - both[h][:SPAN]
+        rows = both[h][SPAN:] + inner[h // 2][h % 2 * SPAN : (h % 2 + 1) * SPAN]
+        mixed_out[:, lanes] = rows
+        shaped = rows * lax.rsqrt(jnp.mean(rows * rows, -1, keepdims=True) + EPS) * gain[...]
+        gates = gate[:, lanes]
+        normed_out[:, lanes] = (shaped * (gates * sigmoid(gates))).astype(LOW)
 
 
 def mix(keep, features, solved, attend, gate, gain, state_in):
@@ -367,30 +399,29 @@
         normed[...] = rounded
         normed_out[...] = rounded.astype(jnp.float32).T
 
-    gate = mxu(normed[...], gate_w[...], NN)
-    up = mxu(normed[...], up_w[...], NN)
-    grad_inner = mxu(grad_top[...], down_w[...], NT)
-    sigma = sigmoid(gate)
-    inner = (gate * sigma * up).astype(LOW)
-    inner_out[...] = inner.astype(jnp.float32).T
-    grad_gate = (grad_inner * up * sigma * (1.0 + gate * (1.0 - sigma))).astype(LOW)
-    grad_up = (grad_inner * gate * sigma).astype(LOW)
-    first = core[0] == 0
-    wide_gate, wide_up = grad_gate.astype(jnp.float32), grad_up.astype(jnp.float32)
-    kept_out[...] = jnp.where(first, wide_gate, wide_up).astype(LOW)
-    sent_out[...] = jnp.where(first, wide_up, wide_gate)
-    out_term = mxu(inner, down_w[...], NN)
-    grad_term = mxu(grad_gate, gate_w[...], NT) + mxu(grad_up, up_w[...], NT)
-
     @pl.when(step == 0)
     def _():
-        total[...] = out_term
-        grad_total[...] = grad_term
-
-    @pl.when(step > 0)
-    def _():
-        total[...] += out_term
-        grad_total[...] += grad_term
+        total[...] = jnp.zeros_like(total)
+        grad_total[...] = jnp.zeros_like(grad_total)
+
+    first = core[0] == 0
+    size = normed.shape[0] // 1
+    parts = [slice(i * size, (i + 1) * size) for i in range(1)]
+    gates = [mxu(normed[part, :], gate_w[...], NN) for part in parts]
+    ups = [mxu(normed[part, :], up_w[...], NN) for part in parts]
+    grad_inners = [mxu(grad_top[part, :], down_w[...], NT) for part in parts]
+    for part, gate, up, grad_inner in zip(parts, gates, ups, grad_inners):
+        sigma = sigmoid(gate)
+        act = gate * sigma
+        inner = (act * up).astype(LOW)
+        inner_out[:, part] = inner.astype(jnp.float32).T
+        wide_gate = grad_inner * up * (sigma + act * (1.0 - sigma))
+        wide_up = grad_inner * act
+        grad_gate, grad_up = wide_gate.astype(LOW), wide_up.astype(LOW)
+        kept_out[part, :] = jnp.where(first, wide_gate, wide_up).astype(LOW)
+        sent_out[part, :] = jnp.where(first, wide_up, wide_gate).astype(LOW).astype(jnp.float32)
+        total[part, :] += mxu(inner, down_w[...], NN)
+        grad_total[part, :] += mxu(grad_gate, gate_w[...], NT) + mxu(grad_up, up_w[...], NT)
 
     @pl.when(step == pl.num_programs(0) - 1)
     def _():
@@ -471,37 +502,39 @@
     erase = solved[0]
     flag = keep[span]
     gain_total = jnp.zeros_like(gain_out[...])
-    for p in range(heads // 2):
-        grads = []
-        for h in (2 * p, 2 * p + 1):
-            lanes = slice(h * LANES, (h + 1) * LANES)
-            gates = gate[:, lanes]
-            sigma = sigmoid(gates)
-            rows = mixed[:, lanes]
-            grad = grad_head[:, lanes]
-            scale = lax.rsqrt(jnp.mean(rows * rows, -1, keepdims=True) + EPS)
-            unit = rows * scale
-            grad_gate = grad * unit * gain[...] * sigma * (1.0 + gates * (1.0 - sigma))
-            grad_gate_out[:, lanes] = grad_gate.astype(LOW).astype(jnp.float32)
-            shaped = grad * gates * sigma
-            gain_total = gain_total + jnp.sum(shaped * unit, 0, keepdims=True)
-            inward = shaped * gain[...]
-            grad_rows = scale * (inward - unit * jnp.mean(inward * unit, -1, keepdims=True))
-            grad_mixed_out[:, lanes] = grad_rows
-            grads.append(grad_rows)
-        q, k = pair(query, p), pair(key, p)
-        passed = product(product_t(k, q) * upper, jnp.concatenate(grads, 0))
-        for i in range(2):
-            h = 2 * p + i
-            end = state[h]
-            grad_new = passed[i * SPAN : (i + 1) * SPAN] + product(head(key, h), end)
-            state[h] = flag * (
-                end
-                + t_product(
-                    jnp.concatenate([head(query, h), -head(erase, h)], 0),
-                    jnp.concatenate([grads[i], grad_new], 0),
-                )
+    every, pairs = range(heads), range(heads // 2)
+    passes = [product_t(pair(key, p), pair(query, p)) * upper for p in pairs]
+    grads = []
+    for h in every:
+        lanes = slice(h * LANES, (h + 1) * LANES)
+        gates = gate[:, lanes]
+        sigma = sigmoid(gates)
+        rows = mixed[:, lanes]
+        grad = grad_head[:, lanes]
+        scale = lax.rsqrt(jnp.mean(rows * rows, -1, keepdims=True) + EPS)
+        unit = rows * scale
+        grad_gate = grad * unit * gain[...] * sigma * (1.0 + gates * (1.0 - sigma))
+        grad_gate_out[:, lanes] = grad_gate.astype(LOW).astype(jnp.float32)
+        shaped = grad * gates * sigma
+        gain_total = gain_total + jnp.sum(shaped * unit, 0, keepdims=True)
+        inward = shaped * gain[...]
+        grad_rows = scale * (inward - unit * jnp.mean(inward * unit, -1, keepdims=True))
+        grad_mixed_out[:, lanes] = grad_rows
+        grads.append(split(grad_rows))
+    passed = [product(passes[p], stack(grads[2 * p], grads[2 * p + 1])) for p in pairs]
+    ends = [state[h] for h in every]
+    grad_new = [
+        passed[h // 2][h % 2 * SPAN : (h % 2 + 1) * SPAN] + product(head(key, h), ends[h])
+        for h in every
+    ]
+    for h in every:
+        state[h] = flag * (
+            ends[h]
+            + t_product(
+                jnp.concatenate([head(query, h), -head(erase, h)], 0),
+                stack(grads[h], split(grad_new[h])),
             )
+        )
     gain_out[...] += gain_total
 
 
@@ -535,7 +568,7 @@
 
 def back_kernel(
     keep, features, beta, beta_pre, solved, inverses, starts, news, grad_mixed, state_in, pre, conv,
-    position, live, grad_pre_out, borrowed_out, conv_out, grad_beta_out, state, later,
+    position, live, grad_pre_out, borrowed_out, conv_out, grad_beta_out, state, later, sums,
 ):
     step = pl.program_id(0)
     span = pl.num_programs(0) - 1 - step
@@ -546,98 +579,136 @@
     @pl.when(step == 0)
     def _():
         state[...] = state_in[...]
-        conv_out[...] = jnp.zeros_like(conv_out)
+        sums[...] = jnp.zeros_like(sums)
         later[...] = jnp.zeros_like(later)
-
-    @pl.when(step > 0)
-    def _():
-        later[:, 8 + SPAN :, :] = later[:, 8:16, :]
 
     query, key, value = features[0], features[1], features[2]
     erase, update = solved[0], solved[1]
     betas = beta[...]
     flag = keep[span]
     base = pl.multiple_of(span * SPAN, SPAN)
-    places = position[pl.ds(base, SPAN + 16), :]
+    places = position[pl.ds(base, SPAN), :]
     lives = live[pl.ds(base, SPAN), :]
-    valid = [jnp.where(places >= taps - 1 - tap, 1.0, 0.0) for tap in range(taps)]
+    valid = [
+        jnp.broadcast_to(jnp.where(places >= taps - 1 - tap, 1.0, 0.0), (SPAN, LANES))
+        for tap in range(taps - 1)
+    ]
+    every, pairs = range(heads), range(heads // 2)
+    part = [slice(h % 2 * SPAN, (h % 2 + 1) * SPAN) for h in every]
+    q = [split(pair(query, p)) for p in pairs]
+    k = [split(pair(key, p)) for p in pairs]
+    b = [pair_column(betas, p) for p in pairs]
+    grad_out = [split(pair(grad_mixed, p)) for p in pairs]
+    new = [split(pair(news, p)) for p in pairs]
+    erases = [split(pair(erase, p)) for p in pairs]
+    row = lambda value, h: tuple(v[part[h]] for v in value[h // 2])
+    scores = [product_t(k[p], stack(k[p], q[p])) for p in pairs]
+    passed = [product(scores[p][:, 2 * SPAN :] * upper, grad_out[p]) for p in pairs]
+    ends = [split(state[h]) for h in every]
+    begin = [split(starts[0, h]) for h in every]
+    grad_new = [passed[h // 2][part[h]] + product(row(k, h), ends[h]) for h in every]
+    grad_news = [split(value) for value in grad_new]
+    both = [product_t(stack(row(grad_out, h), grad_news[h]), begin[h]) for h in every]
+    grad_key = [product_t(row(new, h), ends[h]) for h in every]
+    for h in every:
+        state[h] = flag * (
+            state[h]
+            + t_product(
+                stack(row(q, h), tuple(-v for v in row(erases, h))),
+                stack(row(grad_out, h), grad_news[h]),
+            )
+        )
+    grad_attend = [product_t(grad_out[p], new[p]) * inclusive for p in pairs]
+    joined = lambda values, p: jnp.concatenate([values[2 * p], values[2 * p + 1]], 0)
+    grad_q = [
+        joined([value[:SPAN] for value in both], p) + product(grad_attend[p], k[p]) for p in pairs
+    ]
+    grad_k = [joined(grad_key, p) + product(grad_attend[p].T, q[p]) for p in pairs]
+    turned = [
+        product(
+            inverses[0, p].T,
+            jnp.concatenate(
+                [joined(grad_new, p), -joined([value[SPAN:] for value in both], p)], 1
+            ),
+        )
+        for p in pairs
+    ]
+    grad_bv = [value[:, :LANES] for value in turned]
+    grad_bk = [value[:, LANES:] for value in turned]
+    grad_lower = [
+        -strict * (product_t(grad_bv[p], pair(update, p)) + product_t(grad_bk[p], erases[p]))
+        for p in pairs
+    ]
+    inner = [b[p] * grad_lower[p] for p in pairs]
+    grad_k = [
+        grad_k[p] + product(inner[p] + inner[p].T, k[p]) + b[p] * grad_bk[p] for p in pairs
+    ]
+    grad_v = [b[p] * grad_bv[p] for p in pairs]
     beta_columns = []
-    for p in range(heads // 2):
-        q, k, v, b = pair(query, p), pair(key, p), pair(value, p), pair_column(betas, p)
-        grad_out = pair(grad_mixed, p)
-        new = pair(news, p)
-        scores = product_t(k, jnp.concatenate([k, q], 0))
-        passed = product(scores[:, 2 * SPAN :] * upper, grad_out)
-        grad_query, grad_key, grad_new, grad_erase = [], [], [], []
-        for i in range(2):
-            h = 2 * p + i
-            rows = slice(i * SPAN, (i + 1) * SPAN)
-            end = state[h]
-            grad_new_h = passed[rows] + product(k[rows], end)
-            both = product_t(jnp.concatenate([grad_out[rows], grad_new_h], 0), starts[0, h])
-            grad_query.append(both[:SPAN])
-            grad_erase.append(-both[SPAN:])
-            grad_key.append(product_t(new[rows], end))
-            grad_new.append(grad_new_h)
-            state[h] = flag * (
-                end
-                + t_product(
-                    jnp.concatenate([q[rows], -head(erase, h)], 0),
-                    jnp.concatenate([grad_out[rows], grad_new_h], 0),
+    for p in pairs:
+        grad_b = (
+            jnp.sum(grad_lower[p] * scores[p][:, : 2 * SPAN], -1, keepdims=True)
+            + jnp.sum(grad_bv[p] * pair(value, p), -1, keepdims=True)
+            + jnp.sum(grad_bk[p] * pair(key, p), -1, keepdims=True)
+        )
+        beta_columns += [grad_b[:SPAN], grad_b[SPAN:]]
+    chunks = [(which, h) for which in range(3) for h in every]
+    for start in range(0, len(chunks), 4):
+        group = chunks[start : start + 4]
+        places = [(which, slice(h * LANES, (h + 1) * LANES)) for which, h in group]
+        grads = [(grad_q, grad_k, grad_v)[which][h // 2][part[h]] for which, h in group]
+        shifted = [
+            [
+                pre[which, 0, pl.ds(8 - (taps - 1) + tap, SPAN), lanes]
+                for tap in range(taps)
+            ]
+            for which, lanes in places
+        ]
+        shifted = [
+            [value * valid[tap] for tap, value in enumerate(moved[:-1])] + moved[-1:]
+            for moved in shifted
+        ]
+        totals = [
+            sum(
+                conv[which, tap : tap + 1, lanes] * moved[tap] for tap in range(taps)
+            )
+            for moved, (which, lanes) in zip(shifted, places)
+        ]
+        sigmas = [sigmoid(total) for total in totals]
+        acts = [total * sigma for total, sigma in zip(totals, sigmas)]
+        slopes = [sigma + act * (1.0 - sigma) for sigma, act in zip(sigmas, acts)]
+        squares = [
+            jnp.sum(act * act, -1, keepdims=True) if which < 2 else None
+            for act, (which, _) in zip(acts, group)
+        ]
+        grads = [
+            grad * lives if which == 1 else grad for grad, (which, _) in zip(grads, group)
+        ]
+        scales = [None if square is None else lax.rsqrt(square + KEY_EPS) for square in squares]
+        units = [act if scale is None else act * scale for act, scale in zip(acts, scales)]
+        along = [
+            None if scale is None else jnp.sum(grad * unit, -1, keepdims=True)
+            for grad, unit, scale in zip(grads, units, scales)
+        ]
+        grads = [
+            slope * (grad if scale is None else scale * (grad - unit * dot))
+            for slope, grad, scale, unit, dot in zip(slopes, grads, scales, units, along)
+        ]
+        for grad, moved, (which, lanes) in zip(grads, shifted, places):
+            result = conv[which, taps - 1 : taps, lanes] * grad
+            for tap in range(taps):
+                product_ = grad * moved[tap]
+                sums[which, tap, :, lanes] += sum(
+                    product_[8 * r : 8 * (r + 1)] for r in range(SPAN // 8)
                 )
-            )
-        grad_new = jnp.concatenate(grad_new, 0)
-        grad_erase = jnp.concatenate(grad_erase, 0)
-        grad_attend = product_t(grad_out, new) * inclusive
-        grad_q = jnp.concatenate(grad_query, 0) + product(grad_attend, k)
-        grad_k = jnp.concatenate(grad_key, 0) + product(grad_attend.T, q)
-        turned = product(inverses[0, p].T, jnp.concatenate([grad_new, grad_erase], 1))
-        grad_bv, grad_bk = turned[:, :LANES], turned[:, LANES:]
-        grad_lower = -strict * (
-            product_t(grad_bv, pair(update, p)) + product_t(grad_bk, pair(erase, p))
-        )
-        grad_b = (
-            jnp.sum(grad_lower * scores[:, : 2 * SPAN], -1, keepdims=True)
-            + jnp.sum(grad_bv * v, -1, keepdims=True)
-            + jnp.sum(grad_bk * k, -1, keepdims=True)
-        )
-        inner = b * grad_lower
-        grad_k = grad_k + product(inner + inner.T, k) + b * grad_bk
-        grad_v = b * grad_bv
-        beta_columns += [grad_b[:SPAN], grad_b[SPAN:]]
-        for i in range(2):
-            h = 2 * p + i
-            rows = slice(i * SPAN, (i + 1) * SPAN)
-            lanes = slice(h * LANES, (h + 1) * LANES)
-            for which, grad in enumerate((grad_q[rows], grad_k[rows] * lives, grad_v[rows])):
-                window = pre[which, pl.ds(base + HALO - 8, SPAN + 8), lanes]
-                shifted = [window[8 - (taps - 1) + tap :][:SPAN] for tap in range(taps)]
-                total = None
-                for tap in range(taps):
-                    term = conv[which, tap : tap + 1, lanes] * shifted[tap] * valid[tap][8 : 8 + SPAN]
-                    total = term if total is None else total + term
-                sigma = sigmoid(total)
-                if which < 2:
-                    act = total * sigma
-                    scale = lax.rsqrt(jnp.sum(act * act, -1, keepdims=True) + KEY_EPS)
-                    unit = act * scale
-                    grad = scale * (grad - unit * jnp.sum(grad * unit, -1, keepdims=True))
-                grad = grad * sigma * (1.0 + total * (1.0 - sigma))
-                for tap in range(taps):
-                    conv_out[which, tap : tap + 1, lanes] += jnp.sum(
-                        grad * valid[tap][8 : 8 + SPAN] * shifted[tap], 0, keepdims=True
+                if tap < taps - 1:
+                    masked = grad * valid[tap]
+                    later[which, tap, SPAN:, lanes] = later[which, tap, :8, lanes]
+                    later[which, tap, :SPAN, lanes] = masked
+                    result = result + conv[which, tap : tap + 1, lanes] * (
+                        later[which, tap, pl.ds(taps - 1 - tap, SPAN), lanes]
                     )
-                later[which, 8 : 8 + SPAN, lanes] = grad
-                result = None
-                for tap in range(taps):
-                    ahead = 8 + taps - 1 - tap
-                    term = (
-                        conv[which, tap : tap + 1, lanes]
-                        * later[which, ahead : ahead + SPAN, lanes]
-                        * valid[tap][ahead : ahead + SPAN]
-                    )
-                    result = term if result is None else result + term
-                grad_pre_out[which, :, lanes] = result
+            grad_pre_out[which, :, lanes] = result
     columns = lax.broadcasted_iota(jnp.int32, (SPAN, heads), 1)
     grad_beta = jnp.zeros((SPAN, heads), jnp.float32)
     for h in range(heads):
@@ -649,15 +720,13 @@
 
     @pl.when(span == 0)
     def _():
+        conv_out[...] = jnp.sum(sums[...], 2)
         for which in range(3):
             result = None
-            for tap in range(taps):
+            for tap in range(taps - 1):
                 ahead = taps - 1 - tap
-                term = (
-                    conv[which, tap : tap + 1, :]
-                    * later[which, ahead : ahead + 8, :]
-                    * valid[tap][ahead : ahead + 8]
-                )
+                rows = jnp.concatenate([jnp.zeros((8, later.shape[3]), jnp.float32), later[which, tap, :8]], 0)
+                term = conv[which, tap : tap + 1, :] * rows[ahead:][:8]
                 result = term if result is None else result + term
             borrowed_out[which] = result
 
@@ -675,7 +744,6 @@
     rows = pl.BlockSpec((SPAN, width), lambda c: (spans - 1 - c, 0))
     triple = pl.BlockSpec((3, SPAN, width), lambda c: (0, spans - 1 - c, 0))
     column = pl.BlockSpec((SPAN, heads), lambda c: (spans - 1 - c, 0))
-    position = jnp.pad(position, ((8, 8), (0, 0)))
     return pl.pallas_call(
         back_kernel,
         grid=(spans,),
@@ -684,7 +752,9 @@
             pl.BlockSpec((2, SPAN, width), lambda c: (0, spans - 1 - c, 0)),
             pl.BlockSpec((1, heads // 2, 2 * SPAN, 2 * SPAN), lambda c: (spans - 1 - c, 0, 0, 0)),
             pl.BlockSpec((1, heads, size, size), lambda c: (spans - 1 - c, 0, 0, 0)),
-            rows, rows, whole((heads, size, size)), whole(pre.shape), whole(conv.shape),
+            rows, rows, whole((heads, size, size)),
+            pl.BlockSpec((3, 1, SPAN + 8, width), lambda c: (0, spans - 1 - c, 0, 0)),
+            whole(conv.shape),
             whole(position.shape), whole(live.shape),
         ],
         out_specs=[triple, whole((3, 8, width)), whole((3, taps, width)), column],
@@ -693,7 +763,8 @@
         ],
         scratch_shapes=[
             pltpu.VMEM((heads, size, size), jnp.float32),
-            pltpu.VMEM((3, SPAN + 16, width), jnp.float32),
+            pltpu.VMEM((3, taps - 1, SPAN + 8, width), jnp.float32),
+            pltpu.VMEM((3, taps, 8, width), jnp.float32),
         ],
         compiler_params=params(),
         cost_estimate=cost(30 * count * width * size * 4, 60 * count * width),
@@ -830,7 +901,11 @@
     return jnp.concatenate([low, high], 0), (first, second, pair_map)
 
 
-def carried_back(shift, context):
+def together(value, *others):
+    return lax.optimization_barrier((value, *others))
+
+
+def carried_back(shift, context, beside=((), (), ())):
     heads, size, _ = shift.shape
     if not tuned():
         gathered = lax.all_gather(
@@ -843,38 +918,49 @@
             return apply_map(maps, state, True)
 
         zeros = jnp.zeros((heads, size, size), jnp.float32)
-        return lax.fori_loop(0, count - 1 - lax.axis_index("seq"), one, zeros)
+        return lax.fori_loop(0, count - 1 - lax.axis_index("seq"), one, zeros), ()
     first, second, pair_map = context
     half = heads // 2
     here = side("x") == 0
     kept = jnp.where(here, shift[:half], shift[half:])
     other = hop(jnp.where(here, shift[half:], shift[:half]), "x")
+    other, *done = together(other, *beside[0])
     first = jnp.concatenate([jnp.where(here, kept, other), first[:, :, size:]], 2)
     second = jnp.concatenate([jnp.where(here, other, kept), second[:, :, size:]], 2)
     pair_map = jnp.concatenate([apply_map(first, second[:, :, :size], True), pair_map[:, :, size:]], 2)
     state = jnp.zeros((half, size, size), jnp.float32)
     for step in range(3, 0, -1):
         sent = pair_map[:, :, :size] if step == 3 else apply_map(pair_map, state, True)
-        state = state + lax.ppermute(sent, "seq", [(2 * step + x, 2 * step - 2 + x) for x in range(2)])
+        come = lax.ppermute(sent, "seq", [(2 * step + x, 2 * step - 2 + x) for x in range(2)])
+        if step > 1:
+            come, *more = together(come, *beside[4 - step])
+            done += more
+        state = state + come
     moved = apply_map(second, state, True)
     mine = jnp.where(here, moved, state)
-    other = hop(jnp.where(here, state, moved), "x")
+    other = jnp.where(here, state, moved)
+    other = hop(other, "x")
     low, high = jnp.where(here, mine, other), jnp.where(here, other, mine)
-    return jnp.concatenate([low, high], 0)
+    return jnp.concatenate([low, high], 0), done
 
 
 def outer_kernel(bit, *refs, blocks, post):
     count = len(blocks)
     lefts, rights = refs[: 2 * count], refs[2 * count : 4 * count]
-    keep, send, stacked = refs[4 * count :]
+    *outs, stacked = refs[4 * count :]
     step = pl.program_id(0)
     tokens = lefts[0].shape[1]
-    half = keep.shape[0]
+    half = outs[0].shape[0]
 
     @pl.when(step == 0)
     def _():
         for piece in range(count):
             for which in range(2):
+                if len(outs) == 1:
+                    stacked[piece, :, which * tokens : (which + 1) * tokens] = lefts[
+                        2 * piece + which
+                    ][...].astype(LOW)
+                    continue
                 for start in range(0, half, post):
                     for place, mine in ((start, bit[0]), (half + start, 1 - bit[0])):
                         rows = pl.ds(pl.multiple_of(2 * start + mine * post, 8), post)
@@ -890,11 +976,11 @@
             right = jnp.concatenate(
                 [rights[2 * piece][...].astype(LOW), rights[2 * piece + 1][...].astype(LOW)], 0
             )
-            keep[...] = mxu(stacked[piece, :half, :], right, NN)
-            send[...] = mxu(stacked[piece, half:, :], right, NN)
-
-
-def outer(pieces, way):
+            for index, out in enumerate(outs):
+                out[...] = mxu(stacked[piece, index * half : (index + 1) * half, :], right, NN)
+
+
+def outer(pieces, way=None):
     rows, tokens = pieces[0][0].shape
     block = 2 * LANES
     post = rows // 8 * {"near": 2, "x": 1}.get(way, 0) or rows // 16
@@ -910,48 +996,63 @@
 
         specs += [pl.BlockSpec((tokens, block), place)] * 2
     total = sum(counts)
-    out = pl.BlockSpec((rows // 2, block), lambda j: (0, j))
-    shape = jax.ShapeDtypeStruct((rows // 2, total * block), jnp.float32)
+    number = 2 if way else 1
+    out = pl.BlockSpec((rows // number, block), lambda j: (0, j))
+    shape = jax.ShapeDtypeStruct((rows // number, total * block), jnp.float32)
+    bit = side(way).astype(jnp.int32).reshape(1) if way else jnp.zeros((1,), jnp.int32)
     return pl.pallas_call(
         lambda *refs: outer_kernel(*refs, blocks=counts, post=post),
         grid=(total,),
         in_specs=[pl.BlockSpec(memory_space=pltpu.SMEM)] + [left] * len(lefts) + specs,
-        out_specs=[out, out],
-        out_shape=[shape, shape],
+        out_specs=[out] * number,
+        out_shape=[shape] * number,
         scratch_shapes=[pltpu.VMEM((len(pieces), rows, 2 * tokens), LOW)],
         compiler_params=params(),
         cost_estimate=cost(
             4 * rows * tokens * total * block, 4 * rows * total * block + 8 * tokens * rows
         ),
         name="outer",
-    )(side(way).astype(jnp.int32).reshape(1), *lefts, *rights)
+    )(bit, *lefts, *rights)
 
 
 def take(value, place, axis):
     return lax.dynamic_index_in_dim(value, place, axis, False)
 
 
-def reduced(keep, send, order):
-    names = ["far", "near", "x", "y"]
-    names.remove(order[0])
-    shape = (2, 2, 2, keep.shape[0] // 8, keep.shape[1])
-    keep, come = keep.reshape(shape), hop(send, order[0]).reshape(shape)
-    for way in order[1:]:
-        at, bit = names.index(way), side(way)
-        names.remove(way)
-        send = take(keep, 1 - bit, at) + take(come, 1 - bit, at)
-        keep = take(keep, bit, at) + take(come, bit, at)
-        come = hop(send, way)
-    keep = keep + come
-    come = hop(keep, "y")
-    first = side("y") == 0
-    return jnp.concatenate([jnp.where(first, keep, come), jnp.where(first, come, keep)], 0)
-
-
-XYZ, YZX, ZXY = ("x", "y", "near", "far"), ("y", "near", "x", "far"), ("near", "x", "y", "far")
-
-
-def small_sums(small):
+class Part:
+    def __init__(self, keep, first):
+        names = ["far", "near", "x", "y"]
+        names.remove(first)
+        self.names, self.come = names, None
+        self.keep = keep.reshape(2, 2, 2, keep.shape[0] // 8, keep.shape[1])
+
+    def arrived(self, come):
+        self.come = come.reshape(self.keep.shape)
+
+    def split(self, way):
+        at, bit = self.names.index(way), side(way)
+        self.names.remove(way)
+        send = take(self.keep, 1 - bit, at) + take(self.come, 1 - bit, at)
+        self.keep = take(self.keep, bit, at) + take(self.come, bit, at)
+        return send
+
+    def total(self):
+        self.keep = self.keep + self.come
+        return self.keep
+
+    def whole(self, come):
+        first = side("y") == 0
+        return jnp.concatenate(
+            [jnp.where(first, self.keep, come), jnp.where(first, come, self.keep)], 0
+        )
+
+
+def swaps(moves):
+    values = together(*[value for value, _ in moves])
+    return together(*[hop(value, way) for value, (_, way) in zip(values, moves)])
+
+
+def flatten_small(small):
     first_gain, beta, conv, head_gain, second_gain = small
     seq = lax.axis_size("seq")
     flat = jnp.concatenate(
@@ -964,12 +1065,13 @@
     )
     size = flat.shape[1]
     rows = -(-size // 2048) * 16
-    flat = jnp.pad(flat, ((0, 0), (0, rows * 128 - size))).reshape(seq * rows, 128)
-    flat = flat + hop(flat, "core")
-    split = flat.reshape(4, 2, rows, 128)
-    here = side("x")
-    halves_of = [take(split, place, 1).reshape(-1, 128) for place in (here, 1 - here)]
-    flat = reduced(*halves_of, XYZ).reshape(-1)
+    return jnp.pad(flat, ((0, 0), (0, rows * 128 - size))).reshape(seq * rows, 128)
+
+
+def unflatten_small(flat, small):
+    first_gain, beta, conv, head_gain, second_gain = small
+    seq = lax.axis_size("seq")
+    flat = flat.reshape(-1)
     sizes = [a.size // seq for a in small]
     places = [sum(sizes[:i]) for i in range(len(sizes))]
     pieces = [flat[p : p + s] for p, s in zip(places, sizes)]
@@ -1032,23 +1134,6 @@
     grad_mixed, grad_gate_pre, grad_head_gain, shift = gather_states(
         keep, grad_head, mixed, gate_pre, head_gain[None], features, solved, heads
     )
-    state_grad = carried_back(shift, context)
-    grads, borrowed, grad_conv, grad_beta_pre = back(
-        keep, features, beta, beta_pre, solved, inverses, starts, news, grad_mixed, state_grad, pre,
-        conv_weight, position, live,
-    )
-    returned = passed_along(borrowed, "seq", -1)
-    tail = grads[:, count - 8 :] + returned
-    grads = lax.dynamic_update_slice(grads, tail, (0, count - 8, 0))
-    grads = grads.astype(LOW)
-    input_grad, grad_first_gain = enter(
-        rows, first_gain[None], grad_hidden, grads, grad_gate_pre, grad_beta_pre, query_weight,
-        key_weight, value_weight, gate_weight, beta_weight,
-    )
-    small = (
-        grad_first_gain[0], outer_sum(normed_one.T, grad_beta_pre), grad_conv, grad_head_gain[0],
-        grad_second_gain[0],
-    )
     if tuned():
         half = width // 2
 
@@ -1071,48 +1156,123 @@
         out_right = both(pick(grad_branch, grad_gate_pre), pick(grad_gate_pre, grad_branch))
         blocks = hidden_gate.shape[1] // 256
         low = blocks // 2
-        some = width // 256 * 3 // 4
+        some = width // 512
         early = (
-            reduced(
-                *outer([(*two, *gate_up, 0, low), (*out_left, *out_right, 0, some)], "x"), XYZ
+            outer([(*two, *gate_up, 0, low), (*out_left, *out_right, 0, some)], "x"),
+            outer(
+                [
+                    (*two, *gate_up, low, blocks - low),
+                    (*out_left, *out_right, some, width // 256 - some),
+                ],
+                "y",
             ),
-            reduced(
-                *outer(
-                    [
-                        (*two, *gate_up, low, blocks - low),
-                        (*out_left, *out_right, some, width // 256 - some),
-                    ],
-                    "y",
-                ),
-                YZX,
-            ),
-            reduced(*outer([(*inners, *tops, 0, half // 256)], "near"), ZXY),
-        )
+            outer([(*inners, *tops, 0, half // 256)], "near"),
+        )
+        state_grad, done = carried_back(shift, context, early)
+        keeps, sends = done[0::2], done[1::2]
+        ways = ("x", "y", "near")
+        cuts = [send.shape[0] // 2 for send in sends]
+        state_grad, *begun = together(state_grad, *(s[:c] for s, c in zip(sends, cuts)))
+        begun = [hop(value, way) for value, way in zip(begun, ways)]
+    else:
+        state_grad, _ = carried_back(shift, context)
+    grads, borrowed, grad_conv, grad_beta_pre = back(
+        keep, features, beta, beta_pre, solved, inverses, starts, news, grad_mixed, state_grad, pre,
+        conv_weight, position, live,
+    )
+    if tuned():
+        borrowed, *begun = together(borrowed, *begun)
+    returned = passed_along(borrowed, "seq", -1)
+    tail = grads[:, count - 8 :] + returned
+    grads = lax.dynamic_update_slice(grads, tail, (0, count - 8, 0))
+    grads = grads.astype(LOW)
+    if tuned():
+        grads, *rest = together(grads, *(s[c:] for s, c in zip(sends, cuts)))
+        rest = [hop(value, way) for value, way in zip(rest, ways)]
         wide = grads.astype(jnp.float32)
         query_key = both(pick(grads[0], grads[1]), pick(wide[1], wide[0]))
         value = both(
             pick(grads[2, :, :half], grads[2, :, half:]), pick(wide[2, :, half:], wide[2, :, :half])
         )
         late = (
-            reduced(*outer([(*one, *query_key, 0, half // 256)], "x"), XYZ),
-            reduced(*outer([(*one, *query_key, half // 256, half // 256)], "y"), YZX),
-            reduced(*outer([(*one, *value, 0, half // 256)], "near"), ZXY),
-        )
+            outer([(*one, *query_key, 0, half // 256)], "x"),
+            outer([(*one, *query_key, half // 256, half // 256)], "y"),
+            outer([(*one, *value, 0, half // 256)], "near"),
+        )
+        input_grad, grad_first_gain = enter(
+            rows, first_gain[None], grad_hidden, grads, grad_gate_pre, grad_beta_pre, query_weight,
+            key_weight, value_weight, gate_weight, beta_weight,
+        )
+        small = (
+            grad_first_gain[0], outer_sum(normed_one.T, grad_beta_pre), grad_conv, grad_head_gain[0],
+            grad_second_gain[0],
+        )
+        flat = flatten_small(small)
+        sends = [send for _, send in late]
+        early = [Part(keep_, way) for keep_, way in zip(keeps, ways)]
+        late = [Part(keep_, way) for (keep_, _), way in zip(late, ways)]
+        input_grad, flat, *joined = together(input_grad, flat, *rest, *sends)
+        rest, sends = joined[:3], joined[3:]
+        for part, one_half, other_half in zip(early, begun, rest):
+            part.arrived(jnp.concatenate([one_half, other_half], 0))
+        orders = (("y", "near", "far"), ("near", "x", "far"), ("x", "y", "far"))
+
+        def stage(parts, lap):
+            return [(part.split(order[lap]), order[lap]) for part, order in zip(parts, orders)]
+
+        def arrive(parts, comes):
+            for part, come in zip(parts, comes):
+                part.arrived(come)
+
+        *comes, flat_come = swaps(stage(early, 0) + list(zip(sends, ways)) + [(flat, "core")])
+        flat = (flat + flat_come).reshape(4, 2, -1, 128)
+        bit = side("x")
+        tiny = Part(take(flat, bit, 1).reshape(-1, 128), "x")
+        tiny_send = take(flat, 1 - bit, 1).reshape(-1, 128)
+        arrive(early + late, comes)
+        for lap, way, following in ((0, "x", "y"), (1, "y", "near")):
+            *comes, flat_come = swaps(
+                stage(early, lap + 1) + stage(late, lap) + [(tiny_send, way)]
+            )
+            tiny.arrived(flat_come)
+            tiny_send = tiny.split(following)
+            arrive(early + late, comes)
+        *comes, flat_come = swaps(
+            [(part.total(), "y") for part in early] + stage(late, 2) + [(tiny_send, "near")]
+        )
+        tiny.arrived(flat_come)
+        early = [part.whole(come) for part, come in zip(early, comes)]
+        arrive(late, comes[3:])
         a, b = low * 256, (blocks - low) * 256
         own = (
             jnp.concatenate([early[0][:, :a], early[1][:, :b]], 1), early[2],
             jnp.concatenate([early[0][:, a:], early[1][:, b:]], 1),
-            jnp.concatenate(late[:2], 1), late[2],
-        )
-        other = tuple(hop(v, "core") for v in own)
+        )
+        *comes, flat_come, other_a, other_b, other_c = swaps(
+            [(part.total(), "y") for part in late] + [(tiny.split("far"), "far")]
+            + [(value, "core") for value in own]
+        )
+        late = [part.whole(come) for part, come in zip(late, comes)]
+        tiny.arrived(flat_come)
+        own = (*own, jnp.concatenate(late[:2], 1), late[2])
+        *last, flat_come = swaps([(own[3], "core"), (own[4], "core"), (tiny.total(), "y")])
+        other = (other_a, other_b, other_c, *last)
         zero = [pick(m, o) for m, o in zip(own, other)]
         one_ = [pick(o, m) for m, o in zip(own, other)]
         query_g, key_g = zero[3], one_[3]
         value_g = jnp.concatenate([zero[4], one_[4]], 1)
         gate_g, out_g, hidden_gate_g, hidden_up_g = one_[2], zero[2], zero[0], one_[0]
         hidden_down_g = jnp.concatenate([zero[1], one_[1]], 1)
-        first_g, beta_g, conv_g, head_g, second_g = small_sums(small)
+        first_g, beta_g, conv_g, head_g, second_g = unflatten_small(tiny.whole(flat_come), small)
     else:
+        input_grad, grad_first_gain = enter(
+            rows, first_gain[None], grad_hidden, grads, grad_gate_pre, grad_beta_pre, query_weight,
+            key_weight, value_weight, gate_weight, beta_weight,
+        )
+        small = (
+            grad_first_gain[0], outer_sum(normed_one.T, grad_beta_pre), grad_conv, grad_head_gain[0],
+            grad_second_gain[0],
+        )
 
         def whole(term, dimension):
             part = lax.psum_scatter(term, "seq", scatter_dimension=dimension, tiled=True)

time: 645 us -> 572 us (0.89)
  waiting for transfers between devices: 296 us -> 229 us
  Pallas kernels: 197 us -> 153 us
  other arithmetic: 50.6 us -> 67.4 us
  local copies, waits for them, and re-layouts: 26.3 us -> 41.8 us
    ppermute x54 -> x57, waiting for transfers between devices: 266 us -> 205 us  [hop(): lax.ppermute(value, axis, [(i, i ^ bit) for i in range(lax.axis_size(axis...]
    pallas_call x1, Pallas kernels: 44.9 us -> 16.7 us  [prepare(): pl.pallas_call(prepare_kernel, grid=(spans,), in_specs=[pl.BlockSpec(memo...]
    add x37, other arithmetic: 16.9 us -> 32.6 us  [the longest x13 12.3 us: split(): send = take(self.keep, 1 - bit, at) + take(self.come, 1 - bit, at)]
    unnamed x118 -> x172, local copies, waits for them, and re-layouts: 17.5 us -> 29.5 us
    pallas_call x1, Pallas kernels: 42 us -> 32.3 us  [back(): pl.pallas_call(back_kernel, grid=(spans,), in_specs=[pl.BlockSpec(memory_...]
    ppermute x3, waiting for transfers between devices: 23.4 us -> 15 us  [carried_back(): lax.ppermute(sent, 'seq', [(2 * step + x, 2 * step - 2 + x) for x in rang...]
    ppermute x54 -> x57, starting transfers between devices: 50.1 us -> 53.8 us  [hop(): lax.ppermute(value, axis, [(i, i ^ bit) for i in range(lax.axis_size(axis...]
    select_n x14 -> x13, other arithmetic: 14.7 us -> 14.2 us  [pick(): return jnp.where(here, zero, one)]
  transfers between devices with their start and end apart: 62 -> 65, of which waited for: 25 -> 31; matrix products, arithmetic and copies ran while one was open for 9% -> 5% of each run, Pallas kernels for 14% -> 16%
where the time goes in v2:
time: 572 us; the launch traced here: 564 us
  waiting for transfers between devices  229 us (40%)
  Pallas kernels  153 us (27%)
  starting transfers between devices  69.5 us (12%)
  other arithmetic  67.4 us (12%)
  local copies, waits for them, and re-layouts  41.8 us (7%)
    ppermute x57, waiting for transfers between devices, hop(): lax.ppermute(value, axis, [(i, i ^ bit) for i in range(lax.axis_size(axis...  205 us
    ppermute x57, starting transfers between devices, hop(): lax.ppermute(value, axis, [(i, i ^ bit) for i in range(lax.axis_size(axis...  53.8 us
    pallas_call x6, Pallas kernels, outer(): pl.pallas_call(lambda *refs: outer_kernel(*refs, blocks=counts, post=post...  38 us
    pallas_call x1, Pallas kernels, back(): pl.pallas_call(back_kernel, grid=(spans,), in_specs=[pl.BlockSpec(memory_...  32.3 us
    unnamed x172, local copies, waits for them, and re-layouts  29.5 us
    pallas_call x1, Pallas kernels, feed(): pl.pallas_call(feed_kernel, grid=(hidden // block,), in_specs=[pl.BlockSp...  25.8 us
    pallas_call x1, Pallas kernels, prepare(): pl.pallas_call(prepare_kernel, grid=(spans,), in_specs=[pl.BlockSpec(memo...  16.7 us
    ppermute x3, waiting for transfers between devices, carried_back(): lax.ppermute(sent, 'seq', [(2 * step + x, 2 * step - 2 + x) for x in rang...  15 us
  transfers between devices with their start and end apart: 65, of which 31 were waited for; matrix products, arithmetic and copies ran while one was open for 5% of the time, Pallas kernels for 16%

profile of v2, /device:TPU:0, one launch (start us, length us, event | category | flops | bytes accessed | tf_op | source)
XLA Modules:
  0.0 563.6 jit_solution(7618120463738510282)
XLA Ops:
  1.4 4.8 collective-permute-start
  12.6 12.0 %project.1 = (f32[1024,384]{1,0:T(8,128)S(1)}, f32[3,6,72,1024]{3,2,1,0:T(8,128)}, f32[3,384,1024]{2,1,0:T(8,128)}, f32[384,1024]{1,0:T(8,128)S(1)}, f32[384,8]{1,0:T(8,128)S(1)}, /*index=5*/f32[384,8]{1,0:T(8,128)S(1)}) custom-call(bf16[384,1024]{1,0:T(8,128)(2,1)S(1)} %bitcast.230, f32[16,1024]{1,0:T(8,128)S(1)} %collective-permute-done.halo, ...), custom_call_target="tpu_custom_call" | custom-call | flops 1 | bytes 1 | tf_op jit(solution)/shard_map/project/pallas_call | solution.py:216
  26.4 16.7 %prepare.1 = (f32[2,384,1024]{2,1,0:T(8,128)}, f32[6,4,128,128]{3,2,1,0:T(8,128)S(1)}, f32[6,4,128,128]{3,2,1,0:T(8,128)S(1)}, f32[8,128,256]{2,1,0:T(8,128)S(1)}) custom-call(f32[6]{0:T(128)S(1)} %fusion.42.keep, f32[3,384,1024]{2,1,0:T(8,128)} %get-tuple-element.165.features, f32[384,8]{1,0:T(8,128)S(1)} %get-tuple-element.166.beta), custom_call_target="tpu_custom_call" | custom-call | flops 1 | bytes 1 | tf_op jit(solution)/shard_map/prepare/pallas_call | solution.py:299
  46.0 11.8 %collective-permute-done.1 = f32[4,128,256]{2,1,0:T(8,128)S(1)} collective-permute-done((f32[4,128,256]{2,1,0:T(8,128)S(1)}, f32[4,128,256]{2,1,0:T(8,128)S(1)}, u32[]{:S(2)}, u32[]{:S(2)}) %collective-permute-start.1) | collective-permute-done | bytes 524320 | tf_op jit(solution)/shard_map/ppermute | solution.py:848
  59.8 3.5 collective-permute-start.2
  63.2 4.3 collective-permute-done.2.refs_1_
  71.6 4.8 collective-permute-done.5
  76.6 7.5 %mix.1 = (f32[6,8,128,128]{3,2,1,0:T(8,128)}, f32[384,1024]{1,0:T(8,128)S(1)}, f32[384,1024]{1,0:T(8,128)S(1)}, bf16[384,1024]{1,0:T(8,128)(2,1)S(1)}) custom-call(f32[6]{0:T(128)S(1)} %fusion.42.keep, f32[3,384,1024]{2,1,0:T(8,128)} %get-tuple-element.165.features, f32[2,384,1024]{2,1,0:T(8,128)} %get-tuple-element.167.solved, ...), custom_call_target="tpu_custom_call" | custom-call | flops 1 | bytes 1 | tf_op jit(solution)/shard_map/mix/pallas_call | solution.py:362
  86.4 25.8 %feed.1 = (bf16[384,1024]{1,0:T(8,128)(2,1)}, f32[1024,384]{1,0:T(8,128)S(1)}, f32[2816,384]{1,0:T(8,128)}, bf16[384,2816]{1,0:T(8,128)(2,1)}, f32[384,2816]{1,0...) custom-call(s32[1]{0:T(128)} %bitcast.core, ...), custom_call_target="tpu_custom_call" | custom-call | flops 1 | bytes 1 | tf_op jit(solution)/shard_map/feed/pallas_call | solution.py:456
  115.1 2.3 copy.107
  119.3 8.0 %gather_states.1 = (f32[384,1024]{1,0:T(8,128)S(1)}, f32[384,1024]{1,0:T(8,128)S(1)}, f32[1,128]{1,0:T(1,128)S(1)}, f32[8,128,128]{2,1,0:T(8,128)S(1)}) custom-call(f32[6]{0:T(128)S(1)} %fusion.42.keep, f32[384,1024]{1,0:T(8,128)S(1)} %copy-done.34, f32[384,1024]{1,0:T(8,128)} %copy-done.33, f32[384,1024]{1,0:T(8,128)} %copy-done.19, ...), custom_call_target="tpu_custom_call" | custom-call | flops 1 | bytes 1 | tf_op jit(solution)/shard_map/gather_states/pallas_call | solution.py:549
  127.4 1.6 broadcast_select_fusion
  137.7 10.2 %outer.6 = (f32[512,1792]{1,0:T(8,128)}, f32[512,1792]{1,0:T(8,128)}) custom-call(s32[1]{0:T(128)} %bitcast.13.refs_0_, f32[1024,384]{1,0:T(8,128)S(1)} %copy-done.13, f32[1024,384]{1,0:T(8,128)S(1)} %collective-permute-done.7.refs_2_, f32[1024,384]{1,0:T(8,128)S(1)} %broadcast_select_fusion.3.refs_3_, f32[1024,384]{1,0:T(8,128)} %broadcast_select_fusion.2.refs_4_, ...), custom_call_target="tpu_custom_call" | custom-call | flops 1 | bytes 1 | tf_op jit(solution)/shard_map/outer/pallas_call | solution.py:1003
  153.9 10.8 %outer.7 = (f32[512,2048]{1,0:T(8,128)}, f32[512,2048]{1,0:T(8,128)}) custom-call(s32[1]{0:T(128)} %bitcast.15.refs_0_, f32[1024,384]{1,0:T(8,128)S(1)} %copy-done.14, f32[1024,384]{1,0:T(8,128)S(1)} %copy-done.16, f32[1024,384]{1,0:T(8,128)S(1)} %copy-done.3, f32[1024,384]{1,0:T(8,128)} %broadcast_select_fusion.2.refs_4_, ...), custom_call_target="tpu_custom_call" | custom-call | flops 1 | bytes 1 | tf_op jit(solution)/shard_map/outer/pallas_call | solution.py:1003
  167.0 1.8 collective-permute-start.13
  168.9 8.3 %outer.8 = (f32[1408,512]{1,0:T(8,128)S(1)}, f32[1408,512]{1,0:T(8,128)}) custom-call(s32[1]{0:T(128)} %bitcast.16.refs_0_, f32[2816,384]{1,0:T(8,128)} %get-tuple-element.194.refs_1_, f32[2816,384]{1,0:T(8,128)} %collective-permute-done.14.refs_2_, bf16[384,512]{1,0:T(8,128)(2,1)S(1)} %slice_select_fusion.5.refs_3_, f32[384,512]{1,0:T(8,128)} %collective-permute-done.15.refs_4_), custom_call_target="tpu_custom_call" | custom-call | flops 1 | bytes 1 | tf_op jit(solution)/shard_map/outer/pallas_call | solution.py:1003
  180.4 2.2 fusion.46
  182.6 15.0 %collective-permute-done.16 = f32[4,128,128]{2,1,0:T(8,128)S(1)} collective-permute-done((f32[4,128,128]{2,1,0:T(8,128)S(1)}, f32[4,128,128]{2,1,0:T(8,128)S(1)}, u32[]{:S(2)}, u32[]{:S(2)}) %collective-permute-start.16) | collective-permute-done | bytes 262176 | tf_op jit(solution)/shard_map/ppermute | solution.py:934
  197.7 2.4 fusion.45
  203.4 4.3 collective-permute-done.17
  211.0 32.3 %back.1 = (f32[3,384,1024]{2,1,0:T(8,128)}, f32[3,8,1024]{2,1,0:T(8,128)S(1)}, f32[3,4,1024]{2,1,0:T(4,128)S(1)}, f32[384,8]{1,0:T(8,128)S(1)}) custom-call(f32[6]{0:T(128)S(1)} %fusion.42.keep, f32[3,384,1024]{2,1,0:T(8,128)} %get-tuple-element.165.features, f32[384,8]{1,0:T(8,128)S(1)} %copy-done.43, f32[384,8]{1,0:T(8,128)S(1)} %copy-done.45, ...), custom_call_target="tpu_custom_call" | custom-call | flops 1 | bytes 1 | tf_op jit(solution)/shard_map/back/pallas_call | solution.py:747
  243.3 5.8 %collective-permute-done.18 = f32[256,1792]{1,0:T(8,128)S(1)} collective-permute-done((f32[256,1792]{1,0:T(8,128)S(1)}, f32[256,1792]{1,0:T(8,128)S(1)}, u32[]{:S(2)}, u32[]{:S(2)}) %collective-permute-start.18) | collective-permute-done | bytes 1835040 | tf_op jit(solution)/shard_map/ppermute | solution.py:848
  249.2 4.5 collective-permute-done.19
  255.0 5.2 collective-permute-done.21
  261.7 2.7 convert_element_type.51.grads
  266.1 2.4 collective-permute-start.22
  269.1 1.7 fusion.2
  273.1 2.4 fusion.7
  279.6 9.0 %enter.1 = (bf16[384,1024]{1,0:T(8,128)(2,1)}, f32[1,1024]{1,0:T(1,128)S(1)}) custom-call(bf16[384,1024]{1,0:T(8,128)(2,1)S(1)} %bitcast.232, f32[1,1024]{1,0:T(1,128)S(1)} %bitcast.240, f32[384,1024]{1,0:T(8,128)S(1)} %copy-done.32, bf16[3,384,1024]{2,1,0:T(8,128)(2,1)} %copy-done.52, f32[384,1024]{1,0:T(8,128)S(1)} %copy-done.18, ...), custom_call_target="tpu_custom_call" | custom-call | flops 1 | bytes 1 | tf_op jit(solution)/shard_map/enter/pallas_call | solution.py:810
  291.3 3.2 outer.11
  294.6 2.6 outer.9
  297.2 2.9 outer.10
  300.0 6.2 %collective-permute-done.24 = f32[704,512]{1,0:T(8,128)} collective-permute-done((f32[704,512]{1,0:T(8,128)}, f32[704,512]{1,0:T(8,128)}, u32[]{:S(2)}, u32[]{:S(2)}) %collective-permute-start.24) | collective-permute-done | bytes 1441824 | tf_op jit(solution)/shard_map/ppermute | solution.py:848
  306.2 2.3 collective-permute-done.23
  308.5 1.9 pad_maximum_fusion.1
  313.1 2.2 pad_maximum_fusion
  318.4 1.9 pad_maximum_fusion.2
  321.8 2.5 collective-permute-start.30
  328.5 19.9 %collective-permute-done.30 = f32[512,512]{1,0:T(8,128)S(1)} collective-permute-done((f32[512,512]{1,0:T(8,128)S(1)}, f32[512,512]{1,0:T(8,128)S(1)}, u32[]{:S(2)}, u32[]{:S(2)}) %collective-permute-start.30) | collective-permute-done | bytes 1048608 | tf_op jit(solution)/shard_map/ppermute | solution.py:848
  349.1 36.1 %collective-permute-done.31 = f32[512,512]{1,0:T(8,128)S(1)} collective-permute-done((f32[512,512]{1,0:T(8,128)S(1)}, f32[512,512]{1,0:T(8,128)S(1)}, u32[]{:S(2)}, u32[]{:S(2)}) %collective-permute-start.31) | collective-permute-done | bytes 1048608 | tf_op jit(solution)/shard_map/ppermute | solution.py:848
  385.2 4.2 collective-permute-done.32
  403.0 16.9 %collective-permute-done.40 = f32[128,128]{1,0:T(8,128)S(1)} collective-permute-done((f32[128,128]{1,0:T(8,128)S(1)}, f32[128,128]{1,0:T(8,128)S(1)}, u32[]{:S(2)}, u32[]{:S(2)}) %collective-permute-start.40) | collective-permute-done | bytes 65568 | tf_op jit(solution)/shard_map/ppermute | solution.py:848
  419.8 4.5 collective-permute-start.38
  425.1 6.7 %collective-permute-done.38 = f32[2,2,64,512]{3,2,0,1:T(8,128)} collective-permute-done((f32[2,2,64,512]{3,2,0,1:T(8,128)}, f32[2,2,64,512]{3,2,0,1:T(8,128)}, u32[]{:S(2)}, u32[]{:S(2)}) %collective-permute-start.38) | collective-permute-done | bytes 524320 | tf_op jit(solution)/shard_map/ppermute | solution.py:848
  431.8 2.8 collective-permute-done.39
  434.6 1.9 fusion.17
  436.5 1.9 fusion.16
  438.5 1.8 fusion.18
  440.4 2.0 bitcast_add_fusion.16
  442.3 1.9 bitcast_add_fusion.15
  444.3 3.6 collective-permute-start.42
  447.9 2.9 collective-permute-start.43
  451.3 3.4 collective-permute-done.47
  456.1 5.3 collective-permute-done.45
  462.3 36.4 %collective-permute-done.43 = f32[176,512]{1,0:T(8,128)} collective-permute-done((f32[176,512]{1,0:T(8,128)}, f32[176,512]{1,0:T(8,128)}, u32[]{:S(2)}, u32[]{:S(2)}) %collective-permute-start.43) | collective-permute-done | bytes 360480 | tf_op jit(solution)/shard_map/ppermute | solution.py:848
  509.9 4.1 collective-permute-start.54
  514.0 1.7 collective-permute-done.54
  517.1 3.5 collective-permute-done.51
  520.7 4.2 collective-permute-done.52
  524.9 3.7 collective-permute-done.53
  528.5 6.3 %collective-permute-done.50 = f32[176,512]{1,0:T(8,128)S(1)} collective-permute-done((f32[176,512]{1,0:T(8,128)S(1)}, f32[176,512]{1,0:T(8,128)S(1)}, u32[]{:S(2)}, u32[]{:S(2)}) %collective-permute-start.50) | collective-permute-done | bytes 360480 | tf_op jit(solution)/shard_map/ppermute | solution.py:848
  541.0 4.5 collective-permute-done.58
  547.6 3.8 collective-permute-done.56
  555.0 1.8 broadcast_select_fusion.4
  (384 shorter events, 125.9 us)
Async XLA Ops:
  1.4 8.5 %collective-permute-start = (f32[16,1024]{1,0:T(8,128)S(1)}, f32[16,1024]{1,0:T(8,128)S(1)}, u32[]{:S(2)}, u32[]{:S(2)}) collective-permute-start(f32[16,1024]{1,0:T(8,128)S(1)} %bitcast_convert_fusion), channel_id=1, source_target_pairs={{0,4},{4,8},{8,12},{12,16},{16,20},{20,24},{24,28},{1,5},{5,9},{9,... | collective-permute-start | bytes 196616 | tf_op jit(solution)/shard_map/ppermute | solution.py:836
  44.3 13.4 %collective-permute-start.1 = (f32[4,128,256]{2,1,0:T(8,128)S(1)}, f32[4,128,256]{2,1,0:T(8,128)S(1)}, u32[]{:S(2)}, u32[]{:S(2)}) collective-permute-start(f32[4,128,256]{2,1,0:T(8,128)S(1)} %slice_select_fusion.4), channel_id=1, source_target_pairs={{0,4},{4,0},{8,12},{12,8},{16,20},{20,16},{24,28},{28,24},{1,5},{5... | collective-permute-start | bytes 1572872 | tf_op jit(solution)/shard_map/ppermute | solution.py:848
  59.8 7.8 %collective-permute-start.2 = (f32[4,128,128]{2,1,0:T(8,128)S(1)}, f32[4,128,128]{2,1,0:T(8,128)S(1)}, u32[]{:S(2)}, u32[]{:S(2)}) collective-permute-start(f32[4,128,128]{2,1,0:T(8,128)S(1)} %get-tuple-element.440), channel_id=1, source_target_pairs={{0,8},{4,12},{1,9},{5,13},{2,10},{6,14},{3,11},{7,15}} | collective-permute-start | bytes 786440 | tf_op jit(solution)/shard_map/ppermute | solution.py:896
  68.8 0.9 collective-permute-start.4
  70.0 6.4 %collective-permute-start.5 = (f32[4,128,128]{2,1,0:T(8,128)S(1)}, f32[4,128,128]{2,1,0:T(8,128)S(1)}, u32[]{:S(2)}, u32[]{:S(2)}) collective-permute-start(f32[4,128,128]{2,1,0:T(8,128)S(1)} %broadcast_select_fusion.30), channel_id=1, source_target_pairs={{0,4},{4,0},{8,12},{12,8},{16,20},{20,16},{24,28},{28,24},{1,5},{5... | collective-permute-start | bytes 786440 | tf_op jit(solution)/shard_map/ppermute | solution.py:848
  114.6 22.0 %collective-permute-start.10 = (f32[384,2816]{1,0:T(8,128)}, f32[384,2816]{1,0:T(8,128)}, u32[]{:S(2)}, u32[]{:S(2)}) collective-permute-start(f32[384,2816]{1,0:T(8,128)} %get-tuple-element.185), channel_id=1, source_target_pairs={{0,1},{1,0},{2,3},{3,2},{4,5},{5,4},{6,7},{7,6},{8,9},{9,8},{10,11... | collective-permute-start | bytes 12976136 | tf_op jit(solution)/shard_map/ppermute | solution.py:848
  114.6 54.3 %collective-permute-start.14 = (f32[2816,384]{1,0:T(8,128)}, f32[2816,384]{1,0:T(8,128)}, u32[]{:S(2)}, u32[]{:S(2)}) collective-permute-start(f32[2816,384]{1,0:T(8,128)} %get-tuple-element.194.refs_1_), channel_id=1, source_target_pairs={{0,1},{1,0},{2,3},{3,2},{4,5},{5,4},{6,7},{7,6},{8,9},{9,8},{10,11... | collective-permute-start | bytes 12976136 | tf_op jit(solution)/shard_map/ppermute | solution.py:848
  115.1 14.4 %collective-permute-start.9 = (f32[1024,384]{1,0:T(8,128)S(1)}, f32[1024,384]{1,0:T(8,128)S(1)}, u32[]{:S(2)}, u32[]{:S(2)}) collective-permute-start(f32[1024,384]{1,0:T(8,128)S(1)} %get-tuple-element.183.refs_1_), channel_id=1, source_target_pairs={{0,1},{1,0},{2,3},{3,2},{4,5},{5,4},{6,7},{7,6},{8,9},{9,8},{10,11... | collective-permute-start | bytes 4718600 | tf_op jit(solution)/shard_map/ppermute | solution.py:848
  117.4 17.7 %collective-permute-start.7 = (f32[1024,384]{1,0:T(8,128)}, f32[1024,384]{1,0:T(8,128)S(1)}, u32[]{:S(2)}, u32[]{:S(2)}) collective-permute-start(f32[1024,384]{1,0:T(8,128)} %copy-done.12), channel_id=1, source_target_pairs={{0,1},{1,0},{2,3},{3,2},{4,5},{5,4},{6,7},{7,6},{8,9},{9,8},{10,11... | collective-permute-start | bytes 4718600 | tf_op jit(solution)/shard_map/ppermute | solution.py:848
  119.1 13.0 %collective-permute-start.8 = (f32[1024,384]{1,0:T(8,128)S(1)}, f32[1024,384]{1,0:T(8,128)S(1)}, u32[]{:S(2)}, u32[]{:S(2)}) collective-permute-start(f32[1024,384]{1,0:T(8,128)S(1)} %convert_bitcast_fusion), channel_id=1, source_target_pairs={{0,1},{1,0},{2,3},{3,2},{4,5},{5,4},{6,7},{7,6},{8,9},{9,8},{10,11... | collective-permute-start | bytes 4718600 | tf_op jit(solution)/shard_map/ppermute | solution.py:848
  129.5 7.1 %collective-permute-start.11 = (f32[384,1024]{1,0:T(8,128)S(1)}, f32[384,1024]{1,0:T(8,128)S(1)}, u32[]{:S(2)}, u32[]{:S(2)}) collective-permute-start(f32[384,1024]{1,0:T(8,128)S(1)} %get-tuple-element.391), channel_id=1, source_target_pairs={{0,1},{1,0},{2,3},{3,2},{4,5},{5,4},{6,7},{7,6},{8,9},{9,8},{10,11... | collective-permute-start | bytes 4718600 | tf_op jit(solution)/shard_map/ppermute | solution.py:848
  132.1 15.9 %collective-permute-start.6 = (f32[4,128,128]{2,1,0:T(8,128)S(1)}, f32[4,128,128]{2,1,0:T(8,128)S(1)}, u32[]{:S(2)}, u32[]{:S(2)}) collective-permute-start(f32[4,128,128]{2,1,0:T(8,128)S(1)} %slice_select_fusion.7), channel_id=1, source_target_pairs={{0,4},{4,0},{8,12},{12,8},{16,20},{20,16},{24,28},{28,24},{1,5},{5... | collective-permute-start | bytes 786440 | tf_op jit(solution)/shard_map/ppermute | solution.py:848
  135.0 33.8 %collective-permute-start.15 = (f32[384,512]{1,0:T(8,128)}, f32[384,512]{1,0:T(8,128)}, u32[]{:S(2)}, u32[]{:S(2)}) collective-permute-start(f32[384,512]{1,0:T(8,128)} %slice_select_fusion.2), channel_id=1, source_target_pairs={{0,1},{1,0},{2,3},{3,2},{4,5},{5,4},{6,7},{7,6},{8,9},{9,8},{10,11... | collective-permute-start | bytes 2359304 | tf_op jit(solution)/shard_map/ppermute | solution.py:848
  149.7 16.1 %collective-permute-start.12 = (f32[4,128,128]{2,1,0:T(8,128)}, f32[4,128,128]{2,1,0:T(8,128)}, u32[]{:S(2)}, u32[]{:S(2)}) collective-permute-start(f32[4,128,128]{2,1,0:T(8,128)} %apply_map.12), channel_id=1, source_target_pairs={{24,16},{28,20},{25,17},{29,21},{26,18},{30,22},{27,19},{31,23}} | collective-permute-start | bytes 786440 | tf_op jit(solution)/shard_map/ppermute | solution.py:934
  167.0 10.2 %collective-permute-start.13 = (f32[4,128,128]{2,1,0:T(8,128)S(1)}, f32[4,128,128]{2,1,0:T(8,128)}, u32[]{:S(2)}, u32[]{:S(2)}) collective-permute-start(f32[4,128,128]{2,1,0:T(8,128)S(1)} %apply_map.13), channel_id=1, source_target_pairs={{16,8},{20,12},{17,9},{21,13},{18,10},{22,14},{19,11},{23,15}} | collective-permute-start | bytes 786440 | tf_op jit(solution)/shard_map/ppermute | solution.py:934
  179.0 18.6 %collective-permute-start.16 = (f32[4,128,128]{2,1,0:T(8,128)S(1)}, f32[4,128,128]{2,1,0:T(8,128)S(1)}, u32[]{:S(2)}, u32[]{:S(2)}) collective-permute-start(f32[4,128,128]{2,1,0:T(8,128)S(1)} %apply_map.14), channel_id=1, source_target_pairs={{8,0},{12,4},{9,1},{13,5},{10,2},{14,6},{11,3},{15,7}} | collective-permute-start | bytes 786440 | tf_op jit(solution)/shard_map/ppermute | solution.py:934
  200.3 7.3 %collective-permute-start.17 = (f32[4,128,128]{2,1,0:T(8,128)S(1)}, f32[4,128,128]{2,1,0:T(8,128)S(1)}, u32[]{:S(2)}, u32[]{:S(2)}) collective-permute-start(f32[4,128,128]{2,1,0:T(8,128)S(1)} %broadcast_select_fusion.24), channel_id=1, source_target_pairs={{0,4},{4,0},{8,12},{12,8},{16,20},{20,16},{24,28},{28,24},{1,5},{5... | collective-permute-start | bytes 786440 | tf_op jit(solution)/shard_map/ppermute | solution.py:848
  207.8 45.9 %collective-permute-start.19 = (f32[256,2048]{1,0:T(8,128)}, f32[256,2048]{1,0:T(8,128)S(1)}, u32[]{:S(2)}, u32[]{:S(2)}) collective-permute-start(f32[256,2048]{1,0:T(8,128)} %get-tuple-element.206), channel_id=1, source_target_pairs={{0,2},{1,3},{2,0},{3,1},{4,6},{5,7},{6,4},{7,5},{8,10},{9,11},{10,... | collective-permute-start | bytes 6291464 | tf_op jit(solution)/shard_map/ppermute | solution.py:848
  209.4 39.8 %collective-permute-start.18 = (f32[256,1792]{1,0:T(8,128)S(1)}, f32[256,1792]{1,0:T(8,128)S(1)}, u32[]{:S(2)}, u32[]{:S(2)}) collective-permute-start(f32[256,1792]{1,0:T(8,128)S(1)} %copy-done.67), channel_id=1, source_target_pairs={{0,4},{4,0},{8,12},{12,8},{16,20},{20,16},{24,28},{28,24},{1,5},{5... | collective-permute-start | bytes 5505032 | tf_op jit(solution)/shard_map/ppermute | solution.py:848
  210.9 32.4 %collective-permute-start.20 = (f32[704,512]{1,0:T(8,128)S(1)}, f32[704,512]{1,0:T(8,128)S(1)}, u32[]{:S(2)}, u32[]{:S(2)}) collective-permute-start(f32[704,512]{1,0:T(8,128)S(1)} %get-tuple-element.207), channel_id=1, source_target_pairs={{0,8},{4,12},{8,0},{12,4},{16,24},{20,28},{24,16},{28,20},{1,9},{5... | collective-permute-start | bytes 4325384 | tf_op jit(solution)/shard_map/ppermute | solution.py:848
  253.7 6.5 %collective-permute-start.21 = (f32[3,8,1024]{2,1,0:T(8,128)S(1)}, f32[3,8,1024]{2,1,0:T(8,128)S(1)}, u32[]{:S(2)}, u32[]{:S(2)}) collective-permute-start(f32[3,8,1024]{2,1,0:T(8,128)S(1)} %get-tuple-element.208), channel_id=1, source_target_pairs={{4,0},{8,4},{12,8},{16,12},{20,16},{24,20},{28,24},{5,1},{9,5},{13... | collective-permute-start | bytes 294920 | tf_op jit(solution)/shard_map/ppermute | solution.py:836
  264.5 44.0 %collective-permute-start.23 = (f32[256,2048]{1,0:T(8,128)}, f32[256,2048]{1,0:T(8,128)}, u32[]{:S(2)}, u32[]{:S(2)}) collective-permute-start(f32[256,2048]{1,0:T(8,128)} %get-tuple-element.217), channel_id=1, source_target_pairs={{0,2},{1,3},{2,0},{3,1},{4,6},{5,7},{6,4},{7,5},{8,10},{9,11},{10,... | collective-permute-start | bytes 6291464 | tf_op jit(solution)/shard_map/ppermute | solution.py:848
  266.1 40.1 %collective-permute-start.22 = (f32[256,1792]{1,0:T(8,128)}, f32[256,1792]{1,0:T(8,128)}, u32[]{:S(2)}, u32[]{:S(2)}) collective-permute-start(f32[256,1792]{1,0:T(8,128)} %get-tuple-element.216), channel_id=1, source_target_pairs={{0,4},{4,0},{8,12},{12,8},{16,20},{20,16},{24,28},{28,24},{1,5},{5... | collective-permute-start | bytes 5505032 | tf_op jit(solution)/shard_map/ppermute | solution.py:848
  271.9 22.7 %collective-permute-start.25 = (f32[384,1024]{1,0:T(8,128)}, f32[384,1024]{1,0:T(8,128)}, u32[]{:S(2)}, u32[]{:S(2)}) collective-permute-start(f32[384,1024]{1,0:T(8,128)} %fusion.2), channel_id=1, source_target_pairs={{0,1},{1,0},{2,3},{3,2},{4,5},{5,4},{6,7},{7,6},{8,9},{9,8},{10,11... | collective-permute-start | bytes 4718600 | tf_op jit(solution)/shard_map/ppermute | solution.py:848
  271.9 34.3 %collective-permute-start.24 = (f32[704,512]{1,0:T(8,128)}, f32[704,512]{1,0:T(8,128)}, u32[]{:S(2)}, u32[]{:S(2)}) collective-permute-start(f32[704,512]{1,0:T(8,128)} %get-tuple-element.218), channel_id=1, source_target_pairs={{0,8},{4,12},{8,0},{12,4},{16,24},{20,28},{24,16},{28,20},{1,9},{5... | collective-permute-start | bytes 4325384 | tf_op jit(solution)/shard_map/ppermute | solution.py:848
  275.5 15.8 %collective-permute-start.26 = (f32[384,512]{1,0:T(8,128)}, f32[384,512]{1,0:T(8,128)}, u32[]{:S(2)}, u32[]{:S(2)}) collective-permute-start(f32[384,512]{1,0:T(8,128)} %fusion.7), channel_id=1, source_target_pairs={{0,1},{1,0},{2,3},{3,2},{4,5},{5,4},{6,7},{7,6},{8,9},{9,8},{10,11... | collective-permute-start | bytes 2359304 | tf_op jit(solution)/shard_map/ppermute | solution.py:848
  321.8 26.6 %collective-permute-start.30 = (f32[512,512]{1,0:T(8,128)S(1)}, f32[512,512]{1,0:T(8,128)S(1)}, u32[]{:S(2)}, u32[]{:S(2)}) collective-permute-start(f32[512,512]{1,0:T(8,128)S(1)} %get-tuple-element.239), channel_id=1, source_target_pairs={{0,4},{4,0},{8,12},{12,8},{16,20},{20,16},{24,28},{28,24},{1,5},{5... | collective-permute-start | bytes 3145736 | tf_op jit(solution)/shard_map/ppermute | solution.py:848
  324.3 65.1 %collective-permute-start.28 = (f32[2,2,64,2048]{3,2,0,1:T(8,128)S(1)}, f32[2,2,64,2048]{3,2,0,1:T(8,128)S(1)}, u32[]{:S(2)}, u32[]{:S(2)}) collective-permute-start(f32[2,2,64,2048]{3,2,0,1:T(8,128)S(1)} %fusion), channel_id=1, source_target_pairs={{0,8},{4,12},{8,0},{12,4},{16,24},{20,28},{24,16},{28,20},{1,9},{5... | collective-permute-start | bytes 6291464 | tf_op jit(solution)/shard_map/ppermute | solution.py:848
  325.0 64.4 %collective-permute-start.27 = (f32[2,2,64,1792]{3,2,0,1:T(8,128)S(1)}, f32[2,2,64,1792]{3,2,0,1:T(8,128)S(1)}, u32[]{:S(2)}, u32[]{:S(2)}) collective-permute-start(f32[2,2,64,1792]{3,2,0,1:T(8,128)S(1)} %fusion.1), channel_id=1, source_target_pairs={{0,2},{1,3},{2,0},{3,1},{4,6},{5,7},{6,4},{7,5},{8,10},{9,11},{10,... | collective-permute-start | bytes 5505032 | tf_op jit(solution)/shard_map/ppermute | solution.py:848
  326.6 62.8 %collective-permute-start.29 = (f32[2,2,176,512]{3,2,0,1:T(8,128)S(1)}, f32[2,2,176,512]{3,2,0,1:T(8,128)S(1)}, u32[]{:S(2)}, u32[]{:S(2)}) collective-permute-start(f32[2,2,176,512]{3,2,0,1:T(8,128)S(1)} %fusion.3), channel_id=1, source_target_pairs={{0,4},{4,0},{8,12},{12,8},{16,20},{20,16},{24,28},{28,24},{1,5},{5... | collective-permute-start | bytes 4325384 | tf_op jit(solution)/shard_map/ppermute | solution.py:848
  326.7 1.3 collective-permute-start.33
  328.0 57.2 %collective-permute-start.31 = (f32[512,512]{1,0:T(8,128)S(1)}, f32[512,512]{1,0:T(8,128)S(1)}, u32[]{:S(2)}, u32[]{:S(2)}) collective-permute-start(f32[512,512]{1,0:T(8,128)S(1)} %get-tuple-element.240), channel_id=1, source_target_pairs={{0,2},{1,3},{2,0},{3,1},{4,6},{5,7},{6,4},{7,5},{8,10},{9,11},{10,... | collective-permute-start | bytes 3145736 | tf_op jit(solution)/shard_map/ppermute | solution.py:848
  348.4 41.0 %collective-permute-start.32 = (f32[512,512]{1,0:T(8,128)S(1)}, f32[512,512]{1,0:T(8,128)S(1)}, u32[]{:S(2)}, u32[]{:S(2)}) collective-permute-start(f32[512,512]{1,0:T(8,128)S(1)} %get-tuple-element.241), channel_id=1, source_target_pairs={{0,8},{4,12},{8,0},{12,4},{16,24},{20,28},{24,16},{28,20},{1,9},{5... | collective-permute-start | bytes 3145736 | tf_op jit(solution)/shard_map/ppermute | solution.py:848
  397.2 27.1 %collective-permute-start.37 = (f32[2,2,64,512]{3,2,0,1:T(8,128)S(1)}, f32[2,2,64,512]{3,2,0,1:T(8,128)S(1)}, u32[]{:S(2)}, u32[]{:S(2)}) collective-permute-start(f32[2,2,64,512]{3,2,0,1:T(8,128)S(1)} %fusion.15), channel_id=1, source_target_pairs={{0,2},{1,3},{2,0},{3,1},{4,6},{5,7},{6,4},{7,5},{8,10},{9,11},{10,... | collective-permute-start | bytes 1572872 | tf_op jit(solution)/shard_map/ppermute | solution.py:848
  398.7 35.9 %collective-permute-start.35 = (f32[2,64,2048]{2,1,0:T(8,128)}, f32[2,64,2048]{2,1,0:T(8,128)}, u32[]{:S(2)}, u32[]{:S(2)}) collective-permute-start(f32[2,64,2048]{2,1,0:T(8,128)} %get-tuple-element.254), channel_id=1, source_target_pairs={{0,4},{4,0},{8,12},{12,8},{16,20},{20,16},{24,28},{28,24},{1,5},{5... | collective-permute-start | bytes 3145736 | tf_op jit(solution)/shard_map/ppermute | solution.py:848
  399.4 35.2 %collective-permute-start.34 = (f32[2,64,1792]{2,1,0:T(8,128)}, f32[2,64,1792]{2,1,0:T(8,128)}, u32[]{:S(2)}, u32[]{:S(2)}) collective-permute-start(f32[2,64,1792]{2,1,0:T(8,128)} %get-tuple-element.253), channel_id=1, source_target_pairs={{0,8},{4,12},{8,0},{12,4},{16,24},{20,28},{24,16},{28,20},{1,9},{5... | collective-permute-start | bytes 2752520 | tf_op jit(solution)/shard_map/ppermute | solution.py:848
  400.8 33.8 %collective-permute-start.36 = (f32[2,176,512]{2,1,0:T(8,128)}, f32[2,176,512]{2,1,0:T(8,128)}, u32[]{:S(2)}, u32[]{:S(2)}) collective-permute-start(f32[2,176,512]{2,1,0:T(8,128)} %get-tuple-element.255), channel_id=1, source_target_pairs={{0,2},{1,3},{2,0},{3,1},{4,6},{5,7},{6,4},{7,5},{8,10},{9,11},{10,... | collective-permute-start | bytes 2162696 | tf_op jit(solution)/shard_map/ppermute | solution.py:848
  401.4 18.4 %collective-permute-start.40 = (f32[128,128]{1,0:T(8,128)S(1)}, f32[128,128]{1,0:T(8,128)S(1)}, u32[]{:S(2)}, u32[]{:S(2)}) collective-permute-start(f32[128,128]{1,0:T(8,128)S(1)} %bitcast.258), channel_id=1, source_target_pairs={{0,4},{4,0},{8,12},{12,8},{16,20},{20,16},{24,28},{28,24},{1,5},{5... | collective-permute-start | bytes 196616 | tf_op jit(solution)/shard_map/ppermute | solution.py:848
  419.8 11.9 %collective-permute-start.38 = (f32[2,2,64,512]{3,2,0,1:T(8,128)}, f32[2,2,64,512]{3,2,0,1:T(8,128)}, u32[]{:S(2)}, u32[]{:S(2)}) collective-permute-start(f32[2,2,64,512]{3,2,0,1:T(8,128)} %fusion.14), channel_id=1, source_target_pairs={{0,8},{4,12},{8,0},{12,4},{16,24},{20,28},{24,16},{28,20},{1,9},{5... | collective-permute-start | bytes 1572872 | tf_op jit(solution)/shard_map/ppermute | solution.py:848
  425.1 9.5 %collective-permute-start.39 = (f32[2,2,64,512]{3,2,0,1:T(8,128)}, f32[2,2,64,512]{3,2,0,1:T(8,128)}, u32[]{:S(2)}, u32[]{:S(2)}) collective-permute-start(f32[2,2,64,512]{3,2,0,1:T(8,128)} %fusion.13), channel_id=1, source_target_pairs={{0,4},{4,0},{8,12},{12,8},{16,20},{20,16},{24,28},{28,24},{1,5},{5... | collective-permute-start | bytes 1572872 | tf_op jit(solution)/shard_map/ppermute | solution.py:848
  444.2 11.4 %collective-permute-start.44 = (f32[2,64,512]{2,1,0:T(8,128)S(1)}, f32[2,64,512]{2,1,0:T(8,128)}, u32[]{:S(2)}, u32[]{:S(2)}) collective-permute-start(f32[2,64,512]{2,1,0:T(8,128)S(1)} %get-tuple-element.270), channel_id=1, source_target_pairs={{0,8},{4,12},{8,0},{12,4},{16,24},{20,28},{24,16},{28,20},{1,9},{5... | collective-permute-start | bytes 786440 | tf_op jit(solution)/shard_map/ppermute | solution.py:848
  444.3 55.1 %collective-permute-start.42 = (f32[64,2048]{1,0:T(8,128)}, f32[64,2048]{1,0:T(8,128)}, u32[]{:S(2)}, u32[]{:S(2)}) collective-permute-start(f32[64,2048]{1,0:T(8,128)} %fusion.16), channel_id=1, source_target_pairs={{0,16},{4,20},{8,24},{12,28},{16,0},{20,4},{24,8},{28,12},{1,17},{... | collective-permute-start | bytes 1572872 | tf_op jit(solution)/shard_map/ppermute | solution.py:848
  447.9 50.8 %collective-permute-start.41 = (f32[64,1792]{1,0:T(8,128)}, f32[64,1792]{1,0:T(8,128)S(1)}, u32[]{:S(2)}, u32[]{:S(2)}) collective-permute-start(f32[64,1792]{1,0:T(8,128)} %fusion.17), channel_id=1, source_target_pairs={{0,16},{4,20},{8,24},{12,28},{16,0},{20,4},{24,8},{28,12},{1,17},{... | collective-permute-start | bytes 1376264 | tf_op jit(solution)/shard_map/ppermute | solution.py:848
  447.9 50.8 %collective-permute-start.43 = (f32[176,512]{1,0:T(8,128)}, f32[176,512]{1,0:T(8,128)}, u32[]{:S(2)}, u32[]{:S(2)}) collective-permute-start(f32[176,512]{1,0:T(8,128)} %fusion.18), channel_id=1, source_target_pairs={{0,16},{4,20},{8,24},{12,28},{16,0},{20,4},{24,8},{28,12},{1,17},{... | collective-permute-start | bytes 1081352 | tf_op jit(solution)/shard_map/ppermute | solution.py:848
  450.8 3.9 collective-permute-start.47
  454.7 6.7 %collective-permute-start.45 = (f32[2,64,512]{2,1,0:T(8,128)}, f32[2,64,512]{2,1,0:T(8,128)}, u32[]{:S(2)}, u32[]{:S(2)}) collective-permute-start(f32[2,64,512]{2,1,0:T(8,128)} %get-tuple-element.271), channel_id=1, source_target_pairs={{0,4},{4,0},{8,12},{12,8},{16,20},{20,16},{24,28},{28,24},{1,5},{5... | collective-permute-start | bytes 786440 | tf_op jit(solution)/shard_map/ppermute | solution.py:848
  455.6 6.7 %collective-permute-start.46 = (f32[2,64,512]{2,1,0:T(8,128)}, f32[2,64,512]{2,1,0:T(8,128)}, u32[]{:S(2)}, u32[]{:S(2)}) collective-permute-start(f32[2,64,512]{2,1,0:T(8,128)} %get-tuple-element.272), channel_id=1, source_target_pairs={{0,2},{1,3},{2,0},{3,1},{4,6},{5,7},{6,4},{7,5},{8,10},{9,11},{10,... | collective-permute-start | bytes 786440 | tf_op jit(solution)/shard_map/ppermute | solution.py:848
  507.3 27.4 %collective-permute-start.49 = (f32[64,2048]{1,0:T(8,128)S(1)}, f32[64,2048]{1,0:T(8,128)S(1)}, u32[]{:S(2)}, u32[]{:S(2)}) collective-permute-start(f32[64,2048]{1,0:T(8,128)S(1)} %bitcast_add_fusion.6), channel_id=1, source_target_pairs={{0,2},{1,3},{2,0},{3,1},{4,6},{5,7},{6,4},{7,5},{8,10},{9,11},{10,... | collective-permute-start | bytes 1572872 | tf_op jit(solution)/shard_map/ppermute | solution.py:848
  507.9 26.9 %collective-permute-start.48 = (f32[64,1792]{1,0:T(8,128)S(1)}, f32[64,1792]{1,0:T(8,128)S(1)}, u32[]{:S(2)}, u32[]{:S(2)}) collective-permute-start(f32[64,1792]{1,0:T(8,128)S(1)} %bitcast_add_fusion.9), channel_id=1, source_target_pairs={{0,2},{1,3},{2,0},{3,1},{4,6},{5,7},{6,4},{7,5},{8,10},{9,11},{10,... | collective-permute-start | bytes 1376264 | tf_op jit(solution)/shard_map/ppermute | solution.py:848
  509.4 25.4 %collective-permute-start.50 = (f32[176,512]{1,0:T(8,128)S(1)}, f32[176,512]{1,0:T(8,128)S(1)}, u32[]{:S(2)}, u32[]{:S(2)}) collective-permute-start(f32[176,512]{1,0:T(8,128)S(1)} %bitcast_add_fusion.12), channel_id=1, source_target_pairs={{0,2},{1,3},{2,0},{3,1},{4,6},{5,7},{6,4},{7,5},{8,10},{9,11},{10,... | collective-permute-start | bytes 1081352 | tf_op jit(solution)/shard_map/ppermute | solution.py:848
  509.9 10.7 %collective-permute-start.51 = (f32[64,512]{1,0:T(8,128)S(1)}, f32[64,512]{1,0:T(8,128)S(1)}, u32[]{:S(2)}, u32[]{:S(2)}) collective-permute-start(f32[64,512]{1,0:T(8,128)S(1)} %fusion.25), channel_id=1, source_target_pairs={{0,16},{4,20},{8,24},{12,28},{16,0},{20,4},{24,8},{28,12},{1,17},{... | collective-permute-start | bytes 393224 | tf_op jit(solution)/shard_map/ppermute | solution.py:848
  509.9 5.8 %collective-permute-start.54 = (f32[2,16,128]{2,1,0:T(8,128)S(1)}, f32[2,16,128]{2,1,0:T(8,128)S(1)}, u32[]{:S(2)}, u32[]{:S(2)}) collective-permute-start(f32[2,16,128]{2,1,0:T(8,128)S(1)} %get-tuple-element.287), channel_id=1, source_target_pairs={{0,8},{4,12},{8,0},{12,4},{16,24},{20,28},{24,16},{28,20},{1,9},{5... | collective-permute-start | bytes 49160 | tf_op jit(solution)/shard_map/ppermute | solution.py:848
  515.7 9.2 %collective-permute-start.52 = (f32[64,512]{1,0:T(8,128)}, f32[64,512]{1,0:T(8,128)S(1)}, u32[]{:S(2)}, u32[]{:S(2)}) collective-permute-start(f32[64,512]{1,0:T(8,128)} %fusion.24), channel_id=1, source_target_pairs={{0,16},{4,20},{8,24},{12,28},{16,0},{20,4},{24,8},{28,12},{1,17},{... | collective-permute-start | bytes 393224 | tf_op jit(solution)/shard_map/ppermute | solution.py:848
  520.7 7.9 %collective-permute-start.53 = (f32[64,512]{1,0:T(8,128)}, f32[64,512]{1,0:T(8,128)}, u32[]{:S(2)}, u32[]{:S(2)}) collective-permute-start(f32[64,512]{1,0:T(8,128)} %fusion.23), channel_id=1, source_target_pairs={{0,16},{4,20},{8,24},{12,28},{16,0},{20,4},{24,8},{28,12},{1,17},{... | collective-permute-start | bytes 393224 | tf_op jit(solution)/shard_map/ppermute | solution.py:848
  539.7 13.0 %collective-permute-start.59 = (f32[128,2816]{1,0:T(8,128)S(1)}, f32[128,2816]{1,0:T(8,128)S(1)}, u32[]{:S(2)}, u32[]{:S(2)}) collective-permute-start(f32[128,2816]{1,0:T(8,128)S(1)} %pad_maximum_fusion.3), channel_id=1, source_target_pairs={{0,1},{1,0},{2,3},{3,2},{4,5},{5,4},{6,7},{7,6},{8,9},{9,8},{10,11... | collective-permute-start | bytes 4325384 | tf_op jit(solution)/shard_map/ppermute | solution.py:848
  539.8 13.0 %collective-permute-start.60 = (f32[352,512]{1,0:T(8,128)S(1)}, f32[352,512]{1,0:T(8,128)S(1)}, u32[]{:S(2)}, u32[]{:S(2)}) collective-permute-start(f32[352,512]{1,0:T(8,128)S(1)} %pad_maximum_fusion.5), channel_id=1, source_target_pairs={{0,1},{1,0},{2,3},{3,2},{4,5},{5,4},{6,7},{7,6},{8,9},{9,8},{10,11... | collective-permute-start | bytes 2162696 | tf_op jit(solution)/shard_map/ppermute | solution.py:848
  540.3 12.5 %collective-permute-start.61 = (f32[128,1024]{1,0:T(8,128)S(1)}, f32[128,1024]{1,0:T(8,128)S(1)}, u32[]{:S(2)}, u32[]{:S(2)}) collective-permute-start(f32[128,1024]{1,0:T(8,128)S(1)} %fusion.12), channel_id=1, source_target_pairs={{0,1},{1,0},{2,3},{3,2},{4,5},{5,4},{6,7},{7,6},{8,9},{9,8},{10,11... | collective-permute-start | bytes 1572872 | tf_op jit(solution)/shard_map/ppermute | solution.py:848
  540.4 6.6 %collective-permute-start.55 = (f32[64,512]{1,0:T(8,128)S(1)}, f32[64,512]{1,0:T(8,128)S(1)}, u32[]{:S(2)}, u32[]{:S(2)}) collective-permute-start(f32[64,512]{1,0:T(8,128)S(1)} %bitcast_add_fusion.25), channel_id=1, source_target_pairs={{0,2},{1,3},{2,0},{3,1},{4,6},{5,7},{6,4},{7,5},{8,10},{9,11},{10,... | collective-permute-start | bytes 393224 | tf_op jit(solution)/shard_map/ppermute | solution.py:848
  541.0 4.5 collective-permute-start.58
  545.5 5.8 %collective-permute-start.56 = (f32[64,512]{1,0:T(8,128)S(1)}, f32[64,512]{1,0:T(8,128)S(1)}, u32[]{:S(2)}, u32[]{:S(2)}) collective-permute-start(f32[64,512]{1,0:T(8,128)S(1)} %bitcast_add_fusion.23), channel_id=1, source_target_pairs={{0,2},{1,3},{2,0},{3,1},{4,6},{5,7},{6,4},{7,5},{8,10},{9,11},{10,... | collective-permute-start | bytes 393224 | tf_op jit(solution)/shard_map/ppermute | solution.py:848
  547.0 5.8 %collective-permute-start.57 = (f32[64,512]{1,0:T(8,128)S(1)}, f32[64,512]{1,0:T(8,128)S(1)}, u32[]{:S(2)}, u32[]{:S(2)}) collective-permute-start(f32[64,512]{1,0:T(8,128)S(1)} %bitcast_add_fusion.21), channel_id=1, source_target_pairs={{0,2},{1,3},{2,0},{3,1},{4,6},{5,7},{6,4},{7,5},{8,10},{9,11},{10,... | collective-permute-start | bytes 393224 | tf_op jit(solution)/shard_map/ppermute | solution.py:848
  552.9 5.2 collective-permute-start.62
  553.0 5.1 collective-permute-start.63
  553.5 4.6 collective-permute-start.64
  (86 other events, 486.9 us)

commit v3 on v2

--- a/solution.py
+++ b/solution.py
@@ -35,7 +35,7 @@
 TN = (((0,), (0,)), ((), ()))
 
 
-def params(mib=48):
+def params(mib=52):
     return pltpu.CompilerParams(vmem_limit_bytes=mib * 2**20)
 
 
@@ -319,15 +319,18 @@
 
 
 def mix_kernel(
-    keep, features, solved, attend, gate, gain, state_in, starts_out, new_out, mixed_out, normed_out,
-    state,
+    keep, place, features, solved, attend, gate, gain, state_mine, state_other, starts_out, new_out,
+    mixed_out, normed_out, state,
 ):
     span = pl.program_id(0)
     heads = state.shape[0]
 
     @pl.when(span == 0)
     def _():
-        state[...] = state_in[...]
+        half = heads // 2
+        first = place[0] == 0
+        state[:half] = jnp.where(first, state_mine[...], state_other[...])
+        state[half:] = jnp.where(first, state_other[...], state_mine[...])
 
     query, key = features[0], features[1]
     erase, update = solved[0], solved[1]
@@ -352,9 +355,10 @@
         normed_out[:, lanes] = (shaped * (gates * sigmoid(gates))).astype(LOW)
 
 
-def mix(keep, features, solved, attend, gate, gain, state_in):
+def mix(keep, place, features, solved, attend, gate, gain, state_mine, state_other):
     _, count, width = features.shape
-    heads, size, _ = state_in.shape
+    half, size, _ = state_mine.shape
+    heads = 2 * half
     spans = count // SPAN
     f32 = lambda shape: jax.ShapeDtypeStruct(shape, jnp.float32)
     rows = pl.BlockSpec((SPAN, width), lambda c: (c, 0))
@@ -363,10 +367,11 @@
         mix_kernel,
         grid=(spans,),
         in_specs=[
-            pl.BlockSpec(memory_space=pltpu.SMEM), pairs, pairs,
+            pl.BlockSpec(memory_space=pltpu.SMEM), pl.BlockSpec(memory_space=pltpu.SMEM), pairs, pairs,
             pl.BlockSpec((1, heads // 2, 2 * SPAN, 2 * SPAN), lambda c: (c, 0, 0, 0)),
             rows, pl.BlockSpec((1, size), lambda c: (0, 0)),
-            pl.BlockSpec((heads, size, size), lambda c: (0, 0, 0)),
+            pl.BlockSpec((half, size, size), lambda c: (0, 0, 0)),
+            pl.BlockSpec((half, size, size), lambda c: (0, 0, 0)),
         ],
         out_specs=[
             pl.BlockSpec((1, heads, size, size), lambda c: (c, 0, 0, 0)), rows, rows, rows,
@@ -379,13 +384,13 @@
         compiler_params=params(),
         cost_estimate=cost(8 * count * width * size * 4, 40 * count * width),
         name="mix",
-    )(keep, features, solved, attend, gate, gain, state_in)
+    )(keep, place, features, solved, attend, gate, gain, state_mine, state_other)
 
 
 def feed_kernel(
     core, tokens, normed_head, grad_top, second_gain, out_w, gate_w, up_w, down_w,
     block_out, normed_out, inner_out, kept_out, sent_out, grad_hidden_out, branch_out, grad_head_out,
-    gain_grad_out, hidden, normed, total, grad_total,
+    gain_grad_out, head_turned_out, hidden, normed, total, grad_total,
 ):
     step = pl.program_id(0)
 
@@ -398,6 +403,7 @@
         ).astype(LOW)
         normed[...] = rounded
         normed_out[...] = rounded.astype(jnp.float32).T
+        head_turned_out[...] = normed_head[...].astype(jnp.float32).T
 
     @pl.when(step == 0)
     def _():
@@ -464,12 +470,12 @@
         ],
         out_specs=[
             rows, whole((width, count)), pl.BlockSpec((block, count), lambda j: (j, 0)), columns,
-            columns, rows, rows, rows, whole((1, width)),
+            columns, rows, rows, rows, whole((1, width)), whole((width, count)),
         ],
         out_shape=[
             low((count, width)), f32((width, count)), f32((hidden, count)), low((count, hidden)),
             f32((count, hidden)), f32((count, width)), f32((count, width)), f32((count, width)),
-            f32((1, width)),
+            f32((1, width)), f32((width, count)),
         ],
         scratch_shapes=[
             pltpu.VMEM((count, width), jnp.float32), pltpu.VMEM((count, width), LOW),
@@ -485,8 +491,8 @@
 
 
 def gather_kernel(
-    keep, grad_head, mixed, gate, gain, features, solved, grad_mixed_out, grad_gate_out, gain_out,
-    state,
+    keep, core, grad_head, grad_branch, mixed, gate, gain, features, solved, grad_mixed_out,
+    grad_gate_out, kept_out, sent_out, gain_out, state,
 ):
     step = pl.program_id(0)
     span = pl.num_programs(0) - 1 - step
@@ -514,7 +520,10 @@
         scale = lax.rsqrt(jnp.mean(rows * rows, -1, keepdims=True) + EPS)
         unit = rows * scale
         grad_gate = grad * unit * gain[...] * sigma * (1.0 + gates * (1.0 - sigma))
-        grad_gate_out[:, lanes] = grad_gate.astype(LOW).astype(jnp.float32)
+        grad_gate = grad_gate.astype(LOW).astype(jnp.float32)
+        grad_gate_out[:, lanes] = grad_gate
+        kept_out[:, lanes] = jnp.where(core[0] == 0, grad_branch[:, lanes], grad_gate).astype(LOW)
+        sent_out[:, lanes] = jnp.where(core[0] == 0, grad_gate, grad_branch[:, lanes])
         shaped = grad * gates * sigma
         gain_total = gain_total + jnp.sum(shaped * unit, 0, keepdims=True)
         inward = shaped * gain[...]
@@ -538,7 +547,9 @@
     gain_out[...] += gain_total
 
 
-def gather_states(keep, grad_head, mixed, gate, gain, features, solved, heads):
+def gather_states(
+    keep, core, grad_head, grad_branch, mixed, gate, gain, features, solved, heads
+):
     _, count, width = features.shape
     size = width // heads
     spans = count // SPAN
@@ -550,25 +561,26 @@
         gather_kernel,
         grid=(spans,),
         in_specs=[
-            pl.BlockSpec(memory_space=pltpu.SMEM), rows, rows, rows,
-            pl.BlockSpec((1, size), lambda c: (0, 0)), pairs, one,
+            pl.BlockSpec(memory_space=pltpu.SMEM), pl.BlockSpec(memory_space=pltpu.SMEM), rows, rows,
+            rows, rows, pl.BlockSpec((1, size), lambda c: (0, 0)), pairs, one,
         ],
         out_specs=[
-            rows, rows, pl.BlockSpec((1, size), lambda c: (0, 0)),
+            rows, rows, rows, rows, pl.BlockSpec((1, size), lambda c: (0, 0)),
             pl.BlockSpec((heads, size, size), lambda c: (0, 0, 0)),
         ],
         out_shape=[
-            f32((count, width)), f32((count, width)), f32((1, size)), f32((heads, size, size)),
+            f32((count, width)), f32((count, width)), jax.ShapeDtypeStruct((count, width), LOW),
+            f32((count, width)), f32((1, size)), f32((heads, size, size)),
         ],
         compiler_params=params(),
         cost_estimate=cost(8 * count * width * size * 4, 32 * count * width),
         name="gather_states",
-    )(keep, grad_head, mixed, gate, gain, features, solved)
+    )(keep, core, grad_head, grad_branch, mixed, gate, gain, features, solved)
 
 
 def back_kernel(
-    keep, features, beta, beta_pre, solved, inverses, starts, news, grad_mixed, state_in, pre, conv,
-    position, live, grad_pre_out, borrowed_out, conv_out, grad_beta_out, state, later, sums,
+    keep, place, features, beta, beta_pre, solved, inverses, starts, news, grad_mixed, state_mine,
+    state_other, pre, conv, position, live, grad_pre_out, borrowed_out, conv_out, grad_beta_out, state, later, sums,
 ):
     step = pl.program_id(0)
     span = pl.num_programs(0) - 1 - step
@@ -578,7 +590,10 @@
 
     @pl.when(step == 0)
     def _():
-        state[...] = state_in[...]
+        half = heads // 2
+        first = place[0] == 0
+        state[:half] = jnp.where(first, state_mine[...], state_other[...])
+        state[half:] = jnp.where(first, state_other[...], state_mine[...])
         sums[...] = jnp.zeros_like(sums)
         later[...] = jnp.zeros_like(later)
 
@@ -732,11 +747,12 @@
 
 
 def back(
-    keep, features, beta, beta_pre, solved, inverses, starts, news, grad_mixed, state_in, pre, conv,
-    position, live,
+    keep, place, features, beta, beta_pre, solved, inverses, starts, news, grad_mixed, state_mine,
+    state_other, pre, conv, position, live,
 ):
     _, count, width = features.shape
-    heads, size, _ = state_in.shape
+    half, size, _ = state_mine.shape
+    heads = 2 * half
     spans = count // SPAN
     taps = conv.shape[1]
     f32 = lambda shape: jax.ShapeDtypeStruct(shape, jnp.float32)
@@ -748,11 +764,11 @@
         back_kernel,
         grid=(spans,),
         in_specs=[
-            pl.BlockSpec(memory_space=pltpu.SMEM), triple, column, column,
+            pl.BlockSpec(memory_space=pltpu.SMEM), pl.BlockSpec(memory_space=pltpu.SMEM), triple, column, column,
             pl.BlockSpec((2, SPAN, width), lambda c: (0, spans - 1 - c, 0)),
             pl.BlockSpec((1, heads // 2, 2 * SPAN, 2 * SPAN), lambda c: (spans - 1 - c, 0, 0, 0)),
             pl.BlockSpec((1, heads, size, size), lambda c: (spans - 1 - c, 0, 0, 0)),
-            rows, rows, whole((heads, size, size)),
+            rows, rows, whole((half, size, size)), whole((half, size, size)),
             pl.BlockSpec((3, 1, SPAN + 8, width), lambda c: (0, spans - 1 - c, 0, 0)),
             whole(conv.shape),
             whole(position.shape), whole(live.shape),
@@ -770,8 +786,8 @@
         cost_estimate=cost(30 * count * width * size * 4, 60 * count * width),
         name="back",
     )(
-        keep, features, beta, beta_pre, solved, inverses, starts, news, grad_mixed, state_in, pre,
-        conv, position, live,
+        keep, place, features, beta, beta_pre, solved, inverses, starts, news, grad_mixed,
+        state_mine, state_other, pre, conv, position, live,
     )
 
 
@@ -853,98 +869,140 @@
     return lax.axis_index(axis) // bit % 2
 
 
-def apply_kernel(maps, state, out, *, turned):
+def apply_kernel(shift, maps, *refs, turned):
+    *states, out = refs
     size = maps.shape[1]
     for h in range(maps.shape[0]):
-        matrix = maps[h, :, size:]
-        moved = (t_product if turned else product)(matrix, state[h])
-        if state.shape[2] == size:
-            out[h] = moved + maps[h, :, :size]
+        state = states[0][h]
+        for other in states[1:]:
+            state = state + other[h]
+        moved = (t_product if turned else product)(maps[h, :, size:], state)
+        if state.shape[1] == size:
+            out[h] = moved + shift[h, :, :size]
         else:
-            out[h] = moved + jnp.concatenate([maps[h, :, :size], jnp.zeros_like(matrix)], 1)
-
-
-def apply_map(maps, state, turned=False):
+            out[h] = moved + jnp.concatenate([shift[h, :, :size], jnp.zeros((size, size), jnp.float32)], 1)
+
+
+def apply_map(shift, maps, *states, turned=False):
     return pl.pallas_call(
         lambda *refs: apply_kernel(*refs, turned=turned),
-        out_shape=jax.ShapeDtypeStruct(state.shape, jnp.float32),
-        compiler_params=params(),
-        cost_estimate=cost(2 * maps.size * state.shape[2], 4 * (maps.size + 2 * state.size)),
+        out_shape=jax.ShapeDtypeStruct(states[0].shape, jnp.float32),
+        compiler_params=params(4),
+        cost_estimate=cost(0, 0),
         name="apply_map",
-    )(maps, state)
+    )(shift, maps, *states)
+
+
+def ends_kernel(here, shift, maps, state, come, stay_out, send_out, *, turned):
+    size = maps.shape[1]
+    mine = here[0] == 0
+    for h in range(maps.shape[0]):
+        near = state[h] + come[h]
+        far = (t_product if turned else product)(maps[h, :, size:], near) + shift[h, :, :size]
+        if turned:
+            near, far = far, near
+        stay_out[h] = jnp.where(mine, near, far)
+        send_out[h] = jnp.where(mine, far, near)
+
+
+def pair_ends(here, shift, maps, state, come, turned=False):
+    shape = jax.ShapeDtypeStruct(state.shape, jnp.float32)
+    vmem = pl.BlockSpec(memory_space=pltpu.VMEM)
+    return pl.pallas_call(
+        lambda *refs: ends_kernel(*refs, turned=turned),
+        in_specs=[pl.BlockSpec(memory_space=pltpu.SMEM)] + [vmem] * 4,
+        out_specs=[vmem, vmem],
+        out_shape=[shape, shape],
+        compiler_params=params(4),
+        cost_estimate=cost(0, 0),
+        name="pair_ends",
+    )(here, shift, maps, state, come)
 
 
 def carried_forward(maps):
     heads, size, _ = maps.shape
+    half = heads // 2
     if not tuned():
         gathered = lax.all_gather(maps, "seq")
 
         def one(lap, state):
-            return apply_map(lax.dynamic_index_in_dim(gathered, lap, 0, False), state)
-
-        zeros = jnp.zeros((heads, size, size), jnp.float32)
-        return lax.fori_loop(0, lax.axis_index("seq"), one, zeros), (maps,)
-    half = heads // 2
-    here, z = side("x") == 0, lax.axis_index("seq") // 2
+            each = lax.dynamic_index_in_dim(gathered, lap, 0, False)
+            return apply_map(each, each, state)
+
+        state = lax.fori_loop(
+            0, lax.axis_index("seq"), one, jnp.zeros((heads, size, size), jnp.float32)
+        )
+        return state[:half], state[half:], jnp.zeros((1,), jnp.int32), (maps,)
+    place = side("x").astype(jnp.int32).reshape(1)
+    here = place[0] == 0
     kept = jnp.where(here, maps[:half], maps[half:])
     other = hop(jnp.where(here, maps[half:], maps[:half]), "x")
     first, second = jnp.where(here, kept, other), jnp.where(here, other, kept)
-    pair_map = apply_map(second, first)
+    pair_map = apply_map(second, second, first)
     state = jnp.zeros((half, size, size), jnp.float32)
+    come = state
     for step in range(3):
-        sent = pair_map[:, :, :size] if step == 0 else apply_map(pair_map, state)
-        state = state + lax.ppermute(sent, "seq", [(2 * step + x, 2 * step + 2 + x) for x in range(2)])
-    moved = apply_map(first, state)
-    mine = jnp.where(here, state, moved)
-    other = hop(jnp.where(here, moved, state), "x")
-    low, high = jnp.where(here, mine, other), jnp.where(here, other, mine)
-    return jnp.concatenate([low, high], 0), (first, second, pair_map)
+        if step == 0:
+            sent = pair_map[:, :, :size]
+        else:
+            sent = apply_map(pair_map, pair_map, state, come)
+            state = state + come
+        come = lax.ppermute(sent, "seq", [(2 * step + x, 2 * step + 2 + x) for x in range(2)])
+    mine, send = pair_ends(place, first, first, state, come)
+    return mine, hop(send, "x"), place, (first, second, pair_map)
 
 
 def together(value, *others):
     return lax.optimization_barrier((value, *others))
 
 
-def carried_back(shift, context, beside=((), (), ())):
+def carried_back(shift, context, beside=None):
     heads, size, _ = shift.shape
+    half = heads // 2
     if not tuned():
-        gathered = lax.all_gather(
-            jnp.concatenate([shift, context[0][:, :, size:]], 2), "seq"
-        )
+        gathered = lax.all_gather(jnp.concatenate([shift, context[0][:, :, size:]], 2), "seq")
         count = lax.axis_size("seq")
 
         def one(lap, state):
-            maps = lax.dynamic_index_in_dim(gathered, count - 1 - lap, 0, False)
-            return apply_map(maps, state, True)
+            each = lax.dynamic_index_in_dim(gathered, count - 1 - lap, 0, False)
+            return apply_map(each, each, state, turned=True)
 
         zeros = jnp.zeros((heads, size, size), jnp.float32)
-        return lax.fori_loop(0, count - 1 - lax.axis_index("seq"), one, zeros), ()
+        state = lax.fori_loop(0, count - 1 - lax.axis_index("seq"), one, zeros)
+        return state[:half], state[half:], ()
     first, second, pair_map = context
-    half = heads // 2
-    here = side("x") == 0
+    place = side("x").astype(jnp.int32).reshape(1)
+    here = place[0] == 0
+    done = []
+
+    def step_with(number, sent, go):
+        moves, work = beside[number]
+        sent, *values = together(sent, *[value for value, _ in moves])
+        come, *rest = together(
+            go(sent), *[hop(value, way) for value, (_, way) in zip(values, moves)], *work
+        )
+        done.append(rest)
+        return come
+
     kept = jnp.where(here, shift[:half], shift[half:])
-    other = hop(jnp.where(here, shift[half:], shift[:half]), "x")
-    other, *done = together(other, *beside[0])
-    first = jnp.concatenate([jnp.where(here, kept, other), first[:, :, size:]], 2)
-    second = jnp.concatenate([jnp.where(here, other, kept), second[:, :, size:]], 2)
-    pair_map = jnp.concatenate([apply_map(first, second[:, :, :size], True), pair_map[:, :, size:]], 2)
+    other = step_with(0, jnp.where(here, shift[half:], shift[:half]), lambda value: hop(value, "x"))
+    first_shift, second_shift = jnp.where(here, kept, other), jnp.where(here, other, kept)
+    pair_shift = apply_map(first_shift, first, second_shift, turned=True)
     state = jnp.zeros((half, size, size), jnp.float32)
+    come = state
     for step in range(3, 0, -1):
-        sent = pair_map[:, :, :size] if step == 3 else apply_map(pair_map, state, True)
-        come = lax.ppermute(sent, "seq", [(2 * step + x, 2 * step - 2 + x) for x in range(2)])
-        if step > 1:
-            come, *more = together(come, *beside[4 - step])
-            done += more
-        state = state + come
-    moved = apply_map(second, state, True)
-    mine = jnp.where(here, moved, state)
-    other = jnp.where(here, state, moved)
-    other = hop(other, "x")
-    low, high = jnp.where(here, mine, other), jnp.where(here, other, mine)
-    return jnp.concatenate([low, high], 0), done
-
-
-def outer_kernel(bit, *refs, blocks, post):
+        if step == 3:
+            sent = pair_shift
+        else:
+            sent = apply_map(pair_shift, pair_map, state, come, turned=True)
+            state = state + come
+        pairs = [(2 * step + x, 2 * step - 2 + x) for x in range(2)]
+        come = step_with(4 - step, sent, lambda value: lax.ppermute(value, "seq", pairs))
+    mine, send = pair_ends(place, second_shift, second, state, come, turned=True)
+    return mine, step_with(4, send, lambda value: hop(value, "x")), done
+
+
+def outer_kernel(bit, *refs, blocks, post, pieces):
     count = len(blocks)
     lefts, rights = refs[: 2 * count], refs[2 * count : 4 * count]
     *outs, stacked = refs[4 * count :]
@@ -956,11 +1014,6 @@
     def _():
         for piece in range(count):
             for which in range(2):
-                if len(outs) == 1:
-                    stacked[piece, :, which * tokens : (which + 1) * tokens] = lefts[
-                        2 * piece + which
-                    ][...].astype(LOW)
-                    continue
                 for start in range(0, half, post):
                     for place, mine in ((start, bit[0]), (half + start, 1 - bit[0])):
                         rows = pl.ds(pl.multiple_of(2 * start + mine * post, 8), post)
@@ -976,14 +1029,16 @@
             right = jnp.concatenate(
                 [rights[2 * piece][...].astype(LOW), rights[2 * piece + 1][...].astype(LOW)], 0
             )
-            for index, out in enumerate(outs):
-                out[...] = mxu(stacked[piece, index * half : (index + 1) * half, :], right, NN)
-
-
-def outer(pieces, way=None):
+            place = 0
+            for out, size in zip(outs, (half, *pieces)):
+                out[...] = mxu(stacked[piece, place : place + size, :], right, NN)
+                place += size
+
+
+def outer(pieces, way, parts=1):
     rows, tokens = pieces[0][0].shape
     block = 2 * LANES
-    post = rows // 8 * {"near": 2, "x": 1}.get(way, 0) or rows // 16
+    post = rows // 16 if way == "y" else rows // 8 * {"far": 4, "near": 2, "x": 1}[way]
     counts = [piece[5] for piece in pieces]
     left = pl.BlockSpec((rows, tokens), lambda j: (0, 0), pipeline_mode=pl.Buffered(1))
     lefts, rights, specs = [], [], []
@@ -996,23 +1051,24 @@
 
         specs += [pl.BlockSpec((tokens, block), place)] * 2
     total = sum(counts)
-    number = 2 if way else 1
-    out = pl.BlockSpec((rows // number, block), lambda j: (0, j))
-    shape = jax.ShapeDtypeStruct((rows // number, total * block), jnp.float32)
-    bit = side(way).astype(jnp.int32).reshape(1) if way else jnp.zeros((1,), jnp.int32)
-    return pl.pallas_call(
-        lambda *refs: outer_kernel(*refs, blocks=counts, post=post),
+    eighth = rows // 16
+    sizes = [eighth * 8 // parts // 16 * 16] * (parts - 1)
+    sizes = [*sizes, rows // 2 - sum(sizes)]
+    outs = [rows // 2, *sizes]
+    keep, *sends = pl.pallas_call(
+        lambda *refs: outer_kernel(*refs, blocks=counts, post=post, pieces=sizes),
         grid=(total,),
         in_specs=[pl.BlockSpec(memory_space=pltpu.SMEM)] + [left] * len(lefts) + specs,
-        out_specs=[out] * number,
-        out_shape=[shape] * number,
+        out_specs=[pl.BlockSpec((size, block), lambda j: (0, j)) for size in outs],
+        out_shape=[jax.ShapeDtypeStruct((size, total * block), jnp.float32) for size in outs],
         scratch_shapes=[pltpu.VMEM((len(pieces), rows, 2 * tokens), LOW)],
         compiler_params=params(),
         cost_estimate=cost(
             4 * rows * tokens * total * block, 4 * rows * total * block + 8 * tokens * rows
         ),
         name="outer",
-    )(bit, *lefts, *rights)
+    )(side(way).astype(jnp.int32).reshape(1), *lefts, *rights)
+    return keep, sends
 
 
 def take(value, place, axis):
@@ -1020,36 +1076,72 @@
 
 
 class Part:
-    def __init__(self, keep, first):
-        names = ["far", "near", "x", "y"]
-        names.remove(first)
-        self.names, self.come = names, None
-        self.keep = keep.reshape(2, 2, 2, keep.shape[0] // 8, keep.shape[1])
-
-    def arrived(self, come):
-        self.come = come.reshape(self.keep.shape)
-
-    def split(self, way):
-        at, bit = self.names.index(way), side(way)
-        self.names.remove(way)
-        send = take(self.keep, 1 - bit, at) + take(self.come, 1 - bit, at)
-        self.keep = take(self.keep, bit, at) + take(self.come, bit, at)
-        return send
-
-    def total(self):
-        self.keep = self.keep + self.come
-        return self.keep
+    def __init__(self, keep, order):
+        self.order, self.stage = order, 1
+        self.names = [name for name in ("far", "near", "x", "y") if name != order[0]]
+        shape = (2, 2, 2, keep.shape[0] // 8, keep.shape[1])
+        self.terms = [(keep.reshape(shape), tuple(self.names))]
+
+    def begun(self, pieces):
+        come = pieces[0] if len(pieces) == 1 else jnp.concatenate(pieces, 0)
+        self.absorb(come)
+
+    def absorb(self, come):
+        shape = (2,) * len(self.names) + self.terms[0][0].shape[-2:]
+        self.terms.append((come.reshape(shape), tuple(self.names)))
+
+    def chosen(self, bits):
+        total = None
+        for value, names in self.terms:
+            starts, sizes = [], []
+            for name in names:
+                fixed = name in bits or name not in self.names
+                starts.append(bits.get(name, side(name)) if fixed else 0)
+                sizes.append(1 if fixed else 2)
+            sizes += value.shape[len(names) :]
+            starts = [jnp.asarray(start, jnp.int32) for start in [*starts, 0, 0]]
+            piece = lax.dynamic_slice(value, starts, sizes)
+            piece = piece.reshape([size for size, name in zip(sizes, names) if size > 1] + sizes[-2:])
+            total = piece if total is None else total + piece
+        return total
+
+    def move(self):
+        stage, self.stage = self.stage, self.stage + 1
+        if stage < 4 and (stage < 3 or self.order[3] != "y"):
+            way = self.order[stage]
+            send = self.chosen({way: 1 - side(way)})
+            self.names.remove(way)
+            return send, way
+        if stage < 5:
+            self.stage = 5
+            self.keep = self.chosen({})
+            self.absorb = self.whole if stage == 4 else self.summed
+            return self.keep, "y"
+        self.absorb = lambda come: setattr(self, "other", come)
+        return self.done, "core"
 
     def whole(self, come):
         first = side("y") == 0
-        return jnp.concatenate(
+        self.done = jnp.concatenate(
             [jnp.where(first, self.keep, come), jnp.where(first, come, self.keep)], 0
         )
 
-
-def swaps(moves):
+    def summed(self, come):
+        self.done = (self.keep + come).reshape(-1, come.shape[-1])
+
+
+def swaps(moves, *beside):
     values = together(*[value for value, _ in moves])
-    return together(*[hop(value, way) for value, (_, way) in zip(values, moves)])
+    comes = [hop(value, way) for value, (_, way) in zip(values, moves)]
+    done = together(*comes, *beside)
+    return done[: len(moves)], done[len(moves) :]
+
+
+def advance(parts, extra=()):
+    comes, _ = swaps([part.move() for part in parts] + list(extra))
+    for part, come in zip(parts, comes):
+        part.absorb(come)
+    return comes[len(parts) :]
 
 
 def flatten_small(small):
@@ -1119,23 +1211,20 @@
         gate_weight, beta_weight, conv_weight,
     )
     solved, inverses, attend, maps = prepare(keep, features, beta)
-    state_in, context = carried_forward(maps)
+    state_mine, state_other, place, context = carried_forward(maps)
     starts, news, mixed, normed_head = mix(
-        keep, features, solved, attend, gate_pre, head_gain[None], state_in
-    )
-    head_turned = normed_head.T.astype(jnp.float32)
+        keep, place, features, solved, attend, gate_pre, head_gain[None], state_mine, state_other
+    )
     (
         block_out, two_turned, inner_turned, kept, sent, grad_hidden, grad_branch, grad_head,
-        grad_second_gain,
+        grad_second_gain, head_turned,
     ) = feed(
         core, rows, normed_head, top, second_gain[None], out_weight, hidden_gate, hidden_up,
         hidden_down,
     )
-    grad_mixed, grad_gate_pre, grad_head_gain, shift = gather_states(
-        keep, grad_head, mixed, gate_pre, head_gain[None], features, solved, heads
-    )
     if tuned():
         half = width // 2
+        units = half // 256
 
         def pick(zero, one):
             return jnp.where(here, zero, one)
@@ -1148,57 +1237,72 @@
             pick(top[:, :half], top[:, half:]), pick(wide_top[:, half:], wide_top[:, :half])
         )
         one = both(normed_one)
-        two = both(two_turned)
         inners = both(inner_turned)
         heads_turned = both(head_turned)
+        two = both(two_turned)
         gate_up = both(kept, sent)
+    grad_mixed, grad_gate_pre, out_kept, out_sent, grad_head_gain, shift = gather_states(
+        keep, core, grad_head, grad_branch, mixed, gate_pre, head_gain[None], features, solved, heads
+    )
+    if tuned():
         out_left = pick(heads_turned[0], one[0]), pick(heads_turned[1], one[1])
-        out_right = both(pick(grad_branch, grad_gate_pre), pick(grad_gate_pre, grad_branch))
+        out_right = both(out_kept, out_sent)
         blocks = hidden_gate.shape[1] // 256
-        low = blocks // 2
-        some = width // 512
-        early = (
-            outer([(*two, *gate_up, 0, low), (*out_left, *out_right, 0, some)], "x"),
-            outer(
-                [
-                    (*two, *gate_up, low, blocks - low),
-                    (*out_left, *out_right, some, width // 256 - some),
-                ],
-                "y",
-            ),
-            outer([(*inners, *tops, 0, half // 256)], "near"),
-        )
-        state_grad, done = carried_back(shift, context, early)
-        keeps, sends = done[0::2], done[1::2]
-        ways = ("x", "y", "near")
-        cuts = [send.shape[0] // 2 for send in sends]
-        state_grad, *begun = together(state_grad, *(s[:c] for s, c in zip(sends, cuts)))
-        begun = [hop(value, way) for value, way in zip(begun, ways)]
+        some = blocks * 3 // 11
+        down_keep, down_sends = outer([(*inners, *tops, 0, units)], "y", 5)
+        shift, down_keep, *down_sends = together(shift, down_keep, *down_sends)
+        rest_keep, rest_sends = outer([(*two, *gate_up, some, blocks - some)], "y", 2)
+        out_keep, out_sends = outer([(*out_left, *out_right, 0, width // 256)], "near")
+        some_keep, some_sends = outer([(*two, *gate_up, 0, some)], "x")
+        work = [
+            (rest_keep, *rest_sends), (out_keep, *out_sends), (some_keep, *some_sends), (), (),
+        ]
+        moves = [[(send, "y")] for send in down_sends]
+        grad_mine, grad_other, done = carried_back(
+            shift, context, list(zip(moves, work))
+        )
+        down_come = [value[0] for value in done]
+        rest_keep, *rest_sends = done[0][1:]
+        out_keep, *out_sends = done[1][1:]
+        some_keep, *some_sends = done[2][1:]
+        down = Part(down_keep, ("y", "x", "near", "far"))
+        rest = Part(rest_keep, ("y", "x", "near", "far"))
+        some_part = Part(some_keep, ("x", "near", "far", "y"))
+        out = Part(out_keep, ("near", "far", "y", "x"))
+        down.begun(down_come)
+        moves = [down.move(), (rest_sends[0], "y"), (out_sends[0], "near")]
+        grad_mine, *values = together(grad_mine, *[value for value, _ in moves])
+        comes = [hop(value, way) for value, (_, way) in zip(values, moves)]
     else:
-        state_grad, _ = carried_back(shift, context)
+        grad_mine, grad_other, _ = carried_back(shift, context)
     grads, borrowed, grad_conv, grad_beta_pre = back(
-        keep, features, beta, beta_pre, solved, inverses, starts, news, grad_mixed, state_grad, pre,
-        conv_weight, position, live,
+        keep, place, features, beta, beta_pre, solved, inverses, starts, news, grad_mixed, grad_mine,
+        grad_other, pre, conv_weight, position, live,
     )
     if tuned():
-        borrowed, *begun = together(borrowed, *begun)
+        borrowed, *comes = together(borrowed, *comes)
+        down.absorb(comes[0])
+        rest_come = [comes[1]]
+        out.begun([comes[2]])
     returned = passed_along(borrowed, "seq", -1)
     tail = grads[:, count - 8 :] + returned
     grads = lax.dynamic_update_slice(grads, tail, (0, count - 8, 0))
     grads = grads.astype(LOW)
     if tuned():
-        grads, *rest = together(grads, *(s[c:] for s, c in zip(sends, cuts)))
-        rest = [hop(value, way) for value, way in zip(rest, ways)]
+        moves = [(some_sends[0], "x"), (rest_sends[1], "y"), down.move(), out.move()]
+        grads, *values = together(grads, *[value for value, _ in moves])
+        comes = [hop(value, way) for value, (_, way) in zip(values, moves)]
         wide = grads.astype(jnp.float32)
         query_key = both(pick(grads[0], grads[1]), pick(wide[1], wide[0]))
         value = both(
             pick(grads[2, :, :half], grads[2, :, half:]), pick(wide[2, :, half:], wide[2, :, :half])
         )
+        orders = (("y", "x", "near", "far"), ("near", "y", "x", "far"))
         late = (
-            outer([(*one, *query_key, 0, half // 256)], "x"),
-            outer([(*one, *query_key, half // 256, half // 256)], "y"),
-            outer([(*one, *value, 0, half // 256)], "near"),
-        )
+            outer([(*one, *query_key, 0, units), (*one, *value, 0, units)], "y"),
+            outer([(*one, *query_key, units, units)], "near"),
+        )
+        grads, *late_sends = together(grads, *[send for _, (send,) in late])
         input_grad, grad_first_gain = enter(
             rows, first_gain[None], grad_hidden, grads, grad_gate_pre, grad_beta_pre, query_weight,
             key_weight, value_weight, gate_weight, beta_weight,
@@ -1208,62 +1312,44 @@
             grad_second_gain[0],
         )
         flat = flatten_small(small)
-        sends = [send for _, send in late]
-        early = [Part(keep_, way) for keep_, way in zip(keeps, ways)]
-        late = [Part(keep_, way) for (keep_, _), way in zip(late, ways)]
-        input_grad, flat, *joined = together(input_grad, flat, *rest, *sends)
-        rest, sends = joined[:3], joined[3:]
-        for part, one_half, other_half in zip(early, begun, rest):
-            part.arrived(jnp.concatenate([one_half, other_half], 0))
-        orders = (("y", "near", "far"), ("near", "x", "far"), ("x", "y", "far"))
-
-        def stage(parts, lap):
-            return [(part.split(order[lap]), order[lap]) for part, order in zip(parts, orders)]
-
-        def arrive(parts, comes):
-            for part, come in zip(parts, comes):
-                part.arrived(come)
-
-        *comes, flat_come = swaps(stage(early, 0) + list(zip(sends, ways)) + [(flat, "core")])
+        late_sends[0], *comes = together(late_sends[0], *comes)
+        some_part.begun([comes[0]])
+        rest.begun([*rest_come, comes[1]])
+        down.absorb(comes[2])
+        out.absorb(comes[3])
+        late = [Part(keep_, order) for (keep_, _), order in zip(late, orders)]
+        comes, (flat, input_grad) = swaps(
+            [part.move() for part in (rest, some_part, down)]
+            + [(send, order[0]) for send, order in zip(late_sends, orders)],
+            flat, input_grad,
+        )
+        for part, come in zip((rest, some_part, down), comes):
+            part.absorb(come)
+        for part, come in zip(late, comes[3:]):
+            part.begun([come])
+        (flat_come,) = advance([out, some_part, rest, *late, down], [(flat, "core")])
         flat = (flat + flat_come).reshape(4, 2, -1, 128)
         bit = side("x")
-        tiny = Part(take(flat, bit, 1).reshape(-1, 128), "x")
+        tiny = Part(take(flat, bit, 1).reshape(-1, 128), ("x", "y", "near", "far"))
         tiny_send = take(flat, 1 - bit, 1).reshape(-1, 128)
-        arrive(early + late, comes)
-        for lap, way, following in ((0, "x", "y"), (1, "y", "near")):
-            *comes, flat_come = swaps(
-                stage(early, lap + 1) + stage(late, lap) + [(tiny_send, way)]
-            )
-            tiny.arrived(flat_come)
-            tiny_send = tiny.split(following)
-            arrive(early + late, comes)
-        *comes, flat_come = swaps(
-            [(part.total(), "y") for part in early] + stage(late, 2) + [(tiny_send, "near")]
-        )
-        tiny.arrived(flat_come)
-        early = [part.whole(come) for part, come in zip(early, comes)]
-        arrive(late, comes[3:])
-        a, b = low * 256, (blocks - low) * 256
-        own = (
-            jnp.concatenate([early[0][:, :a], early[1][:, :b]], 1), early[2],
-            jnp.concatenate([early[0][:, a:], early[1][:, b:]], 1),
-        )
-        *comes, flat_come, other_a, other_b, other_c = swaps(
-            [(part.total(), "y") for part in late] + [(tiny.split("far"), "far")]
-            + [(value, "core") for value in own]
-        )
-        late = [part.whole(come) for part, come in zip(late, comes)]
-        tiny.arrived(flat_come)
-        own = (*own, jnp.concatenate(late[:2], 1), late[2])
-        *last, flat_come = swaps([(own[3], "core"), (own[4], "core"), (tiny.total(), "y")])
-        other = (other_a, other_b, other_c, *last)
-        zero = [pick(m, o) for m, o in zip(own, other)]
-        one_ = [pick(o, m) for m, o in zip(own, other)]
-        query_g, key_g = zero[3], one_[3]
-        value_g = jnp.concatenate([zero[4], one_[4]], 1)
-        gate_g, out_g, hidden_gate_g, hidden_up_g = one_[2], zero[2], zero[0], one_[0]
-        hidden_down_g = jnp.concatenate([zero[1], one_[1]], 1)
-        first_g, beta_g, conv_g, head_g, second_g = unflatten_small(tiny.whole(flat_come), small)
+        tiny_come = advance([out, some_part, rest, *late, down], [(tiny_send, "x")])
+        tiny.begun(tiny_come)
+        advance([rest, out, *late, tiny, some_part])
+        advance([*late, tiny, rest, out])
+        advance([*late, tiny])
+        advance([tiny])
+        advance([tiny])
+        zero = lambda part: pick(part.done, part.other)
+        one_ = lambda part: pick(part.other, part.done)
+        columns = half
+        query_g = jnp.concatenate([zero(late[0])[:, :columns], zero(late[1])], 1)
+        key_g = jnp.concatenate([one_(late[0])[:, :columns], one_(late[1])], 1)
+        value_g = jnp.concatenate([zero(late[0])[:, columns:], one_(late[0])[:, columns:]], 1)
+        out_g, gate_g = zero(out), one_(out)
+        hidden_gate_g = jnp.concatenate([zero(some_part), zero(rest)], 1)
+        hidden_up_g = jnp.concatenate([one_(some_part), one_(rest)], 1)
+        hidden_down_g = jnp.concatenate([zero(down), one_(down)], 1)
+        first_g, beta_g, conv_g, head_g, second_g = unflatten_small(tiny.done, small)
     else:
         input_grad, grad_first_gain = enter(
             rows, first_gain[None], grad_hidden, grads, grad_gate_pre, grad_beta_pre, query_weight,

time: 572 us -> 549 us (0.960)
  waiting for transfers between devices: 229 us -> 206 us
  local copies, waits for them, and re-layouts: 41.8 us -> 19.9 us
  Pallas kernels: 153 us -> 163 us
  starting transfers between devices: 69.5 us -> 78.7 us
    ppermute x57 -> x59, waiting for transfers between devices: 205 us -> 189 us  [hop(): lax.ppermute(value, axis, [(i, i ^ bit) for i in range(lax.axis_size(axis...]
    unnamed x172 -> x98, local copies, waits for them, and re-layouts: 29.5 us -> 15.3 us
    ppermute x57 -> x59, starting transfers between devices: 53.8 us -> 64.6 us  [hop(): lax.ppermute(value, axis, [(i, i ^ bit) for i in range(lax.axis_size(axis...]
    add x36 -> x29, other arithmetic: 31.2 us -> 40 us  [the longest x27 39.9 us: chosen(): total = piece if total is None else total + piece]
    slice x6 -> x3, local copies, waits for them, and re-layouts: 6.68 us -> 0.09 us  [the longest x1 0.04 us: local(): one_(late[0])[:, columns:]]
  transfers between devices with their start and end apart: 65 -> 67, of which waited for: 31 -> 31; matrix products, arithmetic and copies ran while one was open for 5% -> 7% of each run, Pallas kernels for 16% -> 18%
where the time goes in v3:
time: 549 us; the launch traced here: 542 us
  waiting for transfers between devices  206 us (38%)
  Pallas kernels  163 us (30%)
  starting transfers between devices  78.7 us (14%)
  other arithmetic  70.3 us (13%)
  local copies, waits for them, and re-layouts  19.9 us (4%)
    ppermute x59, waiting for transfers between devices, hop(): lax.ppermute(value, axis, [(i, i ^ bit) for i in range(lax.axis_size(axis...  189 us
    ppermute x59, starting transfers between devices, hop(): lax.ppermute(value, axis, [(i, i ^ bit) for i in range(lax.axis_size(axis...  64.6 us
    pallas_call x6, Pallas kernels, outer(): pl.pallas_call(lambda *refs: outer_kernel(*refs, blocks=counts, post=post...  43 us
    add x27, other arithmetic, chosen(): total = piece if total is None else total + piece  39.9 us
    pallas_call x1, Pallas kernels, back(): pl.pallas_call(back_kernel, grid=(spans,), in_specs=[pl.BlockSpec(memory_...  32.7 us
    pallas_call x1, Pallas kernels, feed(): pl.pallas_call(feed_kernel, grid=(hidden // block,), in_specs=[pl.BlockSp...  27.2 us
    pallas_call x1, Pallas kernels, prepare(): pl.pallas_call(prepare_kernel, grid=(spans,), in_specs=[pl.BlockSpec(memo...  16.9 us
    unnamed x98, local copies, waits for them, and re-layouts  15.3 us
  transfers between devices with their start and end apart: 67, of which 31 were waited for; matrix products, arithmetic and copies ran while one was open for 7% of the time, Pallas kernels for 18%

profile of v3, /device:TPU:0, one launch (start us, length us, event | category | flops | bytes accessed | tf_op | source)
XLA Modules:
  0.0 542.2 jit_solution(7636664134791385683)
XLA Ops:
  1.4 4.8 collective-permute-start
  12.6 12.8 %project.1 = (f32[1024,384]{1,0:T(8,128)}, f32[3,6,72,1024]{3,2,1,0:T(8,128)}, f32[3,384,1024]{2,1,0:T(8,128)}, f32[384,1024]{1,0:T(8,128)}, f32[384,8]{1,0:T(8,128)S(1)}, /*index=5*/f32[384,8]{1,0:T(8,128)S(1)}) custom-call(bf16[384,1024]{1,0:T(8,128)(2,1)S(1)} %bitcast.241, f32[16,1024]{1,0:T(8,128)S(1)} %collective-permute-done.halo, ...), custom_call_target="tpu_custom_call" | custom-call | flops 1 | bytes 1 | tf_op jit(solution)/shard_map/project/pallas_call | solution.py:216
  26.1 16.9 %prepare.1 = (f32[2,384,1024]{2,1,0:T(8,128)}, f32[6,4,128,128]{3,2,1,0:T(8,128)}, f32[6,4,128,128]{3,2,1,0:T(8,128)}, f32[8,128,256]{2,1,0:T(8,128)S(1)}) custom-call(f32[6]{0:T(128)S(1)} %fusion.32.keep, f32[3,384,1024]{2,1,0:T(8,128)} %get-tuple-element.195.features, f32[384,8]{1,0:T(8,128)S(1)} %get-tuple-element.196.beta), custom_call_target="tpu_custom_call" | custom-call | flops 1 | bytes 1 | tf_op jit(solution)/shard_map/prepare/pallas_call | solution.py:299
  44.7 11.8 %collective-permute-done.1 = f32[4,128,256]{2,1,0:T(8,128)S(1)} collective-permute-done((f32[4,128,256]{2,1,0:T(8,128)S(1)}, f32[4,128,256]{2,1,0:T(8,128)S(1)}, u32[]{:S(2)}, u32[]{:S(2)}) %collective-permute-start.1) | collective-permute-done | bytes 524320 | tf_op jit(solution)/shard_map/ppermute | solution.py:864
  56.9 3.5 collective-permute-start.2
  60.4 4.3 collective-permute-done.2.refs_3_.refs_2_
  68.8 4.8 collective-permute-done.5.state_other
  73.6 8.5 %mix.1 = (f32[6,8,128,128]{3,2,1,0:T(8,128)}, f32[384,1024]{1,0:T(8,128)}, f32[384,1024]{1,0:T(8,128)}, bf16[384,1024]{1,0:T(8,128)(2,1)S(1)}) custom-call(f32[6]{0:T(128)S(1)} %fusion.32.keep, s32[1]{0:T(128)} %bitcast.6.refs_0_.place, f32[3,384,1024]{2,1,0:T(8,128)} %get-tuple-element.195.features, f32[2,384,1024]{2,1,0:T(8,128)} %get-tuple-element.197.solved, ...), custom_call_target="tpu_custom_call" | custom-call | flops 1 | bytes 1 | tf_op jit(solution)/shard_map/mix/pallas_call | solution.py:366
  82.1 27.2 %feed.1 = (bf16[384,1024]{1,0:T(8,128)(2,1)}, f32[1024,384]{1,0:T(8,128)}, f32[2816,384]{1,0:T(8,128)}, bf16[384,2816]{1,0:T(8,128)(2,1)}, f32[384,2816]{1,0:T(8...) custom-call(s32[1]{0:T(128)} %bitcast.core, ...), custom_call_target="tpu_custom_call" | custom-call | flops 1 | bytes 1 | tf_op jit(solution)/shard_map/feed/pallas_call | solution.py:462
  111.4 2.4 slice_select_fusion.2
  114.3 12.4 %collective-permute-done.7.refs_4_ = f32[384,512]{1,0:T(8,128)} collective-permute-done((f32[384,512]{1,0:T(8,128)}, f32[384,512]{1,0:T(8,128)}, u32[]{:S(2)}, u32[]{:S(2)}) %collective-permute-start.7) | collective-permute-done | bytes 786464 | tf_op jit(solution)/shard_map/ppermute | solution.py:864
  128.0 9.2 %gather_states.1 = (f32[384,1024]{1,0:T(8,128)}, f32[384,1024]{1,0:T(8,128)}, bf16[384,1024]{1,0:T(8,128)(2,1)S(1)}, f32[384,1024]{1,0:T(8,128)}, f32[1,128]{1,0:T(1,128)S(1)}, /*index=5*/f32[8,128,128]{2,1,0:T(8,128)S(1)}) custom-call(f32[6]{0:T(128)S(1)} %fusion.32.keep, s32[1]{0:T(128)} %bitcast.core, f32[384,1024]{1,0:T(8,128)} %get-tuple-element.205.grad_head, ...), custom_call_target="tpu_custom_call" | custom-call | flops 1 | bytes 1 | tf_op jit(solution)/shard_map/gather_states/pallas_call | solution.py:560
  138.4 8.3 %outer.6 = (f32[1408,512]{1,0:T(8,128)}, f32[272,512]{1,0:T(8,128)}, f32[272,512]{1,0:T(8,128)S(1)}, f32[272,512]{1,0:T(8,128)}, f32[272,512]{1,0:T(8,128)}, /*index=5*/f32[320,512]{1,0:T(8,128)}) custom-call(s32[1]{0:T(128)} %bitcast.14.refs_0_, f32[2816,384]{1,0:T(8,128)} %get-tuple-element.209.refs_1_, f32[2816,384]{1,0:T(8,128)} %collective-permute-done.6.refs_2_, ...), custom_call_target="tpu_custom_call" | custom-call | flops 1 | bytes 1 | tf_op jit(solution)/shard_map/outer/pallas_call | solution.py:1058
  152.7 10.4 %outer.7 = (f32[512,2048]{1,0:T(8,128)}, f32[256,2048]{1,0:T(8,128)}, f32[256,2048]{1,0:T(8,128)}) custom-call(s32[1]{0:T(128)} %bitcast.14.refs_0_, f32[1024,384]{1,0:T(8,128)S(1)} %copy-done.2, f32[1024,384]{1,0:T(8,128)} %collective-permute-done.10.refs_2_, bf16[384,2816]{1,0:T(8,128)(2,1)} %get-tuple-element.221.refs_3_, ...), custom_call_target="tpu_custom_call" | custom-call | flops 1 | bytes 1 | tf_op jit(solution)/shard_map/outer/pallas_call | solution.py:1058
  168.3 2.7 broadcast_select_fusion.refs_2_
  171.0 6.6 %outer.8 = (f32[512,1024]{1,0:T(8,128)}, f32[512,1024]{1,0:T(8,128)}) custom-call(s32[1]{0:T(128)} %bitcast.16.refs_0_, f32[1024,384]{1,0:T(8,128)} %broadcast_select_fusion.1.refs_1_, f32[1024,384]{1,0:T(8,128)} %broadcast_select_fusion.refs_2_, bf16[384,1024]{1,0:T(8,128)(2,1)S(1)} %copy-done.14, f32[384,1024]{1,0:T(8,128)} %collective-permute-done.16.refs_4_), custom_call_target="tpu_custom_call" | custom-call | flops 1 | bytes 1 | tf_op jit(solution)/shard_map/outer/pallas_call | solution.py:1058
  181.2 5.7 %outer.9 = (f32[512,768]{1,0:T(8,128)S(1)}, f32[512,768]{1,0:T(8,128)}) custom-call(s32[1]{0:T(128)} %bitcast.6.refs_0_.place, f32[1024,384]{1,0:T(8,128)} %get-tuple-element.220.refs_1_, f32[1024,384]{1,0:T(8,128)} %collective-permute-done.10.refs_2_, bf16[384,2816]{1,0:T(8,128)(2,1)} %get-tuple-element.221.refs_3_, f32[384,2816]{1,0:T(8,128)} %collective-permute-done.11.refs_4_), custom_call_target="tpu_custom_call" | custom-call | flops 1 | bytes 1 | tf_op jit(solution)/shard_map/outer/pallas_call | solution.py:1058
  186.9 5.4 collective-permute-done.18
  194.9 12.0 %collective-permute-done.19.refs_4_ = f32[4,128,128]{2,1,0:T(8,128)S(1)} collective-permute-done((f32[4,128,128]{2,1,0:T(8,128)S(1)}, f32[4,128,128]{2,1,0:T(8,128)S(1)}, u32[]{:S(2)}, u32[]{:S(2)}) %collective-permute-start.19) | collective-permute-done | bytes 262176 | tf_op jit(solution)/shard_map/ppermute | solution.py:1000
  212.6 3.6 collective-permute-done.21.state_other
  216.2 5.2 collective-permute-done.22
  224.2 5.9 %collective-permute-start.25 = (f32[512,1024]{1,0:T(8,128)}, f32[512,1024]{1,0:T(8,128)}, u32[]{:S(2)}, u32[]{:S(2)}) collective-permute-start(f32[512,1024]{1,0:T(8,128)} %get-tuple-element.272), channel_id=1, source_target_pairs={{0,8},{4,12},{8,0},{12,4},{16,24},{20,28},{24,16},{28,20},{1,9},{5... | collective-permute-start | bytes 6291464 | tf_op jit(solution)/shard_map/ppermute | solution.py:864
  230.1 1.9 collective-permute-start.23
  232.0 32.7 %back.1 = (f32[3,384,1024]{2,1,0:T(8,128)}, f32[3,8,1024]{2,1,0:T(8,128)S(1)}, f32[3,4,1024]{2,1,0:T(4,128)S(1)}, f32[384,8]{1,0:T(8,128)S(1)}) custom-call(f32[6]{0:T(128)S(1)} %fusion.32.keep, s32[1]{0:T(128)} %bitcast.6.refs_0_.place, f32[3,384,1024]{2,1,0:T(8,128)} %get-tuple-element.195.features, f32[384,8]{1,0:T(8,128)S(1)} %copy-done.12, ...), custom_call_target="tpu_custom_call" | custom-call | flops 1 | bytes 1 | tf_op jit(solution)/shard_map/back/pallas_call | solution.py:763
  264.7 2.6 collective-permute-done.24
  267.3 4.4 collective-permute-done.25
  273.0 2.5 add_bitcast_fusion.3
  275.5 2.6 bitcast_add_fusion.1
  280.0 2.9 collective-permute-start.29
  282.9 8.8 %collective-permute-start.32 = (f32[2,2,64,1024]{3,2,1,0:T(8,128)}, f32[2,2,64,1024]{3,2,1,0:T(8,128)}, u32[]{:S(2)}, u32[]{:S(2)}) collective-permute-start(f32[2,2,64,1024]{3,2,1,0:T(8,128)} %add_bitcast_fusion.3), channel_id=1, source_target_pairs={{0,16},{4,20},{8,24},{12,28},{16,0},{20,4},{24,8},{28,12},{1,17},{... | collective-permute-start | bytes 3145736 | tf_op jit(solution)/shard_map/ppermute | solution.py:864
  295.8 4.6 outer.11
  301.4 7.6 %outer.10 = (f32[512,1024]{1,0:T(8,128)}, f32[512,1024]{1,0:T(8,128)}) custom-call(s32[1]{0:T(128)} %bitcast.14.refs_0_, f32[1024,384]{1,0:T(8,128)} %get-tuple-element.237.refs_1_.refs_3_, f32[1024,384]{1,0:T(8,128)} %collective-permute-done.15.refs_2_.refs_4_, f32[1024,384]{1,0:T(8,128)} %get-tuple-element.237.refs_1_.refs_3_, ...), custom_call_target="tpu_custom_call" | custom-call | flops 1 | bytes 1 | tf_op jit(solution)/shard_map/outer/pallas_call | solution.py:1058
  308.9 21.1 %collective-permute-done.31 = f32[2,176,512]{2,1,0:T(8,128)} collective-permute-done((f32[2,176,512]{2,1,0:T(8,128)}, f32[2,176,512]{2,1,0:T(8,128)}, u32[]{:S(2)}, u32[]{:S(2)}) %collective-permute-start.31) | collective-permute-done | bytes 720928 | tf_op jit(solution)/shard_map/ppermute | solution.py:864
  330.0 7.7 %collective-permute-done.32 = f32[2,2,64,1024]{3,2,1,0:T(8,128)} collective-permute-done((f32[2,2,64,1024]{3,2,1,0:T(8,128)}, f32[2,2,64,1024]{3,2,1,0:T(8,128)}, u32[]{:S(2)}, u32[]{:S(2)}) %collective-permute-start.32) | collective-permute-done | bytes 1048608 | tf_op jit(solution)/shard_map/ppermute | solution.py:864
  337.7 2.2 bitcast_add_fusion.12
  339.9 2.1 add_bitcast_fusion.4
  342.0 2.9 pad_maximum_fusion
  344.9 2.0 copy-done.27
  352.4 2.1 collective-permute-start.35
  354.6 2.6 fusion.2
  358.5 10.1 %enter.1 = (bf16[384,1024]{1,0:T(8,128)(2,1)}, f32[1,1024]{1,0:T(1,128)S(1)}) custom-call(bf16[384,1024]{1,0:T(8,128)(2,1)S(1)} %bitcast.243, f32[1,1024]{1,0:T(1,128)S(1)} %bitcast.252, f32[384,1024]{1,0:T(8,128)} %get-tuple-element.300.grad_hidden, bf16[3,384,1024]{2,1,0:T(8,128)(2,1)} %copy-done.26, f32[384,1024]{1,0:T(8,128)} %get-tuple-element.302.grad_gate, ...), custom_call_target="tpu_custom_call" | custom-call | flops 1 | bytes 1 | tf_op jit(solution)/shard_map/enter/pallas_call | solution.py:826
  368.7 2.3 bitcast_add_fusion.7
  371.0 25.8 %collective-permute-done.35 = f32[176,512]{1,0:T(8,128)} collective-permute-done((f32[176,512]{1,0:T(8,128)}, f32[176,512]{1,0:T(8,128)}, u32[]{:S(2)}, u32[]{:S(2)}) %collective-permute-start.35) | collective-permute-done | bytes 360480 | tf_op jit(solution)/shard_map/ppermute | solution.py:864
  399.8 3.1 bitcast_add_fusion
  403.0 2.1 bitcast_add_fusion.9
  405.0 1.9 add_bitcast_fusion.5
  406.9 2.3 add_bitcast_fusion.2
  409.3 2.7 collective-permute-start.40
  413.6 1.7 collective-permute-start.43
  417.4 7.6 %collective-permute-done.43 = f32[176,512]{1,0:T(8,128)S(1)} collective-permute-done((f32[176,512]{1,0:T(8,128)S(1)}, f32[176,512]{1,0:T(8,128)S(1)}, u32[]{:S(2)}, u32[]{:S(2)}) %collective-permute-start.43) | collective-permute-done | bytes 360480 | tf_op jit(solution)/shard_map/ppermute | solution.py:864
  427.4 14.7 %collective-permute-done.39 = f32[2,64,768]{2,1,0:T(8,128)S(1)} collective-permute-done((f32[2,64,768]{2,1,0:T(8,128)}, f32[2,64,768]{2,1,0:T(8,128)S(1)}, u32[]{:S(2)}, u32[]{:S(2)}) %collective-permute-start.39) | collective-permute-done | bytes 393248 | tf_op jit(solution)/shard_map/ppermute | solution.py:864
  442.2 2.5 collective-permute-done.42
  453.2 1.8 collective-permute-start.47
  456.4 6.3 %collective-permute-done.51 = f32[128,128]{1,0:T(8,128)S(1)} collective-permute-done((f32[128,128]{1,0:T(8,128)S(1)}, f32[128,128]{1,0:T(8,128)S(1)}, u32[]{:S(2)}, u32[]{:S(2)}) %collective-permute-start.51) | collective-permute-done | bytes 65568 | tf_op jit(solution)/shard_map/ppermute | solution.py:864
  465.0 7.1 %collective-permute-done.49 = f32[2,64,512]{2,1,0:T(8,128)S(1)} collective-permute-done((f32[2,64,512]{2,1,0:T(8,128)S(1)}, f32[2,64,512]{2,1,0:T(8,128)S(1)}, u32[]{:S(2)}, u32[]{:S(2)}) %collective-permute-start.49) | collective-permute-done | bytes 262176 | tf_op jit(solution)/shard_map/ppermute | solution.py:864
  473.4 6.0 %collective-permute-done.47 = f32[64,2048]{1,0:T(8,128)S(1)} collective-permute-done((f32[64,2048]{1,0:T(8,128)S(1)}, f32[64,2048]{1,0:T(8,128)S(1)}, u32[]{:S(2)}, u32[]{:S(2)}) %collective-permute-start.47) | collective-permute-done | bytes 524320 | tf_op jit(solution)/shard_map/ppermute | solution.py:864
  485.0 1.8 collective-permute-start.52
  489.0 15.8 %collective-permute-done.56 = f32[2,2,16,128]{3,2,1,0:T(8,128)S(1)} collective-permute-done((f32[2,2,16,128]{3,2,1,0:T(8,128)S(1)}, f32[2,2,16,128]{3,2,1,0:T(8,128)S(1)}, u32[]{:S(2)}, u32[]{:S(2)}) %collective-permute-start.56) | collective-permute-done | bytes 32800 | tf_op jit(solution)/shard_map/ppermute | solution.py:864
  504.8 7.2 %collective-permute-done.55 = f32[64,512]{1,0:T(8,128)S(1)} collective-permute-done((f32[64,512]{1,0:T(8,128)S(1)}, f32[64,512]{1,0:T(8,128)S(1)}, u32[]{:S(2)}, u32[]{:S(2)}) %collective-permute-start.55) | collective-permute-done | bytes 131104 | tf_op jit(solution)/shard_map/ppermute | solution.py:864
  518.6 3.7 collective-permute-done.60
  522.3 5.3 collective-permute-done.59
  528.6 1.8 pad_maximum_fusion.1
  530.4 2.8 collective-permute-done.65
  533.2 1.8 collective-permute-start.66
  (292 shorter events, 104.0 us)
Async XLA Ops:
  1.4 8.5 %collective-permute-start = (f32[16,1024]{1,0:T(8,128)S(1)}, f32[16,1024]{1,0:T(8,128)S(1)}, u32[]{:S(2)}, u32[]{:S(2)}) collective-permute-start(f32[16,1024]{1,0:T(8,128)S(1)} %bitcast_convert_fusion), channel_id=1, source_target_pairs={{0,4},{4,8},{8,12},{12,16},{16,20},{20,24},{24,28},{1,5},{5,9},{9,... | collective-permute-start | bytes 196616 | tf_op jit(solution)/shard_map/ppermute | solution.py:852
  43.0 13.5 %collective-permute-start.1 = (f32[4,128,256]{2,1,0:T(8,128)S(1)}, f32[4,128,256]{2,1,0:T(8,128)S(1)}, u32[]{:S(2)}, u32[]{:S(2)}) collective-permute-start(f32[4,128,256]{2,1,0:T(8,128)S(1)} %slice_select_fusion.3), channel_id=1, source_target_pairs={{0,4},{4,0},{8,12},{12,8},{16,20},{20,16},{24,28},{28,24},{1,5},{5... | collective-permute-start | bytes 1572872 | tf_op jit(solution)/shard_map/ppermute | solution.py:864
  56.9 7.8 %collective-permute-start.2 = (f32[4,128,128]{2,1,0:T(8,128)S(1)}, f32[4,128,128]{2,1,0:T(8,128)S(1)}, u32[]{:S(2)}, u32[]{:S(2)}) collective-permute-start(f32[4,128,128]{2,1,0:T(8,128)S(1)} %slice.129), channel_id=1, source_target_pairs={{0,8},{4,12},{1,9},{5,13},{2,10},{6,14},{3,11},{7,15}} | collective-permute-start | bytes 786440 | tf_op jit(solution)/shard_map/ppermute | solution.py:950
  67.2 6.4 %collective-permute-start.5 = (f32[4,128,128]{2,1,0:T(8,128)S(1)}, f32[4,128,128]{2,1,0:T(8,128)S(1)}, u32[]{:S(2)}, u32[]{:S(2)}) collective-permute-start(f32[4,128,128]{2,1,0:T(8,128)S(1)} %get-tuple-element.202), channel_id=1, source_target_pairs={{0,4},{4,0},{8,12},{12,8},{16,20},{20,16},{24,28},{28,24},{1,5},{5... | collective-permute-start | bytes 786440 | tf_op jit(solution)/shard_map/ppermute | solution.py:864
  109.4 28.7 %collective-permute-start.6 = (f32[2816,384]{1,0:T(8,128)}, f32[2816,384]{1,0:T(8,128)}, u32[]{:S(2)}, u32[]{:S(2)}) collective-permute-start(f32[2816,384]{1,0:T(8,128)} %get-tuple-element.209.refs_1_), channel_id=1, source_target_pairs={{0,1},{1,0},{2,3},{3,2},{4,5},{5,4},{6,7},{7,6},{8,9},{9,8},{10,11... | collective-permute-start | bytes 12976136 | tf_op jit(solution)/shard_map/ppermute | solution.py:864
  109.5 40.3 %collective-permute-start.11 = (f32[384,2816]{1,0:T(8,128)}, f32[384,2816]{1,0:T(8,128)}, u32[]{:S(2)}, u32[]{:S(2)}) collective-permute-start(f32[384,2816]{1,0:T(8,128)} %get-tuple-element.222), channel_id=1, source_target_pairs={{0,1},{1,0},{2,3},{3,2},{4,5},{5,4},{6,7},{7,6},{8,9},{9,8},{10,11... | collective-permute-start | bytes 12976136 | tf_op jit(solution)/shard_map/ppermute | solution.py:864
  110.0 38.3 %collective-permute-start.10 = (f32[1024,384]{1,0:T(8,128)}, f32[1024,384]{1,0:T(8,128)}, u32[]{:S(2)}, u32[]{:S(2)}) collective-permute-start(f32[1024,384]{1,0:T(8,128)} %get-tuple-element.220.refs_1_), channel_id=1, source_target_pairs={{0,1},{1,0},{2,3},{3,2},{4,5},{5,4},{6,7},{7,6},{8,9},{9,8},{10,11... | collective-permute-start | bytes 4718600 | tf_op jit(solution)/shard_map/ppermute | solution.py:864
  113.8 12.9 %collective-permute-start.7 = (f32[384,512]{1,0:T(8,128)}, f32[384,512]{1,0:T(8,128)}, u32[]{:S(2)}, u32[]{:S(2)}) collective-permute-start(f32[384,512]{1,0:T(8,128)} %slice_select_fusion.2), channel_id=1, source_target_pairs={{0,1},{1,0},{2,3},{3,2},{4,5},{5,4},{6,7},{7,6},{8,9},{9,8},{10,11... | collective-permute-start | bytes 2359304 | tf_op jit(solution)/shard_map/ppermute | solution.py:864
  114.2 54.1 %collective-permute-start.15 = (f32[1024,384]{1,0:T(8,128)}, f32[1024,384]{1,0:T(8,128)}, u32[]{:S(2)}, u32[]{:S(2)}) collective-permute-start(f32[1024,384]{1,0:T(8,128)} %get-tuple-element.237.refs_1_.refs_3_), channel_id=1, source_target_pairs={{0,1},{1,0},{2,3},{3,2},{4,5},{5,4},{6,7},{7,6},{8,9},{9,8},{10,11... | collective-permute-start | bytes 4718600 | tf_op jit(solution)/shard_map/ppermute | solution.py:864
  126.7 41.6 %collective-permute-start.14 = (f32[1024,384]{1,0:T(8,128)}, f32[1024,384]{1,0:T(8,128)}, u32[]{:S(2)}, u32[]{:S(2)}) collective-permute-start(f32[1024,384]{1,0:T(8,128)} %get-tuple-element.236), channel_id=1, source_target_pairs={{0,1},{1,0},{2,3},{3,2},{4,5},{5,4},{6,7},{7,6},{8,9},{9,8},{10,11... | collective-permute-start | bytes 4718600 | tf_op jit(solution)/shard_map/ppermute | solution.py:864
  138.0 33.0 %collective-permute-start.16 = (f32[384,1024]{1,0:T(8,128)}, f32[384,1024]{1,0:T(8,128)}, u32[]{:S(2)}, u32[]{:S(2)}) collective-permute-start(f32[384,1024]{1,0:T(8,128)} %get-tuple-element.239), channel_id=1, source_target_pairs={{0,1},{1,0},{2,3},{3,2},{4,5},{5,4},{6,7},{7,6},{8,9},{9,8},{10,11... | collective-permute-start | bytes 4718600 | tf_op jit(solution)/shard_map/ppermute | solution.py:864
  148.2 15.0 %collective-permute-start.9 = (f32[272,512]{1,0:T(8,128)}, f32[272,512]{1,0:T(8,128)}, u32[]{:S(2)}, u32[]{:S(2)}) collective-permute-start(f32[272,512]{1,0:T(8,128)} %get-tuple-element.219), channel_id=1, source_target_pairs={{0,2},{1,3},{2,0},{3,1},{4,6},{5,7},{6,4},{7,5},{8,10},{9,11},{10,... | collective-permute-start | bytes 1671176 | tf_op jit(solution)/shard_map/ppermute | solution.py:864
  149.8 13.4 %collective-permute-start.8 = (f32[4,128,128]{2,1,0:T(8,128)}, f32[4,128,128]{2,1,0:T(8,128)}, u32[]{:S(2)}, u32[]{:S(2)}) collective-permute-start(f32[4,128,128]{2,1,0:T(8,128)} %slice_select_fusion.7), channel_id=1, source_target_pairs={{0,4},{4,0},{8,12},{12,8},{16,20},{20,16},{24,28},{28,24},{1,5},{5... | collective-permute-start | bytes 786440 | tf_op jit(solution)/shard_map/ppermute | solution.py:864
  164.7 14.1 %collective-permute-start.13 = (f32[272,512]{1,0:T(8,128)S(1)}, f32[272,512]{1,0:T(8,128)S(1)}, u32[]{:S(2)}, u32[]{:S(2)}) collective-permute-start(f32[272,512]{1,0:T(8,128)S(1)} %copy-done.24), channel_id=1, source_target_pairs={{0,2},{1,3},{2,0},{3,1},{4,6},{5,7},{6,4},{7,5},{8,10},{9,11},{10,... | collective-permute-start | bytes 1671176 | tf_op jit(solution)/shard_map/ppermute | solution.py:864
  167.5 10.1 %collective-permute-start.12 = (f32[4,128,128]{2,1,0:T(8,128)S(1)}, f32[4,128,128]{2,1,0:T(8,128)S(1)}, u32[]{:S(2)}, u32[]{:S(2)}) collective-permute-start(f32[4,128,128]{2,1,0:T(8,128)S(1)} %apply_map.9.refs_0_), channel_id=1, source_target_pairs={{24,16},{28,20},{25,17},{29,21},{26,18},{30,22},{27,19},{31,23}} | collective-permute-start | bytes 786440 | tf_op jit(solution)/shard_map/ppermute | solution.py:1000
  179.1 13.2 %collective-permute-start.18 = (f32[272,512]{1,0:T(8,128)S(1)}, f32[272,512]{1,0:T(8,128)S(1)}, u32[]{:S(2)}, u32[]{:S(2)}) collective-permute-start(f32[272,512]{1,0:T(8,128)S(1)} %copy-done.45), channel_id=1, source_target_pairs={{0,2},{1,3},{2,0},{3,1},{4,6},{5,7},{6,4},{7,5},{8,10},{9,11},{10,... | collective-permute-start | bytes 1671176 | tf_op jit(solution)/shard_map/ppermute | solution.py:864
  180.3 6.6 %collective-permute-start.17 = (f32[4,128,128]{2,1,0:T(8,128)S(1)}, f32[4,128,128]{2,1,0:T(8,128)S(1)}, u32[]{:S(2)}, u32[]{:S(2)}) collective-permute-start(f32[4,128,128]{2,1,0:T(8,128)S(1)} %apply_map.10), channel_id=1, source_target_pairs={{16,8},{20,12},{17,9},{21,13},{18,10},{22,14},{19,11},{23,15}} | collective-permute-start | bytes 786440 | tf_op jit(solution)/shard_map/ppermute | solution.py:1000
  192.6 14.3 %collective-permute-start.20 = (f32[272,512]{1,0:T(8,128)S(1)}, f32[272,512]{1,0:T(8,128)S(1)}, u32[]{:S(2)}, u32[]{:S(2)}) collective-permute-start(f32[272,512]{1,0:T(8,128)S(1)} %copy-done.44), channel_id=1, source_target_pairs={{0,2},{1,3},{2,0},{3,1},{4,6},{5,7},{6,4},{7,5},{8,10},{9,11},{10,... | collective-permute-start | bytes 1671176 | tf_op jit(solution)/shard_map/ppermute | solution.py:864
  193.6 13.4 %collective-permute-start.19 = (f32[4,128,128]{2,1,0:T(8,128)S(1)}, f32[4,128,128]{2,1,0:T(8,128)S(1)}, u32[]{:S(2)}, u32[]{:S(2)}) collective-permute-start(f32[4,128,128]{2,1,0:T(8,128)S(1)} %apply_map.11), channel_id=1, source_target_pairs={{8,0},{12,4},{9,1},{13,5},{10,2},{14,6},{11,3},{15,7}} | collective-permute-start | bytes 786440 | tf_op jit(solution)/shard_map/ppermute | solution.py:1000
  207.7 13.7 %collective-permute-start.22 = (f32[320,512]{1,0:T(8,128)}, f32[320,512]{1,0:T(8,128)S(1)}, u32[]{:S(2)}, u32[]{:S(2)}) collective-permute-start(f32[320,512]{1,0:T(8,128)} %get-tuple-element.262), channel_id=1, source_target_pairs={{0,2},{1,3},{2,0},{3,1},{4,6},{5,7},{6,4},{7,5},{8,10},{9,11},{10,... | collective-permute-start | bytes 1966088 | tf_op jit(solution)/shard_map/ppermute | solution.py:864
  209.8 6.4 %collective-permute-start.21 = (f32[4,128,128]{2,1,0:T(8,128)S(1)}, f32[4,128,128]{2,1,0:T(8,128)S(1)}, u32[]{:S(2)}, u32[]{:S(2)}) collective-permute-start(f32[4,128,128]{2,1,0:T(8,128)S(1)} %get-tuple-element.261), channel_id=1, source_target_pairs={{0,4},{4,0},{8,12},{12,8},{16,20},{20,16},{24,28},{28,24},{1,5},{5... | collective-permute-start | bytes 786440 | tf_op jit(solution)/shard_map/ppermute | solution.py:864
  223.5 43.8 %collective-permute-start.24 = (f32[256,2048]{1,0:T(8,128)}, f32[256,2048]{1,0:T(8,128)}, u32[]{:S(2)}, u32[]{:S(2)}) collective-permute-start(f32[256,2048]{1,0:T(8,128)} %get-tuple-element.271), channel_id=1, source_target_pairs={{0,2},{1,3},{2,0},{3,1},{4,6},{5,7},{6,4},{7,5},{8,10},{9,11},{10,... | collective-permute-start | bytes 6291464 | tf_op jit(solution)/shard_map/ppermute | solution.py:864
  224.2 47.5 %collective-permute-start.25 = (f32[512,1024]{1,0:T(8,128)}, f32[512,1024]{1,0:T(8,128)}, u32[]{:S(2)}, u32[]{:S(2)}) collective-permute-start(f32[512,1024]{1,0:T(8,128)} %get-tuple-element.272), channel_id=1, source_target_pairs={{0,8},{4,12},{8,0},{12,4},{16,24},{20,28},{24,16},{28,20},{1,9},{5... | collective-permute-start | bytes 6291464 | tf_op jit(solution)/shard_map/ppermute | solution.py:864
  230.1 34.7 %collective-permute-start.23 = (f32[2,2,176,512]{3,2,1,0:T(8,128)}, f32[2,2,176,512]{3,2,1,0:T(8,128)}, u32[]{:S(2)}, u32[]{:S(2)}) collective-permute-start(f32[2,2,176,512]{3,2,1,0:T(8,128)} %add_bitcast_fusion.1), channel_id=1, source_target_pairs={{0,4},{4,0},{8,12},{12,8},{16,20},{20,16},{24,28},{28,24},{1,5},{5... | collective-permute-start | bytes 4325384 | tf_op jit(solution)/shard_map/ppermute | solution.py:864
  271.7 6.6 %collective-permute-start.26 = (f32[3,8,1024]{2,1,0:T(8,128)S(1)}, f32[3,8,1024]{2,1,0:T(8,128)S(1)}, u32[]{:S(2)}, u32[]{:S(2)}) collective-permute-start(f32[3,8,1024]{2,1,0:T(8,128)S(1)} %get-tuple-element.275), channel_id=1, source_target_pairs={{4,0},{8,4},{12,8},{16,12},{20,16},{24,20},{28,24},{5,1},{9,5},{13... | collective-permute-start | bytes 294920 | tf_op jit(solution)/shard_map/ppermute | solution.py:852
  279.5 12.4 %collective-permute-start.27 = (f32[384,1024]{1,0:T(8,128)S(1)}, f32[384,1024]{1,0:T(8,128)}, u32[]{:S(2)}, u32[]{:S(2)}) collective-permute-start(f32[384,1024]{1,0:T(8,128)S(1)} %fusion), channel_id=1, source_target_pairs={{0,1},{1,0},{2,3},{3,2},{4,5},{5,4},{6,7},{7,6},{8,9},{9,8},{10,11... | collective-permute-start | bytes 4718600 | tf_op jit(solution)/shard_map/ppermute | solution.py:864
  279.6 58.1 %collective-permute-start.30 = (f32[256,2048]{1,0:T(8,128)}, f32[256,2048]{1,0:T(8,128)}, u32[]{:S(2)}, u32[]{:S(2)}) collective-permute-start(f32[256,2048]{1,0:T(8,128)} %get-tuple-element.286), channel_id=1, source_target_pairs={{0,2},{1,3},{2,0},{3,1},{4,6},{5,7},{6,4},{7,5},{8,10},{9,11},{10,... | collective-permute-start | bytes 6291464 | tf_op jit(solution)/shard_map/ppermute | solution.py:864
  280.0 57.7 %collective-permute-start.29 = (f32[512,768]{1,0:T(8,128)}, f32[512,768]{1,0:T(8,128)}, u32[]{:S(2)}, u32[]{:S(2)}) collective-permute-start(f32[512,768]{1,0:T(8,128)} %get-tuple-element.285), channel_id=1, source_target_pairs={{0,4},{4,0},{8,12},{12,8},{16,20},{20,16},{24,28},{28,24},{1,5},{5... | collective-permute-start | bytes 4718600 | tf_op jit(solution)/shard_map/ppermute | solution.py:864
  282.9 54.8 %collective-permute-start.32 = (f32[2,2,64,1024]{3,2,1,0:T(8,128)}, f32[2,2,64,1024]{3,2,1,0:T(8,128)}, u32[]{:S(2)}, u32[]{:S(2)}) collective-permute-start(f32[2,2,64,1024]{3,2,1,0:T(8,128)} %add_bitcast_fusion.3), channel_id=1, source_target_pairs={{0,16},{4,20},{8,24},{12,28},{16,0},{20,4},{24,8},{28,12},{1,17},{... | collective-permute-start | bytes 3145736 | tf_op jit(solution)/shard_map/ppermute | solution.py:864
  291.9 9.5 %collective-permute-start.28 = (f32[384,512]{1,0:T(8,128)S(1)}, f32[384,512]{1,0:T(8,128)S(1)}, u32[]{:S(2)}, u32[]{:S(2)}) collective-permute-start(f32[384,512]{1,0:T(8,128)S(1)} %fusion.1), channel_id=1, source_target_pairs={{0,1},{1,0},{2,3},{3,2},{4,5},{5,4},{6,7},{7,6},{8,9},{9,8},{10,11... | collective-permute-start | bytes 2359304 | tf_op jit(solution)/shard_map/ppermute | solution.py:864
  292.0 38.0 %collective-permute-start.31 = (f32[2,176,512]{2,1,0:T(8,128)}, f32[2,176,512]{2,1,0:T(8,128)}, u32[]{:S(2)}, u32[]{:S(2)}) collective-permute-start(f32[2,176,512]{2,1,0:T(8,128)} %bitcast_add_fusion.1), channel_id=1, source_target_pairs={{0,8},{4,12},{8,0},{12,4},{16,24},{20,28},{24,16},{28,20},{1,9},{5... | collective-permute-start | bytes 2162696 | tf_op jit(solution)/shard_map/ppermute | solution.py:864
  348.6 49.6 %collective-permute-start.33 = (f32[2,2,64,2048]{3,2,1,0:T(8,128)}, f32[2,2,64,2048]{3,2,1,0:T(8,128)}, u32[]{:S(2)}, u32[]{:S(2)}) collective-permute-start(f32[2,2,64,2048]{3,2,1,0:T(8,128)} %add_bitcast_fusion), channel_id=1, source_target_pairs={{0,4},{4,0},{8,12},{12,8},{16,20},{20,16},{24,28},{28,24},{1,5},{5... | collective-permute-start | bytes 6291464 | tf_op jit(solution)/shard_map/ppermute | solution.py:864
  348.9 49.4 %collective-permute-start.36 = (f32[512,1024]{1,0:T(8,128)}, f32[512,1024]{1,0:T(8,128)}, u32[]{:S(2)}, u32[]{:S(2)}) collective-permute-start(f32[512,1024]{1,0:T(8,128)} %get-tuple-element.298), channel_id=1, source_target_pairs={{0,2},{1,3},{2,0},{3,1},{4,6},{5,7},{6,4},{7,5},{8,10},{9,11},{10,... | collective-permute-start | bytes 6291464 | tf_op jit(solution)/shard_map/ppermute | solution.py:864
  349.2 49.1 %collective-permute-start.37 = (f32[512,512]{1,0:T(8,128)}, f32[512,512]{1,0:T(8,128)}, u32[]{:S(2)}, u32[]{:S(2)}) collective-permute-start(f32[512,512]{1,0:T(8,128)} %get-tuple-element.299), channel_id=1, source_target_pairs={{0,8},{4,12},{8,0},{12,4},{16,24},{20,28},{24,16},{28,20},{1,9},{5... | collective-permute-start | bytes 3145736 | tf_op jit(solution)/shard_map/ppermute | solution.py:864
  349.9 48.3 %collective-permute-start.34 = (f32[2,2,64,768]{3,2,1,0:T(8,128)}, f32[2,2,64,768]{3,2,1,0:T(8,128)}, u32[]{:S(2)}, u32[]{:S(2)}) collective-permute-start(f32[2,2,64,768]{3,2,1,0:T(8,128)} %add_bitcast_fusion.4), channel_id=1, source_target_pairs={{0,8},{4,12},{8,0},{12,4},{16,24},{20,28},{24,16},{28,20},{1,9},{5... | collective-permute-start | bytes 2359304 | tf_op jit(solution)/shard_map/ppermute | solution.py:864
  352.4 44.4 %collective-permute-start.35 = (f32[176,512]{1,0:T(8,128)}, f32[176,512]{1,0:T(8,128)}, u32[]{:S(2)}, u32[]{:S(2)}) collective-permute-start(f32[176,512]{1,0:T(8,128)} %bitcast_add_fusion.12), channel_id=1, source_target_pairs={{0,16},{4,20},{8,24},{12,28},{16,0},{20,4},{24,8},{28,12},{1,17},{... | collective-permute-start | bytes 1081352 | tf_op jit(solution)/shard_map/ppermute | solution.py:864
  409.3 35.5 %collective-permute-start.40 = (f32[2,64,2048]{2,1,0:T(8,128)}, f32[2,64,2048]{2,1,0:T(8,128)}, u32[]{:S(2)}, u32[]{:S(2)}) collective-permute-start(f32[2,64,2048]{2,1,0:T(8,128)} %bitcast_add_fusion), channel_id=1, source_target_pairs={{0,8},{4,12},{8,0},{12,4},{16,24},{20,28},{24,16},{28,20},{1,9},{5... | collective-permute-start | bytes 3145736 | tf_op jit(solution)/shard_map/ppermute | solution.py:864
  412.0 32.7 %collective-permute-start.41 = (f32[2,2,64,1024]{3,2,1,0:T(8,128)}, f32[2,2,64,1024]{3,2,1,0:T(8,128)}, u32[]{:S(2)}, u32[]{:S(2)}) collective-permute-start(f32[2,2,64,1024]{3,2,1,0:T(8,128)} %add_bitcast_fusion.2), channel_id=1, source_target_pairs={{0,4},{4,0},{8,12},{12,8},{16,20},{20,16},{24,28},{28,24},{1,5},{5... | collective-permute-start | bytes 3145736 | tf_op jit(solution)/shard_map/ppermute | solution.py:864
  413.6 11.3 %collective-permute-start.43 = (f32[176,512]{1,0:T(8,128)S(1)}, f32[176,512]{1,0:T(8,128)S(1)}, u32[]{:S(2)}, u32[]{:S(2)}) collective-permute-start(f32[176,512]{1,0:T(8,128)S(1)} %fusion.6), channel_id=1, source_target_pairs={{0,2},{1,3},{2,0},{3,1},{4,6},{5,7},{6,4},{7,5},{8,10},{9,11},{10,... | collective-permute-start | bytes 1081352 | tf_op jit(solution)/shard_map/ppermute | solution.py:864
  415.4 26.8 %collective-permute-start.38 = (f32[2,64,1024]{2,1,0:T(8,128)}, f32[2,64,1024]{2,1,0:T(8,128)}, u32[]{:S(2)}, u32[]{:S(2)}) collective-permute-start(f32[2,64,1024]{2,1,0:T(8,128)} %bitcast_add_fusion.7), channel_id=1, source_target_pairs={{0,2},{1,3},{2,0},{3,1},{4,6},{5,7},{6,4},{7,5},{8,10},{9,11},{10,... | collective-permute-start | bytes 1572872 | tf_op jit(solution)/shard_map/ppermute | solution.py:864
  416.7 28.0 %collective-permute-start.42 = (f32[2,2,64,512]{3,2,1,0:T(8,128)}, f32[2,2,64,512]{3,2,1,0:T(8,128)}, u32[]{:S(2)}, u32[]{:S(2)}) collective-permute-start(f32[2,2,64,512]{3,2,1,0:T(8,128)} %add_bitcast_fusion.5), channel_id=1, source_target_pairs={{0,2},{1,3},{2,0},{3,1},{4,6},{5,7},{6,4},{7,5},{8,10},{9,11},{10,... | collective-permute-start | bytes 1572872 | tf_op jit(solution)/shard_map/ppermute | solution.py:864
  425.7 16.5 %collective-permute-start.39 = (f32[2,64,768]{2,1,0:T(8,128)}, f32[2,64,768]{2,1,0:T(8,128)S(1)}, u32[]{:S(2)}, u32[]{:S(2)}) collective-permute-start(f32[2,64,768]{2,1,0:T(8,128)} %bitcast_add_fusion.9), channel_id=1, source_target_pairs={{0,16},{4,20},{8,24},{12,28},{16,0},{20,4},{24,8},{28,12},{1,17},{... | collective-permute-start | bytes 1179656 | tf_op jit(solution)/shard_map/ppermute | solution.py:864
  452.5 27.3 %collective-permute-start.50 = (f32[352,512]{1,0:T(8,128)S(1)}, f32[352,512]{1,0:T(8,128)S(1)}, u32[]{:S(2)}, u32[]{:S(2)}) collective-permute-start(f32[352,512]{1,0:T(8,128)S(1)} %pad_maximum_fusion.5), channel_id=1, source_target_pairs={{0,1},{1,0},{2,3},{3,2},{4,5},{5,4},{6,7},{7,6},{8,9},{9,8},{10,11... | collective-permute-start | bytes 2162696 | tf_op jit(solution)/shard_map/ppermute | solution.py:864
  452.6 11.9 %collective-permute-start.45 = (f32[64,1024]{1,0:T(8,128)S(1)}, f32[64,1024]{1,0:T(8,128)S(1)}, u32[]{:S(2)}, u32[]{:S(2)}) collective-permute-start(f32[64,1024]{1,0:T(8,128)S(1)} %bitcast_add_fusion.21), channel_id=1, source_target_pairs={{0,4},{4,0},{8,12},{12,8},{16,20},{20,16},{24,28},{28,24},{1,5},{5... | collective-permute-start | bytes 786440 | tf_op jit(solution)/shard_map/ppermute | solution.py:864
  453.2 26.2 %collective-permute-start.47 = (f32[64,2048]{1,0:T(8,128)S(1)}, f32[64,2048]{1,0:T(8,128)S(1)}, u32[]{:S(2)}, u32[]{:S(2)}) collective-permute-start(f32[64,2048]{1,0:T(8,128)S(1)} %bitcast_add_fusion.5), channel_id=1, source_target_pairs={{0,16},{4,20},{8,24},{12,28},{16,0},{20,4},{24,8},{28,12},{1,17},{... | collective-permute-start | bytes 1572872 | tf_op jit(solution)/shard_map/ppermute | solution.py:864
  455.0 24.8 %collective-permute-start.48 = (f32[2,64,1024]{2,1,0:T(8,128)S(1)}, f32[2,64,1024]{2,1,0:T(8,128)S(1)}, u32[]{:S(2)}, u32[]{:S(2)}) collective-permute-start(f32[2,64,1024]{2,1,0:T(8,128)S(1)} %bitcast_add_fusion.4), channel_id=1, source_target_pairs={{0,8},{4,12},{8,0},{12,4},{16,24},{20,28},{24,16},{28,20},{1,9},{5... | collective-permute-start | bytes 1572872 | tf_op jit(solution)/shard_map/ppermute | solution.py:864
  455.6 7.2 %collective-permute-start.51 = (f32[128,128]{1,0:T(8,128)S(1)}, f32[128,128]{1,0:T(8,128)S(1)}, u32[]{:S(2)}, u32[]{:S(2)}) collective-permute-start(f32[128,128]{1,0:T(8,128)S(1)} %bitcast.295), channel_id=1, source_target_pairs={{0,4},{4,0},{8,12},{12,8},{16,20},{20,16},{24,28},{28,24},{1,5},{5... | collective-permute-start | bytes 196616 | tf_op jit(solution)/shard_map/ppermute | solution.py:864
  462.7 10.7 %collective-permute-start.46 = (f32[2,64,768]{2,1,0:T(8,128)S(1)}, f32[2,64,768]{2,1,0:T(8,128)S(1)}, u32[]{:S(2)}, u32[]{:S(2)}) collective-permute-start(f32[2,64,768]{2,1,0:T(8,128)S(1)} %fusion.5), channel_id=1, source_target_pairs={{0,2},{1,3},{2,0},{3,1},{4,6},{5,7},{6,4},{7,5},{8,10},{9,11},{10,... | collective-permute-start | bytes 1179656 | tf_op jit(solution)/shard_map/ppermute | solution.py:864
  464.5 7.6 %collective-permute-start.49 = (f32[2,64,512]{2,1,0:T(8,128)S(1)}, f32[2,64,512]{2,1,0:T(8,128)S(1)}, u32[]{:S(2)}, u32[]{:S(2)}) collective-permute-start(f32[2,64,512]{2,1,0:T(8,128)S(1)} %bitcast_add_fusion.20), channel_id=1, source_target_pairs={{0,4},{4,0},{8,12},{12,8},{16,20},{20,16},{24,28},{28,24},{1,5},{5... | collective-permute-start | bytes 786440 | tf_op jit(solution)/shard_map/ppermute | solution.py:864
  485.0 27.0 %collective-permute-start.52 = (f32[64,2048]{1,0:T(8,128)S(1)}, f32[64,2048]{1,0:T(8,128)S(1)}, u32[]{:S(2)}, u32[]{:S(2)}) collective-permute-start(f32[64,2048]{1,0:T(8,128)S(1)} %fusion.4), channel_id=1, source_target_pairs={{0,2},{1,3},{2,0},{3,1},{4,6},{5,7},{6,4},{7,5},{8,10},{9,11},{10,... | collective-permute-start | bytes 1572872 | tf_op jit(solution)/shard_map/ppermute | solution.py:864
  486.8 25.2 %collective-permute-start.57 = (f32[128,768]{1,0:T(8,128)S(1)}, f32[128,768]{1,0:T(8,128)S(1)}, u32[]{:S(2)}, u32[]{:S(2)}) collective-permute-start(f32[128,768]{1,0:T(8,128)S(1)} %bitcast.284), channel_id=1, source_target_pairs={{0,1},{1,0},{2,3},{3,2},{4,5},{5,4},{6,7},{7,6},{8,9},{9,8},{10,11... | collective-permute-start | bytes 1179656 | tf_op jit(solution)/shard_map/ppermute | solution.py:864
  486.8 25.2 %collective-permute-start.53 = (f32[64,1024]{1,0:T(8,128)S(1)}, f32[64,1024]{1,0:T(8,128)S(1)}, u32[]{:S(2)}, u32[]{:S(2)}) collective-permute-start(f32[64,1024]{1,0:T(8,128)S(1)} %fusion.8), channel_id=1, source_target_pairs={{0,2},{1,3},{2,0},{3,1},{4,6},{5,7},{6,4},{7,5},{8,10},{9,11},{10,... | collective-permute-start | bytes 786440 | tf_op jit(solution)/shard_map/ppermute | solution.py:864
  487.1 24.9 %collective-permute-start.54 = (f32[64,1024]{1,0:T(8,128)S(1)}, f32[64,1024]{1,0:T(8,128)S(1)}, u32[]{:S(2)}, u32[]{:S(2)}) collective-permute-start(f32[64,1024]{1,0:T(8,128)S(1)} %bitcast_add_fusion.16), channel_id=1, source_target_pairs={{0,16},{4,20},{8,24},{12,28},{16,0},{20,4},{24,8},{28,12},{1,17},{... | collective-permute-start | bytes 786440 | tf_op jit(solution)/shard_map/ppermute | solution.py:864
  487.2 17.5 %collective-permute-start.56 = (f32[2,2,16,128]{3,2,1,0:T(8,128)S(1)}, f32[2,2,16,128]{3,2,1,0:T(8,128)S(1)}, u32[]{:S(2)}, u32[]{:S(2)}) collective-permute-start(f32[2,2,16,128]{3,2,1,0:T(8,128)S(1)} %add_bitcast_fusion.6), channel_id=1, source_target_pairs={{0,2},{1,3},{2,0},{3,1},{4,6},{5,7},{6,4},{7,5},{8,10},{9,11},{10,... | collective-permute-start | bytes 98312 | tf_op jit(solution)/shard_map/ppermute | solution.py:864
  504.8 7.2 %collective-permute-start.55 = (f32[64,512]{1,0:T(8,128)S(1)}, f32[64,512]{1,0:T(8,128)S(1)}, u32[]{:S(2)}, u32[]{:S(2)}) collective-permute-start(f32[64,512]{1,0:T(8,128)S(1)} %bitcast_add_fusion.25), channel_id=1, source_target_pairs={{0,16},{4,20},{8,24},{12,28},{16,0},{20,4},{24,8},{28,12},{1,17},{... | collective-permute-start | bytes 393224 | tf_op jit(solution)/shard_map/ppermute | solution.py:864
  514.5 13.1 %collective-permute-start.61 = (f32[128,2048]{1,0:T(8,128)S(1)}, f32[128,2048]{1,0:T(8,128)S(1)}, u32[]{:S(2)}, u32[]{:S(2)}) collective-permute-start(f32[128,2048]{1,0:T(8,128)S(1)} %pad_maximum_fusion.4), channel_id=1, source_target_pairs={{0,1},{1,0},{2,3},{3,2},{4,5},{5,4},{6,7},{7,6},{8,9},{9,8},{10,11... | collective-permute-start | bytes 3145736 | tf_op jit(solution)/shard_map/ppermute | solution.py:864
  514.6 13.0 %collective-permute-start.62 = (f32[128,1024]{1,0:T(8,128)S(1)}, f32[128,1024]{1,0:T(8,128)S(1)}, u32[]{:S(2)}, u32[]{:S(2)}) collective-permute-start(f32[128,1024]{1,0:T(8,128)S(1)} %pad_maximum_fusion.6), channel_id=1, source_target_pairs={{0,1},{1,0},{2,3},{3,2},{4,5},{5,4},{6,7},{7,6},{8,9},{9,8},{10,11... | collective-permute-start | bytes 1572872 | tf_op jit(solution)/shard_map/ppermute | solution.py:864
  516.5 11.1 %collective-permute-start.58 = (f32[64,1024]{1,0:T(8,128)S(1)}, f32[64,1024]{1,0:T(8,128)S(1)}, u32[]{:S(2)}, u32[]{:S(2)}) collective-permute-start(f32[64,1024]{1,0:T(8,128)S(1)} %fusion.7), channel_id=1, source_target_pairs={{0,2},{1,3},{2,0},{3,1},{4,6},{5,7},{6,4},{7,5},{8,10},{9,11},{10,... | collective-permute-start | bytes 786440 | tf_op jit(solution)/shard_map/ppermute | solution.py:864
  518.2 9.4 %collective-permute-start.59 = (f32[64,512]{1,0:T(8,128)S(1)}, f32[64,512]{1,0:T(8,128)S(1)}, u32[]{:S(2)}, u32[]{:S(2)}) collective-permute-start(f32[64,512]{1,0:T(8,128)S(1)} %fusion.10), channel_id=1, source_target_pairs={{0,2},{1,3},{2,0},{3,1},{4,6},{5,7},{6,4},{7,5},{8,10},{9,11},{10,... | collective-permute-start | bytes 393224 | tf_op jit(solution)/shard_map/ppermute | solution.py:864
  518.5 3.7 collective-permute-start.60
  527.8 5.4 collective-permute-start.63
  528.1 5.1 collective-permute-start.64
  528.6 4.5 collective-permute-start.65
  533.2 5.6 %collective-permute-start.66 = (f32[16,128]{1,0:T(8,128)S(1)}, f32[16,128]{1,0:T(8,128)S(1)}, u32[]{:S(2)}, u32[]{:S(2)}) collective-permute-start(f32[16,128]{1,0:T(8,128)S(1)} %fusion.24), channel_id=1, source_target_pairs={{0,2},{1,3},{2,0},{3,1},{4,6},{5,7},{6,4},{7,5},{8,10},{9,11},{10,... | collective-permute-start | bytes 24584 | tf_op jit(solution)/shard_map/ppermute | solution.py:864
  (49 other events, 404.4 us)

commit v4 on v3

--- a/solution.py
+++ b/solution.py
@@ -167,7 +167,7 @@
         rounded = norm(tokens[...].astype(jnp.float32))
         normed[HALO:, :] = rounded
         normed_out[...] = rounded.astype(jnp.float32).T
-        beta_pre = mxu(rounded, beta_w[...], NN)
+        beta_pre = mxu(rounded, beta_w[...], NT)
         beta_pre_out[...] = beta_pre
         beta_out[...] = sigmoid(beta_pre) * live[...]
 
@@ -208,7 +208,7 @@
 
 def project(tokens, halo, gain, position, live, query_w, key_w, value_w, gate_w, beta_w, conv):
     count, width = tokens.shape
-    heads = beta_w.shape[1]
+    heads = beta_w.shape[0]
     block = 2 * LANES
     whole = lambda shape: pl.BlockSpec(shape, lambda j: (0,) * len(shape))
     weight = pl.BlockSpec((width, block), lambda j: (0, j))
@@ -218,7 +218,7 @@
         grid=(width // block,),
         in_specs=[
             whole((count, width)), whole((HALO, width)), whole((1, width)), whole((count, 1)),
-            whole((count, 1)), weight, weight, weight, weight, whole((width, heads)),
+            whole((count, 1)), weight, weight, weight, weight, whole((heads, width)),
             pl.BlockSpec((3, conv.shape[1], block), lambda j: (0, 0, j)),
         ],
         out_specs=[
@@ -522,8 +522,6 @@
         grad_gate = grad * unit * gain[...] * sigma * (1.0 + gates * (1.0 - sigma))
         grad_gate = grad_gate.astype(LOW).astype(jnp.float32)
         grad_gate_out[:, lanes] = grad_gate
-        kept_out[:, lanes] = jnp.where(core[0] == 0, grad_branch[:, lanes], grad_gate).astype(LOW)
-        sent_out[:, lanes] = jnp.where(core[0] == 0, grad_gate, grad_branch[:, lanes])
         shaped = grad * gates * sigma
         gain_total = gain_total + jnp.sum(shaped * unit, 0, keepdims=True)
         inward = shaped * gain[...]
@@ -545,6 +543,12 @@
             )
         )
     gain_out[...] += gain_total
+    half = grad_branch.shape[1] // 2
+    first = core[0] == 0
+    for place, source in ((0, grad_branch), (half, grad_gate_out)):
+        low, high = source[:, :half], source[:, half:]
+        kept_out[:, place : place + half] = jnp.where(first, low, high).astype(LOW)
+        sent_out[:, place : place + half] = jnp.where(first, high, low)
 
 
 def gather_states(
@@ -802,7 +806,7 @@
 
     @pl.when(step == 0)
     def _():
-        total[...] = term + mxu(grad_beta[...].astype(LOW), beta_w[...], NT)
+        total[...] = term + mxu(grad_beta[...].astype(LOW), beta_w[...], NN)
 
     @pl.when(step > 0)
     def _():
@@ -819,7 +823,7 @@
     tokens, gain, grad_hidden, grads, grad_gate, grad_beta, query_w, key_w, value_w, gate_w, beta_w
 ):
     count, width = tokens.shape
-    heads = beta_w.shape[1]
+    heads = beta_w.shape[0]
     block = 2 * LANES
     whole = lambda shape: pl.BlockSpec(shape, lambda j: (0,) * len(shape))
     weight = pl.BlockSpec((width, block), lambda j: (0, j))
@@ -830,7 +834,7 @@
             whole((count, width)), whole((1, width)), whole((count, width)),
             pl.BlockSpec((3, count, block), lambda j: (0, 0, j)),
             pl.BlockSpec((count, block), lambda j: (0, j)), whole((count, heads)),
-            weight, weight, weight, weight, whole((width, heads)),
+            weight, weight, weight, weight, whole((heads, width)),
         ],
         out_specs=[whole((count, width)), whole((1, width))],
         out_shape=[
@@ -859,9 +863,14 @@
 HOPS = {"core": ("doc", 1), "y": ("doc", 2), "x": ("seq", 1), "near": ("seq", 2), "far": ("seq", 4)}
 
 
-def hop(value, way):
-    axis, bit = HOPS[way]
-    return lax.ppermute(value, axis, [(i, i ^ bit) for i in range(lax.axis_size(axis))])
+def hop(value, way, other_way=None):
+    if other_way in (None, way):
+        axis, bit = HOPS[way]
+        return lax.ppermute(value, axis, [(i, i ^ bit) for i in range(lax.axis_size(axis))])
+    size = lax.axis_size("doc")
+    masks = [bit * size if axis == "seq" else bit for axis, bit in (HOPS[way], HOPS[other_way])]
+    pairs = [(i, i ^ masks[i % 2]) for i in range(lax.axis_size("seq") * size)]
+    return lax.ppermute(value, ("seq", "doc"), pairs)
 
 
 def side(way):
@@ -919,7 +928,11 @@
     )(here, shift, maps, state, come)
 
 
-def carried_forward(maps):
+def together(value, *others):
+    return lax.optimization_barrier((value, *others))
+
+
+def carried_forward(maps, beside):
     heads, size, _ = maps.shape
     half = heads // 2
     if not tuned():
@@ -937,6 +950,7 @@
     here = place[0] == 0
     kept = jnp.where(here, maps[:half], maps[half:])
     other = hop(jnp.where(here, maps[half:], maps[:half]), "x")
+    other, *beside = together(other, *beside)
     first, second = jnp.where(here, kept, other), jnp.where(here, other, kept)
     pair_map = apply_map(second, second, first)
     state = jnp.zeros((half, size, size), jnp.float32)
@@ -949,11 +963,7 @@
             state = state + come
         come = lax.ppermute(sent, "seq", [(2 * step + x, 2 * step + 2 + x) for x in range(2)])
     mine, send = pair_ends(place, first, first, state, come)
-    return mine, hop(send, "x"), place, (first, second, pair_map)
-
-
-def together(value, *others):
-    return lax.optimization_barrier((value, *others))
+    return mine, hop(send, "x"), place, (first, second, pair_map), *beside
 
 
 def carried_back(shift, context, beside=None):
@@ -977,9 +987,9 @@
 
     def step_with(number, sent, go):
         moves, work = beside[number]
-        sent, *values = together(sent, *[value for value, _ in moves])
+        sent, *values = together(sent, *[move[0] for move in moves])
         come, *rest = together(
-            go(sent), *[hop(value, way) for value, (_, way) in zip(values, moves)], *work
+            go(sent), *[hop(value, *move[1:]) for value, move in zip(values, moves)], *work
         )
         done.append(rest)
         return come
@@ -1002,24 +1012,23 @@
     return mine, step_with(4, send, lambda value: hop(value, "x")), done
 
 
-def outer_kernel(bit, *refs, blocks, post, pieces):
+def outer_kernel(table, *refs, blocks, pieces):
     count = len(blocks)
     lefts, rights = refs[: 2 * count], refs[2 * count : 4 * count]
     *outs, stacked = refs[4 * count :]
     step = pl.program_id(0)
     tokens = lefts[0].shape[1]
-    half = outs[0].shape[0]
+    size = outs[0].shape[0] // 8
 
     @pl.when(step == 0)
     def _():
         for piece in range(count):
             for which in range(2):
-                for start in range(0, half, post):
-                    for place, mine in ((start, bit[0]), (half + start, 1 - bit[0])):
-                        rows = pl.ds(pl.multiple_of(2 * start + mine * post, 8), post)
-                        stacked[
-                            piece, place : place + post, which * tokens : (which + 1) * tokens
-                        ] = lefts[2 * piece + which][rows, :].astype(LOW)
+                for place in range(16):
+                    rows = pl.ds(pl.multiple_of(table[place] * size, 16), size)
+                    stacked[
+                        piece, place * size : (place + 1) * size, which * tokens : (which + 1) * tokens
+                    ] = lefts[2 * piece + which][rows, :].astype(LOW)
 
     for piece in range(count):
         low = sum(blocks[:piece])
@@ -1030,15 +1039,31 @@
                 [rights[2 * piece][...].astype(LOW), rights[2 * piece + 1][...].astype(LOW)], 0
             )
             place = 0
-            for out, size in zip(outs, (half, *pieces)):
-                out[...] = mxu(stacked[piece, place : place + size, :], right, NN)
-                place += size
-
-
-def outer(pieces, way, parts=1):
+            for out, number in zip(outs, (8 * size, *pieces)):
+                out[...] = mxu(stacked[piece, place : place + number, :], right, NN)
+                place += number
+
+
+WEIGHTS = {"far": 8, "near": 4, "x": 2, "y": 1}
+
+
+def by_core(values):
+    return jnp.where(side("core") == 0, values[0], values[1])
+
+
+def outer(pieces, orders, parts=(1,)):
     rows, tokens = pieces[0][0].shape
     block = 2 * LANES
-    post = rows // 16 if way == "y" else rows // 8 * {"far": 4, "near": 2, "x": 1}[way]
+    table = []
+    for place in range(16):
+        entries = []
+        for order in orders:
+            bits = [place >> 3 & 1, place >> 2 & 1, place >> 1 & 1, place & 1]
+            first = side(order[0]) ^ bits[0]
+            rest = sum(bit * WEIGHTS[way] for bit, way in zip(bits[1:], order[1:]))
+            entries.append(first * WEIGHTS[order[0]] + rest)
+        table.append(by_core(entries))
+    table = jnp.stack(table).astype(jnp.int32)
     counts = [piece[5] for piece in pieces]
     left = pl.BlockSpec((rows, tokens), lambda j: (0, 0), pipeline_mode=pl.Buffered(1))
     lefts, rights, specs = [], [], []
@@ -1051,23 +1076,19 @@
 
         specs += [pl.BlockSpec((tokens, block), place)] * 2
     total = sum(counts)
-    eighth = rows // 16
-    sizes = [eighth * 8 // parts // 16 * 16] * (parts - 1)
-    sizes = [*sizes, rows // 2 - sum(sizes)]
+    sizes = [rows // 2 * part // sum(parts) for part in parts]
     outs = [rows // 2, *sizes]
     keep, *sends = pl.pallas_call(
-        lambda *refs: outer_kernel(*refs, blocks=counts, post=post, pieces=sizes),
+        lambda *refs: outer_kernel(*refs, blocks=counts, pieces=sizes),
         grid=(total,),
         in_specs=[pl.BlockSpec(memory_space=pltpu.SMEM)] + [left] * len(lefts) + specs,
         out_specs=[pl.BlockSpec((size, block), lambda j: (0, j)) for size in outs],
         out_shape=[jax.ShapeDtypeStruct((size, total * block), jnp.float32) for size in outs],
         scratch_shapes=[pltpu.VMEM((len(pieces), rows, 2 * tokens), LOW)],
         compiler_params=params(),
-        cost_estimate=cost(
-            4 * rows * tokens * total * block, 4 * rows * total * block + 8 * tokens * rows
-        ),
+        cost_estimate=cost(0, 0),
         name="outer",
-    )(side(way).astype(jnp.int32).reshape(1), *lefts, *rights)
+    )(table, *lefts, *rights)
     return keep, sends
 
 
@@ -1076,72 +1097,78 @@
 
 
 class Part:
-    def __init__(self, keep, order):
-        self.order, self.stage = order, 1
-        self.names = [name for name in ("far", "near", "x", "y") if name != order[0]]
-        shape = (2, 2, 2, keep.shape[0] // 8, keep.shape[1])
-        self.terms = [(keep.reshape(shape), tuple(self.names))]
-
-    def begun(self, pieces):
-        come = pieces[0] if len(pieces) == 1 else jnp.concatenate(pieces, 0)
-        self.absorb(come)
-
-    def absorb(self, come):
-        shape = (2,) * len(self.names) + self.terms[0][0].shape[-2:]
-        self.terms.append((come.reshape(shape), tuple(self.names)))
-
-    def chosen(self, bits):
+    def __init__(self, keeps, comes, orders, split_y=True):
+        self.orders, self.split_y, self.stage = orders, split_y, 1
+        self.groups = [[self.shaped(value) for value in group] for group in zip(keeps, comes)]
+        self.terms = []
+
+    def shaped(self, value):
+        left = tuple(range(self.stage, len(self.orders[0])))
+        columns = value.shape[-1]
+        rows = value.size // columns // 2 ** len(left)
+        return value.reshape((2,) * len(left) + (rows, columns)), left
+
+    def add(self, come):
+        self.terms.append(self.shaped(come))
+
+    def place(self, stage):
+        return by_core([side(order[stage]) for order in self.orders])
+
+    def chosen(self, here):
+        sums = [self.added(group, here) for group in self.groups]
+        total = sums[0] if len(sums) == 1 else jnp.concatenate(sums, -1)
+        return total + self.added(self.terms, here) if self.terms else total
+
+    def added(self, terms, here):
         total = None
-        for value, names in self.terms:
+        for value, left in terms:
             starts, sizes = [], []
-            for name in names:
-                fixed = name in bits or name not in self.names
-                starts.append(bits.get(name, side(name)) if fixed else 0)
+            for stage in left:
+                fixed = stage <= self.stage
+                place = self.place(stage) if fixed else 0
+                starts.append(1 - place if stage == self.stage and not here else place)
                 sizes.append(1 if fixed else 2)
-            sizes += value.shape[len(names) :]
+            sizes += value.shape[len(left) :]
             starts = [jnp.asarray(start, jnp.int32) for start in [*starts, 0, 0]]
             piece = lax.dynamic_slice(value, starts, sizes)
-            piece = piece.reshape([size for size, name in zip(sizes, names) if size > 1] + sizes[-2:])
+            piece = piece.reshape([size for size in sizes[:-2] if size > 1] + sizes[-2:])
             total = piece if total is None else total + piece
         return total
 
     def move(self):
-        stage, self.stage = self.stage, self.stage + 1
-        if stage < 4 and (stage < 3 or self.order[3] != "y"):
-            way = self.order[stage]
-            send = self.chosen({way: 1 - side(way)})
-            self.names.remove(way)
-            return send, way
-        if stage < 5:
-            self.stage = 5
-            self.keep = self.chosen({})
-            self.absorb = self.whole if stage == 4 else self.summed
-            return self.keep, "y"
+        if self.stage < len(self.orders[0]):
+            send = self.chosen(False)
+            ways = [order[self.stage] for order in self.orders]
+            self.stage += 1
+            self.absorb = self.add
+            return send, *ways
+        if self.stage == len(self.orders[0]):
+            mine = self.chosen(True)
+            self.stage += 1
+
+            def absorb(come):
+                self.done = in_order(mine, come) if self.split_y else mine + come
+
+            self.absorb = absorb
+            return mine, "y"
         self.absorb = lambda come: setattr(self, "other", come)
         return self.done, "core"
 
-    def whole(self, come):
-        first = side("y") == 0
-        self.done = jnp.concatenate(
-            [jnp.where(first, self.keep, come), jnp.where(first, come, self.keep)], 0
-        )
-
-    def summed(self, come):
-        self.done = (self.keep + come).reshape(-1, come.shape[-1])
-
-
-def swaps(moves, *beside):
-    values = together(*[value for value, _ in moves])
-    comes = [hop(value, way) for value, (_, way) in zip(values, moves)]
+
+def in_order(mine, come):
+    first = side("y") == 0
+    return jnp.concatenate([jnp.where(first, mine, come), jnp.where(first, come, mine)], 0)
+
+
+def advance(parts, extra=(), beside=()):
+    moves = [part.move() for part in parts] + list(extra)
+    values = together(*[move[0] for move in moves])
+    comes = [hop(value, *move[1:]) for value, move in zip(values, moves)]
     done = together(*comes, *beside)
-    return done[: len(moves)], done[len(moves) :]
-
-
-def advance(parts, extra=()):
-    comes, _ = swaps([part.move() for part in parts] + list(extra))
-    for part, come in zip(parts, comes):
+    for part, come in zip(parts, done):
         part.absorb(come)
-    return comes[len(parts) :]
+    done = done[len(parts) :]
+    return done[: len(extra)], done[len(extra) :]
 
 
 def flatten_small(small):
@@ -1208,10 +1235,29 @@
     halo = passed_along(rows[count - HALO :].astype(jnp.float32), "seq", 1)
     normed_one, pre, features, gate_pre, beta_pre, beta = project(
         rows, halo, first_gain[None], position, live, query_weight, key_weight, value_weight,
-        gate_weight, beta_weight, conv_weight,
+        gate_weight, beta_weight.T, conv_weight,
     )
     solved, inverses, attend, maps = prepare(keep, features, beta)
-    state_mine, state_other, place, context = carried_forward(maps)
+    if tuned():
+        half = width // 2
+        units = half // 256
+
+        def pick(zero, one):
+            return jnp.where(here, zero, one)
+
+        def both(value, send=None):
+            return value, hop(value if send is None else send, "core")
+
+        wide_top = top.astype(jnp.float32)
+        tops = both(
+            pick(top[:, :half], top[:, half:]), pick(wide_top[:, half:], wide_top[:, :half])
+        )
+        one = both(normed_one)
+    state_mine, state_other, place, context, *beside = carried_forward(
+        maps, (*tops, *one) if tuned() else ()
+    )
+    if tuned():
+        tops, one = beside[:2], beside[2:]
     starts, news, mixed, normed_head = mix(
         keep, place, features, solved, attend, gate_pre, head_gain[None], state_mine, state_other
     )
@@ -1223,21 +1269,6 @@
         hidden_down,
     )
     if tuned():
-        half = width // 2
-        units = half // 256
-
-        def pick(zero, one):
-            return jnp.where(here, zero, one)
-
-        def both(value, send=None):
-            return value, hop(value if send is None else send, "core")
-
-        wide_top = top.astype(jnp.float32)
-        tops = both(
-            pick(top[:, :half], top[:, half:]), pick(wide_top[:, half:], wide_top[:, :half])
-        )
-        one = both(normed_one)
-        inners = both(inner_turned)
         heads_turned = both(head_turned)
         two = both(two_turned)
         gate_up = both(kept, sent)
@@ -1245,34 +1276,39 @@
         keep, core, grad_head, grad_branch, mixed, gate_pre, head_gain[None], features, solved, heads
     )
     if tuned():
-        out_left = pick(heads_turned[0], one[0]), pick(heads_turned[1], one[1])
         out_right = both(out_kept, out_sent)
         blocks = hidden_gate.shape[1] // 256
         some = blocks * 3 // 11
-        down_keep, down_sends = outer([(*inners, *tops, 0, units)], "y", 5)
-        shift, down_keep, *down_sends = together(shift, down_keep, *down_sends)
-        rest_keep, rest_sends = outer([(*two, *gate_up, some, blocks - some)], "y", 2)
-        out_keep, out_sends = outer([(*out_left, *out_right, 0, width // 256)], "near")
-        some_keep, some_sends = outer([(*two, *gate_up, 0, some)], "x")
-        work = [
-            (rest_keep, *rest_sends), (out_keep, *out_sends), (some_keep, *some_sends), (), (),
-        ]
-        moves = [[(send, "y")] for send in down_sends]
-        grad_mine, grad_other, done = carried_back(
-            shift, context, list(zip(moves, work))
-        )
-        down_come = [value[0] for value in done]
-        rest_keep, *rest_sends = done[0][1:]
-        out_keep, *out_sends = done[1][1:]
-        some_keep, *some_sends = done[2][1:]
-        down = Part(down_keep, ("y", "x", "near", "far"))
-        rest = Part(rest_keep, ("y", "x", "near", "far"))
-        some_part = Part(some_keep, ("x", "near", "far", "y"))
-        out = Part(out_keep, ("near", "far", "y", "x"))
-        down.begun(down_come)
-        moves = [down.move(), (rest_sends[0], "y"), (out_sends[0], "near")]
-        grad_mine, *values = together(grad_mine, *[value for value, _ in moves])
-        comes = [hop(value, way) for value, (_, way) in zip(values, moves)]
+        blocks = hidden_gate.shape[1] // 256
+        low = blocks * 9 // 11
+        orders = ("x", "y", "near", "far"), ("y", "x", "far", "near")
+        down_orders = ("near", "x", "y", "far"), ("near", "y", "x", "far")
+        firsts = [order[0] for order in orders]
+        shift, two_other, gate_up_other, inner_turned = together(
+            shift, two[1], gate_up[1], inner_turned
+        )
+        inners = both(inner_turned)
+        two, gate_up = (two[0], two_other), (gate_up[0], gate_up_other)
+        out_right = both(out_kept, out_sent)
+        wide_keep, wide_sends = outer([(*two, *gate_up, 0, low)], orders, (1, 2, 2, 2, 1))
+        shift, wide_keep, *wide_sends = together(shift, wide_keep, *wide_sends)
+        down_keep, down_sends = outer([(*inners, *tops, 0, units)], down_orders, (1, 1))
+        rest_keep, rest_sends = outer(
+            [
+                (*two, *gate_up, low, blocks - low), (*heads_turned, *out_right, 0, units),
+                (*one, *out_right, units, units),
+            ],
+            orders,
+        )
+        work = [(down_keep, *down_sends), (rest_keep, *rest_sends), (), (), ()]
+        moves = [[(send, *firsts)] for send in wide_sends]
+        grad_mine, grad_other, done = carried_back(shift, context, list(zip(moves, work)))
+        down_keep, *down_sends = done[0][1:]
+        rest_keep, *rest_sends = done[1][1:]
+        wide_come = jnp.concatenate([value[0] for value in done], 0)
+        moves = [(rest_sends[0], *firsts), (down_sends[0], "near")]
+        grad_other, *values = together(grad_other, *[move[0] for move in moves])
+        comes = [hop(value, *move[1:]) for value, move in zip(values, moves)]
     else:
         grad_mine, grad_other, _ = carried_back(shift, context)
     grads, borrowed, grad_conv, grad_beta_pre = back(
@@ -1281,79 +1317,67 @@
     )
     if tuned():
         borrowed, *comes = together(borrowed, *comes)
-        down.absorb(comes[0])
-        rest_come = [comes[1]]
-        out.begun([comes[2]])
+        wide_part = Part((wide_keep, rest_keep), (wide_come, comes[0]), orders)
+        down_come = comes[1]
     returned = passed_along(borrowed, "seq", -1)
     tail = grads[:, count - 8 :] + returned
     grads = lax.dynamic_update_slice(grads, tail, (0, count - 8, 0))
     grads = grads.astype(LOW)
     if tuned():
-        moves = [(some_sends[0], "x"), (rest_sends[1], "y"), down.move(), out.move()]
-        grads, *values = together(grads, *[value for value, _ in moves])
-        comes = [hop(value, way) for value, (_, way) in zip(values, moves)]
+        moves = [wide_part.move(), (down_sends[1], "near")]
+        grads, *values = together(grads, *[move[0] for move in moves])
+        comes = [hop(value, *move[1:]) for value, move in zip(values, moves)]
         wide = grads.astype(jnp.float32)
         query_key = both(pick(grads[0], grads[1]), pick(wide[1], wide[0]))
         value = both(
             pick(grads[2, :, :half], grads[2, :, half:]), pick(wide[2, :, half:], wide[2, :, :half])
         )
-        orders = (("y", "x", "near", "far"), ("near", "y", "x", "far"))
-        late = (
-            outer([(*one, *query_key, 0, units), (*one, *value, 0, units)], "y"),
-            outer([(*one, *query_key, units, units)], "near"),
-        )
-        grads, *late_sends = together(grads, *[send for _, (send,) in late])
+        late_keep, (late_send,) = outer(
+            [(*one, *query_key, 0, 2 * units), (*one, *value, 0, units)], orders
+        )
+        grads, late_send, *comes = together(grads, late_send, *comes)
+        wide_part.absorb(comes[0])
+        down = Part((down_keep,), (jnp.concatenate([down_come, comes[1]], 0),), down_orders)
         input_grad, grad_first_gain = enter(
             rows, first_gain[None], grad_hidden, grads, grad_gate_pre, grad_beta_pre, query_weight,
-            key_weight, value_weight, gate_weight, beta_weight,
+            key_weight, value_weight, gate_weight, beta_weight.T,
         )
         small = (
             grad_first_gain[0], outer_sum(normed_one.T, grad_beta_pre), grad_conv, grad_head_gain[0],
             grad_second_gain[0],
         )
         flat = flatten_small(small)
-        late_sends[0], *comes = together(late_sends[0], *comes)
-        some_part.begun([comes[0]])
-        rest.begun([*rest_come, comes[1]])
-        down.absorb(comes[2])
-        out.absorb(comes[3])
-        late = [Part(keep_, order) for (keep_, _), order in zip(late, orders)]
-        comes, (flat, input_grad) = swaps(
-            [part.move() for part in (rest, some_part, down)]
-            + [(send, order[0]) for send, order in zip(late_sends, orders)],
-            flat, input_grad,
-        )
-        for part, come in zip((rest, some_part, down), comes):
-            part.absorb(come)
-        for part, come in zip(late, comes[3:]):
-            part.begun([come])
-        (flat_come,) = advance([out, some_part, rest, *late, down], [(flat, "core")])
-        flat = (flat + flat_come).reshape(4, 2, -1, 128)
+        (come,), (flat, input_grad) = advance(
+            [wide_part, down], [(late_send, *firsts)], (flat, input_grad)
+        )
+        late = Part((late_keep,), (come,), orders)
+        (come,), _ = advance([late, wide_part, down], [(flat, "core")])
+        flat = (flat + come).reshape(2, 2, 2, -1, 128).transpose(2, 1, 0, 3, 4)
         bit = side("x")
-        tiny = Part(take(flat, bit, 1).reshape(-1, 128), ("x", "y", "near", "far"))
-        tiny_send = take(flat, 1 - bit, 1).reshape(-1, 128)
-        tiny_come = advance([out, some_part, rest, *late, down], [(tiny_send, "x")])
-        tiny.begun(tiny_come)
-        advance([rest, out, *late, tiny, some_part])
-        advance([*late, tiny, rest, out])
-        advance([*late, tiny])
-        advance([tiny])
-        advance([tiny])
+        tiny_keep, tiny_send = (take(flat, place, 0).reshape(-1, 128) for place in (bit, 1 - bit))
+        (come,), _ = advance([late, down, wide_part], [(tiny_send, "x")])
+        tiny = Part((tiny_keep,), (come,), (("x", "near", "far"),) * 2, False)
+        advance([late, down, wide_part, tiny])
+        advance([late, down, tiny])
+        advance([late, tiny])
         zero = lambda part: pick(part.done, part.other)
         one_ = lambda part: pick(part.other, part.done)
-        columns = half
-        query_g = jnp.concatenate([zero(late[0])[:, :columns], zero(late[1])], 1)
-        key_g = jnp.concatenate([one_(late[0])[:, :columns], one_(late[1])], 1)
-        value_g = jnp.concatenate([zero(late[0])[:, columns:], one_(late[0])[:, columns:]], 1)
-        out_g, gate_g = zero(out), one_(out)
-        hidden_gate_g = jnp.concatenate([zero(some_part), zero(rest)], 1)
-        hidden_up_g = jnp.concatenate([one_(some_part), one_(rest)], 1)
+        split = blocks * 256
+        hidden_gate_g, hidden_up_g = (
+            of(wide_part)[:, : blocks * 256] for of in (zero, one_)
+        )
+        out_g, gate_g = (
+            jnp.concatenate([zero(wide_part)[:, places], one_(wide_part)[:, places]], 1)
+            for places in (slice(split, split + half), slice(split + half, split + width))
+        )
+        query_g, key_g = zero(late)[:, :width], one_(late)[:, :width]
+        value_g = jnp.concatenate([zero(late)[:, width:], one_(late)[:, width:]], 1)
         hidden_down_g = jnp.concatenate([zero(down), one_(down)], 1)
         first_g, beta_g, conv_g, head_g, second_g = unflatten_small(tiny.done, small)
     else:
         input_grad, grad_first_gain = enter(
             rows, first_gain[None], grad_hidden, grads, grad_gate_pre, grad_beta_pre, query_weight,
-            key_weight, value_weight, gate_weight, beta_weight,
+            key_weight, value_weight, gate_weight, beta_weight.T,
         )
         small = (
             grad_first_gain[0], outer_sum(normed_one.T, grad_beta_pre), grad_conv, grad_head_gain[0],

time: 549 us -> 519 us (0.945)
  waiting for transfers between devices: 206 us -> 172 us
  local copies, waits for them, and re-layouts: 19.9 us -> 25.5 us
  other arithmetic: 70.3 us -> 64.7 us
    ppermute x59 -> x27, waiting for transfers between devices: 189 us -> 73.1 us  [hop(): lax.ppermute(value, axis, [(i, i ^ bit) for i in range(lax.axis_size(axis...]
    ppermute x0 -> x15, waiting for transfers between devices: none -> 80.1 us  [hop(): return lax.ppermute(value, ('seq', 'doc'), pairs)]
    ppermute x0 -> x15, starting transfers between devices: none -> 28.6 us  [hop(): return lax.ppermute(value, ('seq', 'doc'), pairs)]
    ppermute x59 -> x27, starting transfers between devices: 64.6 us -> 40.2 us  [hop(): lax.ppermute(value, axis, [(i, i ^ bit) for i in range(lax.axis_size(axis...]
    select_n x13 -> x9, other arithmetic: 12.2 us -> 6.26 us  [pick(): return jnp.where(here, zero, one)]
    add x29 -> x22, other arithmetic: 40.9 us -> 38.9 us  [the longest x11 21 us: chosen(): return total + self.added(self.terms, here) if self.terms else total]
    unnamed x98 -> x107, local copies, waits for them, and re-layouts: 15.3 us -> 16.9 us
    pallas_call x6 -> x4, Pallas kernels: 43 us -> 41.8 us  [outer(): pl.pallas_call(lambda *refs: outer_kernel(*refs, blocks=counts, pieces=si...]
  transfers between devices with their start and end apart: 67 -> 50, of which waited for: 31 -> 24; matrix products, arithmetic and copies ran while one was open for 7% -> 7% of each run, Pallas kernels for 18% -> 22%
where the time goes in v4:
time: 519 us; the launch traced here: 510 us
  waiting for transfers between devices  172 us (33%)
  Pallas kernels  162 us (31%)
  starting transfers between devices  83.8 us (16%)
  other arithmetic  64.7 us (12%)
  local copies, waits for them, and re-layouts  25.5 us (5%)
    ppermute x15, waiting for transfers between devices, hop(): return lax.ppermute(value, ('seq', 'doc'), pairs)  80.1 us
    ppermute x27, waiting for transfers between devices, hop(): lax.ppermute(value, axis, [(i, i ^ bit) for i in range(lax.axis_size(axis...  73.1 us
    pallas_call x4, Pallas kernels, outer(): pl.pallas_call(lambda *refs: outer_kernel(*refs, blocks=counts, pieces=si...  41.8 us
    ppermute x27, starting transfers between devices, hop(): lax.ppermute(value, axis, [(i, i ^ bit) for i in range(lax.axis_size(axis...  40.2 us
    pallas_call x1, Pallas kernels, back(): pl.pallas_call(back_kernel, grid=(spans,), in_specs=[pl.BlockSpec(memory_...  32.8 us
    ppermute x15, starting transfers between devices, hop(): return lax.ppermute(value, ('seq', 'doc'), pairs)  28.6 us
    pallas_call x1, Pallas kernels, feed(): pl.pallas_call(feed_kernel, grid=(hidden // block,), in_specs=[pl.BlockSp...  27.2 us
    add x11, other arithmetic, chosen(): return total + self.added(self.terms, here) if self.terms else total  21 us
  transfers between devices with their start and end apart: 50, of which 24 were waited for; matrix products, arithmetic and copies ran while one was open for 7% of the time, Pallas kernels for 22%

profile of v4, /device:TPU:0, one launch (start us, length us, event | category | flops | bytes accessed | tf_op | source)
XLA Modules:
  0.0 510.1 jit_solution(17339732888859933311)
XLA Ops:
  1.4 4.8 collective-permute-start
  12.3 12.9 %project.1 = (f32[1024,384]{1,0:T(8,128)}, f32[3,6,72,1024]{3,2,1,0:T(8,128)}, f32[3,384,1024]{2,1,0:T(8,128)}, f32[384,1024]{1,0:T(8,128)}, f32[384,8]{1,0:T(8,128)S(1)}, /*index=5*/f32[384,8]{1,0:T(8,128)S(1)}) custom-call(bf16[384,1024]{1,0:T(8,128)(2,1)S(1)} %bitcast.195, f32[16,1024]{1,0:T(8,128)S(1)} %collective-permute-done.halo, ...), custom_call_target="tpu_custom_call" | custom-call | flops 1 | bytes 1 | tf_op jit(solution)/shard_map/project/pallas_call | solution.py:216
  26.9 16.8 %prepare.1 = (f32[2,384,1024]{2,1,0:T(8,128)}, f32[6,4,128,128]{3,2,1,0:T(8,128)}, f32[6,4,128,128]{3,2,1,0:T(8,128)}, f32[8,128,256]{2,1,0:T(8,128)S(1)}) custom-call(f32[6]{0:T(128)S(1)} %fusion.15.keep, f32[3,384,1024]{2,1,0:T(8,128)} %get-tuple-element.164.features, f32[384,8]{1,0:T(8,128)S(1)} %get-tuple-element.165.beta), custom_call_target="tpu_custom_call" | custom-call | flops 1 | bytes 1 | tf_op jit(solution)/shard_map/prepare/pallas_call | solution.py:299
  43.8 1.6 collective-permute-start.1
  46.2 11.5 %collective-permute-done.1 = f32[4,128,256]{2,1,0:T(8,128)S(1)} collective-permute-done((f32[4,128,256]{2,1,0:T(8,128)S(1)}, f32[4,128,256]{2,1,0:T(8,128)S(1)}, u32[]{:S(2)}, u32[]{:S(2)}) %collective-permute-start.1) | collective-permute-done | bytes 524320 | tf_op jit(solution)/shard_map/ppermute | solution.py:869
  59.1 4.5 collective-permute-start.4
  63.5 4.9 collective-permute-done.4.refs_3_.refs_2_
  71.5 5.9 %collective-permute-done.7.state_other = f32[4,128,128]{2,1,0:T(8,128)S(1)} collective-permute-done((f32[4,128,128]{2,1,0:T(8,128)S(1)}, f32[4,128,128]{2,1,0:T(8,128)S(1)}, u32[]{:S(2)}, u32[]{:S(2)}) %collective-permute-start.7) | collective-permute-done | bytes 262176 | tf_op jit(solution)/shard_map/ppermute | solution.py:869
  77.4 8.5 %mix.1 = (f32[6,8,128,128]{3,2,1,0:T(8,128)}, f32[384,1024]{1,0:T(8,128)}, f32[384,1024]{1,0:T(8,128)}, bf16[384,1024]{1,0:T(8,128)(2,1)S(1)}) custom-call(f32[6]{0:T(128)S(1)} %fusion.15.keep, s32[1]{0:T(128)} %bitcast.6.refs_0_.place, f32[3,384,1024]{2,1,0:T(8,128)} %get-tuple-element.164.features, f32[2,384,1024]{2,1,0:T(8,128)} %get-tuple-element.166.solved, ...), custom_call_target="tpu_custom_call" | custom-call | flops 1 | bytes 1 | tf_op jit(solution)/shard_map/mix/pallas_call | solution.py:366
  85.9 27.2 %feed.1 = (bf16[384,1024]{1,0:T(8,128)(2,1)}, f32[1024,384]{1,0:T(8,128)}, f32[2816,384]{1,0:T(8,128)}, bf16[384,2816]{1,0:T(8,128)(2,1)}, f32[384,2816]{1,0:T(8...) custom-call(s32[1]{0:T(128)} %bitcast.core, ...), custom_call_target="tpu_custom_call" | custom-call | flops 1 | bytes 1 | tf_op jit(solution)/shard_map/feed/pallas_call | solution.py:462
  113.7 9.4 %gather_states.1 = (f32[384,1024]{1,0:T(8,128)}, f32[384,1024]{1,0:T(8,128)}, bf16[384,1024]{1,0:T(8,128)(2,1)S(1)}, f32[384,1024]{1,0:T(8,128)}, f32[1,128]{1,0:T(1,128)S(1)}, /*index=5*/f32[8,128,128]{2,1,0:T(8,128)S(1)}) custom-call(f32[6]{0:T(128)S(1)} %fusion.15.keep, s32[1]{0:T(128)} %bitcast.core, f32[384,1024]{1,0:T(8,128)} %get-tuple-element.176.grad_head, ...), custom_call_target="tpu_custom_call" | custom-call | flops 1 | bytes 1 | tf_op jit(solution)/shard_map/gather_states/pallas_call | solution.py:564
  124.1 12.6 %outer.4 = (f32[512,2304]{1,0:T(8,128)}, f32[64,2304]{1,0:T(8,128)}, f32[128,2304]{1,0:T(8,128)}, f32[128,2304]{1,0:T(8,128)}, f32[128,2304]{1,0:T(8,128)}, /*index=5*/f32[64,2304]{1,0:T(8,128)S(1)}) custom-call(s32[16]{0:T(128)S(1)} %stack.152.refs_0_, f32[1024,384]{1,0:T(8,128)} %get-tuple-element.180.refs_1_, f32[1024,384]{1,0:T(8,128)} %collective-permute-done.8.refs_2_, ...), custom_call_target="tpu_custom_call" | custom-call | flops 1 | bytes 1 | tf_op jit(solution)/shard_map/outer/pallas_call | solution.py:1081
  142.5 8.3 %outer.5 = (f32[1408,512]{1,0:T(8,128)}, f32[704,512]{1,0:T(8,128)}, f32[704,512]{1,0:T(8,128)}) custom-call(s32[16]{0:T(128)S(1)} %stack.169.refs_0_, f32[2816,384]{1,0:T(8,128)} %get-tuple-element.198.refs_1_, f32[2816,384]{1,0:T(8,128)} %collective-permute-done.12.refs_2_, bf16[384,512]{1,0:T(8,128)(2,1)S(1)} %copy-done.9, f32[384,512]{1,0:T(8,128)S(1)} %copy-done.13), custom_call_target="tpu_custom_call" | custom-call | flops 1 | bytes 1 | tf_op jit(solution)/shard_map/outer/pallas_call | solution.py:1081
  150.8 2.7 collective-permute-done.10
  156.2 11.1 %outer.6 = (f32[512,1536]{1,0:T(8,128)}, f32[512,1536]{1,0:T(8,128)}) custom-call(s32[16]{0:T(128)S(1)} %stack.152.refs_0_, f32[1024,384]{1,0:T(8,128)} %get-tuple-element.180.refs_1_, f32[1024,384]{1,0:T(8,128)} %collective-permute-done.8.refs_2_, f32[1024,384]{1,0:T(8,128)} %get-tuple-element.209.refs_3_, f32[1024,384]{1,0:T(8,128)} %collective-permute-done.15.refs_4_, ...), custom_call_target="tpu_custom_call" | custom-call | flops 1 | bytes 1 | tf_op jit(solution)/shard_map/outer/pallas_call | solution.py:1081
  167.3 3.8 collective-permute-done.14
  174.0 14.7 %collective-permute-done.18 = f32[128,2304]{1,0:T(8,128)S(1)} collective-permute-done((f32[128,2304]{1,0:T(8,128)S(1)}, f32[128,2304]{1,0:T(8,128)S(1)}, u32[]{:S(2)}, u32[]{:S(2)}) %collective-permute-start.18) | collective-permute-done | bytes 1179680 | tf_op jit(solution)/shard_map/ppermute | solution.py:873
  191.1 11.5 %collective-permute-done.19.refs_4_ = f32[4,128,128]{2,1,0:T(8,128)S(1)} collective-permute-done((f32[4,128,128]{2,1,0:T(8,128)S(1)}, f32[4,128,128]{2,1,0:T(8,128)S(1)}, u32[]{:S(2)}, u32[]{:S(2)}) %collective-permute-start.19) | collective-permute-done | bytes 262176 | tf_op jit(solution)/shard_map/ppermute | solution.py:1010
  202.6 3.6 collective-permute-done.20
  208.5 10.7 %collective-permute-done.21.state_other = f32[4,128,128]{2,1,0:T(8,128)S(1)} collective-permute-done((f32[4,128,128]{2,1,0:T(8,128)S(1)}, f32[4,128,128]{2,1,0:T(8,128)S(1)}, u32[]{:S(2)}, u32[]{:S(2)}) %collective-permute-start.21) | collective-permute-done | bytes 262176 | tf_op jit(solution)/shard_map/ppermute | solution.py:869
  222.4 7.3 %collective-permute-start.24 = (f32[704,512]{1,0:T(8,128)}, f32[704,512]{1,0:T(8,128)}, u32[]{:S(2)}, u32[]{:S(2)}) collective-permute-start(f32[704,512]{1,0:T(8,128)} %get-tuple-element.247), channel_id=1, source_target_pairs={{0,8},{4,12},{8,0},{12,4},{16,24},{20,28},{24,16},{28,20},{1,9},{5... | collective-permute-start | bytes 4325384 | tf_op jit(solution)/shard_map/ppermute | solution.py:869
  231.2 32.8 %back.1 = (f32[3,384,1024]{2,1,0:T(8,128)}, f32[3,8,1024]{2,1,0:T(8,128)S(1)}, f32[3,4,1024]{2,1,0:T(4,128)S(1)}, f32[384,8]{1,0:T(8,128)S(1)}) custom-call(f32[6]{0:T(128)S(1)} %fusion.15.keep, s32[1]{0:T(128)} %bitcast.6.refs_0_.place, f32[3,384,1024]{2,1,0:T(8,128)} %get-tuple-element.164.features, f32[384,8]{1,0:T(8,128)S(1)} %copy-done.11, ...), custom_call_target="tpu_custom_call" | custom-call | flops 1 | bytes 1 | tf_op jit(solution)/shard_map/back/pallas_call | solution.py:767
  264.1 3.9 add_bitcast_fusion
  269.3 1.9 add_bitcast_fusion.2
  271.2 2.2 pad_maximum_fusion
  273.4 2.3 collective-permute-done.25
  277.8 1.6 fusion
  280.5 1.8 collective-permute-start.29
  282.3 1.5 fusion.2
  284.1 1.7 add_bitcast_fusion.4
  285.9 1.6 add_bitcast_fusion.5
  288.2 9.8 %outer.7 = (f32[512,1536]{1,0:T(8,128)}, f32[512,1536]{1,0:T(8,128)}) custom-call(s32[16]{0:T(128)S(1)} %stack.152.refs_0_, f32[1024,384]{1,0:T(8,128)} %get-tuple-element.210.refs_5_.refs_1_.refs_3_, f32[1024,384]{1,0:T(8,128)} %collective-permute-done.3.refs_6_.refs_2_.refs_4_, f32[1024,384]{1,0:T(8,128)} %get-tuple-element.210.refs_5_.refs_1_.refs_3_, ...), custom_call_target="tpu_custom_call" | custom-call | flops 1 | bytes 1 | tf_op jit(solution)/shard_map/outer/pallas_call | solution.py:1081
  297.9 16.9 %collective-permute-done.29 = f32[704,512]{1,0:T(8,128)} collective-permute-done((f32[704,512]{1,0:T(8,128)}, f32[704,512]{1,0:T(8,128)}, u32[]{:S(2)}, u32[]{:S(2)}) %collective-permute-start.29) | collective-permute-done | bytes 1441824 | tf_op jit(solution)/shard_map/ppermute | solution.py:869
  314.9 7.2 %collective-permute-done.28 = f32[2,2,64,3840]{3,2,1,0:T(8,128)} collective-permute-done((f32[2,2,64,3840]{3,2,1,0:T(8,128)}, f32[2,2,64,3840]{3,2,1,0:T(8,128)}, u32[]{:S(2)}, u32[]{:S(2)}) %collective-permute-start.28) | collective-permute-done | bytes 3932192 | tf_op jit(solution)/shard_map/ppermute | solution.py:873
  322.1 2.2 pad_maximum_fusion.1
  324.8 1.6 add_bitcast_fusion.3
  326.4 3.3 maximum_add_fusion
  331.0 6.3 %collective-permute-start.30 = (f32[2,64,3840]{2,1,0:T(8,128)}, f32[2,64,3840]{2,1,0:T(8,128)}, u32[]{:S(2)}, u32[]{:S(2)}) collective-permute-start(f32[2,64,3840]{2,1,0:T(8,128)} %maximum_add_fusion), channel_id=1, source_target_pairs={{0,8},{1,17},{2,10},{3,19},{4,12},{5,21},{6,14},{7,23},{8,0},{9,25... | collective-permute-start | bytes 5898248 | tf_op jit(solution)/shard_map/ppermute | solution.py:873
  339.3 1.7 add_bitcast_fusion.6
  342.5 10.1 %enter.1 = (bf16[384,1024]{1,0:T(8,128)(2,1)}, f32[1,1024]{1,0:T(1,128)S(1)}) custom-call(bf16[384,1024]{1,0:T(8,128)(2,1)S(1)} %bitcast.197, f32[1,1024]{1,0:T(1,128)S(1)} %bitcast.201, f32[384,1024]{1,0:T(8,128)} %get-tuple-element.264.grad_hidden, bf16[3,384,1024]{2,1,0:T(8,128)(2,1)} %copy-done.26, f32[384,1024]{1,0:T(8,128)} %get-tuple-element.266.grad_gate, ...), custom_call_target="tpu_custom_call" | custom-call | flops 1 | bytes 1 | tf_op jit(solution)/shard_map/enter/pallas_call | solution.py:830
  352.7 30.0 %collective-permute-done.31 = f32[2,2,176,512]{3,2,1,0:T(8,128)} collective-permute-done((f32[2,2,176,512]{3,2,1,0:T(8,128)}, f32[2,2,176,512]{3,2,1,0:T(8,128)}, u32[]{:S(2)}, u32[]{:S(2)}) %collective-permute-start.31) | collective-permute-done | bytes 1441824 | tf_op jit(solution)/shard_map/ppermute | solution.py:873
  382.7 2.6 bitcast_add_fusion.3
  385.3 3.2 add_bitcast_fusion.1
  388.6 2.6 maximum_add_fusion.1
  392.4 8.7 %collective-permute-start.34 = (f32[64,3840]{1,0:T(8,128)}, f32[64,3840]{1,0:T(8,128)S(1)}, u32[]{:S(2)}, u32[]{:S(2)}) collective-permute-start(f32[64,3840]{1,0:T(8,128)} %maximum_add_fusion.1), channel_id=1, source_target_pairs={{0,16},{1,9},{2,18},{3,11},{4,20},{5,13},{6,22},{7,15},{8,24},{9,1... | collective-permute-start | bytes 2949128 | tf_op jit(solution)/shard_map/ppermute | solution.py:873
  403.2 16.3 %collective-permute-done.35 = f32[2,176,512]{2,1,0:T(8,128)S(1)} collective-permute-done((f32[2,176,512]{2,1,0:T(8,128)}, f32[2,176,512]{2,1,0:T(8,128)S(1)}, u32[]{:S(2)}, u32[]{:S(2)}) %collective-permute-start.35) | collective-permute-done | bytes 720928 | tf_op jit(solution)/shard_map/ppermute | solution.py:873
  419.6 4.3 collective-permute-done.34
  424.7 1.8 bitcast_add_fusion.2
  426.5 2.1 fusion.10
  428.6 2.0 maximum_add_fusion.2
  431.5 2.4 collective-permute-start.37
  433.9 4.9 collective-permute-start.38
  438.8 4.5 collective-permute-done.40
  443.4 8.8 %collective-permute-done.38 = f32[176,512]{1,0:T(8,128)} collective-permute-done((f32[176,512]{1,0:T(8,128)}, f32[176,512]{1,0:T(8,128)}, u32[]{:S(2)}, u32[]{:S(2)}) %collective-permute-start.38) | collective-permute-done | bytes 360480 | tf_op jit(solution)/shard_map/ppermute | solution.py:869
  453.3 2.1 fusion.7
  455.4 1.6 broadcast_select_fusion.3
  460.7 8.1 %collective-permute-start.43 = (f32[128,3840]{1,0:T(8,128)}, f32[128,3840]{1,0:T(8,128)}, u32[]{:S(2)}, u32[]{:S(2)}) collective-permute-start(f32[128,3840]{1,0:T(8,128)} %pad_maximum_fusion.2), channel_id=1, source_target_pairs={{0,1},{1,0},{2,3},{3,2},{4,5},{5,4},{6,7},{7,6},{8,9},{9,8},{10,11... | collective-permute-start | bytes 5898248 | tf_op jit(solution)/shard_map/ppermute | solution.py:869
  468.9 2.8 collective-permute-start.41
  472.2 2.4 collective-permute-start.44
  474.7 4.8 collective-permute-done.44
  485.4 3.3 collective-permute-start.47
  488.8 1.8 broadcast_select_fusion.1
  490.6 4.6 collective-permute-done.45
  500.3 1.7 collective-permute-start.49
  (257 shorter events, 75.5 us)
Async XLA Ops:
  1.4 7.4 %collective-permute-start = (f32[16,1024]{1,0:T(8,128)S(1)}, f32[16,1024]{1,0:T(8,128)S(1)}, u32[]{:S(2)}, u32[]{:S(2)}) collective-permute-start(f32[16,1024]{1,0:T(8,128)S(1)} %bitcast_convert_fusion), channel_id=1, source_target_pairs={{0,4},{4,8},{8,12},{12,16},{16,20},{20,24},{24,28},{1,5},{5,9},{9,... | collective-permute-start | bytes 196616 | tf_op jit(solution)/shard_map/ppermute | solution.py:856
  8.7 16.5 %copy-start.5 = (s32[384,1]{1,0:T(8,128)}, s32[384,1]{1,0:T(8,128)S(1)}, u32[]{:S(2)}) copy-start(s32[384,1]{1,0:T(8,128)S(1)} %reshape_subtract_fusion.position) | copy-start | bytes 4612
  8.8 16.3 %copy-start.7 = (f32[384,1]{1,0:T(8,128)}, f32[384,1]{1,0:T(8,128)S(1)}, u32[]{:S(2)}) copy-start(f32[384,1]{1,0:T(8,128)S(1)} %fusion.11.live) | copy-start | bytes 4612
  12.3 13.6 %copy-start.31 = (bf16[1,384,1024]{2,1,0:T(8,128)(2,1)S(1)}, bf16[1,384,1024]{2,1,0:T(8,128)(2,1)}, u32[]{:S(2)}) copy-start(bf16[1,384,1024]{2,1,0:T(8,128)(2,1)} %param.18) | copy-start | bytes 2359300
  25.9 32.8 %collective-permute-start.3 = (f32[1024,384]{1,0:T(8,128)}, f32[1024,384]{1,0:T(8,128)}, u32[]{:S(2)}, u32[]{:S(2)}) collective-permute-start(f32[1024,384]{1,0:T(8,128)} %get-tuple-element.210.refs_5_.refs_1_.refs_3_), channel_id=1, source_target_pairs={{0,1},{1,0},{2,3},{3,2},{4,5},{5,4},{6,7},{7,6},{8,9},{9,8},{10,11... | collective-permute-start | bytes 4718600 | tf_op jit(solution)/shard_map/ppermute | solution.py:869
  26.2 31.5 %collective-permute-start.2 = (f32[384,512]{1,0:T(8,128)S(1)}, f32[384,512]{1,0:T(8,128)S(1)}, u32[]{:S(2)}, u32[]{:S(2)}) collective-permute-start(f32[384,512]{1,0:T(8,128)S(1)} %slice_select_fusion.2), channel_id=1, source_target_pairs={{0,1},{1,0},{2,3},{3,2},{4,5},{5,4},{6,7},{7,6},{8,9},{9,8},{10,11... | collective-permute-start | bytes 2359304 | tf_op jit(solution)/shard_map/ppermute | solution.py:869
  43.8 13.9 %collective-permute-start.1 = (f32[4,128,256]{2,1,0:T(8,128)S(1)}, f32[4,128,256]{2,1,0:T(8,128)S(1)}, u32[]{:S(2)}, u32[]{:S(2)}) collective-permute-start(f32[4,128,256]{2,1,0:T(8,128)S(1)} %slice_select_fusion.3), channel_id=1, source_target_pairs={{0,4},{4,0},{8,12},{12,8},{16,20},{20,16},{24,28},{28,24},{1,5},{5... | collective-permute-start | bytes 1572872 | tf_op jit(solution)/shard_map/ppermute | solution.py:869
  59.1 9.4 %collective-permute-start.4 = (f32[4,128,128]{2,1,0:T(8,128)S(1)}, f32[4,128,128]{2,1,0:T(8,128)S(1)}, u32[]{:S(2)}, u32[]{:S(2)}) collective-permute-start(f32[4,128,128]{2,1,0:T(8,128)S(1)} %slice.155), channel_id=1, source_target_pairs={{0,8},{4,12},{1,9},{5,13},{2,10},{6,14},{3,11},{7,15}} | collective-permute-start | bytes 786440 | tf_op jit(solution)/shard_map/ppermute | solution.py:964
  68.7 0.7 collective-permute-start.5
  69.6 0.9 collective-permute-start.6
  70.8 6.5 %collective-permute-start.7 = (f32[4,128,128]{2,1,0:T(8,128)S(1)}, f32[4,128,128]{2,1,0:T(8,128)S(1)}, u32[]{:S(2)}, u32[]{:S(2)}) collective-permute-start(f32[4,128,128]{2,1,0:T(8,128)S(1)} %get-tuple-element.173), channel_id=1, source_target_pairs={{0,4},{4,0},{8,12},{12,8},{16,20},{20,16},{24,28},{28,24},{1,5},{5... | collective-permute-start | bytes 786440 | tf_op jit(solution)/shard_map/ppermute | solution.py:869
  113.1 10.8 %collective-permute-start.9 = (f32[384,2816]{1,0:T(8,128)}, f32[384,2816]{1,0:T(8,128)}, u32[]{:S(2)}, u32[]{:S(2)}) collective-permute-start(f32[384,2816]{1,0:T(8,128)} %get-tuple-element.181), channel_id=1, source_target_pairs={{0,1},{1,0},{2,3},{3,2},{4,5},{5,4},{6,7},{7,6},{8,9},{9,8},{10,11... | collective-permute-start | bytes 12976136 | tf_op jit(solution)/shard_map/ppermute | solution.py:869
  113.2 10.7 %collective-permute-start.8 = (f32[1024,384]{1,0:T(8,128)}, f32[1024,384]{1,0:T(8,128)}, u32[]{:S(2)}, u32[]{:S(2)}) collective-permute-start(f32[1024,384]{1,0:T(8,128)} %get-tuple-element.180.refs_1_), channel_id=1, source_target_pairs={{0,1},{1,0},{2,3},{3,2},{4,5},{5,4},{6,7},{7,6},{8,9},{9,8},{10,11... | collective-permute-start | bytes 4718600 | tf_op jit(solution)/shard_map/ppermute | solution.py:869
  123.9 16.4 %collective-permute-start.12 = (f32[2816,384]{1,0:T(8,128)}, f32[2816,384]{1,0:T(8,128)}, u32[]{:S(2)}, u32[]{:S(2)}) collective-permute-start(f32[2816,384]{1,0:T(8,128)} %get-tuple-element.198.refs_1_), channel_id=1, source_target_pairs={{0,1},{1,0},{2,3},{3,2},{4,5},{5,4},{6,7},{7,6},{8,9},{9,8},{10,11... | collective-permute-start | bytes 12976136 | tf_op jit(solution)/shard_map/ppermute | solution.py:869
  124.1 12.6 %copy-start.3 = (f32[8,128,128]{2,1,0:T(8,128)S(1)}, f32[8,128,128]{2,1,0:T(8,128)}, u32[]{:S(2)}) copy-start(f32[8,128,128]{2,1,0:T(8,128)} %copy-done.2) | copy-start | bytes 1572868
  137.7 15.8 %collective-permute-start.11 = (f32[64,2304]{1,0:T(8,128)}, f32[64,2304]{1,0:T(8,128)}, u32[]{:S(2)}, u32[]{:S(2)}) collective-permute-start(f32[64,2304]{1,0:T(8,128)} %get-tuple-element.197), channel_id=1, source_target_pairs={{0,4},{1,3},{2,6},{3,1},{4,0},{5,7},{6,2},{7,5},{8,12},{9,11},{10,... | collective-permute-start | bytes 1769480 | tf_op jit(solution)/shard_map/ppermute | solution.py:873
  138.3 15.2 %collective-permute-start.10 = (f32[4,128,128]{2,1,0:T(8,128)}, f32[4,128,128]{2,1,0:T(8,128)}, u32[]{:S(2)}, u32[]{:S(2)}) collective-permute-start(f32[4,128,128]{2,1,0:T(8,128)} %slice_select_fusion.7), channel_id=1, source_target_pairs={{0,4},{4,0},{8,12},{12,8},{16,20},{20,16},{24,28},{28,24},{1,5},{5... | collective-permute-start | bytes 786440 | tf_op jit(solution)/shard_map/ppermute | solution.py:869
  139.7 16.5 %collective-permute-start.16 = (f32[384,1024]{1,0:T(8,128)}, f32[384,1024]{1,0:T(8,128)}, u32[]{:S(2)}, u32[]{:S(2)}) collective-permute-start(f32[384,1024]{1,0:T(8,128)} %get-tuple-element.213), channel_id=1, source_target_pairs={{0,1},{1,0},{2,3},{3,2},{4,5},{5,4},{6,7},{7,6},{8,9},{9,8},{10,11... | collective-permute-start | bytes 4718600 | tf_op jit(solution)/shard_map/ppermute | solution.py:869
  139.7 16.5 %collective-permute-start.15 = (f32[1024,384]{1,0:T(8,128)}, f32[1024,384]{1,0:T(8,128)}, u32[]{:S(2)}, u32[]{:S(2)}) collective-permute-start(f32[1024,384]{1,0:T(8,128)} %get-tuple-element.209.refs_3_), channel_id=1, source_target_pairs={{0,1},{1,0},{2,3},{3,2},{4,5},{5,4},{6,7},{7,6},{8,9},{9,8},{10,11... | collective-permute-start | bytes 4718600 | tf_op jit(solution)/shard_map/ppermute | solution.py:869
  140.3 13.2 %copy-start.4 = (f32[8,128,128]{2,1,0:T(8,128)S(1)}, f32[8,128,128]{2,1,0:T(8,128)}, u32[]{:S(2)}) copy-start(f32[8,128,128]{2,1,0:T(8,128)} %copy-done.2) | copy-start | bytes 1572868
  154.8 16.3 %collective-permute-start.14 = (f32[128,2304]{1,0:T(8,128)S(1)}, f32[128,2304]{1,0:T(8,128)S(1)}, u32[]{:S(2)}, u32[]{:S(2)}) collective-permute-start(f32[128,2304]{1,0:T(8,128)S(1)} %copy-done.48), channel_id=1, source_target_pairs={{0,4},{1,3},{2,6},{3,1},{4,0},{5,7},{6,2},{7,5},{8,12},{9,11},{10,... | collective-permute-start | bytes 3538952 | tf_op jit(solution)/shard_map/ppermute | solution.py:873
  155.5 11.8 %collective-permute-start.13 = (f32[4,128,128]{2,1,0:T(8,128)S(1)}, f32[4,128,128]{2,1,0:T(8,128)S(1)}, u32[]{:S(2)}, u32[]{:S(2)}) collective-permute-start(f32[4,128,128]{2,1,0:T(8,128)S(1)} %apply_map.9.refs_0_), channel_id=1, source_target_pairs={{24,16},{28,20},{25,17},{29,21},{26,18},{30,22},{27,19},{31,23}} | collective-permute-start | bytes 786440 | tf_op jit(solution)/shard_map/ppermute | solution.py:1010
  156.2 16.2 %copy-start.47 = (f32[128,2304]{1,0:T(8,128)S(1)}, f32[128,2304]{1,0:T(8,128)}, u32[]{:S(2)}) copy-start(f32[128,2304]{1,0:T(8,128)} %get-tuple-element.220) | copy-start | bytes 3538948
  167.3 21.7 %copy-start.46 = (f32[128,2304]{1,0:T(8,128)S(1)}, f32[128,2304]{1,0:T(8,128)}, u32[]{:S(2)}) copy-start(f32[128,2304]{1,0:T(8,128)} %get-tuple-element.225) | copy-start | bytes 3538948
  172.4 34.0 %copy-start.25 = (f32[64,2304]{1,0:T(8,128)S(1)}, f32[64,2304]{1,0:T(8,128)}, u32[]{:S(2)}) copy-start(f32[64,2304]{1,0:T(8,128)} %copy-done.24) | copy-start | bytes 1769476
  172.4 16.3 %collective-permute-start.18 = (f32[128,2304]{1,0:T(8,128)S(1)}, f32[128,2304]{1,0:T(8,128)S(1)}, u32[]{:S(2)}, u32[]{:S(2)}) collective-permute-start(f32[128,2304]{1,0:T(8,128)S(1)} %copy-done.47), channel_id=1, source_target_pairs={{0,4},{1,3},{2,6},{3,1},{4,0},{5,7},{6,2},{7,5},{8,12},{9,11},{10,... | collective-permute-start | bytes 3538952 | tf_op jit(solution)/shard_map/ppermute | solution.py:873
  173.1 0.9 collective-permute-start.17
  189.0 17.1 %collective-permute-start.20 = (f32[128,2304]{1,0:T(8,128)S(1)}, f32[128,2304]{1,0:T(8,128)S(1)}, u32[]{:S(2)}, u32[]{:S(2)}) collective-permute-start(f32[128,2304]{1,0:T(8,128)S(1)} %copy-done.46), channel_id=1, source_target_pairs={{0,4},{1,3},{2,6},{3,1},{4,0},{5,7},{6,2},{7,5},{8,12},{9,11},{10,... | collective-permute-start | bytes 3538952 | tf_op jit(solution)/shard_map/ppermute | solution.py:873
  189.7 12.8 %collective-permute-start.19 = (f32[4,128,128]{2,1,0:T(8,128)S(1)}, f32[4,128,128]{2,1,0:T(8,128)S(1)}, u32[]{:S(2)}, u32[]{:S(2)}) collective-permute-start(f32[4,128,128]{2,1,0:T(8,128)S(1)} %apply_map.11), channel_id=1, source_target_pairs={{8,0},{12,4},{9,1},{13,5},{10,2},{14,6},{11,3},{15,7}} | collective-permute-start | bytes 786440 | tf_op jit(solution)/shard_map/ppermute | solution.py:1010
  206.1 13.1 %copy-start.38 = (f32[128,2304]{1,0:T(8,128)}, f32[128,2304]{1,0:T(8,128)S(1)}, u32[]{:S(2)}) copy-start(f32[128,2304]{1,0:T(8,128)S(1)} %collective-permute-done.20) | copy-start | bytes 3538948
  206.4 12.8 %collective-permute-start.22 = (f32[64,2304]{1,0:T(8,128)S(1)}, f32[64,2304]{1,0:T(8,128)S(1)}, u32[]{:S(2)}, u32[]{:S(2)}) collective-permute-start(f32[64,2304]{1,0:T(8,128)S(1)} %copy-done.25), channel_id=1, source_target_pairs={{0,4},{1,3},{2,6},{3,1},{4,0},{5,7},{6,2},{7,5},{8,12},{9,11},{10,... | collective-permute-start | bytes 1769480 | tf_op jit(solution)/shard_map/ppermute | solution.py:873
  207.1 12.1 %collective-permute-start.21 = (f32[4,128,128]{2,1,0:T(8,128)S(1)}, f32[4,128,128]{2,1,0:T(8,128)S(1)}, u32[]{:S(2)}, u32[]{:S(2)}) collective-permute-start(f32[4,128,128]{2,1,0:T(8,128)S(1)} %get-tuple-element.230), channel_id=1, source_target_pairs={{0,4},{4,0},{8,12},{12,8},{16,20},{20,16},{24,28},{28,24},{1,5},{5... | collective-permute-start | bytes 786440 | tf_op jit(solution)/shard_map/ppermute | solution.py:869
  219.2 48.8 %collective-permute-start.23 = (f32[512,1536]{1,0:T(8,128)}, f32[512,1536]{1,0:T(8,128)}, u32[]{:S(2)}, u32[]{:S(2)}) collective-permute-start(f32[512,1536]{1,0:T(8,128)} %get-tuple-element.246), channel_id=1, source_target_pairs={{0,4},{1,3},{2,6},{3,1},{4,0},{5,7},{6,2},{7,5},{8,12},{9,11},{10,... | collective-permute-start | bytes 9437192 | tf_op jit(solution)/shard_map/ppermute | solution.py:873
  220.9 10.2 %copy-start.39 = (f32[128,2304]{1,0:T(8,128)S(1)}, f32[128,2304]{1,0:T(8,128)}, u32[]{:S(2)}) copy-start(f32[128,2304]{1,0:T(8,128)} %copy-done.38) | copy-start | bytes 3538948
  222.4 8.8 %copy-start.6 = (s32[384,1]{1,0:T(8,128)S(1)}, s32[384,1]{1,0:T(8,128)}, u32[]{:S(2)}) copy-start(s32[384,1]{1,0:T(8,128)} %copy-done.5) | copy-start | bytes 4612
  222.4 8.8 %copy-start.8 = (f32[384,1]{1,0:T(8,128)S(1)}, f32[384,1]{1,0:T(8,128)}, u32[]{:S(2)}) copy-start(f32[384,1]{1,0:T(8,128)} %copy-done.7) | copy-start | bytes 4612
  222.4 45.6 %collective-permute-start.24 = (f32[704,512]{1,0:T(8,128)}, f32[704,512]{1,0:T(8,128)}, u32[]{:S(2)}, u32[]{:S(2)}) collective-permute-start(f32[704,512]{1,0:T(8,128)} %get-tuple-element.247), channel_id=1, source_target_pairs={{0,8},{4,12},{8,0},{12,4},{16,24},{20,28},{24,16},{28,20},{1,9},{5... | collective-permute-start | bytes 4325384 | tf_op jit(solution)/shard_map/ppermute | solution.py:869
  268.0 7.6 %collective-permute-start.25 = (f32[3,8,1024]{2,1,0:T(8,128)S(1)}, f32[3,8,1024]{2,1,0:T(8,128)S(1)}, u32[]{:S(2)}, u32[]{:S(2)}) collective-permute-start(f32[3,8,1024]{2,1,0:T(8,128)S(1)} %get-tuple-element.250), channel_id=1, source_target_pairs={{4,0},{8,4},{12,8},{16,12},{20,16},{24,20},{28,24},{5,1},{9,5},{13... | collective-permute-start | bytes 294920 | tf_op jit(solution)/shard_map/ppermute | solution.py:856
  276.0 46.1 %collective-permute-start.28 = (f32[2,2,64,3840]{3,2,1,0:T(8,128)}, f32[2,2,64,3840]{3,2,1,0:T(8,128)}, u32[]{:S(2)}, u32[]{:S(2)}) collective-permute-start(f32[2,2,64,3840]{3,2,1,0:T(8,128)} %pad_maximum_fusion), channel_id=1, source_target_pairs={{0,2},{1,5},{2,0},{3,7},{4,6},{5,1},{6,4},{7,3},{8,10},{9,13},{10,... | collective-permute-start | bytes 11796488 | tf_op jit(solution)/shard_map/ppermute | solution.py:873
  280.5 7.7 %collective-permute-start.26 = (f32[384,1024]{1,0:T(8,128)}, f32[384,1024]{1,0:T(8,128)}, u32[]{:S(2)}, u32[]{:S(2)}) collective-permute-start(f32[384,1024]{1,0:T(8,128)} %fusion), channel_id=1, source_target_pairs={{0,1},{1,0},{2,3},{3,2},{4,5},{5,4},{6,7},{7,6},{8,9},{9,8},{10,11... | collective-permute-start | bytes 4718600 | tf_op jit(solution)/shard_map/ppermute | solution.py:869
  280.5 34.4 %collective-permute-start.29 = (f32[704,512]{1,0:T(8,128)}, f32[704,512]{1,0:T(8,128)}, u32[]{:S(2)}, u32[]{:S(2)}) collective-permute-start(f32[704,512]{1,0:T(8,128)} %get-tuple-element.255), channel_id=1, source_target_pairs={{0,8},{4,12},{8,0},{12,4},{16,24},{20,28},{24,16},{28,20},{1,9},{5... | collective-permute-start | bytes 4325384 | tf_op jit(solution)/shard_map/ppermute | solution.py:869
  283.8 4.3 collective-permute-start.27
  326.4 12.2 %copy-start.28 = (f32[1024,384]{1,0:T(8,128)S(1)}, f32[1024,384]{1,0:T(8,128)}, u32[]{:S(2)}) copy-start(f32[1024,384]{1,0:T(8,128)} %get-tuple-element.210.refs_5_.refs_1_.refs_3_) | copy-start | bytes 4718596
  329.7 53.0 %collective-permute-start.32 = (f32[512,1536]{1,0:T(8,128)}, f32[512,1536]{1,0:T(8,128)}, u32[]{:S(2)}, u32[]{:S(2)}) collective-permute-start(f32[512,1536]{1,0:T(8,128)} %get-tuple-element.263), channel_id=1, source_target_pairs={{0,4},{1,3},{2,6},{3,1},{4,0},{5,7},{6,2},{7,5},{8,12},{9,11},{10,... | collective-permute-start | bytes 9437192 | tf_op jit(solution)/shard_map/ppermute | solution.py:873
  331.0 51.7 %collective-permute-start.30 = (f32[2,64,3840]{2,1,0:T(8,128)}, f32[2,64,3840]{2,1,0:T(8,128)}, u32[]{:S(2)}, u32[]{:S(2)}) collective-permute-start(f32[2,64,3840]{2,1,0:T(8,128)} %maximum_add_fusion), channel_id=1, source_target_pairs={{0,8},{1,17},{2,10},{3,19},{4,12},{5,21},{6,14},{7,23},{8,0},{9,25... | collective-permute-start | bytes 5898248 | tf_op jit(solution)/shard_map/ppermute | solution.py:873
  337.3 45.4 %collective-permute-start.31 = (f32[2,2,176,512]{3,2,1,0:T(8,128)}, f32[2,2,176,512]{3,2,1,0:T(8,128)}, u32[]{:S(2)}, u32[]{:S(2)}) collective-permute-start(f32[2,2,176,512]{3,2,1,0:T(8,128)} %add_bitcast_fusion.3), channel_id=1, source_target_pairs={{0,4},{1,3},{2,6},{3,1},{4,0},{5,7},{6,2},{7,5},{8,12},{9,11},{10,... | collective-permute-start | bytes 4325384 | tf_op jit(solution)/shard_map/ppermute | solution.py:873
  391.2 32.7 %collective-permute-start.33 = (f32[2,2,64,1536]{3,2,1,0:T(8,128)}, f32[2,2,64,1536]{3,2,1,0:T(8,128)}, u32[]{:S(2)}, u32[]{:S(2)}) collective-permute-start(f32[2,2,64,1536]{3,2,1,0:T(8,128)} %add_bitcast_fusion.1), channel_id=1, source_target_pairs={{0,2},{1,5},{2,0},{3,7},{4,6},{5,1},{6,4},{7,3},{8,10},{9,13},{10,... | collective-permute-start | bytes 4718600 | tf_op jit(solution)/shard_map/ppermute | solution.py:873
  392.4 31.5 %collective-permute-start.34 = (f32[64,3840]{1,0:T(8,128)}, f32[64,3840]{1,0:T(8,128)S(1)}, u32[]{:S(2)}, u32[]{:S(2)}) collective-permute-start(f32[64,3840]{1,0:T(8,128)} %maximum_add_fusion.1), channel_id=1, source_target_pairs={{0,16},{1,9},{2,18},{3,11},{4,20},{5,13},{6,22},{7,15},{8,24},{9,1... | collective-permute-start | bytes 2949128 | tf_op jit(solution)/shard_map/ppermute | solution.py:873
  401.1 18.5 %collective-permute-start.35 = (f32[2,176,512]{2,1,0:T(8,128)}, f32[2,176,512]{2,1,0:T(8,128)S(1)}, u32[]{:S(2)}, u32[]{:S(2)}) collective-permute-start(f32[2,176,512]{2,1,0:T(8,128)} %bitcast_add_fusion.3), channel_id=1, source_target_pairs={{0,2},{1,5},{2,0},{3,7},{4,6},{5,1},{6,4},{7,3},{8,10},{9,13},{10,... | collective-permute-start | bytes 2162696 | tf_op jit(solution)/shard_map/ppermute | solution.py:873
  401.9 1.3 collective-permute-start.36
  430.6 21.7 %copy-start.33 = (f32[64,3840]{1,0:T(8,128)}, f32[64,3840]{1,0:T(8,128)S(1)}, u32[]{:S(2)}) copy-start(f32[64,3840]{1,0:T(8,128)S(1)} %maximum_add_fusion.2) | copy-start | bytes 2949124
  430.7 21.7 %collective-permute-start.39 = (f32[64,3840]{1,0:T(8,128)S(1)}, f32[64,3840]{1,0:T(8,128)S(1)}, u32[]{:S(2)}, u32[]{:S(2)}) collective-permute-start(f32[64,3840]{1,0:T(8,128)S(1)} %maximum_add_fusion.2), channel_id=1, source_target_pairs={{0,2},{1,3},{2,0},{3,1},{4,6},{5,7},{6,4},{7,5},{8,10},{9,11},{10,... | collective-permute-start | bytes 2949128 | tf_op jit(solution)/shard_map/ppermute | solution.py:869
  431.5 20.8 %collective-permute-start.37 = (f32[2,64,1536]{2,1,0:T(8,128)S(1)}, f32[2,64,1536]{2,1,0:T(8,128)S(1)}, u32[]{:S(2)}, u32[]{:S(2)}) collective-permute-start(f32[2,64,1536]{2,1,0:T(8,128)S(1)} %bitcast_add_fusion.2), channel_id=1, source_target_pairs={{0,8},{1,17},{2,10},{3,19},{4,12},{5,21},{6,14},{7,23},{8,0},{9,25... | collective-permute-start | bytes 2359304 | tf_op jit(solution)/shard_map/ppermute | solution.py:873
  433.9 18.3 %collective-permute-start.38 = (f32[176,512]{1,0:T(8,128)}, f32[176,512]{1,0:T(8,128)}, u32[]{:S(2)}, u32[]{:S(2)}) collective-permute-start(f32[176,512]{1,0:T(8,128)} %fusion.10), channel_id=1, source_target_pairs={{0,16},{4,20},{8,24},{12,28},{16,0},{20,4},{24,8},{28,12},{1,17},{... | collective-permute-start | bytes 1081352 | tf_op jit(solution)/shard_map/ppermute | solution.py:869
  438.8 4.6 collective-permute-start.40
  460.7 19.5 %collective-permute-start.43 = (f32[128,3840]{1,0:T(8,128)}, f32[128,3840]{1,0:T(8,128)}, u32[]{:S(2)}, u32[]{:S(2)}) collective-permute-start(f32[128,3840]{1,0:T(8,128)} %pad_maximum_fusion.2), channel_id=1, source_target_pairs={{0,1},{1,0},{2,3},{3,2},{4,5},{5,4},{6,7},{7,6},{8,9},{9,8},{10,11... | collective-permute-start | bytes 5898248 | tf_op jit(solution)/shard_map/ppermute | solution.py:869
  468.9 11.4 %collective-permute-start.41 = (f32[64,1536]{1,0:T(8,128)}, f32[64,1536]{1,0:T(8,128)S(1)}, u32[]{:S(2)}, u32[]{:S(2)}) collective-permute-start(f32[64,1536]{1,0:T(8,128)} %fusion.7), channel_id=1, source_target_pairs={{0,16},{1,9},{2,18},{3,11},{4,20},{5,13},{6,22},{7,15},{8,24},{9,1... | collective-permute-start | bytes 1179656 | tf_op jit(solution)/shard_map/ppermute | solution.py:873
  471.7 8.5 %collective-permute-start.42 = (f32[176,512]{1,0:T(8,128)S(1)}, f32[176,512]{1,0:T(8,128)}, u32[]{:S(2)}, u32[]{:S(2)}) collective-permute-start(f32[176,512]{1,0:T(8,128)S(1)} %fusion.9), channel_id=1, source_target_pairs={{0,2},{1,3},{2,0},{3,1},{4,6},{5,7},{6,4},{7,5},{8,10},{9,11},{10,... | collective-permute-start | bytes 1081352 | tf_op jit(solution)/shard_map/ppermute | solution.py:869
  472.2 7.3 %collective-permute-start.44 = (f32[2,32,128]{2,1,0:T(8,128)S(1)}, f32[2,32,128]{2,1,0:T(8,128)}, u32[]{:S(2)}, u32[]{:S(2)}) collective-permute-start(f32[2,32,128]{2,1,0:T(8,128)S(1)} %bitcast_add_fusion.8), channel_id=1, source_target_pairs={{0,8},{4,12},{8,0},{12,4},{16,24},{20,28},{24,16},{28,20},{1,9},{5... | collective-permute-start | bytes 98312 | tf_op jit(solution)/shard_map/ppermute | solution.py:869
  483.5 11.6 %collective-permute-start.46 = (f32[352,512]{1,0:T(8,128)S(1)}, f32[352,512]{1,0:T(8,128)S(1)}, u32[]{:S(2)}, u32[]{:S(2)}) collective-permute-start(f32[352,512]{1,0:T(8,128)S(1)} %pad_maximum_fusion.5), channel_id=1, source_target_pairs={{0,1},{1,0},{2,3},{3,2},{4,5},{5,4},{6,7},{7,6},{8,9},{9,8},{10,11... | collective-permute-start | bytes 2162696 | tf_op jit(solution)/shard_map/ppermute | solution.py:869
  484.1 11.1 %collective-permute-start.45 = (f32[64,1536]{1,0:T(8,128)S(1)}, f32[64,1536]{1,0:T(8,128)S(1)}, u32[]{:S(2)}, u32[]{:S(2)}) collective-permute-start(f32[64,1536]{1,0:T(8,128)S(1)} %fusion.6), channel_id=1, source_target_pairs={{0,2},{1,3},{2,0},{3,1},{4,6},{5,7},{6,4},{7,5},{8,10},{9,11},{10,... | collective-permute-start | bytes 1179656 | tf_op jit(solution)/shard_map/ppermute | solution.py:869
  485.4 5.2 %collective-permute-start.47 = (f32[32,128]{1,0:T(8,128)S(1)}, f32[32,128]{1,0:T(8,128)S(1)}, u32[]{:S(2)}, u32[]{:S(2)}) collective-permute-start(f32[32,128]{1,0:T(8,128)S(1)} %bitcast_add_fusion.9), channel_id=1, source_target_pairs={{0,16},{4,20},{8,24},{12,28},{16,0},{20,4},{24,8},{28,12},{1,17},{... | collective-permute-start | bytes 49160 | tf_op jit(solution)/shard_map/ppermute | solution.py:869
  496.1 7.9 %collective-permute-start.48 = (f32[128,1536]{1,0:T(8,128)S(1)}, f32[128,1536]{1,0:T(8,128)S(1)}, u32[]{:S(2)}, u32[]{:S(2)}) collective-permute-start(f32[128,1536]{1,0:T(8,128)S(1)} %pad_maximum_fusion.4), channel_id=1, source_target_pairs={{0,1},{1,0},{2,3},{3,2},{4,5},{5,4},{6,7},{7,6},{8,9},{9,8},{10,11... | collective-permute-start | bytes 2359304 | tf_op jit(solution)/shard_map/ppermute | solution.py:869
  500.3 3.7 collective-permute-start.49
  (37 other events, 120.3 us)

commit v5 on v4

--- a/solution.py
+++ b/solution.py
@@ -35,7 +35,7 @@
 TN = (((0,), (0,)), ((), ()))
 
 
-def params(mib=52):
+def params(mib=54):
     return pltpu.CompilerParams(vmem_limit_bytes=mib * 2**20)
 
 
@@ -1076,7 +1076,8 @@
 
         specs += [pl.BlockSpec((tokens, block), place)] * 2
     total = sum(counts)
-    sizes = [rows // 2 * part // sum(parts) for part in parts]
+    sizes = [rows // 2 * part // sum(parts) // 16 * 16 for part in parts[:-1]]
+    sizes = [*sizes, rows // 2 - sum(sizes)]
     outs = [rows // 2, *sizes]
     keep, *sends = pl.pallas_call(
         lambda *refs: outer_kernel(*refs, blocks=counts, pieces=sizes),
@@ -1280,7 +1281,7 @@
         blocks = hidden_gate.shape[1] // 256
         some = blocks * 3 // 11
         blocks = hidden_gate.shape[1] // 256
-        low = blocks * 9 // 11
+        low = blocks * 8 // 11
         orders = ("x", "y", "near", "far"), ("y", "x", "far", "near")
         down_orders = ("near", "x", "y", "far"), ("near", "y", "x", "far")
         firsts = [order[0] for order in orders]
@@ -1290,9 +1291,8 @@
         inners = both(inner_turned)
         two, gate_up = (two[0], two_other), (gate_up[0], gate_up_other)
         out_right = both(out_kept, out_sent)
-        wide_keep, wide_sends = outer([(*two, *gate_up, 0, low)], orders, (1, 2, 2, 2, 1))
-        shift, wide_keep, *wide_sends = together(shift, wide_keep, *wide_sends)
-        down_keep, down_sends = outer([(*inners, *tops, 0, units)], down_orders, (1, 1))
+        wide_keep, wide_sends = outer([(*two, *gate_up, 0, low)], orders, (9, 9, 9, 5))
+        down_keep, down_sends = outer([(*inners, *tops, 0, units)], down_orders, (3, 4))
         rest_keep, rest_sends = outer(
             [
                 (*two, *gate_up, low, blocks - low), (*heads_turned, *out_right, 0, units),
@@ -1300,12 +1300,14 @@
             ],
             orders,
         )
-        work = [(down_keep, *down_sends), (rest_keep, *rest_sends), (), (), ()]
-        moves = [[(send, *firsts)] for send in wide_sends]
+        work = [
+            (wide_keep, *wide_sends), (down_keep, *down_sends), (rest_keep, *rest_sends), (), (),
+        ]
+        moves = [(), *([(send, *firsts)] for send in wide_sends)]
         grad_mine, grad_other, done = carried_back(shift, context, list(zip(moves, work)))
-        down_keep, *down_sends = done[0][1:]
-        rest_keep, *rest_sends = done[1][1:]
-        wide_come = jnp.concatenate([value[0] for value in done], 0)
+        down_keep, *down_sends = done[1][1:]
+        rest_keep, *rest_sends = done[2][1:]
+        wide_come = jnp.concatenate([value[0] for value in done[1:]], 0)
         moves = [(rest_sends[0], *firsts), (down_sends[0], "near")]
         grad_other, *values = together(grad_other, *[move[0] for move in moves])
         comes = [hop(value, *move[1:]) for value, move in zip(values, moves)]

time: 519 us -> 504 us (0.971)
  waiting for transfers between devices: 172 us -> 147 us
  starting transfers between devices: 83.8 us -> 92.1 us
    ppermute x15 -> x14, waiting for transfers between devices: 80.1 us -> 64.7 us  [hop(): return lax.ppermute(value, ('seq', 'doc'), pairs)]
    ppermute x27, waiting for transfers between devices: 73.1 us -> 63.6 us  [hop(): lax.ppermute(value, axis, [(i, i ^ bit) for i in range(lax.axis_size(axis...]
    unnamed x107 -> x79, local copies, waits for them, and re-layouts: 16.9 us -> 10.6 us
    ppermute x27, starting transfers between devices: 40.2 us -> 45.7 us  [hop(): lax.ppermute(value, axis, [(i, i ^ bit) for i in range(lax.axis_size(axis...]
    ppermute x15 -> x14, starting transfers between devices: 28.6 us -> 32.4 us  [hop(): return lax.ppermute(value, ('seq', 'doc'), pairs)]
  transfers between devices with their start and end apart: 50 -> 49, of which waited for: 24 -> 23; matrix products, arithmetic and copies ran while one was open for 7% -> 8% of each run, Pallas kernels for 22% -> 23%
where the time goes in v5:
time: 504 us; the launch traced here: 497 us
  Pallas kernels  165 us (33%)
  waiting for transfers between devices  147 us (29%)
  starting transfers between devices  92.1 us (18%)
  other arithmetic  67.8 us (13%)
  local copies, waits for them, and re-layouts  22.5 us (4%)
    ppermute x14, waiting for transfers between devices, hop(): return lax.ppermute(value, ('seq', 'doc'), pairs)  64.7 us
    ppermute x27, waiting for transfers between devices, hop(): lax.ppermute(value, axis, [(i, i ^ bit) for i in range(lax.axis_size(axis...  63.6 us
    ppermute x27, starting transfers between devices, hop(): lax.ppermute(value, axis, [(i, i ^ bit) for i in range(lax.axis_size(axis...  45.7 us
    pallas_call x4, Pallas kernels, outer(): pl.pallas_call(lambda *refs: outer_kernel(*refs, blocks=counts, pieces=si...  42.8 us
    pallas_call x1, Pallas kernels, back(): pl.pallas_call(back_kernel, grid=(spans,), in_specs=[pl.BlockSpec(memory_...  33.2 us
    ppermute x14, starting transfers between devices, hop(): return lax.ppermute(value, ('seq', 'doc'), pairs)  32.4 us
    pallas_call x1, Pallas kernels, feed(): pl.pallas_call(feed_kernel, grid=(hidden // block,), in_specs=[pl.BlockSp...  27.5 us
    add x11, other arithmetic, chosen(): return total + self.added(self.terms, here) if self.terms else total  22 us
  transfers between devices with their start and end apart: 49, of which 23 were waited for; matrix products, arithmetic and copies ran while one was open for 8% of the time, Pallas kernels for 23%

profile of v5, /device:TPU:0, one launch (start us, length us, event | category | flops | bytes accessed | tf_op | source)
XLA Modules:
  0.0 496.7 jit_solution(382463787319650085)
XLA Ops:
  1.4 4.8 collective-permute-start
  10.8 12.9 %project.1 = (f32[1024,384]{1,0:T(8,128)}, f32[3,6,72,1024]{3,2,1,0:T(8,128)}, f32[3,384,1024]{2,1,0:T(8,128)}, f32[384,1024]{1,0:T(8,128)}, f32[384,8]{1,0:T(8,128)}, /*index=5*/f32[384,8]{1,0:T(8,128)}) custom-call(bf16[384,1024]{1,0:T(8,128)(2,1)} %bitcast.202, f32[16,1024]{1,0:T(8,128)} %copy-done.30, f32[1,1024]{1,0:T(1,128)} %bitcast.236, ...), custom_call_target="tpu_custom_call" | custom-call | flops 1 | bytes 1 | tf_op jit(solution)/shard_map/project/pallas_call | solution.py:216
  25.3 17.2 %prepare.1 = (f32[2,384,1024]{2,1,0:T(8,128)}, f32[6,4,128,128]{3,2,1,0:T(8,128)}, f32[6,4,128,128]{3,2,1,0:T(8,128)}, f32[8,128,256]{2,1,0:T(8,128)}) custom-call(f32[6]{0:T(128)} %fusion.15.keep, f32[3,384,1024]{2,1,0:T(8,128)} %get-tuple-element.153.features, f32[384,8]{1,0:T(8,128)} %get-tuple-element.154.beta), custom_call_target="tpu_custom_call" | custom-call | flops 1 | bytes 1 | tf_op jit(solution)/shard_map/prepare/pallas_call | solution.py:299
  43.8 1.6 collective-permute-start.1
  46.2 11.5 %collective-permute-done.1 = f32[4,128,256]{2,1,0:T(8,128)S(1)} collective-permute-done((f32[4,128,256]{2,1,0:T(8,128)S(1)}, f32[4,128,256]{2,1,0:T(8,128)S(1)}, u32[]{:S(2)}, u32[]{:S(2)}) %collective-permute-start.1) | collective-permute-done | bytes 524320 | tf_op jit(solution)/shard_map/ppermute | solution.py:869
  59.1 3.5 collective-permute-start.4
  62.6 4.9 collective-permute-done.4.refs_3_.refs_2_
  72.1 4.9 collective-permute-done.7.state_other
  77.8 8.6 %mix.1 = (f32[6,8,128,128]{3,2,1,0:T(8,128)}, f32[384,1024]{1,0:T(8,128)}, f32[384,1024]{1,0:T(8,128)}, bf16[384,1024]{1,0:T(8,128)(2,1)}) custom-call(f32[6]{0:T(128)} %fusion.15.keep, s32[1]{0:T(128)} %bitcast.6.refs_0_.place, f32[3,384,1024]{2,1,0:T(8,128)} %get-tuple-element.153.features, f32[2,384,1024]{2,1,0:T(8,128)} %get-tuple-element.155.solved, ...), custom_call_target="tpu_custom_call" | custom-call | flops 1 | bytes 1 | tf_op jit(solution)/shard_map/mix/pallas_call | solution.py:366
  86.4 27.5 %feed.1 = (bf16[384,1024]{1,0:T(8,128)(2,1)}, f32[1024,384]{1,0:T(8,128)}, f32[2816,384]{1,0:T(8,128)}, bf16[384,2816]{1,0:T(8,128)(2,1)}, f32[384,2816]{1,0:T(8...) custom-call(s32[1]{0:T(128)} %bitcast.core, ...), custom_call_target="tpu_custom_call" | custom-call | flops 1 | bytes 1 | tf_op jit(solution)/shard_map/feed/pallas_call | solution.py:462
  114.4 9.7 %gather_states.1 = (f32[384,1024]{1,0:T(8,128)}, f32[384,1024]{1,0:T(8,128)}, bf16[384,1024]{1,0:T(8,128)(2,1)}, f32[384,1024]{1,0:T(8,128)}, f32[1,128]{1,0:T(1,128)}, /*index=5*/f32[8,128,128]{2,1,0:T(8,128)}) custom-call(f32[6]{0:T(128)} %fusion.15.keep, s32[1]{0:T(128)} %bitcast.core, f32[384,1024]{1,0:T(8,128)} %get-tuple-element.166.grad_head, ...), custom_call_target="tpu_custom_call" | custom-call | flops 1 | bytes 1 | tf_op jit(solution)/shard_map/gather_states/pallas_call | solution.py:564
  124.3 2.1 slice_select_fusion.6
  128.6 10.9 %outer.4 = (f32[512,2048]{1,0:T(8,128)}, f32[144,2048]{1,0:T(8,128)}, f32[144,2048]{1,0:T(8,128)}, f32[144,2048]{1,0:T(8,128)}, f32[80,2048]{1,0:T(8,128)}) custom-call(s32[16]{0:T(128)} %stack.152.refs_0_, f32[1024,384]{1,0:T(8,128)} %get-tuple-element.165.refs_1_, f32[1024,384]{1,0:T(8,128)} %copy-done.9, ...), custom_call_target="tpu_custom_call" | custom-call | flops 1 | bytes 1 | tf_op jit(solution)/shard_map/outer/pallas_call | solution.py:1082
  143.3 8.6 %outer.5 = (f32[1408,512]{1,0:T(8,128)}, f32[592,512]{1,0:T(8,128)}, f32[816,512]{1,0:T(8,128)}) custom-call(s32[16]{0:T(128)} %stack.169.refs_0_, f32[2816,384]{1,0:T(8,128)} %get-tuple-element.184.refs_1_, f32[2816,384]{1,0:T(8,128)} %collective-permute-done.13.refs_2_, bf16[384,512]{1,0:T(8,128)(2,1)} %slice_select_fusion.5.refs_3_, f32[384,512]{1,0:T(8,128)} %copy-done.25), custom_call_target="tpu_custom_call" | custom-call | flops 1 | bytes 1 | tf_op jit(solution)/shard_map/outer/pallas_call | solution.py:1082
  151.9 5.4 %collective-permute-done.12 = f32[144,2048]{1,0:T(8,128)S(1)} collective-permute-done((f32[144,2048]{1,0:T(8,128)}, f32[144,2048]{1,0:T(8,128)S(1)}, u32[]{:S(2)}, u32[]{:S(2)}) %collective-permute-start.12) | collective-permute-done | bytes 1179680 | tf_op jit(solution)/shard_map/ppermute | solution.py:873
  158.8 12.8 %outer.6 = (f32[512,1792]{1,0:T(8,128)}, f32[512,1792]{1,0:T(8,128)}) custom-call(s32[16]{0:T(128)} %stack.152.refs_0_, f32[1024,384]{1,0:T(8,128)} %get-tuple-element.165.refs_1_, f32[1024,384]{1,0:T(8,128)} %copy-done.9, f32[1024,384]{1,0:T(8,128)} %get-tuple-element.194.refs_3_, f32[1024,384]{1,0:T(8,128)} %collective-permute-done.16.refs_4_, ...), custom_call_target="tpu_custom_call" | custom-call | flops 1 | bytes 1 | tf_op jit(solution)/shard_map/outer/pallas_call | solution.py:1082
  171.7 2.2 collective-permute-done.15
  176.2 12.3 %collective-permute-done.18.refs_4_ = f32[4,128,128]{2,1,0:T(8,128)S(1)} collective-permute-done((f32[4,128,128]{2,1,0:T(8,128)S(1)}, f32[4,128,128]{2,1,0:T(8,128)S(1)}, u32[]{:S(2)}, u32[]{:S(2)}) %collective-permute-start.18) | collective-permute-done | bytes 262176 | tf_op jit(solution)/shard_map/ppermute | solution.py:1010
  188.5 1.9 collective-permute-done.19
  193.6 11.7 %collective-permute-done.20.state_other = f32[4,128,128]{2,1,0:T(8,128)S(1)} collective-permute-done((f32[4,128,128]{2,1,0:T(8,128)S(1)}, f32[4,128,128]{2,1,0:T(8,128)S(1)}, u32[]{:S(2)}, u32[]{:S(2)}) %collective-permute-start.20) | collective-permute-done | bytes 262176 | tf_op jit(solution)/shard_map/ppermute | solution.py:869
  205.8 7.2 %collective-permute-start.23 = (f32[592,512]{1,0:T(8,128)}, f32[592,512]{1,0:T(8,128)S(1)}, u32[]{:S(2)}, u32[]{:S(2)}) collective-permute-start(f32[592,512]{1,0:T(8,128)} %get-tuple-element.225), channel_id=1, source_target_pairs={{0,8},{4,12},{8,0},{12,4},{16,24},{20,28},{24,16},{28,20},{1,9},{5... | collective-permute-start | bytes 3637256 | tf_op jit(solution)/shard_map/ppermute | solution.py:869
  213.0 33.2 %back.1 = (f32[3,384,1024]{2,1,0:T(8,128)}, f32[3,8,1024]{2,1,0:T(8,128)}, f32[3,4,1024]{2,1,0:T(4,128)}, f32[384,8]{1,0:T(8,128)}) custom-call(f32[6]{0:T(128)} %fusion.15.keep, s32[1]{0:T(128)} %bitcast.6.refs_0_.place, f32[3,384,1024]{2,1,0:T(8,128)} %get-tuple-element.153.features, f32[384,8]{1,0:T(8,128)} %get-tuple-element.154.beta, ...), custom_call_target="tpu_custom_call" | custom-call | flops 1 | bytes 1 | tf_op jit(solution)/shard_map/back/pallas_call | solution.py:767
  246.6 3.3 copy-done.10
  252.5 1.9 add_bitcast_fusion.1
  254.4 2.2 pad_maximum_fusion.1
  256.6 2.0 collective-permute-done.24
  260.3 5.7 %collective-permute-start.28 = (f32[816,512]{1,0:T(8,128)}, f32[816,512]{1,0:T(8,128)}, u32[]{:S(2)}, u32[]{:S(2)}) collective-permute-start(f32[816,512]{1,0:T(8,128)} %get-tuple-element.233), channel_id=1, source_target_pairs={{0,8},{4,12},{8,0},{12,4},{16,24},{20,28},{24,16},{28,20},{1,9},{5... | collective-permute-start | bytes 5013512 | tf_op jit(solution)/shard_map/ppermute | solution.py:869
  266.5 1.6 fusion
  271.3 1.7 add_bitcast_fusion.4
  273.0 1.6 add_bitcast_fusion.5
  277.2 10.4 %outer.7 = (f32[512,1536]{1,0:T(8,128)}, f32[512,1536]{1,0:T(8,128)}) custom-call(s32[16]{0:T(128)} %stack.152.refs_0_, f32[1024,384]{1,0:T(8,128)} %get-tuple-element.195.refs_5_.refs_1_.refs_3_, f32[1024,384]{1,0:T(8,128)} %collective-permute-done.3.refs_6_.refs_2_.refs_4_, f32[1024,384]{1,0:T(8,128)} %get-tuple-element.195.refs_5_.refs_1_.refs_3_, ...), custom_call_target="tpu_custom_call" | custom-call | flops 1 | bytes 1 | tf_op jit(solution)/shard_map/outer/pallas_call | solution.py:1082
  287.6 9.6 %collective-permute-done.28 = f32[816,512]{1,0:T(8,128)} collective-permute-done((f32[816,512]{1,0:T(8,128)}, f32[816,512]{1,0:T(8,128)}, u32[]{:S(2)}, u32[]{:S(2)}) %collective-permute-start.28) | collective-permute-done | bytes 1671200 | tf_op jit(solution)/shard_map/ppermute | solution.py:869
  297.2 7.8 %collective-permute-done.27 = f32[2,2,64,3840]{3,2,1,0:T(8,128)} collective-permute-done((f32[2,2,64,3840]{3,2,1,0:T(8,128)}, f32[2,2,64,3840]{3,2,1,0:T(8,128)}, u32[]{:S(2)}, u32[]{:S(2)}) %collective-permute-start.27) | collective-permute-done | bytes 3932192 | tf_op jit(solution)/shard_map/ppermute | solution.py:873
  305.1 1.7 pad_maximum_fusion.2
  306.8 4.1 maximum_add_fusion
  312.3 4.3 collective-permute-start.31
  316.6 6.7 %collective-permute-start.29 = (f32[2,64,3840]{2,1,0:T(8,128)}, f32[2,64,3840]{2,1,0:T(8,128)}, u32[]{:S(2)}, u32[]{:S(2)}) collective-permute-start(f32[2,64,3840]{2,1,0:T(8,128)} %maximum_add_fusion), channel_id=1, source_target_pairs={{0,8},{1,17},{2,10},{3,19},{4,12},{5,21},{6,14},{7,23},{8,0},{9,25... | collective-permute-start | bytes 5898248 | tf_op jit(solution)/shard_map/ppermute | solution.py:873
  325.9 2.4 add_bitcast_fusion.6
  328.4 2.4 add_bitcast_fusion.8
  330.8 10.5 %enter.1 = (bf16[384,1024]{1,0:T(8,128)(2,1)}, f32[1,1024]{1,0:T(1,128)}) custom-call(bf16[384,1024]{1,0:T(8,128)(2,1)} %bitcast.204, f32[1,1024]{1,0:T(1,128)} %bitcast.237, f32[384,1024]{1,0:T(8,128)} %get-tuple-element.242.grad_hidden, bf16[3,384,1024]{2,1,0:T(8,128)(2,1)} %copy-done.2, f32[384,1024]{1,0:T(8,128)} %get-tuple-element.244.grad_gate, ...), custom_call_target="tpu_custom_call" | custom-call | flops 1 | bytes 1 | tf_op jit(solution)/shard_map/enter/pallas_call | solution.py:830
  343.8 23.8 %collective-permute-done.30 = f32[2,2,176,512]{3,2,1,0:T(8,128)} collective-permute-done((f32[2,2,176,512]{3,2,1,0:T(8,128)}, f32[2,2,176,512]{3,2,1,0:T(8,128)}, u32[]{:S(2)}, u32[]{:S(2)}) %collective-permute-start.30) | collective-permute-done | bytes 1441824 | tf_op jit(solution)/shard_map/ppermute | solution.py:873
  367.6 2.4 bitcast_add_fusion.3
  370.1 3.3 add_bitcast_fusion.2
  373.4 2.6 maximum_add_fusion.1
  377.2 9.8 %collective-permute-start.33 = (f32[64,3840]{1,0:T(8,128)}, f32[64,3840]{1,0:T(8,128)}, u32[]{:S(2)}, u32[]{:S(2)}) collective-permute-start(f32[64,3840]{1,0:T(8,128)} %maximum_add_fusion.1), channel_id=1, source_target_pairs={{0,16},{1,9},{2,18},{3,11},{4,20},{5,13},{6,22},{7,15},{8,24},{9,1... | collective-permute-start | bytes 2949128 | tf_op jit(solution)/shard_map/ppermute | solution.py:873
  389.1 15.3 %collective-permute-done.34 = f32[2,176,512]{2,1,0:T(8,128)} collective-permute-done((f32[2,176,512]{2,1,0:T(8,128)}, f32[2,176,512]{2,1,0:T(8,128)}, u32[]{:S(2)}, u32[]{:S(2)}) %collective-permute-start.34) | collective-permute-done | bytes 720928 | tf_op jit(solution)/shard_map/ppermute | solution.py:873
  404.4 5.4 %collective-permute-done.33 = f32[64,3840]{1,0:T(8,128)} collective-permute-done((f32[64,3840]{1,0:T(8,128)}, f32[64,3840]{1,0:T(8,128)}, u32[]{:S(2)}, u32[]{:S(2)}) %collective-permute-start.33) | collective-permute-done | bytes 983072 | tf_op jit(solution)/shard_map/ppermute | solution.py:873
  410.0 2.7 bitcast_add_fusion.2
  412.7 2.1 fusion.10
  414.7 3.0 maximum_add_fusion.2
  418.5 1.7 collective-permute-start.36
  420.2 5.5 %collective-permute-start.37 = (f32[176,512]{1,0:T(8,128)}, f32[176,512]{1,0:T(8,128)S(1)}, u32[]{:S(2)}, u32[]{:S(2)}) collective-permute-start(f32[176,512]{1,0:T(8,128)} %fusion.10), channel_id=1, source_target_pairs={{0,16},{4,20},{8,24},{12,28},{16,0},{20,4},{24,8},{28,12},{1,17},{... | collective-permute-start | bytes 1081352 | tf_op jit(solution)/shard_map/ppermute | solution.py:869
  426.3 3.7 collective-permute-done.39
  430.0 7.4 %collective-permute-done.37 = f32[176,512]{1,0:T(8,128)S(1)} collective-permute-done((f32[176,512]{1,0:T(8,128)}, f32[176,512]{1,0:T(8,128)S(1)}, u32[]{:S(2)}, u32[]{:S(2)}) %collective-permute-start.37) | collective-permute-done | bytes 360480 | tf_op jit(solution)/shard_map/ppermute | solution.py:869
  437.4 1.9 collective-permute-done.36
  439.3 2.2 fusion.7
  442.9 1.6 broadcast_select_fusion.3
  446.0 7.0 %collective-permute-start.42 = (f32[128,3840]{1,0:T(8,128)}, f32[128,3840]{1,0:T(8,128)}, u32[]{:S(2)}, u32[]{:S(2)}) collective-permute-start(f32[128,3840]{1,0:T(8,128)} %pad_maximum_fusion.3), channel_id=1, source_target_pairs={{0,1},{1,0},{2,3},{3,2},{4,5},{5,4},{6,7},{7,6},{8,9},{9,8},{10,11... | collective-permute-start | bytes 5898248 | tf_op jit(solution)/shard_map/ppermute | solution.py:869
  453.0 3.9 collective-permute-start.40
  457.9 2.5 collective-permute-start.43
  460.4 3.4 collective-permute-done.43
  466.9 4.8 collective-permute-start.46
  472.7 1.8 broadcast_select_fusion.1
  474.5 7.9 %collective-permute-done.44 = f32[64,1536]{1,0:T(8,128)S(1)} collective-permute-done((f32[64,1536]{1,0:T(8,128)S(1)}, f32[64,1536]{1,0:T(8,128)S(1)}, u32[]{:S(2)}, u32[]{:S(2)}) %collective-permute-start.44) | collective-permute-done | bytes 393248 | tf_op jit(solution)/shard_map/ppermute | solution.py:869
  (227 shorter events, 73.4 us)
Async XLA Ops:
  1.4 8.8 %collective-permute-start = (f32[16,1024]{1,0:T(8,128)S(1)}, f32[16,1024]{1,0:T(8,128)S(1)}, u32[]{:S(2)}, u32[]{:S(2)}) collective-permute-start(f32[16,1024]{1,0:T(8,128)S(1)} %bitcast_convert_fusion), channel_id=1, source_target_pairs={{0,4},{4,8},{8,12},{12,16},{16,20},{20,24},{24,28},{1,5},{5,9},{9,... | collective-permute-start | bytes 196616 | tf_op jit(solution)/shard_map/ppermute | solution.py:856
  23.7 35.0 %collective-permute-start.3 = (f32[1024,384]{1,0:T(8,128)}, f32[1024,384]{1,0:T(8,128)}, u32[]{:S(2)}, u32[]{:S(2)}) collective-permute-start(f32[1024,384]{1,0:T(8,128)} %get-tuple-element.195.refs_5_.refs_1_.refs_3_), channel_id=1, source_target_pairs={{0,1},{1,0},{2,3},{3,2},{4,5},{5,4},{6,7},{7,6},{8,9},{9,8},{10,11... | collective-permute-start | bytes 4718600 | tf_op jit(solution)/shard_map/ppermute | solution.py:869
  24.1 33.7 %collective-permute-start.2 = (f32[384,512]{1,0:T(8,128)S(1)}, f32[384,512]{1,0:T(8,128)S(1)}, u32[]{:S(2)}, u32[]{:S(2)}) collective-permute-start(f32[384,512]{1,0:T(8,128)S(1)} %slice_select_fusion.2), channel_id=1, source_target_pairs={{0,1},{1,0},{2,3},{3,2},{4,5},{5,4},{6,7},{7,6},{8,9},{9,8},{10,11... | collective-permute-start | bytes 2359304 | tf_op jit(solution)/shard_map/ppermute | solution.py:869
  42.5 16.2 %copy-start.11 = (f32[8,128,256]{2,1,0:T(8,128)S(1)}, f32[8,128,256]{2,1,0:T(8,128)}, u32[]{:S(2)}) copy-start(f32[8,128,256]{2,1,0:T(8,128)} %get-tuple-element.158) | copy-start | bytes 3145732
  43.8 13.9 %collective-permute-start.1 = (f32[4,128,256]{2,1,0:T(8,128)S(1)}, f32[4,128,256]{2,1,0:T(8,128)S(1)}, u32[]{:S(2)}, u32[]{:S(2)}) collective-permute-start(f32[4,128,256]{2,1,0:T(8,128)S(1)} %slice_select_fusion.3), channel_id=1, source_target_pairs={{0,4},{4,0},{8,12},{12,8},{16,20},{20,16},{24,28},{28,24},{1,5},{5... | collective-permute-start | bytes 1572872 | tf_op jit(solution)/shard_map/ppermute | solution.py:869
  59.1 8.4 %collective-permute-start.4 = (f32[4,128,128]{2,1,0:T(8,128)S(1)}, f32[4,128,128]{2,1,0:T(8,128)S(1)}, u32[]{:S(2)}, u32[]{:S(2)}) collective-permute-start(f32[4,128,128]{2,1,0:T(8,128)S(1)} %slice.155), channel_id=1, source_target_pairs={{0,8},{4,12},{1,9},{5,13},{2,10},{6,14},{3,11},{7,15}} | collective-permute-start | bytes 786440 | tf_op jit(solution)/shard_map/ppermute | solution.py:964
  67.8 0.7 collective-permute-start.5
  68.7 0.9 collective-permute-start.6
  70.6 6.5 %collective-permute-start.7 = (f32[4,128,128]{2,1,0:T(8,128)S(1)}, f32[4,128,128]{2,1,0:T(8,128)S(1)}, u32[]{:S(2)}, u32[]{:S(2)}) collective-permute-start(f32[4,128,128]{2,1,0:T(8,128)S(1)} %get-tuple-element.162), channel_id=1, source_target_pairs={{0,4},{4,0},{8,12},{12,8},{16,20},{20,16},{24,28},{28,24},{1,5},{5... | collective-permute-start | bytes 786440 | tf_op jit(solution)/shard_map/ppermute | solution.py:869
  113.9 10.3 %collective-permute-start.9 = (f32[384,2816]{1,0:T(8,128)}, f32[384,2816]{1,0:T(8,128)}, u32[]{:S(2)}, u32[]{:S(2)}) collective-permute-start(f32[384,2816]{1,0:T(8,128)} %get-tuple-element.170), channel_id=1, source_target_pairs={{0,1},{1,0},{2,3},{3,2},{4,5},{5,4},{6,7},{7,6},{8,9},{9,8},{10,11... | collective-permute-start | bytes 12976136 | tf_op jit(solution)/shard_map/ppermute | solution.py:869
  113.9 10.2 %collective-permute-start.8 = (f32[1024,384]{1,0:T(8,128)}, f32[1024,384]{1,0:T(8,128)S(1)}, u32[]{:S(2)}, u32[]{:S(2)}) collective-permute-start(f32[1024,384]{1,0:T(8,128)} %get-tuple-element.165.refs_1_), channel_id=1, source_target_pairs={{0,1},{1,0},{2,3},{3,2},{4,5},{5,4},{6,7},{7,6},{8,9},{9,8},{10,11... | collective-permute-start | bytes 4718600 | tf_op jit(solution)/shard_map/ppermute | solution.py:869
  124.1 19.2 %collective-permute-start.13 = (f32[2816,384]{1,0:T(8,128)}, f32[2816,384]{1,0:T(8,128)}, u32[]{:S(2)}, u32[]{:S(2)}) collective-permute-start(f32[2816,384]{1,0:T(8,128)} %get-tuple-element.184.refs_1_), channel_id=1, source_target_pairs={{0,1},{1,0},{2,3},{3,2},{4,5},{5,4},{6,7},{7,6},{8,9},{9,8},{10,11... | collective-permute-start | bytes 12976136 | tf_op jit(solution)/shard_map/ppermute | solution.py:869
  126.4 13.1 %collective-permute-start.10 = (f32[4,128,128]{2,1,0:T(8,128)}, f32[4,128,128]{2,1,0:T(8,128)}, u32[]{:S(2)}, u32[]{:S(2)}) collective-permute-start(f32[4,128,128]{2,1,0:T(8,128)} %slice_select_fusion.6), channel_id=1, source_target_pairs={{0,4},{4,0},{8,12},{12,8},{16,20},{20,16},{24,28},{28,24},{1,5},{5... | collective-permute-start | bytes 786440 | tf_op jit(solution)/shard_map/ppermute | solution.py:869
  140.8 16.5 %collective-permute-start.12 = (f32[144,2048]{1,0:T(8,128)}, f32[144,2048]{1,0:T(8,128)S(1)}, u32[]{:S(2)}, u32[]{:S(2)}) collective-permute-start(f32[144,2048]{1,0:T(8,128)} %get-tuple-element.183), channel_id=1, source_target_pairs={{0,4},{1,3},{2,6},{3,1},{4,0},{5,7},{6,2},{7,5},{8,12},{9,11},{10,... | collective-permute-start | bytes 3538952 | tf_op jit(solution)/shard_map/ppermute | solution.py:873
  141.4 17.5 %collective-permute-start.16 = (f32[1024,384]{1,0:T(8,128)}, f32[1024,384]{1,0:T(8,128)}, u32[]{:S(2)}, u32[]{:S(2)}) collective-permute-start(f32[1024,384]{1,0:T(8,128)} %get-tuple-element.194.refs_3_), channel_id=1, source_target_pairs={{0,1},{1,0},{2,3},{3,2},{4,5},{5,4},{6,7},{7,6},{8,9},{9,8},{10,11... | collective-permute-start | bytes 4718600 | tf_op jit(solution)/shard_map/ppermute | solution.py:869
  141.9 16.9 %collective-permute-start.17 = (f32[384,1024]{1,0:T(8,128)}, f32[384,1024]{1,0:T(8,128)}, u32[]{:S(2)}, u32[]{:S(2)}) collective-permute-start(f32[384,1024]{1,0:T(8,128)} %get-tuple-element.198), channel_id=1, source_target_pairs={{0,1},{1,0},{2,3},{3,2},{4,5},{5,4},{6,7},{7,6},{8,9},{9,8},{10,11... | collective-permute-start | bytes 4718600 | tf_op jit(solution)/shard_map/ppermute | solution.py:869
  141.9 10.0 %collective-permute-start.11 = (f32[4,128,128]{2,1,0:T(8,128)S(1)}, f32[4,128,128]{2,1,0:T(8,128)S(1)}, u32[]{:S(2)}, u32[]{:S(2)}) collective-permute-start(f32[4,128,128]{2,1,0:T(8,128)S(1)} %apply_map.9.refs_0_), channel_id=1, source_target_pairs={{24,16},{28,20},{25,17},{29,21},{26,18},{30,22},{27,19},{31,23}} | collective-permute-start | bytes 786440 | tf_op jit(solution)/shard_map/ppermute | solution.py:1010
  143.3 14.3 %copy-start.33 = (f32[144,2048]{1,0:T(8,128)S(1)}, f32[144,2048]{1,0:T(8,128)}, u32[]{:S(2)}) copy-start(f32[144,2048]{1,0:T(8,128)} %get-tuple-element.193) | copy-start | bytes 3538948
  157.6 16.3 %collective-permute-start.15 = (f32[144,2048]{1,0:T(8,128)S(1)}, f32[144,2048]{1,0:T(8,128)S(1)}, u32[]{:S(2)}, u32[]{:S(2)}) collective-permute-start(f32[144,2048]{1,0:T(8,128)S(1)} %copy-done.33), channel_id=1, source_target_pairs={{0,4},{1,3},{2,6},{3,1},{4,0},{5,7},{6,2},{7,5},{8,12},{9,11},{10,... | collective-permute-start | bytes 3538952 | tf_op jit(solution)/shard_map/ppermute | solution.py:873
  158.1 13.6 %collective-permute-start.14 = (f32[4,128,128]{2,1,0:T(8,128)S(1)}, f32[4,128,128]{2,1,0:T(8,128)S(1)}, u32[]{:S(2)}, u32[]{:S(2)}) collective-permute-start(f32[4,128,128]{2,1,0:T(8,128)S(1)} %apply_map.10), channel_id=1, source_target_pairs={{16,8},{20,12},{17,9},{21,13},{18,10},{22,14},{19,11},{23,15}} | collective-permute-start | bytes 786440 | tf_op jit(solution)/shard_map/ppermute | solution.py:1010
  158.8 15.3 %copy-start.32 = (f32[144,2048]{1,0:T(8,128)S(1)}, f32[144,2048]{1,0:T(8,128)}, u32[]{:S(2)}) copy-start(f32[144,2048]{1,0:T(8,128)} %get-tuple-element.204) | copy-start | bytes 3538948
  171.7 19.8 %copy-start.34 = (f32[80,2048]{1,0:T(8,128)S(1)}, f32[80,2048]{1,0:T(8,128)}, u32[]{:S(2)}) copy-start(f32[80,2048]{1,0:T(8,128)} %get-tuple-element.209) | copy-start | bytes 1966084
  173.9 31.4 %copy-start.20 = (f32[144,2048]{1,0:T(8,128)}, f32[144,2048]{1,0:T(8,128)S(1)}, u32[]{:S(2)}) copy-start(f32[144,2048]{1,0:T(8,128)S(1)} %collective-permute-done.15) | copy-start | bytes 3538948
  174.2 16.3 %collective-permute-start.19 = (f32[144,2048]{1,0:T(8,128)S(1)}, f32[144,2048]{1,0:T(8,128)S(1)}, u32[]{:S(2)}, u32[]{:S(2)}) collective-permute-start(f32[144,2048]{1,0:T(8,128)S(1)} %copy-done.32), channel_id=1, source_target_pairs={{0,4},{1,3},{2,6},{3,1},{4,0},{5,7},{6,2},{7,5},{8,12},{9,11},{10,... | collective-permute-start | bytes 3538952 | tf_op jit(solution)/shard_map/ppermute | solution.py:873
  174.7 13.8 %collective-permute-start.18 = (f32[4,128,128]{2,1,0:T(8,128)S(1)}, f32[4,128,128]{2,1,0:T(8,128)S(1)}, u32[]{:S(2)}, u32[]{:S(2)}) collective-permute-start(f32[4,128,128]{2,1,0:T(8,128)S(1)} %apply_map.11), channel_id=1, source_target_pairs={{8,0},{12,4},{9,1},{13,5},{10,2},{14,6},{11,3},{15,7}} | collective-permute-start | bytes 786440 | tf_op jit(solution)/shard_map/ppermute | solution.py:1010
  190.4 15.3 %copy-start.22 = (f32[144,2048]{1,0:T(8,128)}, f32[144,2048]{1,0:T(8,128)S(1)}, u32[]{:S(2)}) copy-start(f32[144,2048]{1,0:T(8,128)S(1)} %collective-permute-done.19) | copy-start | bytes 3538948
  191.5 13.7 %collective-permute-start.21 = (f32[80,2048]{1,0:T(8,128)S(1)}, f32[80,2048]{1,0:T(8,128)S(1)}, u32[]{:S(2)}, u32[]{:S(2)}) collective-permute-start(f32[80,2048]{1,0:T(8,128)S(1)} %copy-done.34), channel_id=1, source_target_pairs={{0,4},{1,3},{2,6},{3,1},{4,0},{5,7},{6,2},{7,5},{8,12},{9,11},{10,... | collective-permute-start | bytes 1966088 | tf_op jit(solution)/shard_map/ppermute | solution.py:873
  192.0 13.2 %collective-permute-start.20 = (f32[4,128,128]{2,1,0:T(8,128)S(1)}, f32[4,128,128]{2,1,0:T(8,128)S(1)}, u32[]{:S(2)}, u32[]{:S(2)}) collective-permute-start(f32[4,128,128]{2,1,0:T(8,128)S(1)} %get-tuple-element.208), channel_id=1, source_target_pairs={{0,4},{4,0},{8,12},{12,8},{16,20},{20,16},{24,28},{28,24},{1,5},{5... | collective-permute-start | bytes 786440 | tf_op jit(solution)/shard_map/ppermute | solution.py:869
  205.2 45.0 %collective-permute-start.22 = (f32[512,1792]{1,0:T(8,128)}, f32[512,1792]{1,0:T(8,128)}, u32[]{:S(2)}, u32[]{:S(2)}) collective-permute-start(f32[512,1792]{1,0:T(8,128)} %get-tuple-element.224), channel_id=1, source_target_pairs={{0,4},{1,3},{2,6},{3,1},{4,0},{5,7},{6,2},{7,5},{8,12},{9,11},{10,... | collective-permute-start | bytes 11010056 | tf_op jit(solution)/shard_map/ppermute | solution.py:873
  205.8 44.5 %collective-permute-start.23 = (f32[592,512]{1,0:T(8,128)}, f32[592,512]{1,0:T(8,128)S(1)}, u32[]{:S(2)}, u32[]{:S(2)}) collective-permute-start(f32[592,512]{1,0:T(8,128)} %get-tuple-element.225), channel_id=1, source_target_pairs={{0,8},{4,12},{8,0},{12,4},{16,24},{20,28},{24,16},{28,20},{1,9},{5... | collective-permute-start | bytes 3637256 | tf_op jit(solution)/shard_map/ppermute | solution.py:869
  213.0 33.2 %copy-start.21 = (f32[144,2048]{1,0:T(8,128)S(1)}, f32[144,2048]{1,0:T(8,128)}, u32[]{:S(2)}) copy-start(f32[144,2048]{1,0:T(8,128)} %copy-done.20) | copy-start | bytes 3538948
  213.0 33.2 %copy-start.23 = (f32[144,2048]{1,0:T(8,128)S(1)}, f32[144,2048]{1,0:T(8,128)}, u32[]{:S(2)}) copy-start(f32[144,2048]{1,0:T(8,128)} %copy-done.22) | copy-start | bytes 3538948
  250.8 7.7 %collective-permute-start.24 = (f32[3,8,1024]{2,1,0:T(8,128)S(1)}, f32[3,8,1024]{2,1,0:T(8,128)S(1)}, u32[]{:S(2)}, u32[]{:S(2)}) collective-permute-start(f32[3,8,1024]{2,1,0:T(8,128)S(1)} %copy-done.35), channel_id=1, source_target_pairs={{4,0},{8,4},{12,8},{16,12},{20,16},{24,20},{28,24},{5,1},{9,5},{13... | collective-permute-start | bytes 294920 | tf_op jit(solution)/shard_map/ppermute | solution.py:856
  259.0 16.4 %copy-start.2 = (bf16[3,384,1024]{2,1,0:T(8,128)(2,1)}, bf16[3,384,1024]{2,1,0:T(8,128)(2,1)S(1)}, u32[]{:S(2)}) copy-start(bf16[3,384,1024]{2,1,0:T(8,128)(2,1)S(1)} %convert_element_type.43.grads) | copy-start | bytes 7077892
  259.0 46.1 %collective-permute-start.27 = (f32[2,2,64,3840]{3,2,1,0:T(8,128)}, f32[2,2,64,3840]{3,2,1,0:T(8,128)}, u32[]{:S(2)}, u32[]{:S(2)}) collective-permute-start(f32[2,2,64,3840]{3,2,1,0:T(8,128)} %pad_maximum_fusion.1), channel_id=1, source_target_pairs={{0,2},{1,5},{2,0},{3,7},{4,6},{5,1},{6,4},{7,3},{8,10},{9,13},{10,... | collective-permute-start | bytes 11796488 | tf_op jit(solution)/shard_map/ppermute | solution.py:873
  260.3 37.0 %collective-permute-start.28 = (f32[816,512]{1,0:T(8,128)}, f32[816,512]{1,0:T(8,128)}, u32[]{:S(2)}, u32[]{:S(2)}) collective-permute-start(f32[816,512]{1,0:T(8,128)} %get-tuple-element.233), channel_id=1, source_target_pairs={{0,8},{4,12},{8,0},{12,4},{16,24},{20,28},{24,16},{28,20},{1,9},{5... | collective-permute-start | bytes 5013512 | tf_op jit(solution)/shard_map/ppermute | solution.py:869
  269.2 7.1 %collective-permute-start.25 = (f32[384,1024]{1,0:T(8,128)}, f32[384,1024]{1,0:T(8,128)}, u32[]{:S(2)}, u32[]{:S(2)}) collective-permute-start(f32[384,1024]{1,0:T(8,128)} %fusion), channel_id=1, source_target_pairs={{0,1},{1,0},{2,3},{3,2},{4,5},{5,4},{6,7},{7,6},{8,9},{9,8},{10,11... | collective-permute-start | bytes 4718600 | tf_op jit(solution)/shard_map/ppermute | solution.py:869
  270.7 5.6 %collective-permute-start.26 = (f32[384,512]{1,0:T(8,128)S(1)}, f32[384,512]{1,0:T(8,128)S(1)}, u32[]{:S(2)}, u32[]{:S(2)}) collective-permute-start(f32[384,512]{1,0:T(8,128)S(1)} %fusion.2), channel_id=1, source_target_pairs={{0,1},{1,0},{2,3},{3,2},{4,5},{5,4},{6,7},{7,6},{8,9},{9,8},{10,11... | collective-permute-start | bytes 2359304 | tf_op jit(solution)/shard_map/ppermute | solution.py:869
  276.3 28.8 %copy-start.19 = (f32[592,512]{1,0:T(8,128)S(1)}, f32[592,512]{1,0:T(8,128)}, u32[]{:S(2)}) copy-start(f32[592,512]{1,0:T(8,128)} %copy-done.18) | copy-start | bytes 3637252
  310.9 13.0 %copy-start.36 = (f32[1,128]{1,0:T(1,128)S(1)}, f32[1,128]{1,0:T(1,128)}, u32[]{:S(2)}) copy-start(f32[1,128]{1,0:T(1,128)} %get-tuple-element.248) | copy-start | bytes 1540
  310.9 13.7 %copy-start.31 = (f32[3,4,1024]{2,1,0:T(4,128)S(1)}, f32[3,4,1024]{2,1,0:T(4,128)}, u32[]{:S(2)}) copy-start(f32[3,4,1024]{2,1,0:T(4,128)} %get-tuple-element.247) | copy-start | bytes 147460
  310.9 13.8 %copy-start.3 = (f32[1024,384]{1,0:T(8,128)S(1)}, f32[1024,384]{1,0:T(8,128)}, u32[]{:S(2)}) copy-start(f32[1024,384]{1,0:T(8,128)} %get-tuple-element.195.refs_5_.refs_1_.refs_3_) | copy-start | bytes 4718596
  310.9 13.8 %copy-start.24 = (f32[384,8]{1,0:T(8,128)S(1)}, f32[384,8]{1,0:T(8,128)}, u32[]{:S(2)}) copy-start(f32[384,8]{1,0:T(8,128)} %get-tuple-element.245.grad_beta) | copy-start | bytes 36868
  312.3 55.3 %collective-permute-start.31 = (f32[512,1536]{1,0:T(8,128)}, f32[512,1536]{1,0:T(8,128)}, u32[]{:S(2)}, u32[]{:S(2)}) collective-permute-start(f32[512,1536]{1,0:T(8,128)} %get-tuple-element.241), channel_id=1, source_target_pairs={{0,4},{1,3},{2,6},{3,1},{4,0},{5,7},{6,2},{7,5},{8,12},{9,11},{10,... | collective-permute-start | bytes 9437192 | tf_op jit(solution)/shard_map/ppermute | solution.py:873
  316.6 51.0 %collective-permute-start.29 = (f32[2,64,3840]{2,1,0:T(8,128)}, f32[2,64,3840]{2,1,0:T(8,128)}, u32[]{:S(2)}, u32[]{:S(2)}) collective-permute-start(f32[2,64,3840]{2,1,0:T(8,128)} %maximum_add_fusion), channel_id=1, source_target_pairs={{0,8},{1,17},{2,10},{3,19},{4,12},{5,21},{6,14},{7,23},{8,0},{9,25... | collective-permute-start | bytes 5898248 | tf_op jit(solution)/shard_map/ppermute | solution.py:873
  323.4 44.3 %collective-permute-start.30 = (f32[2,2,176,512]{3,2,1,0:T(8,128)}, f32[2,2,176,512]{3,2,1,0:T(8,128)}, u32[]{:S(2)}, u32[]{:S(2)}) collective-permute-start(f32[2,2,176,512]{3,2,1,0:T(8,128)} %add_bitcast_fusion.3), channel_id=1, source_target_pairs={{0,4},{1,3},{2,6},{3,1},{4,0},{5,7},{6,2},{7,5},{8,12},{9,11},{10,... | collective-permute-start | bytes 4325384 | tf_op jit(solution)/shard_map/ppermute | solution.py:873
  330.8 36.8 %copy-start.7 = (f32[1408,512]{1,0:T(8,128)S(1)}, f32[1408,512]{1,0:T(8,128)}, u32[]{:S(2)}) copy-start(f32[1408,512]{1,0:T(8,128)} %copy-done.6) | copy-start | bytes 8650756
  376.0 33.9 %collective-permute-start.32 = (f32[2,2,64,1536]{3,2,1,0:T(8,128)}, f32[2,2,64,1536]{3,2,1,0:T(8,128)}, u32[]{:S(2)}, u32[]{:S(2)}) collective-permute-start(f32[2,2,64,1536]{3,2,1,0:T(8,128)} %add_bitcast_fusion.2), channel_id=1, source_target_pairs={{0,2},{1,5},{2,0},{3,7},{4,6},{5,1},{6,4},{7,3},{8,10},{9,13},{10,... | collective-permute-start | bytes 4718600 | tf_op jit(solution)/shard_map/ppermute | solution.py:873
  377.2 32.7 %collective-permute-start.33 = (f32[64,3840]{1,0:T(8,128)}, f32[64,3840]{1,0:T(8,128)}, u32[]{:S(2)}, u32[]{:S(2)}) collective-permute-start(f32[64,3840]{1,0:T(8,128)} %maximum_add_fusion.1), channel_id=1, source_target_pairs={{0,16},{1,9},{2,18},{3,11},{4,20},{5,13},{6,22},{7,15},{8,24},{9,1... | collective-permute-start | bytes 2949128 | tf_op jit(solution)/shard_map/ppermute | solution.py:873
  386.9 17.5 %collective-permute-start.34 = (f32[2,176,512]{2,1,0:T(8,128)}, f32[2,176,512]{2,1,0:T(8,128)}, u32[]{:S(2)}, u32[]{:S(2)}) collective-permute-start(f32[2,176,512]{2,1,0:T(8,128)} %bitcast_add_fusion.3), channel_id=1, source_target_pairs={{0,2},{1,5},{2,0},{3,7},{4,6},{5,1},{6,4},{7,3},{8,10},{9,13},{10,... | collective-permute-start | bytes 2162696 | tf_op jit(solution)/shard_map/ppermute | solution.py:873
  387.8 1.3 collective-permute-start.35
  417.7 21.6 %collective-permute-start.38 = (f32[64,3840]{1,0:T(8,128)}, f32[64,3840]{1,0:T(8,128)}, u32[]{:S(2)}, u32[]{:S(2)}) collective-permute-start(f32[64,3840]{1,0:T(8,128)} %maximum_add_fusion.2), channel_id=1, source_target_pairs={{0,2},{1,3},{2,0},{3,1},{4,6},{5,7},{6,4},{7,5},{8,10},{9,11},{10,... | collective-permute-start | bytes 2949128 | tf_op jit(solution)/shard_map/ppermute | solution.py:869
  418.5 20.7 %collective-permute-start.36 = (f32[2,64,1536]{2,1,0:T(8,128)}, f32[2,64,1536]{2,1,0:T(8,128)}, u32[]{:S(2)}, u32[]{:S(2)}) collective-permute-start(f32[2,64,1536]{2,1,0:T(8,128)} %bitcast_add_fusion.2), channel_id=1, source_target_pairs={{0,8},{1,17},{2,10},{3,19},{4,12},{5,21},{6,14},{7,23},{8,0},{9,25... | collective-permute-start | bytes 2359304 | tf_op jit(solution)/shard_map/ppermute | solution.py:873
  420.2 17.2 %collective-permute-start.37 = (f32[176,512]{1,0:T(8,128)}, f32[176,512]{1,0:T(8,128)S(1)}, u32[]{:S(2)}, u32[]{:S(2)}) collective-permute-start(f32[176,512]{1,0:T(8,128)} %fusion.10), channel_id=1, source_target_pairs={{0,16},{4,20},{8,24},{12,28},{16,0},{20,4},{24,8},{28,12},{1,17},{... | collective-permute-start | bytes 1081352 | tf_op jit(solution)/shard_map/ppermute | solution.py:869
  425.7 4.3 collective-permute-start.39
  446.0 19.3 %collective-permute-start.42 = (f32[128,3840]{1,0:T(8,128)}, f32[128,3840]{1,0:T(8,128)}, u32[]{:S(2)}, u32[]{:S(2)}) collective-permute-start(f32[128,3840]{1,0:T(8,128)} %pad_maximum_fusion.3), channel_id=1, source_target_pairs={{0,1},{1,0},{2,3},{3,2},{4,5},{5,4},{6,7},{7,6},{8,9},{9,8},{10,11... | collective-permute-start | bytes 5898248 | tf_op jit(solution)/shard_map/ppermute | solution.py:869
  453.0 12.3 %collective-permute-start.40 = (f32[64,1536]{1,0:T(8,128)}, f32[64,1536]{1,0:T(8,128)S(1)}, u32[]{:S(2)}, u32[]{:S(2)}) collective-permute-start(f32[64,1536]{1,0:T(8,128)} %fusion.7), channel_id=1, source_target_pairs={{0,16},{1,9},{2,18},{3,11},{4,20},{5,13},{6,22},{7,15},{8,24},{9,1... | collective-permute-start | bytes 1179656 | tf_op jit(solution)/shard_map/ppermute | solution.py:873
  457.0 7.4 %collective-permute-start.41 = (f32[176,512]{1,0:T(8,128)S(1)}, f32[176,512]{1,0:T(8,128)S(1)}, u32[]{:S(2)}, u32[]{:S(2)}) collective-permute-start(f32[176,512]{1,0:T(8,128)S(1)} %fusion.9), channel_id=1, source_target_pairs={{0,2},{1,3},{2,0},{3,1},{4,6},{5,7},{6,4},{7,5},{8,10},{9,11},{10,... | collective-permute-start | bytes 1081352 | tf_op jit(solution)/shard_map/ppermute | solution.py:869
  457.9 5.9 %collective-permute-start.43 = (f32[2,32,128]{2,1,0:T(8,128)S(1)}, f32[2,32,128]{2,1,0:T(8,128)S(1)}, u32[]{:S(2)}, u32[]{:S(2)}) collective-permute-start(f32[2,32,128]{2,1,0:T(8,128)S(1)} %bitcast_add_fusion.8), channel_id=1, source_target_pairs={{0,8},{4,12},{8,0},{12,4},{16,24},{20,28},{24,16},{28,20},{1,9},{5... | collective-permute-start | bytes 98312 | tf_op jit(solution)/shard_map/ppermute | solution.py:869
  466.9 7.6 %collective-permute-start.46 = (f32[32,128]{1,0:T(8,128)S(1)}, f32[32,128]{1,0:T(8,128)S(1)}, u32[]{:S(2)}, u32[]{:S(2)}) collective-permute-start(f32[32,128]{1,0:T(8,128)S(1)} %bitcast_add_fusion.9), channel_id=1, source_target_pairs={{0,16},{4,20},{8,24},{12,28},{16,0},{20,4},{24,8},{28,12},{1,17},{... | collective-permute-start | bytes 49160 | tf_op jit(solution)/shard_map/ppermute | solution.py:869
  471.8 10.6 %collective-permute-start.44 = (f32[64,1536]{1,0:T(8,128)S(1)}, f32[64,1536]{1,0:T(8,128)S(1)}, u32[]{:S(2)}, u32[]{:S(2)}) collective-permute-start(f32[64,1536]{1,0:T(8,128)S(1)} %fusion.6), channel_id=1, source_target_pairs={{0,2},{1,3},{2,0},{3,1},{4,6},{5,7},{6,4},{7,5},{8,10},{9,11},{10,... | collective-permute-start | bytes 1179656 | tf_op jit(solution)/shard_map/ppermute | solution.py:869
  472.7 9.7 %collective-permute-start.45 = (f32[352,512]{1,0:T(8,128)S(1)}, f32[352,512]{1,0:T(8,128)S(1)}, u32[]{:S(2)}, u32[]{:S(2)}) collective-permute-start(f32[352,512]{1,0:T(8,128)S(1)} %pad_maximum_fusion.6), channel_id=1, source_target_pairs={{0,1},{1,0},{2,3},{3,2},{4,5},{5,4},{6,7},{7,6},{8,9},{9,8},{10,11... | collective-permute-start | bytes 2162696 | tf_op jit(solution)/shard_map/ppermute | solution.py:869
  482.5 8.0 %collective-permute-start.47 = (f32[128,1536]{1,0:T(8,128)S(1)}, f32[128,1536]{1,0:T(8,128)S(1)}, u32[]{:S(2)}, u32[]{:S(2)}) collective-permute-start(f32[128,1536]{1,0:T(8,128)S(1)} %pad_maximum_fusion.5), channel_id=1, source_target_pairs={{0,1},{1,0},{2,3},{3,2},{4,5},{5,4},{6,7},{7,6},{8,9},{9,8},{10,11... | collective-permute-start | bytes 2359304 | tf_op jit(solution)/shard_map/ppermute | solution.py:869
  486.8 3.7 collective-permute-start.48
  (24 other events, 91.7 us)

commit v6 on v5

--- a/solution.py
+++ b/solution.py
@@ -11,20 +11,6 @@
 EPS = 1e-05
 KEY_EPS = 1e-06
 HIGH = lax.Precision.HIGHEST
-
-
-def doc_info(lengths, first, count):
-    padded = (lengths + CK - 1) // CK * CK
-    ends = jnp.cumsum(padded)
-    starts = ends - padded
-    place = first + jnp.arange(count, dtype=jnp.int32)
-    inside = ((place[:, None] >= starts[None, :]) & (place[:, None] < ends[None, :])).astype(
-        jnp.int32
-    )
-    position = place - jnp.sum(inside * starts[None, :], 1)
-    length = jnp.sum(inside * lengths[None, :], 1)
-    live = (position < length).astype(jnp.float32)
-    return (position, live)
 
 
 SPAN = CK
@@ -147,12 +133,36 @@
     return 1.0 / (1.0 + jnp.exp(-value))
 
 
+def doc_starts(docs):
+    begin = jnp.int32(0)
+    for index in range(1, docs.shape[0]):
+        yield begin, docs[index]
+        begin = begin + jnp.bitwise_and(docs[index] + (SPAN - 1), -SPAN)
+
+
+def span_flag(docs, span):
+    place, flag = docs[0] + span * SPAN, jnp.float32(1.0)
+    for begin, _ in doc_starts(docs):
+        flag = jnp.where(begin == place, 0.0, flag)
+    return flag
+
+
+def token_places(docs, count):
+    place = docs[0] + lax.broadcasted_iota(jnp.int32, (count, 1), 0)
+    position, live = place, jnp.zeros((count, 1), jnp.float32)
+    for begin, length in doc_starts(docs):
+        here = place >= begin
+        position = jnp.where(here, place - begin, position)
+        live = jnp.where(here, jnp.where(place - begin < length, 1.0, 0.0), live)
+    return position, live
+
+
 HALO = 16
 
 
 def project_kernel(
-    tokens, halo, gain, position, live, query_w, key_w, value_w, gate_w, beta_w, conv,
-    normed_out, pre_out, feature_out, gate_out, beta_pre_out, beta_out, normed, pre,
+    docs, tokens, halo, gain, query_w, key_w, value_w, gate_w, beta_w, conv,
+    normed_out, pre_out, feature_out, gate_out, beta_pre_out, beta_out, position, live, normed, pre,
 ):
     count = tokens.shape[0]
 
@@ -169,6 +179,7 @@
         normed_out[...] = rounded.astype(jnp.float32).T
         beta_pre = mxu(rounded, beta_w[...], NT)
         beta_pre_out[...] = beta_pre
+        position[...], live[...] = token_places(docs, count)
         beta_out[...] = sigmoid(beta_pre) * live[...]
 
     gate_out[...] = mxu(normed[HALO:, :], gate_w[...], NN)
@@ -206,7 +217,7 @@
     return total
 
 
-def project(tokens, halo, gain, position, live, query_w, key_w, value_w, gate_w, beta_w, conv):
+def project(docs, tokens, halo, gain, query_w, key_w, value_w, gate_w, beta_w, conv):
     count, width = tokens.shape
     heads = beta_w.shape[0]
     block = 2 * LANES
@@ -217,8 +228,8 @@
         project_kernel,
         grid=(width // block,),
         in_specs=[
-            whole((count, width)), whole((HALO, width)), whole((1, width)), whole((count, 1)),
-            whole((count, 1)), weight, weight, weight, weight, whole((heads, width)),
+            pl.BlockSpec(memory_space=pltpu.SMEM), whole((count, width)), whole((HALO, width)),
+            whole((1, width)), weight, weight, weight, weight, whole((heads, width)),
             pl.BlockSpec((3, conv.shape[1], block), lambda j: (0, 0, j)),
         ],
         out_specs=[
@@ -226,11 +237,12 @@
             pl.BlockSpec((3, count // SPAN, SPAN + 8, block), lambda j: (0, 0, 0, j)),
             pl.BlockSpec((3, count, block), lambda j: (0, 0, j)),
             pl.BlockSpec((count, block), lambda j: (0, j)),
-            whole((count, heads)), whole((count, heads)),
+            whole((count, heads)), whole((count, heads)), whole((count, 1)), whole((count, 1)),
         ],
         out_shape=[
             f32((width, count)), f32((3, count // SPAN, SPAN + 8, width)), f32((3, count, width)),
             f32((count, width)), f32((count, heads)), f32((count, heads)),
+            jax.ShapeDtypeStruct((count, 1), jnp.int32), f32((count, 1)),
         ],
         scratch_shapes=[
             pltpu.VMEM((HALO + count, width), LOW),
@@ -239,10 +251,10 @@
         compiler_params=params(),
         cost_estimate=cost(8 * count * width * width, 8 * width * width + 40 * count * width),
         name="project",
-    )(tokens, halo, gain, position, live, query_w, key_w, value_w, gate_w, beta_w, conv)
-
-
-def prepare_kernel(keep, features, beta, solved_out, inverse_out, attend_out, state):
+    )(docs, tokens, halo, gain, query_w, key_w, value_w, gate_w, beta_w, conv)
+
+
+def prepare_kernel(docs, features, beta, solved_out, inverse_out, attend_out, state):
     span = pl.program_id(0)
     heads = state.shape[0]
     size = state.shape[1]
@@ -257,7 +269,7 @@
 
     query, key, value = features[0], features[1], features[2]
     betas = beta[...]
-    flag = keep[span]
+    flag = span_flag(docs, span)
     pairs = range(heads // 2)
     keys = [split(pair(key, p)) for p in pairs]
     columns = [pair_column(betas, p) for p in pairs]
@@ -289,7 +301,7 @@
         state[h] = starts[h] + t_product(tuple(k[rows] for k in keys[h // 2]), news[h])
 
 
-def prepare(keep, features, beta):
+def prepare(docs, features, beta):
     _, count, width = features.shape
     heads = beta.shape[1]
     size = width // heads
@@ -315,11 +327,11 @@
         compiler_params=params(),
         cost_estimate=cost(40 * count * width * size * 4, 60 * count * width),
         name="prepare",
-    )(keep, features, beta)
+    )(docs, features, beta)
 
 
 def mix_kernel(
-    keep, place, features, solved, attend, gate, gain, state_mine, state_other, starts_out, new_out,
+    docs, place, features, solved, attend, gate, gain, state_mine, state_other, starts_out, new_out,
     mixed_out, normed_out, state,
 ):
     span = pl.program_id(0)
@@ -334,7 +346,7 @@
 
     query, key = features[0], features[1]
     erase, update = solved[0], solved[1]
-    flag = keep[span]
+    flag = span_flag(docs, span)
     every, pairs = range(heads), range(heads // 2)
     starts = [state[h] * flag for h in every]
     both = [
@@ -355,7 +367,7 @@
         normed_out[:, lanes] = (shaped * (gates * sigmoid(gates))).astype(LOW)
 
 
-def mix(keep, place, features, solved, attend, gate, gain, state_mine, state_other):
+def mix(docs, place, features, solved, attend, gate, gain, state_mine, state_other):
     _, count, width = features.shape
     half, size, _ = state_mine.shape
     heads = 2 * half
@@ -384,7 +396,7 @@
         compiler_params=params(),
         cost_estimate=cost(8 * count * width * size * 4, 40 * count * width),
         name="mix",
-    )(keep, place, features, solved, attend, gate, gain, state_mine, state_other)
+    )(docs, place, features, solved, attend, gate, gain, state_mine, state_other)
 
 
 def feed_kernel(
@@ -491,7 +503,7 @@
 
 
 def gather_kernel(
-    keep, core, grad_head, grad_branch, mixed, gate, gain, features, solved, grad_mixed_out,
+    docs, core, grad_head, grad_branch, mixed, gate, gain, features, solved, grad_mixed_out,
     grad_gate_out, kept_out, sent_out, gain_out, state,
 ):
     step = pl.program_id(0)
@@ -506,7 +518,7 @@
 
     query, key = features[0], features[1]
     erase = solved[0]
-    flag = keep[span]
+    flag = span_flag(docs, span)
     gain_total = jnp.zeros_like(gain_out[...])
     every, pairs = range(heads), range(heads // 2)
     passes = [product_t(pair(key, p), pair(query, p)) * upper for p in pairs]
@@ -552,7 +564,7 @@
 
 
 def gather_states(
-    keep, core, grad_head, grad_branch, mixed, gate, gain, features, solved, heads
+    docs, core, grad_head, grad_branch, mixed, gate, gain, features, solved, heads
 ):
     _, count, width = features.shape
     size = width // heads
@@ -579,11 +591,11 @@
         compiler_params=params(),
         cost_estimate=cost(8 * count * width * size * 4, 32 * count * width),
         name="gather_states",
-    )(keep, core, grad_head, grad_branch, mixed, gate, gain, features, solved)
+    )(docs, core, grad_head, grad_branch, mixed, gate, gain, features, solved)
 
 
 def back_kernel(
-    keep, place, features, beta, beta_pre, solved, inverses, starts, news, grad_mixed, state_mine,
+    docs, place, features, beta, beta_pre, solved, inverses, starts, news, grad_mixed, state_mine,
     state_other, pre, conv, position, live, grad_pre_out, borrowed_out, conv_out, grad_beta_out, state, later, sums,
 ):
     step = pl.program_id(0)
@@ -604,7 +616,7 @@
     query, key, value = features[0], features[1], features[2]
     erase, update = solved[0], solved[1]
     betas = beta[...]
-    flag = keep[span]
+    flag = span_flag(docs, span)
     base = pl.multiple_of(span * SPAN, SPAN)
     places = position[pl.ds(base, SPAN), :]
     lives = live[pl.ds(base, SPAN), :]
@@ -751,7 +763,7 @@
 
 
 def back(
-    keep, place, features, beta, beta_pre, solved, inverses, starts, news, grad_mixed, state_mine,
+    docs, place, features, beta, beta_pre, solved, inverses, starts, news, grad_mixed, state_mine,
     state_other, pre, conv, position, live,
 ):
     _, count, width = features.shape
@@ -790,7 +802,7 @@
         cost_estimate=cost(30 * count * width * size * 4, 60 * count * width),
         name="back",
     )(
-        keep, place, features, beta, beta_pre, solved, inverses, starts, news, grad_mixed,
+        docs, place, features, beta, beta_pre, solved, inverses, starts, news, grad_mixed,
         state_mine, state_other, pre, conv, position, live,
     )
 
@@ -1053,7 +1065,8 @@
 
 def outer(pieces, orders, parts=(1,)):
     rows, tokens = pieces[0][0].shape
-    block = 2 * LANES
+    double = all(piece[4] % 2 == 0 and piece[5] % 2 == 0 for piece in pieces)
+    block = (4 if double else 2) * LANES
     table = []
     for place in range(16):
         entries = []
@@ -1064,6 +1077,8 @@
             entries.append(first * WEIGHTS[order[0]] + rest)
         table.append(by_core(entries))
     table = jnp.stack(table).astype(jnp.int32)
+    if double:
+        pieces = [(*piece[:4], piece[4] // 2, piece[5] // 2) for piece in pieces]
     counts = [piece[5] for piece in pieces]
     left = pl.BlockSpec((rows, tokens), lambda j: (0, 0), pipeline_mode=pl.Buffered(1))
     lefts, rights, specs = [], [], []
@@ -1227,18 +1242,16 @@
     heads = beta_weight.shape[1]
     reach = conv_weight.shape[1] - 1
     first = lax.axis_index("seq") * count
-    position, live = doc_info(doc_lengths[0], first, count)
-    keep = 1.0 - (position[::CK] == 0).astype(jnp.float32)
-    position, live = position[:, None], live[:, None]
+    docs = jnp.concatenate([first.astype(jnp.int32)[None], doc_lengths[0]])
     core = (lax.axis_index("doc") % 2).astype(jnp.int32).reshape(1)
     here = core[0] == 0
     rows, top = tokens[0], out_grad[0]
     halo = passed_along(rows[count - HALO :].astype(jnp.float32), "seq", 1)
-    normed_one, pre, features, gate_pre, beta_pre, beta = project(
-        rows, halo, first_gain[None], position, live, query_weight, key_weight, value_weight,
+    normed_one, pre, features, gate_pre, beta_pre, beta, position, live = project(
+        docs, rows, halo, first_gain[None], query_weight, key_weight, value_weight,
         gate_weight, beta_weight.T, conv_weight,
     )
-    solved, inverses, attend, maps = prepare(keep, features, beta)
+    solved, inverses, attend, maps = prepare(docs, features, beta)
     if tuned():
         half = width // 2
         units = half // 256
@@ -1260,7 +1273,7 @@
     if tuned():
         tops, one = beside[:2], beside[2:]
     starts, news, mixed, normed_head = mix(
-        keep, place, features, solved, attend, gate_pre, head_gain[None], state_mine, state_other
+        docs, place, features, solved, attend, gate_pre, head_gain[None], state_mine, state_other
     )
     (
         block_out, two_turned, inner_turned, kept, sent, grad_hidden, grad_branch, grad_head,
@@ -1274,7 +1287,7 @@
         two = both(two_turned)
         gate_up = both(kept, sent)
     grad_mixed, grad_gate_pre, out_kept, out_sent, grad_head_gain, shift = gather_states(
-        keep, core, grad_head, grad_branch, mixed, gate_pre, head_gain[None], features, solved, heads
+        docs, core, grad_head, grad_branch, mixed, gate_pre, head_gain[None], features, solved, heads
     )
     if tuned():
         out_right = both(out_kept, out_sent)
@@ -1314,7 +1327,7 @@
     else:
         grad_mine, grad_other, _ = carried_back(shift, context)
     grads, borrowed, grad_conv, grad_beta_pre = back(
-        keep, place, features, beta, beta_pre, solved, inverses, starts, news, grad_mixed, grad_mine,
+        docs, place, features, beta, beta_pre, solved, inverses, starts, news, grad_mixed, grad_mine,
         grad_other, pre, conv_weight, position, live,
     )
     if tuned():

time: 504 us -> 500 us (level)
  transfers between devices with their start and end apart: 49 -> 49, of which waited for: 23 -> 24; matrix products, arithmetic and copies ran while one was open for 8% -> 8% of each run, Pallas kernels for 23% -> 22%
where the time goes in v6:
time: 500 us; the launch traced here: 494 us
  Pallas kernels  161 us (32%)
  waiting for transfers between devices  149 us (30%)
  starting transfers between devices  94.3 us (19%)
  other arithmetic  64.7 us (13%)
  local copies, waits for them, and re-layouts  22.4 us (4%)
    ppermute x27, waiting for transfers between devices, hop(): lax.ppermute(value, axis, [(i, i ^ bit) for i in range(lax.axis_size(axis...  64.9 us
    ppermute x14, waiting for transfers between devices, hop(): return lax.ppermute(value, ('seq', 'doc'), pairs)  64.8 us
    ppermute x27, starting transfers between devices, hop(): lax.ppermute(value, axis, [(i, i ^ bit) for i in range(lax.axis_size(axis...  42.9 us
    pallas_call x4, Pallas kernels, outer(): pl.pallas_call(lambda *refs: outer_kernel(*refs, blocks=counts, pieces=si...  39 us
    ppermute x14, starting transfers between devices, hop(): return lax.ppermute(value, ('seq', 'doc'), pairs)  36.2 us
    pallas_call x1, Pallas kernels, back(): pl.pallas_call(back_kernel, grid=(spans,), in_specs=[pl.BlockSpec(memory_...  33.2 us
    pallas_call x1, Pallas kernels, feed(): pl.pallas_call(feed_kernel, grid=(hidden // block,), in_specs=[pl.BlockSp...  27.5 us
    add x11, other arithmetic, chosen(): return total + self.added(self.terms, here) if self.terms else total  22 us
  transfers between devices with their start and end apart: 49, of which 24 were waited for; matrix products, arithmetic and copies ran while one was open for 8% of the time, Pallas kernels for 22%

profile of v6, /device:TPU:0, one launch (start us, length us, event | category | flops | bytes accessed | tf_op | source)
XLA Modules:
  0.0 493.6 jit_solution(1296539603075627275)
XLA Ops:
  1.4 4.8 collective-permute-start
  8.8 13.0 %project.1 = (f32[1024,384]{1,0:T(8,128)}, f32[3,6,72,1024]{3,2,1,0:T(8,128)}, f32[3,384,1024]{2,1,0:T(8,128)}, f32[384,1024]{1,0:T(8,128)}, f32[384,8]{1,0:T(8,...) custom-call(s32[5]{0:T(128)} %pad_add_fusion.docs, bf16[384,1024]{1,0:T(8,128)(2,1)} %bitcast.186, ...), custom_call_target="tpu_custom_call" | custom-call | flops 1 | bytes 1 | tf_op jit(solution)/shard_map/project/pallas_call | solution.py:227
  22.8 17.2 %prepare.1 = (f32[2,384,1024]{2,1,0:T(8,128)}, f32[6,4,128,128]{3,2,1,0:T(8,128)}, f32[6,4,128,128]{3,2,1,0:T(8,128)}, f32[8,128,256]{2,1,0:T(8,128)}) custom-call(s32[5]{0:T(128)} %pad_add_fusion.docs, f32[3,384,1024]{2,1,0:T(8,128)} %get-tuple-element.155.features, f32[384,8]{1,0:T(8,128)} %get-tuple-element.156.beta), custom_call_target="tpu_custom_call" | custom-call | flops 1 | bytes 1 | tf_op jit(solution)/shard_map/prepare/pallas_call | solution.py:311
  41.3 2.4 collective-permute-start.1
  44.5 11.4 %collective-permute-done.1 = f32[4,128,256]{2,1,0:T(8,128)S(1)} collective-permute-done((f32[4,128,256]{2,1,0:T(8,128)S(1)}, f32[4,128,256]{2,1,0:T(8,128)S(1)}, u32[]{:S(2)}, u32[]{:S(2)}) %collective-permute-start.1) | collective-permute-done | bytes 524320 | tf_op jit(solution)/shard_map/ppermute | solution.py:881
  57.3 4.7 collective-permute-start.4
  61.9 4.9 collective-permute-done.4.refs_3_.refs_2_
  70.5 5.9 %collective-permute-done.7.state_other = f32[4,128,128]{2,1,0:T(8,128)S(1)} collective-permute-done((f32[4,128,128]{2,1,0:T(8,128)S(1)}, f32[4,128,128]{2,1,0:T(8,128)S(1)}, u32[]{:S(2)}, u32[]{:S(2)}) %collective-permute-start.7) | collective-permute-done | bytes 262176 | tf_op jit(solution)/shard_map/ppermute | solution.py:881
  77.1 8.9 %mix.1 = (f32[6,8,128,128]{3,2,1,0:T(8,128)}, f32[384,1024]{1,0:T(8,128)}, f32[384,1024]{1,0:T(8,128)}, bf16[384,1024]{1,0:T(8,128)(2,1)}) custom-call(s32[5]{0:T(128)} %pad_add_fusion.docs, s32[1]{0:T(128)} %bitcast.4.refs_0_.place, f32[3,384,1024]{2,1,0:T(8,128)} %get-tuple-element.155.features, f32[2,384,1024]{2,1,0:T(8,128)} %get-tuple-element.157.solved, ...), custom_call_target="tpu_custom_call" | custom-call | flops 1 | bytes 1 | tf_op jit(solution)/shard_map/mix/pallas_call | solution.py:378
  86.0 27.5 %feed.1 = (bf16[384,1024]{1,0:T(8,128)(2,1)}, f32[1024,384]{1,0:T(8,128)}, f32[2816,384]{1,0:T(8,128)}, bf16[384,2816]{1,0:T(8,128)(2,1)}, f32[384,2816]{1,0:T(8...) custom-call(s32[1]{0:T(128)} %bitcast.core, ...), custom_call_target="tpu_custom_call" | custom-call | flops 1 | bytes 1 | tf_op jit(solution)/shard_map/feed/pallas_call | solution.py:474
  114.1 9.7 %gather_states.1 = (f32[384,1024]{1,0:T(8,128)}, f32[384,1024]{1,0:T(8,128)}, bf16[384,1024]{1,0:T(8,128)(2,1)}, f32[384,1024]{1,0:T(8,128)}, f32[1,128]{1,0:T(1,128)}, /*index=5*/f32[8,128,128]{2,1,0:T(8,128)}) custom-call(s32[5]{0:T(128)} %pad_add_fusion.docs, s32[1]{0:T(128)} %bitcast.core, f32[384,1024]{1,0:T(8,128)} %get-tuple-element.168.grad_head, ...), custom_call_target="tpu_custom_call" | custom-call | flops 1 | bytes 1 | tf_op jit(solution)/shard_map/gather_states/pallas_call | solution.py:576
  123.9 2.1 slice_select_fusion.6
  127.4 9.1 %outer.4 = (f32[512,2048]{1,0:T(8,128)}, f32[144,2048]{1,0:T(8,128)}, f32[144,2048]{1,0:T(8,128)}, f32[144,2048]{1,0:T(8,128)}, f32[80,2048]{1,0:T(8,128)}) custom-call(s32[16]{0:T(128)} %stack.152.refs_0_, f32[1024,384]{1,0:T(8,128)} %get-tuple-element.167.refs_1_, f32[1024,384]{1,0:T(8,128)} %copy-done.9, ...), custom_call_target="tpu_custom_call" | custom-call | flops 1 | bytes 1 | tf_op jit(solution)/shard_map/outer/pallas_call | solution.py:1097
  141.1 7.7 %outer.5 = (f32[1408,512]{1,0:T(8,128)}, f32[592,512]{1,0:T(8,128)}, f32[816,512]{1,0:T(8,128)}) custom-call(s32[16]{0:T(128)} %stack.169.refs_0_, f32[2816,384]{1,0:T(8,128)} %get-tuple-element.186.refs_1_, f32[2816,384]{1,0:T(8,128)} %collective-permute-done.13.refs_2_, bf16[384,512]{1,0:T(8,128)(2,1)} %slice_select_fusion.5.refs_3_, f32[384,512]{1,0:T(8,128)} %copy-done.25), custom_call_target="tpu_custom_call" | custom-call | flops 1 | bytes 1 | tf_op jit(solution)/shard_map/outer/pallas_call | solution.py:1097
  148.9 5.4 %collective-permute-done.12 = f32[144,2048]{1,0:T(8,128)S(1)} collective-permute-done((f32[144,2048]{1,0:T(8,128)}, f32[144,2048]{1,0:T(8,128)S(1)}, u32[]{:S(2)}, u32[]{:S(2)}) %collective-permute-start.12) | collective-permute-done | bytes 1179680 | tf_op jit(solution)/shard_map/ppermute | solution.py:885
  157.0 12.8 %outer.6 = (f32[512,1792]{1,0:T(8,128)}, f32[512,1792]{1,0:T(8,128)}) custom-call(s32[16]{0:T(128)} %stack.152.refs_0_, f32[1024,384]{1,0:T(8,128)} %get-tuple-element.167.refs_1_, f32[1024,384]{1,0:T(8,128)} %copy-done.9, f32[1024,384]{1,0:T(8,128)} %get-tuple-element.196.refs_3_, f32[1024,384]{1,0:T(8,128)} %collective-permute-done.16.refs_4_, ...), custom_call_target="tpu_custom_call" | custom-call | flops 1 | bytes 1 | tf_op jit(solution)/shard_map/outer/pallas_call | solution.py:1097
  173.9 11.5 %collective-permute-done.18.refs_4_ = f32[4,128,128]{2,1,0:T(8,128)S(1)} collective-permute-done((f32[4,128,128]{2,1,0:T(8,128)S(1)}, f32[4,128,128]{2,1,0:T(8,128)S(1)}, u32[]{:S(2)}, u32[]{:S(2)}) %collective-permute-start.18) | collective-permute-done | bytes 262176 | tf_op jit(solution)/shard_map/ppermute | solution.py:1022
  185.5 1.9 collective-permute-done.19
  190.5 11.7 %collective-permute-done.20.state_other = f32[4,128,128]{2,1,0:T(8,128)S(1)} collective-permute-done((f32[4,128,128]{2,1,0:T(8,128)S(1)}, f32[4,128,128]{2,1,0:T(8,128)S(1)}, u32[]{:S(2)}, u32[]{:S(2)}) %collective-permute-start.20) | collective-permute-done | bytes 262176 | tf_op jit(solution)/shard_map/ppermute | solution.py:881
  202.2 1.5 collective-permute-start.22
  203.7 7.2 %collective-permute-start.23 = (f32[592,512]{1,0:T(8,128)}, f32[592,512]{1,0:T(8,128)S(1)}, u32[]{:S(2)}, u32[]{:S(2)}) collective-permute-start(f32[592,512]{1,0:T(8,128)} %get-tuple-element.229), channel_id=1, source_target_pairs={{0,8},{4,12},{8,0},{12,4},{16,24},{20,28},{24,16},{28,20},{1,9},{5... | collective-permute-start | bytes 3637256 | tf_op jit(solution)/shard_map/ppermute | solution.py:881
  210.9 33.2 %back.1 = (f32[3,384,1024]{2,1,0:T(8,128)}, f32[3,8,1024]{2,1,0:T(8,128)}, f32[3,4,1024]{2,1,0:T(4,128)}, f32[384,8]{1,0:T(8,128)}) custom-call(s32[5]{0:T(128)} %pad_add_fusion.docs, s32[1]{0:T(128)} %bitcast.4.refs_0_.place, f32[3,384,1024]{2,1,0:T(8,128)} %get-tuple-element.155.features, f32[384,8]{1,0:T(8,128)} %get-tuple-element.156.beta, ...), custom_call_target="tpu_custom_call" | custom-call | flops 1 | bytes 1 | tf_op jit(solution)/shard_map/back/pallas_call | solution.py:779
  244.5 3.3 copy-done.10
  250.4 1.9 add_bitcast_fusion.1
  252.3 2.2 pad_maximum_fusion.1
  254.5 2.0 collective-permute-done.24
  258.2 4.8 collective-permute-start.28
  263.5 1.6 fusion
  266.2 1.5 fusion.2
  268.3 1.7 add_bitcast_fusion.4
  269.9 1.6 add_bitcast_fusion.5
  274.1 9.4 %outer.7 = (f32[512,1536]{1,0:T(8,128)}, f32[512,1536]{1,0:T(8,128)}) custom-call(s32[16]{0:T(128)} %stack.152.refs_0_, f32[1024,384]{1,0:T(8,128)} %get-tuple-element.197.refs_5_.refs_1_.refs_3_, f32[1024,384]{1,0:T(8,128)} %collective-permute-done.3.refs_6_.refs_2_.refs_4_, f32[1024,384]{1,0:T(8,128)} %get-tuple-element.197.refs_5_.refs_1_.refs_3_, ...), custom_call_target="tpu_custom_call" | custom-call | flops 1 | bytes 1 | tf_op jit(solution)/shard_map/outer/pallas_call | solution.py:1097
  283.5 10.9 %collective-permute-done.28 = f32[816,512]{1,0:T(8,128)} collective-permute-done((f32[816,512]{1,0:T(8,128)}, f32[816,512]{1,0:T(8,128)}, u32[]{:S(2)}, u32[]{:S(2)}) %collective-permute-start.28) | collective-permute-done | bytes 1671200 | tf_op jit(solution)/shard_map/ppermute | solution.py:881
  294.3 8.6 %collective-permute-done.27 = f32[2,2,64,3840]{3,2,1,0:T(8,128)} collective-permute-done((f32[2,2,64,3840]{3,2,1,0:T(8,128)}, f32[2,2,64,3840]{3,2,1,0:T(8,128)}, u32[]{:S(2)}, u32[]{:S(2)}) %collective-permute-start.27) | collective-permute-done | bytes 3932192 | tf_op jit(solution)/shard_map/ppermute | solution.py:885
  303.0 1.7 pad_maximum_fusion.2
  304.7 4.1 maximum_add_fusion
  310.2 3.3 collective-permute-start.31
  313.6 6.7 %collective-permute-start.29 = (f32[2,64,3840]{2,1,0:T(8,128)}, f32[2,64,3840]{2,1,0:T(8,128)}, u32[]{:S(2)}, u32[]{:S(2)}) collective-permute-start(f32[2,64,3840]{2,1,0:T(8,128)} %maximum_add_fusion), channel_id=1, source_target_pairs={{0,8},{1,17},{2,10},{3,19},{4,12},{5,21},{6,14},{7,23},{8,0},{9,25... | collective-permute-start | bytes 5898248 | tf_op jit(solution)/shard_map/ppermute | solution.py:885
  322.9 2.4 add_bitcast_fusion.6
  325.3 2.4 add_bitcast_fusion.8
  327.8 10.5 %enter.1 = (bf16[384,1024]{1,0:T(8,128)(2,1)}, f32[1,1024]{1,0:T(1,128)}) custom-call(bf16[384,1024]{1,0:T(8,128)(2,1)} %bitcast.188, f32[1,1024]{1,0:T(1,128)} %bitcast.221, f32[384,1024]{1,0:T(8,128)} %get-tuple-element.246.grad_hidden, bf16[3,384,1024]{2,1,0:T(8,128)(2,1)} %copy-done.2, f32[384,1024]{1,0:T(8,128)} %get-tuple-element.248.grad_gate, ...), custom_call_target="tpu_custom_call" | custom-call | flops 1 | bytes 1 | tf_op jit(solution)/shard_map/enter/pallas_call | solution.py:842
  340.7 23.8 %collective-permute-done.30 = f32[2,2,176,512]{3,2,1,0:T(8,128)} collective-permute-done((f32[2,2,176,512]{3,2,1,0:T(8,128)}, f32[2,2,176,512]{3,2,1,0:T(8,128)}, u32[]{:S(2)}, u32[]{:S(2)}) %collective-permute-start.30) | collective-permute-done | bytes 1441824 | tf_op jit(solution)/shard_map/ppermute | solution.py:885
  364.6 2.4 bitcast_add_fusion.3
  367.0 3.3 add_bitcast_fusion.2
  370.3 2.6 maximum_add_fusion.1
  374.2 10.2 %collective-permute-start.33 = (f32[64,3840]{1,0:T(8,128)}, f32[64,3840]{1,0:T(8,128)}, u32[]{:S(2)}, u32[]{:S(2)}) collective-permute-start(f32[64,3840]{1,0:T(8,128)} %maximum_add_fusion.1), channel_id=1, source_target_pairs={{0,16},{1,9},{2,18},{3,11},{4,20},{5,13},{6,22},{7,15},{8,24},{9,1... | collective-permute-start | bytes 2949128 | tf_op jit(solution)/shard_map/ppermute | solution.py:885
  386.5 14.9 %collective-permute-done.34 = f32[2,176,512]{2,1,0:T(8,128)} collective-permute-done((f32[2,176,512]{2,1,0:T(8,128)}, f32[2,176,512]{2,1,0:T(8,128)}, u32[]{:S(2)}, u32[]{:S(2)}) %collective-permute-start.34) | collective-permute-done | bytes 720928 | tf_op jit(solution)/shard_map/ppermute | solution.py:885
  401.4 5.9 %collective-permute-done.33 = f32[64,3840]{1,0:T(8,128)} collective-permute-done((f32[64,3840]{1,0:T(8,128)}, f32[64,3840]{1,0:T(8,128)}, u32[]{:S(2)}, u32[]{:S(2)}) %collective-permute-start.33) | collective-permute-done | bytes 983072 | tf_op jit(solution)/shard_map/ppermute | solution.py:885
  407.3 2.7 bitcast_add_fusion.2
  410.0 2.1 fusion.10
  412.1 3.0 maximum_add_fusion.2
  417.2 5.5 %collective-permute-start.37 = (f32[176,512]{1,0:T(8,128)}, f32[176,512]{1,0:T(8,128)S(1)}, u32[]{:S(2)}, u32[]{:S(2)}) collective-permute-start(f32[176,512]{1,0:T(8,128)} %fusion.10), channel_id=1, source_target_pairs={{0,16},{4,20},{8,24},{12,28},{16,0},{20,4},{24,8},{28,12},{1,17},{... | collective-permute-start | bytes 1081352 | tf_op jit(solution)/shard_map/ppermute | solution.py:881
  423.8 3.1 collective-permute-done.39
  426.9 7.4 %collective-permute-done.37 = f32[176,512]{1,0:T(8,128)S(1)} collective-permute-done((f32[176,512]{1,0:T(8,128)}, f32[176,512]{1,0:T(8,128)S(1)}, u32[]{:S(2)}, u32[]{:S(2)}) %collective-permute-start.37) | collective-permute-done | bytes 360480 | tf_op jit(solution)/shard_map/ppermute | solution.py:881
  434.3 2.3 collective-permute-done.36
  436.6 2.2 fusion.7
  440.3 1.6 broadcast_select_fusion.3
  443.4 6.6 %collective-permute-start.42 = (f32[128,3840]{1,0:T(8,128)}, f32[128,3840]{1,0:T(8,128)}, u32[]{:S(2)}, u32[]{:S(2)}) collective-permute-start(f32[128,3840]{1,0:T(8,128)} %pad_maximum_fusion.3), channel_id=1, source_target_pairs={{0,1},{1,0},{2,3},{3,2},{4,5},{5,4},{6,7},{7,6},{8,9},{9,8},{10,11... | collective-permute-start | bytes 5898248 | tf_op jit(solution)/shard_map/ppermute | solution.py:881
  450.0 4.0 collective-permute-start.40
  454.9 2.5 collective-permute-start.43
  457.4 3.3 collective-permute-done.43
  463.9 4.8 collective-permute-start.46
  469.7 1.8 broadcast_select_fusion.1
  471.5 7.8 %collective-permute-done.44 = f32[64,1536]{1,0:T(8,128)S(1)} collective-permute-done((f32[64,1536]{1,0:T(8,128)S(1)}, f32[64,1536]{1,0:T(8,128)S(1)}, u32[]{:S(2)}, u32[]{:S(2)}) %collective-permute-start.44) | collective-permute-done | bytes 393248 | tf_op jit(solution)/shard_map/ppermute | solution.py:881
  (218 shorter events, 72.6 us)
Async XLA Ops:
  1.4 6.7 %collective-permute-start = (f32[16,1024]{1,0:T(8,128)S(1)}, f32[16,1024]{1,0:T(8,128)S(1)}, u32[]{:S(2)}, u32[]{:S(2)}) collective-permute-start(f32[16,1024]{1,0:T(8,128)S(1)} %bitcast_convert_fusion), channel_id=1, source_target_pairs={{0,4},{4,8},{8,12},{12,16},{16,20},{20,24},{24,28},{1,5},{5,9},{9,... | collective-permute-start | bytes 196616 | tf_op jit(solution)/shard_map/ppermute | solution.py:868
  8.8 13.1 %copy-start.8 = (bf16[1,384,1024]{2,1,0:T(8,128)(2,1)S(1)}, bf16[1,384,1024]{2,1,0:T(8,128)(2,1)}, u32[]{:S(2)}) copy-start(bf16[1,384,1024]{2,1,0:T(8,128)(2,1)} %param.18) | copy-start | bytes 2359300
  21.8 35.0 %collective-permute-start.3 = (f32[1024,384]{1,0:T(8,128)}, f32[1024,384]{1,0:T(8,128)}, u32[]{:S(2)}, u32[]{:S(2)}) collective-permute-start(f32[1024,384]{1,0:T(8,128)} %get-tuple-element.197.refs_5_.refs_1_.refs_3_), channel_id=1, source_target_pairs={{0,1},{1,0},{2,3},{3,2},{4,5},{5,4},{6,7},{7,6},{8,9},{9,8},{10,11... | collective-permute-start | bytes 4718600 | tf_op jit(solution)/shard_map/ppermute | solution.py:881
  22.2 33.7 %collective-permute-start.2 = (f32[384,512]{1,0:T(8,128)S(1)}, f32[384,512]{1,0:T(8,128)S(1)}, u32[]{:S(2)}, u32[]{:S(2)}) collective-permute-start(f32[384,512]{1,0:T(8,128)S(1)} %slice_select_fusion.2), channel_id=1, source_target_pairs={{0,1},{1,0},{2,3},{3,2},{4,5},{5,4},{6,7},{7,6},{8,9},{9,8},{10,11... | collective-permute-start | bytes 2359304 | tf_op jit(solution)/shard_map/ppermute | solution.py:881
  40.0 16.8 %copy-start.11 = (f32[8,128,256]{2,1,0:T(8,128)S(1)}, f32[8,128,256]{2,1,0:T(8,128)}, u32[]{:S(2)}) copy-start(f32[8,128,256]{2,1,0:T(8,128)} %get-tuple-element.160) | copy-start | bytes 3145732
  41.3 14.6 %collective-permute-start.1 = (f32[4,128,256]{2,1,0:T(8,128)S(1)}, f32[4,128,256]{2,1,0:T(8,128)S(1)}, u32[]{:S(2)}, u32[]{:S(2)}) collective-permute-start(f32[4,128,256]{2,1,0:T(8,128)S(1)} %slice_select_fusion.3), channel_id=1, source_target_pairs={{0,4},{4,0},{8,12},{12,8},{16,20},{20,16},{24,28},{28,24},{1,5},{5... | collective-permute-start | bytes 1572872 | tf_op jit(solution)/shard_map/ppermute | solution.py:881
  57.3 9.6 %collective-permute-start.4 = (f32[4,128,128]{2,1,0:T(8,128)S(1)}, f32[4,128,128]{2,1,0:T(8,128)S(1)}, u32[]{:S(2)}, u32[]{:S(2)}) collective-permute-start(f32[4,128,128]{2,1,0:T(8,128)S(1)} %slice.151), channel_id=1, source_target_pairs={{0,8},{4,12},{1,9},{5,13},{2,10},{6,14},{3,11},{7,15}} | collective-permute-start | bytes 786440 | tf_op jit(solution)/shard_map/ppermute | solution.py:976
  67.1 0.7 collective-permute-start.5
  68.0 0.9 collective-permute-start.6
  69.9 6.5 %collective-permute-start.7 = (f32[4,128,128]{2,1,0:T(8,128)S(1)}, f32[4,128,128]{2,1,0:T(8,128)S(1)}, u32[]{:S(2)}, u32[]{:S(2)}) collective-permute-start(f32[4,128,128]{2,1,0:T(8,128)S(1)} %get-tuple-element.164), channel_id=1, source_target_pairs={{0,4},{4,0},{8,12},{12,8},{16,20},{20,16},{24,28},{28,24},{1,5},{5... | collective-permute-start | bytes 786440 | tf_op jit(solution)/shard_map/ppermute | solution.py:881
  113.5 10.3 %collective-permute-start.9 = (f32[384,2816]{1,0:T(8,128)}, f32[384,2816]{1,0:T(8,128)}, u32[]{:S(2)}, u32[]{:S(2)}) collective-permute-start(f32[384,2816]{1,0:T(8,128)} %get-tuple-element.172), channel_id=1, source_target_pairs={{0,1},{1,0},{2,3},{3,2},{4,5},{5,4},{6,7},{7,6},{8,9},{9,8},{10,11... | collective-permute-start | bytes 12976136 | tf_op jit(solution)/shard_map/ppermute | solution.py:881
  113.6 10.2 %collective-permute-start.8 = (f32[1024,384]{1,0:T(8,128)}, f32[1024,384]{1,0:T(8,128)S(1)}, u32[]{:S(2)}, u32[]{:S(2)}) collective-permute-start(f32[1024,384]{1,0:T(8,128)} %get-tuple-element.167.refs_1_), channel_id=1, source_target_pairs={{0,1},{1,0},{2,3},{3,2},{4,5},{5,4},{6,7},{7,6},{8,9},{9,8},{10,11... | collective-permute-start | bytes 4718600 | tf_op jit(solution)/shard_map/ppermute | solution.py:881
  123.8 17.3 %collective-permute-start.13 = (f32[2816,384]{1,0:T(8,128)}, f32[2816,384]{1,0:T(8,128)}, u32[]{:S(2)}, u32[]{:S(2)}) collective-permute-start(f32[2816,384]{1,0:T(8,128)} %get-tuple-element.186.refs_1_), channel_id=1, source_target_pairs={{0,1},{1,0},{2,3},{3,2},{4,5},{5,4},{6,7},{7,6},{8,9},{9,8},{10,11... | collective-permute-start | bytes 12976136 | tf_op jit(solution)/shard_map/ppermute | solution.py:881
  126.1 10.4 %collective-permute-start.10 = (f32[4,128,128]{2,1,0:T(8,128)}, f32[4,128,128]{2,1,0:T(8,128)}, u32[]{:S(2)}, u32[]{:S(2)}) collective-permute-start(f32[4,128,128]{2,1,0:T(8,128)} %slice_select_fusion.6), channel_id=1, source_target_pairs={{0,4},{4,0},{8,12},{12,8},{16,20},{20,16},{24,28},{28,24},{1,5},{5... | collective-permute-start | bytes 786440 | tf_op jit(solution)/shard_map/ppermute | solution.py:881
  137.8 16.5 %collective-permute-start.12 = (f32[144,2048]{1,0:T(8,128)}, f32[144,2048]{1,0:T(8,128)S(1)}, u32[]{:S(2)}, u32[]{:S(2)}) collective-permute-start(f32[144,2048]{1,0:T(8,128)} %get-tuple-element.185), channel_id=1, source_target_pairs={{0,4},{1,3},{2,6},{3,1},{4,0},{5,7},{6,2},{7,5},{8,12},{9,11},{10,... | collective-permute-start | bytes 3538952 | tf_op jit(solution)/shard_map/ppermute | solution.py:885
  139.3 17.7 %collective-permute-start.16 = (f32[1024,384]{1,0:T(8,128)}, f32[1024,384]{1,0:T(8,128)}, u32[]{:S(2)}, u32[]{:S(2)}) collective-permute-start(f32[1024,384]{1,0:T(8,128)} %get-tuple-element.196.refs_3_), channel_id=1, source_target_pairs={{0,1},{1,0},{2,3},{3,2},{4,5},{5,4},{6,7},{7,6},{8,9},{9,8},{10,11... | collective-permute-start | bytes 4718600 | tf_op jit(solution)/shard_map/ppermute | solution.py:881
  139.3 17.7 %collective-permute-start.17 = (f32[384,1024]{1,0:T(8,128)}, f32[384,1024]{1,0:T(8,128)}, u32[]{:S(2)}, u32[]{:S(2)}) collective-permute-start(f32[384,1024]{1,0:T(8,128)} %get-tuple-element.200), channel_id=1, source_target_pairs={{0,1},{1,0},{2,3},{3,2},{4,5},{5,4},{6,7},{7,6},{8,9},{9,8},{10,11... | collective-permute-start | bytes 4718600 | tf_op jit(solution)/shard_map/ppermute | solution.py:881
  139.8 9.1 %collective-permute-start.11 = (f32[4,128,128]{2,1,0:T(8,128)S(1)}, f32[4,128,128]{2,1,0:T(8,128)S(1)}, u32[]{:S(2)}, u32[]{:S(2)}) collective-permute-start(f32[4,128,128]{2,1,0:T(8,128)S(1)} %apply_map.9.refs_0_), channel_id=1, source_target_pairs={{24,16},{28,20},{25,17},{29,21},{26,18},{30,22},{27,19},{31,23}} | collective-permute-start | bytes 786440 | tf_op jit(solution)/shard_map/ppermute | solution.py:1022
  141.1 13.4 %copy-start.33 = (f32[144,2048]{1,0:T(8,128)S(1)}, f32[144,2048]{1,0:T(8,128)}, u32[]{:S(2)}) copy-start(f32[144,2048]{1,0:T(8,128)} %get-tuple-element.195) | copy-start | bytes 3538948
  154.5 16.3 %collective-permute-start.15 = (f32[144,2048]{1,0:T(8,128)S(1)}, f32[144,2048]{1,0:T(8,128)S(1)}, u32[]{:S(2)}, u32[]{:S(2)}) collective-permute-start(f32[144,2048]{1,0:T(8,128)S(1)} %copy-done.33), channel_id=1, source_target_pairs={{0,4},{1,3},{2,6},{3,1},{4,0},{5,7},{6,2},{7,5},{8,12},{9,11},{10,... | collective-permute-start | bytes 3538952 | tf_op jit(solution)/shard_map/ppermute | solution.py:885
  156.0 13.8 %collective-permute-start.14 = (f32[4,128,128]{2,1,0:T(8,128)S(1)}, f32[4,128,128]{2,1,0:T(8,128)S(1)}, u32[]{:S(2)}, u32[]{:S(2)}) collective-permute-start(f32[4,128,128]{2,1,0:T(8,128)S(1)} %apply_map.10), channel_id=1, source_target_pairs={{16,8},{20,12},{17,9},{21,13},{18,10},{22,14},{19,11},{23,15}} | collective-permute-start | bytes 786440 | tf_op jit(solution)/shard_map/ppermute | solution.py:1022
  156.9 14.2 %copy-start.32 = (f32[144,2048]{1,0:T(8,128)S(1)}, f32[144,2048]{1,0:T(8,128)}, u32[]{:S(2)}) copy-start(f32[144,2048]{1,0:T(8,128)} %get-tuple-element.206) | copy-start | bytes 3538948
  169.8 18.7 %copy-start.34 = (f32[80,2048]{1,0:T(8,128)S(1)}, f32[80,2048]{1,0:T(8,128)}, u32[]{:S(2)}) copy-start(f32[80,2048]{1,0:T(8,128)} %get-tuple-element.211) | copy-start | bytes 1966084
  170.8 31.4 %copy-start.20 = (f32[144,2048]{1,0:T(8,128)}, f32[144,2048]{1,0:T(8,128)S(1)}, u32[]{:S(2)}) copy-start(f32[144,2048]{1,0:T(8,128)S(1)} %collective-permute-done.15) | copy-start | bytes 3538948
  171.1 16.3 %collective-permute-start.19 = (f32[144,2048]{1,0:T(8,128)S(1)}, f32[144,2048]{1,0:T(8,128)S(1)}, u32[]{:S(2)}, u32[]{:S(2)}) collective-permute-start(f32[144,2048]{1,0:T(8,128)S(1)} %copy-done.32), channel_id=1, source_target_pairs={{0,4},{1,3},{2,6},{3,1},{4,0},{5,7},{6,2},{7,5},{8,12},{9,11},{10,... | collective-permute-start | bytes 3538952 | tf_op jit(solution)/shard_map/ppermute | solution.py:885
  172.6 12.9 %collective-permute-start.18 = (f32[4,128,128]{2,1,0:T(8,128)S(1)}, f32[4,128,128]{2,1,0:T(8,128)S(1)}, u32[]{:S(2)}, u32[]{:S(2)}) collective-permute-start(f32[4,128,128]{2,1,0:T(8,128)S(1)} %apply_map.11), channel_id=1, source_target_pairs={{8,0},{12,4},{9,1},{13,5},{10,2},{14,6},{11,3},{15,7}} | collective-permute-start | bytes 786440 | tf_op jit(solution)/shard_map/ppermute | solution.py:1022
  187.4 16.3 %copy-start.22 = (f32[144,2048]{1,0:T(8,128)}, f32[144,2048]{1,0:T(8,128)S(1)}, u32[]{:S(2)}) copy-start(f32[144,2048]{1,0:T(8,128)S(1)} %collective-permute-done.19) | copy-start | bytes 3538948
  188.5 13.7 %collective-permute-start.21 = (f32[80,2048]{1,0:T(8,128)S(1)}, f32[80,2048]{1,0:T(8,128)S(1)}, u32[]{:S(2)}, u32[]{:S(2)}) collective-permute-start(f32[80,2048]{1,0:T(8,128)S(1)} %copy-done.34), channel_id=1, source_target_pairs={{0,4},{1,3},{2,6},{3,1},{4,0},{5,7},{6,2},{7,5},{8,12},{9,11},{10,... | collective-permute-start | bytes 1966088 | tf_op jit(solution)/shard_map/ppermute | solution.py:885
  189.9 12.3 %collective-permute-start.20 = (f32[4,128,128]{2,1,0:T(8,128)S(1)}, f32[4,128,128]{2,1,0:T(8,128)S(1)}, u32[]{:S(2)}, u32[]{:S(2)}) collective-permute-start(f32[4,128,128]{2,1,0:T(8,128)S(1)} %get-tuple-element.210), channel_id=1, source_target_pairs={{0,4},{4,0},{8,12},{12,8},{16,20},{20,16},{24,28},{28,24},{1,5},{5... | collective-permute-start | bytes 786440 | tf_op jit(solution)/shard_map/ppermute | solution.py:881
  202.2 46.0 %collective-permute-start.22 = (f32[512,1792]{1,0:T(8,128)}, f32[512,1792]{1,0:T(8,128)}, u32[]{:S(2)}, u32[]{:S(2)}) collective-permute-start(f32[512,1792]{1,0:T(8,128)} %get-tuple-element.228), channel_id=1, source_target_pairs={{0,4},{1,3},{2,6},{3,1},{4,0},{5,7},{6,2},{7,5},{8,12},{9,11},{10,... | collective-permute-start | bytes 11010056 | tf_op jit(solution)/shard_map/ppermute | solution.py:885
  203.7 44.5 %collective-permute-start.23 = (f32[592,512]{1,0:T(8,128)}, f32[592,512]{1,0:T(8,128)S(1)}, u32[]{:S(2)}, u32[]{:S(2)}) collective-permute-start(f32[592,512]{1,0:T(8,128)} %get-tuple-element.229), channel_id=1, source_target_pairs={{0,8},{4,12},{8,0},{12,4},{16,24},{20,28},{24,16},{28,20},{1,9},{5... | collective-permute-start | bytes 3637256 | tf_op jit(solution)/shard_map/ppermute | solution.py:881
  210.9 33.2 %copy-start.21 = (f32[144,2048]{1,0:T(8,128)S(1)}, f32[144,2048]{1,0:T(8,128)}, u32[]{:S(2)}) copy-start(f32[144,2048]{1,0:T(8,128)} %copy-done.20) | copy-start | bytes 3538948
  210.9 33.2 %copy-start.23 = (f32[144,2048]{1,0:T(8,128)S(1)}, f32[144,2048]{1,0:T(8,128)}, u32[]{:S(2)}) copy-start(f32[144,2048]{1,0:T(8,128)} %copy-done.22) | copy-start | bytes 3538948
  248.7 7.7 %collective-permute-start.24 = (f32[3,8,1024]{2,1,0:T(8,128)S(1)}, f32[3,8,1024]{2,1,0:T(8,128)S(1)}, u32[]{:S(2)}, u32[]{:S(2)}) collective-permute-start(f32[3,8,1024]{2,1,0:T(8,128)S(1)} %copy-done.35), channel_id=1, source_target_pairs={{4,0},{8,4},{12,8},{16,12},{20,16},{24,20},{28,24},{5,1},{9,5},{13... | collective-permute-start | bytes 294920 | tf_op jit(solution)/shard_map/ppermute | solution.py:868
  256.9 15.4 %copy-start.2 = (bf16[3,384,1024]{2,1,0:T(8,128)(2,1)}, bf16[3,384,1024]{2,1,0:T(8,128)(2,1)S(1)}, u32[]{:S(2)}) copy-start(bf16[3,384,1024]{2,1,0:T(8,128)(2,1)S(1)} %convert_element_type.27.grads) | copy-start | bytes 7077892
  256.9 46.1 %collective-permute-start.27 = (f32[2,2,64,3840]{3,2,1,0:T(8,128)}, f32[2,2,64,3840]{3,2,1,0:T(8,128)}, u32[]{:S(2)}, u32[]{:S(2)}) collective-permute-start(f32[2,2,64,3840]{3,2,1,0:T(8,128)} %pad_maximum_fusion.1), channel_id=1, source_target_pairs={{0,2},{1,5},{2,0},{3,7},{4,6},{5,1},{6,4},{7,3},{8,10},{9,13},{10,... | collective-permute-start | bytes 11796488 | tf_op jit(solution)/shard_map/ppermute | solution.py:885
  258.2 36.2 %collective-permute-start.28 = (f32[816,512]{1,0:T(8,128)}, f32[816,512]{1,0:T(8,128)}, u32[]{:S(2)}, u32[]{:S(2)}) collective-permute-start(f32[816,512]{1,0:T(8,128)} %get-tuple-element.237), channel_id=1, source_target_pairs={{0,8},{4,12},{8,0},{12,4},{16,24},{20,28},{24,16},{28,20},{1,9},{5... | collective-permute-start | bytes 5013512 | tf_op jit(solution)/shard_map/ppermute | solution.py:881
  266.2 7.1 %collective-permute-start.25 = (f32[384,1024]{1,0:T(8,128)}, f32[384,1024]{1,0:T(8,128)}, u32[]{:S(2)}, u32[]{:S(2)}) collective-permute-start(f32[384,1024]{1,0:T(8,128)} %fusion), channel_id=1, source_target_pairs={{0,1},{1,0},{2,3},{3,2},{4,5},{5,4},{6,7},{7,6},{8,9},{9,8},{10,11... | collective-permute-start | bytes 4718600 | tf_op jit(solution)/shard_map/ppermute | solution.py:881
  267.7 5.6 %collective-permute-start.26 = (f32[384,512]{1,0:T(8,128)S(1)}, f32[384,512]{1,0:T(8,128)S(1)}, u32[]{:S(2)}, u32[]{:S(2)}) collective-permute-start(f32[384,512]{1,0:T(8,128)S(1)} %fusion.2), channel_id=1, source_target_pairs={{0,1},{1,0},{2,3},{3,2},{4,5},{5,4},{6,7},{7,6},{8,9},{9,8},{10,11... | collective-permute-start | bytes 2359304 | tf_op jit(solution)/shard_map/ppermute | solution.py:881
  273.2 29.7 %copy-start.19 = (f32[592,512]{1,0:T(8,128)S(1)}, f32[592,512]{1,0:T(8,128)}, u32[]{:S(2)}) copy-start(f32[592,512]{1,0:T(8,128)} %copy-done.18) | copy-start | bytes 3637252
  308.8 12.8 %copy-start.31 = (f32[3,4,1024]{2,1,0:T(4,128)S(1)}, f32[3,4,1024]{2,1,0:T(4,128)}, u32[]{:S(2)}) copy-start(f32[3,4,1024]{2,1,0:T(4,128)} %get-tuple-element.251) | copy-start | bytes 147460
  308.8 12.8 %copy-start.3 = (f32[1024,384]{1,0:T(8,128)S(1)}, f32[1024,384]{1,0:T(8,128)}, u32[]{:S(2)}) copy-start(f32[1024,384]{1,0:T(8,128)} %get-tuple-element.197.refs_5_.refs_1_.refs_3_) | copy-start | bytes 4718596
  308.8 12.8 %copy-start.24 = (f32[384,8]{1,0:T(8,128)S(1)}, f32[384,8]{1,0:T(8,128)}, u32[]{:S(2)}) copy-start(f32[384,8]{1,0:T(8,128)} %get-tuple-element.249.grad_beta) | copy-start | bytes 36868
  310.2 54.3 %collective-permute-start.31 = (f32[512,1536]{1,0:T(8,128)}, f32[512,1536]{1,0:T(8,128)}, u32[]{:S(2)}, u32[]{:S(2)}) collective-permute-start(f32[512,1536]{1,0:T(8,128)} %get-tuple-element.245), channel_id=1, source_target_pairs={{0,4},{1,3},{2,6},{3,1},{4,0},{5,7},{6,2},{7,5},{8,12},{9,11},{10,... | collective-permute-start | bytes 9437192 | tf_op jit(solution)/shard_map/ppermute | solution.py:885
  313.6 51.0 %collective-permute-start.29 = (f32[2,64,3840]{2,1,0:T(8,128)}, f32[2,64,3840]{2,1,0:T(8,128)}, u32[]{:S(2)}, u32[]{:S(2)}) collective-permute-start(f32[2,64,3840]{2,1,0:T(8,128)} %maximum_add_fusion), channel_id=1, source_target_pairs={{0,8},{1,17},{2,10},{3,19},{4,12},{5,21},{6,14},{7,23},{8,0},{9,25... | collective-permute-start | bytes 5898248 | tf_op jit(solution)/shard_map/ppermute | solution.py:885
  320.3 44.3 %collective-permute-start.30 = (f32[2,2,176,512]{3,2,1,0:T(8,128)}, f32[2,2,176,512]{3,2,1,0:T(8,128)}, u32[]{:S(2)}, u32[]{:S(2)}) collective-permute-start(f32[2,2,176,512]{3,2,1,0:T(8,128)} %add_bitcast_fusion.3), channel_id=1, source_target_pairs={{0,4},{1,3},{2,6},{3,1},{4,0},{5,7},{6,2},{7,5},{8,12},{9,11},{10,... | collective-permute-start | bytes 4325384 | tf_op jit(solution)/shard_map/ppermute | solution.py:885
  327.8 36.8 %copy-start.7 = (f32[1408,512]{1,0:T(8,128)S(1)}, f32[1408,512]{1,0:T(8,128)}, u32[]{:S(2)}) copy-start(f32[1408,512]{1,0:T(8,128)} %copy-done.6) | copy-start | bytes 8650756
  372.9 34.3 %collective-permute-start.32 = (f32[2,2,64,1536]{3,2,1,0:T(8,128)}, f32[2,2,64,1536]{3,2,1,0:T(8,128)}, u32[]{:S(2)}, u32[]{:S(2)}) collective-permute-start(f32[2,2,64,1536]{3,2,1,0:T(8,128)} %add_bitcast_fusion.2), channel_id=1, source_target_pairs={{0,2},{1,5},{2,0},{3,7},{4,6},{5,1},{6,4},{7,3},{8,10},{9,13},{10,... | collective-permute-start | bytes 4718600 | tf_op jit(solution)/shard_map/ppermute | solution.py:885
  374.2 33.1 %collective-permute-start.33 = (f32[64,3840]{1,0:T(8,128)}, f32[64,3840]{1,0:T(8,128)}, u32[]{:S(2)}, u32[]{:S(2)}) collective-permute-start(f32[64,3840]{1,0:T(8,128)} %maximum_add_fusion.1), channel_id=1, source_target_pairs={{0,16},{1,9},{2,18},{3,11},{4,20},{5,13},{6,22},{7,15},{8,24},{9,1... | collective-permute-start | bytes 2949128 | tf_op jit(solution)/shard_map/ppermute | solution.py:885
  384.3 17.1 %collective-permute-start.34 = (f32[2,176,512]{2,1,0:T(8,128)}, f32[2,176,512]{2,1,0:T(8,128)}, u32[]{:S(2)}, u32[]{:S(2)}) collective-permute-start(f32[2,176,512]{2,1,0:T(8,128)} %bitcast_add_fusion.3), channel_id=1, source_target_pairs={{0,2},{1,5},{2,0},{3,7},{4,6},{5,1},{6,4},{7,3},{8,10},{9,13},{10,... | collective-permute-start | bytes 2162696 | tf_op jit(solution)/shard_map/ppermute | solution.py:885
  385.1 1.3 collective-permute-start.35
  415.1 21.5 %collective-permute-start.38 = (f32[64,3840]{1,0:T(8,128)}, f32[64,3840]{1,0:T(8,128)}, u32[]{:S(2)}, u32[]{:S(2)}) collective-permute-start(f32[64,3840]{1,0:T(8,128)} %maximum_add_fusion.2), channel_id=1, source_target_pairs={{0,2},{1,3},{2,0},{3,1},{4,6},{5,7},{6,4},{7,5},{8,10},{9,11},{10,... | collective-permute-start | bytes 2949128 | tf_op jit(solution)/shard_map/ppermute | solution.py:881
  415.9 20.7 %collective-permute-start.36 = (f32[2,64,1536]{2,1,0:T(8,128)}, f32[2,64,1536]{2,1,0:T(8,128)}, u32[]{:S(2)}, u32[]{:S(2)}) collective-permute-start(f32[2,64,1536]{2,1,0:T(8,128)} %bitcast_add_fusion.2), channel_id=1, source_target_pairs={{0,8},{1,17},{2,10},{3,19},{4,12},{5,21},{6,14},{7,23},{8,0},{9,25... | collective-permute-start | bytes 2359304 | tf_op jit(solution)/shard_map/ppermute | solution.py:885
  417.2 17.1 %collective-permute-start.37 = (f32[176,512]{1,0:T(8,128)}, f32[176,512]{1,0:T(8,128)S(1)}, u32[]{:S(2)}, u32[]{:S(2)}) collective-permute-start(f32[176,512]{1,0:T(8,128)} %fusion.10), channel_id=1, source_target_pairs={{0,16},{4,20},{8,24},{12,28},{16,0},{20,4},{24,8},{28,12},{1,17},{... | collective-permute-start | bytes 1081352 | tf_op jit(solution)/shard_map/ppermute | solution.py:881
  422.7 4.3 collective-permute-start.39
  443.4 18.9 %collective-permute-start.42 = (f32[128,3840]{1,0:T(8,128)}, f32[128,3840]{1,0:T(8,128)}, u32[]{:S(2)}, u32[]{:S(2)}) collective-permute-start(f32[128,3840]{1,0:T(8,128)} %pad_maximum_fusion.3), channel_id=1, source_target_pairs={{0,1},{1,0},{2,3},{3,2},{4,5},{5,4},{6,7},{7,6},{8,9},{9,8},{10,11... | collective-permute-start | bytes 5898248 | tf_op jit(solution)/shard_map/ppermute | solution.py:881
  450.0 12.3 %collective-permute-start.40 = (f32[64,1536]{1,0:T(8,128)}, f32[64,1536]{1,0:T(8,128)S(1)}, u32[]{:S(2)}, u32[]{:S(2)}) collective-permute-start(f32[64,1536]{1,0:T(8,128)} %fusion.7), channel_id=1, source_target_pairs={{0,16},{1,9},{2,18},{3,11},{4,20},{5,13},{6,22},{7,15},{8,24},{9,1... | collective-permute-start | bytes 1179656 | tf_op jit(solution)/shard_map/ppermute | solution.py:885
  453.9 7.4 %collective-permute-start.41 = (f32[176,512]{1,0:T(8,128)S(1)}, f32[176,512]{1,0:T(8,128)S(1)}, u32[]{:S(2)}, u32[]{:S(2)}) collective-permute-start(f32[176,512]{1,0:T(8,128)S(1)} %fusion.9), channel_id=1, source_target_pairs={{0,2},{1,3},{2,0},{3,1},{4,6},{5,7},{6,4},{7,5},{8,10},{9,11},{10,... | collective-permute-start | bytes 1081352 | tf_op jit(solution)/shard_map/ppermute | solution.py:881
  454.9 5.8 %collective-permute-start.43 = (f32[2,32,128]{2,1,0:T(8,128)S(1)}, f32[2,32,128]{2,1,0:T(8,128)S(1)}, u32[]{:S(2)}, u32[]{:S(2)}) collective-permute-start(f32[2,32,128]{2,1,0:T(8,128)S(1)} %bitcast_add_fusion.8), channel_id=1, source_target_pairs={{0,8},{4,12},{8,0},{12,4},{16,24},{20,28},{24,16},{28,20},{1,9},{5... | collective-permute-start | bytes 98312 | tf_op jit(solution)/shard_map/ppermute | solution.py:881
  463.9 7.6 %collective-permute-start.46 = (f32[32,128]{1,0:T(8,128)S(1)}, f32[32,128]{1,0:T(8,128)S(1)}, u32[]{:S(2)}, u32[]{:S(2)}) collective-permute-start(f32[32,128]{1,0:T(8,128)S(1)} %bitcast_add_fusion.9), channel_id=1, source_target_pairs={{0,16},{4,20},{8,24},{12,28},{16,0},{20,4},{24,8},{28,12},{1,17},{... | collective-permute-start | bytes 49160 | tf_op jit(solution)/shard_map/ppermute | solution.py:881
  468.8 10.6 %collective-permute-start.44 = (f32[64,1536]{1,0:T(8,128)S(1)}, f32[64,1536]{1,0:T(8,128)S(1)}, u32[]{:S(2)}, u32[]{:S(2)}) collective-permute-start(f32[64,1536]{1,0:T(8,128)S(1)} %fusion.6), channel_id=1, source_target_pairs={{0,2},{1,3},{2,0},{3,1},{4,6},{5,7},{6,4},{7,5},{8,10},{9,11},{10,... | collective-permute-start | bytes 1179656 | tf_op jit(solution)/shard_map/ppermute | solution.py:881
  469.7 9.6 %collective-permute-start.45 = (f32[352,512]{1,0:T(8,128)S(1)}, f32[352,512]{1,0:T(8,128)S(1)}, u32[]{:S(2)}, u32[]{:S(2)}) collective-permute-start(f32[352,512]{1,0:T(8,128)S(1)} %pad_maximum_fusion.6), channel_id=1, source_target_pairs={{0,1},{1,0},{2,3},{3,2},{4,5},{5,4},{6,7},{7,6},{8,9},{9,8},{10,11... | collective-permute-start | bytes 2162696 | tf_op jit(solution)/shard_map/ppermute | solution.py:881
  479.5 8.0 %collective-permute-start.47 = (f32[128,1536]{1,0:T(8,128)S(1)}, f32[128,1536]{1,0:T(8,128)S(1)}, u32[]{:S(2)}, u32[]{:S(2)}) collective-permute-start(f32[128,1536]{1,0:T(8,128)S(1)} %pad_maximum_fusion.5), channel_id=1, source_target_pairs={{0,1},{1,0},{2,3},{3,2},{4,5},{5,4},{6,7},{7,6},{8,9},{9,8},{10,11... | collective-permute-start | bytes 2359304 | tf_op jit(solution)/shard_map/ppermute | solution.py:881
  483.8 3.7 collective-permute-start.48
  (24 other events, 89.4 us)

commit v7 on v6

--- a/solution.py
+++ b/solution.py
@@ -176,12 +176,13 @@
         normed[:HALO, :] = norm(halo[...])
         rounded = norm(tokens[...].astype(jnp.float32))
         normed[HALO:, :] = rounded
-        normed_out[...] = rounded.astype(jnp.float32).T
         beta_pre = mxu(rounded, beta_w[...], NT)
         beta_pre_out[...] = beta_pre
         position[...], live[...] = token_places(docs, count)
         beta_out[...] = sigmoid(beta_pre) * live[...]
 
+    lanes = pl.ds(pl.multiple_of(pl.program_id(0) * normed_out.shape[0], LANES), normed_out.shape[0])
+    normed_out[...] = normed[HALO:, lanes].astype(jnp.float32).T
     gate_out[...] = mxu(normed[HALO:, :], gate_w[...], NN)
     valid = [
         jnp.broadcast_to(
@@ -233,7 +234,7 @@
             pl.BlockSpec((3, conv.shape[1], block), lambda j: (0, 0, j)),
         ],
         out_specs=[
-            whole((width, count)),
+            pl.BlockSpec((block, count), lambda j: (j, 0)),
             pl.BlockSpec((3, count // SPAN, SPAN + 8, block), lambda j: (0, 0, 0, j)),
             pl.BlockSpec((3, count, block), lambda j: (0, 0, j)),
             pl.BlockSpec((count, block), lambda j: (0, j)),
@@ -414,8 +415,6 @@
             state * lax.rsqrt(jnp.mean(state * state, -1, keepdims=True) + EPS) * second_gain[...]
         ).astype(LOW)
         normed[...] = rounded
-        normed_out[...] = rounded.astype(jnp.float32).T
-        head_turned_out[...] = normed_head[...].astype(jnp.float32).T
 
     @pl.when(step == 0)
     def _():
@@ -425,6 +424,12 @@
     first = core[0] == 0
     size = normed.shape[0] // 1
     parts = [slice(i * size, (i + 1) * size) for i in range(1)]
+    @pl.when(step < normed.shape[1] // LANES)
+    def _():
+        lanes = pl.ds(pl.multiple_of(step * LANES, LANES), LANES)
+        normed_out[...] = normed[:, lanes].astype(jnp.float32).T
+        head_turned_out[...] = normed_head[:, lanes].astype(jnp.float32).T
+
     gates = [mxu(normed[part, :], gate_w[...], NN) for part in parts]
     ups = [mxu(normed[part, :], up_w[...], NN) for part in parts]
     grad_inners = [mxu(grad_top[part, :], down_w[...], NT) for part in parts]
@@ -450,7 +455,7 @@
         grad_hidden = grad_top[...].astype(jnp.float32) + part
         grad_hidden_out[...] = grad_hidden
         branch = grad_hidden.astype(LOW)
-        branch_out[...] = branch.astype(jnp.float32)
+        branch_out[...] = branch
         grad_head_out[...] = mxu(branch, out_w[...], NT)
 
 
@@ -471,6 +476,7 @@
     low = lambda shape: jax.ShapeDtypeStruct(shape, LOW)
     rows = whole((count, width))
     columns = pl.BlockSpec((count, block), lambda j: (0, j))
+    turned = pl.BlockSpec((LANES, count), lambda j: (jnp.minimum(j, width // LANES - 1), 0))
     return pl.pallas_call(
         feed_kernel,
         grid=(hidden // block,),
@@ -481,12 +487,12 @@
             pl.BlockSpec((block, width), lambda j: (j, 0)),
         ],
         out_specs=[
-            rows, whole((width, count)), pl.BlockSpec((block, count), lambda j: (j, 0)), columns,
-            columns, rows, rows, rows, whole((1, width)), whole((width, count)),
+            rows, turned, pl.BlockSpec((block, count), lambda j: (j, 0)), columns,
+            columns, rows, rows, rows, whole((1, width)), turned,
         ],
         out_shape=[
             low((count, width)), f32((width, count)), f32((hidden, count)), low((count, hidden)),
-            f32((count, hidden)), f32((count, width)), f32((count, width)), f32((count, width)),
+            f32((count, hidden)), f32((count, width)), low((count, width)), f32((count, width)),
             f32((1, width)), f32((width, count)),
         ],
         scratch_shapes=[
@@ -559,6 +565,7 @@
     first = core[0] == 0
     for place, source in ((0, grad_branch), (half, grad_gate_out)):
         low, high = source[:, :half], source[:, half:]
+        low, high = low.astype(jnp.float32), high.astype(jnp.float32)
         kept_out[:, place : place + half] = jnp.where(first, low, high).astype(LOW)
         sent_out[:, place : place + half] = jnp.where(first, high, low)
 

time: 500 us -> 500 us (level)
  no operation moved by 1% of the time
where the time goes in v7:
time: 500 us; the launch traced here: 493 us
  Pallas kernels  161 us (32%)
  waiting for transfers between devices  149 us (30%)
  starting transfers between devices  94.3 us (19%)
  other arithmetic  64.7 us (13%)
  local copies, waits for them, and re-layouts  22.4 us (4%)
    ppermute x14, waiting for transfers between devices, hop(): return lax.ppermute(value, ('seq', 'doc'), pairs)  64.9 us
    ppermute x27, waiting for transfers between devices, hop(): lax.ppermute(value, axis, [(i, i ^ bit) for i in range(lax.axis_size(axis...  64.8 us
    ppermute x27, starting transfers between devices, hop(): lax.ppermute(value, axis, [(i, i ^ bit) for i in range(lax.axis_size(axis...  43 us
    pallas_call x4, Pallas kernels, outer(): pl.pallas_call(lambda *refs: outer_kernel(*refs, blocks=counts, pieces=si...  39 us
    ppermute x14, starting transfers between devices, hop(): return lax.ppermute(value, ('seq', 'doc'), pairs)  36.1 us
    pallas_call x1, Pallas kernels, back(): pl.pallas_call(back_kernel, grid=(spans,), in_specs=[pl.BlockSpec(memory_...  33.2 us
    pallas_call x1, Pallas kernels, feed(): pl.pallas_call(feed_kernel, grid=(hidden // block,), in_specs=[pl.BlockSp...  27.4 us
    add x11, other arithmetic, chosen(): return total + self.added(self.terms, here) if self.terms else total  22 us
  transfers between devices with their start and end apart: 49, of which 24 were waited for; matrix products, arithmetic and copies ran while one was open for 8% of the time, Pallas kernels for 22%

profile of v7, /device:TPU:0, one launch (start us, length us, event | category | flops | bytes accessed | tf_op | source)
XLA Modules:
  0.0 493.3 jit_solution(15002232677714802912)
XLA Ops:
  1.4 4.8 collective-permute-start
  8.8 13.0 %project.1 = (f32[1024,384]{1,0:T(8,128)}, f32[3,6,72,1024]{3,2,1,0:T(8,128)}, f32[3,384,1024]{2,1,0:T(8,128)}, f32[384,1024]{1,0:T(8,128)}, f32[384,8]{1,0:T(8,...) custom-call(s32[5]{0:T(128)} %pad_add_fusion.docs, bf16[384,1024]{1,0:T(8,128)(2,1)} %bitcast.186, ...), custom_call_target="tpu_custom_call" | custom-call | flops 1 | bytes 1 | tf_op jit(solution)/shard_map/project/pallas_call | solution.py:228
  22.7 17.2 %prepare.1 = (f32[2,384,1024]{2,1,0:T(8,128)}, f32[6,4,128,128]{3,2,1,0:T(8,128)}, f32[6,4,128,128]{3,2,1,0:T(8,128)}, f32[8,128,256]{2,1,0:T(8,128)}) custom-call(s32[5]{0:T(128)} %pad_add_fusion.docs, f32[3,384,1024]{2,1,0:T(8,128)} %get-tuple-element.155.features, f32[384,8]{1,0:T(8,128)} %get-tuple-element.156.beta), custom_call_target="tpu_custom_call" | custom-call | flops 1 | bytes 1 | tf_op jit(solution)/shard_map/prepare/pallas_call | solution.py:312
  41.3 2.4 collective-permute-start.1
  44.5 11.4 %collective-permute-done.1 = f32[4,128,256]{2,1,0:T(8,128)S(1)} collective-permute-done((f32[4,128,256]{2,1,0:T(8,128)S(1)}, f32[4,128,256]{2,1,0:T(8,128)S(1)}, u32[]{:S(2)}, u32[]{:S(2)}) %collective-permute-start.1) | collective-permute-done | bytes 524320 | tf_op jit(solution)/shard_map/ppermute | solution.py:888
  57.2 4.6 collective-permute-start.4
  61.8 4.9 collective-permute-done.4.refs_3_.refs_2_
  70.5 5.9 %collective-permute-done.7.state_other = f32[4,128,128]{2,1,0:T(8,128)S(1)} collective-permute-done((f32[4,128,128]{2,1,0:T(8,128)S(1)}, f32[4,128,128]{2,1,0:T(8,128)S(1)}, u32[]{:S(2)}, u32[]{:S(2)}) %collective-permute-start.7) | collective-permute-done | bytes 262176 | tf_op jit(solution)/shard_map/ppermute | solution.py:888
  77.0 8.9 %mix.1 = (f32[6,8,128,128]{3,2,1,0:T(8,128)}, f32[384,1024]{1,0:T(8,128)}, f32[384,1024]{1,0:T(8,128)}, bf16[384,1024]{1,0:T(8,128)(2,1)}) custom-call(s32[5]{0:T(128)} %pad_add_fusion.docs, s32[1]{0:T(128)} %bitcast.4.refs_0_.place, f32[3,384,1024]{2,1,0:T(8,128)} %get-tuple-element.155.features, f32[2,384,1024]{2,1,0:T(8,128)} %get-tuple-element.157.solved, ...), custom_call_target="tpu_custom_call" | custom-call | flops 1 | bytes 1 | tf_op jit(solution)/shard_map/mix/pallas_call | solution.py:379
  85.9 27.4 %feed.1 = (bf16[384,1024]{1,0:T(8,128)(2,1)}, f32[1024,384]{1,0:T(8,128)}, f32[2816,384]{1,0:T(8,128)}, bf16[384,2816]{1,0:T(8,128)(2,1)}, f32[384,2816]{1,0:T(8...) custom-call(s32[1]{0:T(128)} %bitcast.core, ...), custom_call_target="tpu_custom_call" | custom-call | flops 1 | bytes 1 | tf_op jit(solution)/shard_map/feed/pallas_call | solution.py:480
  113.9 9.5 %gather_states.1 = (f32[384,1024]{1,0:T(8,128)}, f32[384,1024]{1,0:T(8,128)}, bf16[384,1024]{1,0:T(8,128)(2,1)}, f32[384,1024]{1,0:T(8,128)}, f32[1,128]{1,0:T(1,128)}, /*index=5*/f32[8,128,128]{2,1,0:T(8,128)}) custom-call(s32[5]{0:T(128)} %pad_add_fusion.docs, s32[1]{0:T(128)} %bitcast.core, f32[384,1024]{1,0:T(8,128)} %get-tuple-element.168.grad_head, ...), custom_call_target="tpu_custom_call" | custom-call | flops 1 | bytes 1 | tf_op jit(solution)/shard_map/gather_states/pallas_call | solution.py:583
  123.5 2.2 slice_select_fusion.6
  127.0 9.1 %outer.4 = (f32[512,2048]{1,0:T(8,128)}, f32[144,2048]{1,0:T(8,128)}, f32[144,2048]{1,0:T(8,128)}, f32[144,2048]{1,0:T(8,128)}, f32[80,2048]{1,0:T(8,128)}) custom-call(s32[16]{0:T(128)} %stack.152.refs_0_, f32[1024,384]{1,0:T(8,128)} %get-tuple-element.167.refs_1_, f32[1024,384]{1,0:T(8,128)} %copy-done.9, ...), custom_call_target="tpu_custom_call" | custom-call | flops 1 | bytes 1 | tf_op jit(solution)/shard_map/outer/pallas_call | solution.py:1104
  140.7 7.7 %outer.5 = (f32[1408,512]{1,0:T(8,128)}, f32[592,512]{1,0:T(8,128)}, f32[816,512]{1,0:T(8,128)}) custom-call(s32[16]{0:T(128)} %stack.169.refs_0_, f32[2816,384]{1,0:T(8,128)} %get-tuple-element.186.refs_1_, f32[2816,384]{1,0:T(8,128)} %collective-permute-done.13.refs_2_, bf16[384,512]{1,0:T(8,128)(2,1)} %slice_select_fusion.5.refs_3_, f32[384,512]{1,0:T(8,128)} %copy-done.25), custom_call_target="tpu_custom_call" | custom-call | flops 1 | bytes 1 | tf_op jit(solution)/shard_map/outer/pallas_call | solution.py:1104
  148.5 5.4 %collective-permute-done.12 = f32[144,2048]{1,0:T(8,128)S(1)} collective-permute-done((f32[144,2048]{1,0:T(8,128)}, f32[144,2048]{1,0:T(8,128)S(1)}, u32[]{:S(2)}, u32[]{:S(2)}) %collective-permute-start.12) | collective-permute-done | bytes 1179680 | tf_op jit(solution)/shard_map/ppermute | solution.py:892
  156.6 12.8 %outer.6 = (f32[512,1792]{1,0:T(8,128)}, f32[512,1792]{1,0:T(8,128)}) custom-call(s32[16]{0:T(128)} %stack.152.refs_0_, f32[1024,384]{1,0:T(8,128)} %get-tuple-element.167.refs_1_, f32[1024,384]{1,0:T(8,128)} %copy-done.9, f32[1024,384]{1,0:T(8,128)} %get-tuple-element.196.refs_3_, f32[1024,384]{1,0:T(8,128)} %collective-permute-done.16.refs_4_, ...), custom_call_target="tpu_custom_call" | custom-call | flops 1 | bytes 1 | tf_op jit(solution)/shard_map/outer/pallas_call | solution.py:1104
  173.5 11.6 %collective-permute-done.18.refs_4_ = f32[4,128,128]{2,1,0:T(8,128)S(1)} collective-permute-done((f32[4,128,128]{2,1,0:T(8,128)S(1)}, f32[4,128,128]{2,1,0:T(8,128)S(1)}, u32[]{:S(2)}, u32[]{:S(2)}) %collective-permute-start.18) | collective-permute-done | bytes 262176 | tf_op jit(solution)/shard_map/ppermute | solution.py:1029
  185.1 1.9 collective-permute-done.19
  190.1 11.7 %collective-permute-done.20.state_other = f32[4,128,128]{2,1,0:T(8,128)S(1)} collective-permute-done((f32[4,128,128]{2,1,0:T(8,128)S(1)}, f32[4,128,128]{2,1,0:T(8,128)S(1)}, u32[]{:S(2)}, u32[]{:S(2)}) %collective-permute-start.20) | collective-permute-done | bytes 262176 | tf_op jit(solution)/shard_map/ppermute | solution.py:888
  201.8 1.5 collective-permute-start.22
  203.3 7.2 %collective-permute-start.23 = (f32[592,512]{1,0:T(8,128)}, f32[592,512]{1,0:T(8,128)S(1)}, u32[]{:S(2)}, u32[]{:S(2)}) collective-permute-start(f32[592,512]{1,0:T(8,128)} %get-tuple-element.229), channel_id=1, source_target_pairs={{0,8},{4,12},{8,0},{12,4},{16,24},{20,28},{24,16},{28,20},{1,9},{5... | collective-permute-start | bytes 3637256 | tf_op jit(solution)/shard_map/ppermute | solution.py:888
  210.6 33.2 %back.1 = (f32[3,384,1024]{2,1,0:T(8,128)}, f32[3,8,1024]{2,1,0:T(8,128)}, f32[3,4,1024]{2,1,0:T(4,128)}, f32[384,8]{1,0:T(8,128)}) custom-call(s32[5]{0:T(128)} %pad_add_fusion.docs, s32[1]{0:T(128)} %bitcast.4.refs_0_.place, f32[3,384,1024]{2,1,0:T(8,128)} %get-tuple-element.155.features, f32[384,8]{1,0:T(8,128)} %get-tuple-element.156.beta, ...), custom_call_target="tpu_custom_call" | custom-call | flops 1 | bytes 1 | tf_op jit(solution)/shard_map/back/pallas_call | solution.py:786
  244.1 3.3 copy-done.10
  250.0 1.9 add_bitcast_fusion.1
  252.0 2.2 pad_maximum_fusion.1
  254.1 2.0 collective-permute-done.24
  257.8 4.8 collective-permute-start.28
  263.1 1.6 fusion
  265.8 1.5 fusion.2
  267.9 1.7 add_bitcast_fusion.4
  269.6 1.6 add_bitcast_fusion.5
  273.8 9.4 %outer.7 = (f32[512,1536]{1,0:T(8,128)}, f32[512,1536]{1,0:T(8,128)}) custom-call(s32[16]{0:T(128)} %stack.152.refs_0_, f32[1024,384]{1,0:T(8,128)} %get-tuple-element.197.refs_5_.refs_1_.refs_3_, f32[1024,384]{1,0:T(8,128)} %collective-permute-done.3.refs_6_.refs_2_.refs_4_, f32[1024,384]{1,0:T(8,128)} %get-tuple-element.197.refs_5_.refs_1_.refs_3_, ...), custom_call_target="tpu_custom_call" | custom-call | flops 1 | bytes 1 | tf_op jit(solution)/shard_map/outer/pallas_call | solution.py:1104
  283.1 10.8 %collective-permute-done.28 = f32[816,512]{1,0:T(8,128)} collective-permute-done((f32[816,512]{1,0:T(8,128)}, f32[816,512]{1,0:T(8,128)}, u32[]{:S(2)}, u32[]{:S(2)}) %collective-permute-start.28) | collective-permute-done | bytes 1671200 | tf_op jit(solution)/shard_map/ppermute | solution.py:888
  294.0 8.6 %collective-permute-done.27 = f32[2,2,64,3840]{3,2,1,0:T(8,128)} collective-permute-done((f32[2,2,64,3840]{3,2,1,0:T(8,128)}, f32[2,2,64,3840]{3,2,1,0:T(8,128)}, u32[]{:S(2)}, u32[]{:S(2)}) %collective-permute-start.27) | collective-permute-done | bytes 3932192 | tf_op jit(solution)/shard_map/ppermute | solution.py:892
  302.6 1.7 pad_maximum_fusion.2
  304.3 4.1 maximum_add_fusion
  309.9 3.3 collective-permute-start.31
  313.2 6.7 %collective-permute-start.29 = (f32[2,64,3840]{2,1,0:T(8,128)}, f32[2,64,3840]{2,1,0:T(8,128)}, u32[]{:S(2)}, u32[]{:S(2)}) collective-permute-start(f32[2,64,3840]{2,1,0:T(8,128)} %maximum_add_fusion), channel_id=1, source_target_pairs={{0,8},{1,17},{2,10},{3,19},{4,12},{5,21},{6,14},{7,23},{8,0},{9,25... | collective-permute-start | bytes 5898248 | tf_op jit(solution)/shard_map/ppermute | solution.py:892
  322.5 2.4 add_bitcast_fusion.6
  324.9 2.4 add_bitcast_fusion.8
  327.4 10.5 %enter.1 = (bf16[384,1024]{1,0:T(8,128)(2,1)}, f32[1,1024]{1,0:T(1,128)}) custom-call(bf16[384,1024]{1,0:T(8,128)(2,1)} %bitcast.188, f32[1,1024]{1,0:T(1,128)} %bitcast.221, f32[384,1024]{1,0:T(8,128)} %get-tuple-element.246.grad_hidden, bf16[3,384,1024]{2,1,0:T(8,128)(2,1)} %copy-done.2, f32[384,1024]{1,0:T(8,128)} %get-tuple-element.248.grad_gate, ...), custom_call_target="tpu_custom_call" | custom-call | flops 1 | bytes 1 | tf_op jit(solution)/shard_map/enter/pallas_call | solution.py:849
  340.4 23.8 %collective-permute-done.30 = f32[2,2,176,512]{3,2,1,0:T(8,128)} collective-permute-done((f32[2,2,176,512]{3,2,1,0:T(8,128)}, f32[2,2,176,512]{3,2,1,0:T(8,128)}, u32[]{:S(2)}, u32[]{:S(2)}) %collective-permute-start.30) | collective-permute-done | bytes 1441824 | tf_op jit(solution)/shard_map/ppermute | solution.py:892
  364.2 2.4 bitcast_add_fusion.3
  366.6 3.3 add_bitcast_fusion.2
  369.9 2.6 maximum_add_fusion.1
  373.8 10.2 %collective-permute-start.33 = (f32[64,3840]{1,0:T(8,128)}, f32[64,3840]{1,0:T(8,128)}, u32[]{:S(2)}, u32[]{:S(2)}) collective-permute-start(f32[64,3840]{1,0:T(8,128)} %maximum_add_fusion.1), channel_id=1, source_target_pairs={{0,16},{1,9},{2,18},{3,11},{4,20},{5,13},{6,22},{7,15},{8,24},{9,1... | collective-permute-start | bytes 2949128 | tf_op jit(solution)/shard_map/ppermute | solution.py:892
  386.1 14.9 %collective-permute-done.34 = f32[2,176,512]{2,1,0:T(8,128)} collective-permute-done((f32[2,176,512]{2,1,0:T(8,128)}, f32[2,176,512]{2,1,0:T(8,128)}, u32[]{:S(2)}, u32[]{:S(2)}) %collective-permute-start.34) | collective-permute-done | bytes 720928 | tf_op jit(solution)/shard_map/ppermute | solution.py:892
  401.0 5.9 %collective-permute-done.33 = f32[64,3840]{1,0:T(8,128)} collective-permute-done((f32[64,3840]{1,0:T(8,128)}, f32[64,3840]{1,0:T(8,128)}, u32[]{:S(2)}, u32[]{:S(2)}) %collective-permute-start.33) | collective-permute-done | bytes 983072 | tf_op jit(solution)/shard_map/ppermute | solution.py:892
  407.0 2.7 bitcast_add_fusion.2
  409.7 2.1 fusion.10
  411.8 3.0 maximum_add_fusion.2
  416.8 5.5 %collective-permute-start.37 = (f32[176,512]{1,0:T(8,128)}, f32[176,512]{1,0:T(8,128)S(1)}, u32[]{:S(2)}, u32[]{:S(2)}) collective-permute-start(f32[176,512]{1,0:T(8,128)} %fusion.10), channel_id=1, source_target_pairs={{0,16},{4,20},{8,24},{12,28},{16,0},{20,4},{24,8},{28,12},{1,17},{... | collective-permute-start | bytes 1081352 | tf_op jit(solution)/shard_map/ppermute | solution.py:888
  423.5 3.1 collective-permute-done.39
  426.6 7.4 %collective-permute-done.37 = f32[176,512]{1,0:T(8,128)S(1)} collective-permute-done((f32[176,512]{1,0:T(8,128)}, f32[176,512]{1,0:T(8,128)S(1)}, u32[]{:S(2)}, u32[]{:S(2)}) %collective-permute-start.37) | collective-permute-done | bytes 360480 | tf_op jit(solution)/shard_map/ppermute | solution.py:888
  434.0 2.3 collective-permute-done.36
  436.2 2.2 fusion.7
  439.9 1.6 broadcast_select_fusion.3
  443.0 6.6 %collective-permute-start.42 = (f32[128,3840]{1,0:T(8,128)}, f32[128,3840]{1,0:T(8,128)}, u32[]{:S(2)}, u32[]{:S(2)}) collective-permute-start(f32[128,3840]{1,0:T(8,128)} %pad_maximum_fusion.3), channel_id=1, source_target_pairs={{0,1},{1,0},{2,3},{3,2},{4,5},{5,4},{6,7},{7,6},{8,9},{9,8},{10,11... | collective-permute-start | bytes 5898248 | tf_op jit(solution)/shard_map/ppermute | solution.py:888
  449.6 4.0 collective-permute-start.40
  454.5 2.5 collective-permute-start.43
  457.0 3.3 collective-permute-done.43
  463.6 4.8 collective-permute-start.46
  469.4 1.8 broadcast_select_fusion.1
  471.2 7.8 %collective-permute-done.44 = f32[64,1536]{1,0:T(8,128)S(1)} collective-permute-done((f32[64,1536]{1,0:T(8,128)S(1)}, f32[64,1536]{1,0:T(8,128)S(1)}, u32[]{:S(2)}, u32[]{:S(2)}) %collective-permute-start.44) | collective-permute-done | bytes 393248 | tf_op jit(solution)/shard_map/ppermute | solution.py:888
  (218 shorter events, 72.7 us)
Async XLA Ops:
  1.4 6.7 %collective-permute-start = (f32[16,1024]{1,0:T(8,128)S(1)}, f32[16,1024]{1,0:T(8,128)S(1)}, u32[]{:S(2)}, u32[]{:S(2)}) collective-permute-start(f32[16,1024]{1,0:T(8,128)S(1)} %bitcast_convert_fusion), channel_id=1, source_target_pairs={{0,4},{4,8},{8,12},{12,16},{16,20},{20,24},{24,28},{1,5},{5,9},{9,... | collective-permute-start | bytes 196616 | tf_op jit(solution)/shard_map/ppermute | solution.py:875
  8.8 13.1 %copy-start.8 = (bf16[1,384,1024]{2,1,0:T(8,128)(2,1)S(1)}, bf16[1,384,1024]{2,1,0:T(8,128)(2,1)}, u32[]{:S(2)}) copy-start(bf16[1,384,1024]{2,1,0:T(8,128)(2,1)} %param.18) | copy-start | bytes 2359300
  21.8 35.0 %collective-permute-start.3 = (f32[1024,384]{1,0:T(8,128)}, f32[1024,384]{1,0:T(8,128)}, u32[]{:S(2)}, u32[]{:S(2)}) collective-permute-start(f32[1024,384]{1,0:T(8,128)} %get-tuple-element.197.refs_5_.refs_1_.refs_3_), channel_id=1, source_target_pairs={{0,1},{1,0},{2,3},{3,2},{4,5},{5,4},{6,7},{7,6},{8,9},{9,8},{10,11... | collective-permute-start | bytes 4718600 | tf_op jit(solution)/shard_map/ppermute | solution.py:888
  22.2 33.7 %collective-permute-start.2 = (f32[384,512]{1,0:T(8,128)S(1)}, f32[384,512]{1,0:T(8,128)S(1)}, u32[]{:S(2)}, u32[]{:S(2)}) collective-permute-start(f32[384,512]{1,0:T(8,128)S(1)} %slice_select_fusion.2), channel_id=1, source_target_pairs={{0,1},{1,0},{2,3},{3,2},{4,5},{5,4},{6,7},{7,6},{8,9},{9,8},{10,11... | collective-permute-start | bytes 2359304 | tf_op jit(solution)/shard_map/ppermute | solution.py:888
  39.9 16.9 %copy-start.11 = (f32[8,128,256]{2,1,0:T(8,128)S(1)}, f32[8,128,256]{2,1,0:T(8,128)}, u32[]{:S(2)}) copy-start(f32[8,128,256]{2,1,0:T(8,128)} %get-tuple-element.160) | copy-start | bytes 3145732
  41.3 14.6 %collective-permute-start.1 = (f32[4,128,256]{2,1,0:T(8,128)S(1)}, f32[4,128,256]{2,1,0:T(8,128)S(1)}, u32[]{:S(2)}, u32[]{:S(2)}) collective-permute-start(f32[4,128,256]{2,1,0:T(8,128)S(1)} %slice_select_fusion.3), channel_id=1, source_target_pairs={{0,4},{4,0},{8,12},{12,8},{16,20},{20,16},{24,28},{28,24},{1,5},{5... | collective-permute-start | bytes 1572872 | tf_op jit(solution)/shard_map/ppermute | solution.py:888
  57.2 9.5 %collective-permute-start.4 = (f32[4,128,128]{2,1,0:T(8,128)S(1)}, f32[4,128,128]{2,1,0:T(8,128)S(1)}, u32[]{:S(2)}, u32[]{:S(2)}) collective-permute-start(f32[4,128,128]{2,1,0:T(8,128)S(1)} %slice.151), channel_id=1, source_target_pairs={{0,8},{4,12},{1,9},{5,13},{2,10},{6,14},{3,11},{7,15}} | collective-permute-start | bytes 786440 | tf_op jit(solution)/shard_map/ppermute | solution.py:983
  67.0 0.7 collective-permute-start.5
  68.0 0.9 collective-permute-start.6
  69.8 6.5 %collective-permute-start.7 = (f32[4,128,128]{2,1,0:T(8,128)S(1)}, f32[4,128,128]{2,1,0:T(8,128)S(1)}, u32[]{:S(2)}, u32[]{:S(2)}) collective-permute-start(f32[4,128,128]{2,1,0:T(8,128)S(1)} %get-tuple-element.164), channel_id=1, source_target_pairs={{0,4},{4,0},{8,12},{12,8},{16,20},{20,16},{24,28},{28,24},{1,5},{5... | collective-permute-start | bytes 786440 | tf_op jit(solution)/shard_map/ppermute | solution.py:888
  113.3 10.1 %collective-permute-start.9 = (f32[384,2816]{1,0:T(8,128)}, f32[384,2816]{1,0:T(8,128)}, u32[]{:S(2)}, u32[]{:S(2)}) collective-permute-start(f32[384,2816]{1,0:T(8,128)} %get-tuple-element.172), channel_id=1, source_target_pairs={{0,1},{1,0},{2,3},{3,2},{4,5},{5,4},{6,7},{7,6},{8,9},{9,8},{10,11... | collective-permute-start | bytes 12976136 | tf_op jit(solution)/shard_map/ppermute | solution.py:888
  113.4 10.0 %collective-permute-start.8 = (f32[1024,384]{1,0:T(8,128)}, f32[1024,384]{1,0:T(8,128)S(1)}, u32[]{:S(2)}, u32[]{:S(2)}) collective-permute-start(f32[1024,384]{1,0:T(8,128)} %get-tuple-element.167.refs_1_), channel_id=1, source_target_pairs={{0,1},{1,0},{2,3},{3,2},{4,5},{5,4},{6,7},{7,6},{8,9},{9,8},{10,11... | collective-permute-start | bytes 4718600 | tf_op jit(solution)/shard_map/ppermute | solution.py:888
  123.4 17.3 %collective-permute-start.13 = (f32[2816,384]{1,0:T(8,128)}, f32[2816,384]{1,0:T(8,128)}, u32[]{:S(2)}, u32[]{:S(2)}) collective-permute-start(f32[2816,384]{1,0:T(8,128)} %get-tuple-element.186.refs_1_), channel_id=1, source_target_pairs={{0,1},{1,0},{2,3},{3,2},{4,5},{5,4},{6,7},{7,6},{8,9},{9,8},{10,11... | collective-permute-start | bytes 12976136 | tf_op jit(solution)/shard_map/ppermute | solution.py:888
  125.7 10.4 %collective-permute-start.10 = (f32[4,128,128]{2,1,0:T(8,128)}, f32[4,128,128]{2,1,0:T(8,128)}, u32[]{:S(2)}, u32[]{:S(2)}) collective-permute-start(f32[4,128,128]{2,1,0:T(8,128)} %slice_select_fusion.6), channel_id=1, source_target_pairs={{0,4},{4,0},{8,12},{12,8},{16,20},{20,16},{24,28},{28,24},{1,5},{5... | collective-permute-start | bytes 786440 | tf_op jit(solution)/shard_map/ppermute | solution.py:888
  137.4 16.5 %collective-permute-start.12 = (f32[144,2048]{1,0:T(8,128)}, f32[144,2048]{1,0:T(8,128)S(1)}, u32[]{:S(2)}, u32[]{:S(2)}) collective-permute-start(f32[144,2048]{1,0:T(8,128)} %get-tuple-element.185), channel_id=1, source_target_pairs={{0,4},{1,3},{2,6},{3,1},{4,0},{5,7},{6,2},{7,5},{8,12},{9,11},{10,... | collective-permute-start | bytes 3538952 | tf_op jit(solution)/shard_map/ppermute | solution.py:892
  138.9 17.7 %collective-permute-start.16 = (f32[1024,384]{1,0:T(8,128)}, f32[1024,384]{1,0:T(8,128)}, u32[]{:S(2)}, u32[]{:S(2)}) collective-permute-start(f32[1024,384]{1,0:T(8,128)} %get-tuple-element.196.refs_3_), channel_id=1, source_target_pairs={{0,1},{1,0},{2,3},{3,2},{4,5},{5,4},{6,7},{7,6},{8,9},{9,8},{10,11... | collective-permute-start | bytes 4718600 | tf_op jit(solution)/shard_map/ppermute | solution.py:888
  138.9 17.7 %collective-permute-start.17 = (f32[384,1024]{1,0:T(8,128)}, f32[384,1024]{1,0:T(8,128)}, u32[]{:S(2)}, u32[]{:S(2)}) collective-permute-start(f32[384,1024]{1,0:T(8,128)} %get-tuple-element.200), channel_id=1, source_target_pairs={{0,1},{1,0},{2,3},{3,2},{4,5},{5,4},{6,7},{7,6},{8,9},{9,8},{10,11... | collective-permute-start | bytes 4718600 | tf_op jit(solution)/shard_map/ppermute | solution.py:888
  139.4 9.1 %collective-permute-start.11 = (f32[4,128,128]{2,1,0:T(8,128)S(1)}, f32[4,128,128]{2,1,0:T(8,128)S(1)}, u32[]{:S(2)}, u32[]{:S(2)}) collective-permute-start(f32[4,128,128]{2,1,0:T(8,128)S(1)} %apply_map.9.refs_0_), channel_id=1, source_target_pairs={{24,16},{28,20},{25,17},{29,21},{26,18},{30,22},{27,19},{31,23}} | collective-permute-start | bytes 786440 | tf_op jit(solution)/shard_map/ppermute | solution.py:1029
  140.7 13.4 %copy-start.33 = (f32[144,2048]{1,0:T(8,128)S(1)}, f32[144,2048]{1,0:T(8,128)}, u32[]{:S(2)}) copy-start(f32[144,2048]{1,0:T(8,128)} %get-tuple-element.195) | copy-start | bytes 3538948
  154.2 16.3 %collective-permute-start.15 = (f32[144,2048]{1,0:T(8,128)S(1)}, f32[144,2048]{1,0:T(8,128)S(1)}, u32[]{:S(2)}, u32[]{:S(2)}) collective-permute-start(f32[144,2048]{1,0:T(8,128)S(1)} %copy-done.33), channel_id=1, source_target_pairs={{0,4},{1,3},{2,6},{3,1},{4,0},{5,7},{6,2},{7,5},{8,12},{9,11},{10,... | collective-permute-start | bytes 3538952 | tf_op jit(solution)/shard_map/ppermute | solution.py:892
  155.6 13.8 %collective-permute-start.14 = (f32[4,128,128]{2,1,0:T(8,128)S(1)}, f32[4,128,128]{2,1,0:T(8,128)S(1)}, u32[]{:S(2)}, u32[]{:S(2)}) collective-permute-start(f32[4,128,128]{2,1,0:T(8,128)S(1)} %apply_map.10), channel_id=1, source_target_pairs={{16,8},{20,12},{17,9},{21,13},{18,10},{22,14},{19,11},{23,15}} | collective-permute-start | bytes 786440 | tf_op jit(solution)/shard_map/ppermute | solution.py:1029
  156.6 14.2 %copy-start.32 = (f32[144,2048]{1,0:T(8,128)S(1)}, f32[144,2048]{1,0:T(8,128)}, u32[]{:S(2)}) copy-start(f32[144,2048]{1,0:T(8,128)} %get-tuple-element.206) | copy-start | bytes 3538948
  169.4 18.7 %copy-start.34 = (f32[80,2048]{1,0:T(8,128)S(1)}, f32[80,2048]{1,0:T(8,128)}, u32[]{:S(2)}) copy-start(f32[80,2048]{1,0:T(8,128)} %get-tuple-element.211) | copy-start | bytes 1966084
  170.5 31.4 %copy-start.20 = (f32[144,2048]{1,0:T(8,128)}, f32[144,2048]{1,0:T(8,128)S(1)}, u32[]{:S(2)}) copy-start(f32[144,2048]{1,0:T(8,128)S(1)} %collective-permute-done.15) | copy-start | bytes 3538948
  170.8 16.3 %collective-permute-start.19 = (f32[144,2048]{1,0:T(8,128)S(1)}, f32[144,2048]{1,0:T(8,128)S(1)}, u32[]{:S(2)}, u32[]{:S(2)}) collective-permute-start(f32[144,2048]{1,0:T(8,128)S(1)} %copy-done.32), channel_id=1, source_target_pairs={{0,4},{1,3},{2,6},{3,1},{4,0},{5,7},{6,2},{7,5},{8,12},{9,11},{10,... | collective-permute-start | bytes 3538952 | tf_op jit(solution)/shard_map/ppermute | solution.py:892
  172.2 12.9 %collective-permute-start.18 = (f32[4,128,128]{2,1,0:T(8,128)S(1)}, f32[4,128,128]{2,1,0:T(8,128)S(1)}, u32[]{:S(2)}, u32[]{:S(2)}) collective-permute-start(f32[4,128,128]{2,1,0:T(8,128)S(1)} %apply_map.11), channel_id=1, source_target_pairs={{8,0},{12,4},{9,1},{13,5},{10,2},{14,6},{11,3},{15,7}} | collective-permute-start | bytes 786440 | tf_op jit(solution)/shard_map/ppermute | solution.py:1029
  187.0 16.3 %copy-start.22 = (f32[144,2048]{1,0:T(8,128)}, f32[144,2048]{1,0:T(8,128)S(1)}, u32[]{:S(2)}) copy-start(f32[144,2048]{1,0:T(8,128)S(1)} %collective-permute-done.19) | copy-start | bytes 3538948
  188.1 13.7 %collective-permute-start.21 = (f32[80,2048]{1,0:T(8,128)S(1)}, f32[80,2048]{1,0:T(8,128)S(1)}, u32[]{:S(2)}, u32[]{:S(2)}) collective-permute-start(f32[80,2048]{1,0:T(8,128)S(1)} %copy-done.34), channel_id=1, source_target_pairs={{0,4},{1,3},{2,6},{3,1},{4,0},{5,7},{6,2},{7,5},{8,12},{9,11},{10,... | collective-permute-start | bytes 1966088 | tf_op jit(solution)/shard_map/ppermute | solution.py:892
  189.5 12.3 %collective-permute-start.20 = (f32[4,128,128]{2,1,0:T(8,128)S(1)}, f32[4,128,128]{2,1,0:T(8,128)S(1)}, u32[]{:S(2)}, u32[]{:S(2)}) collective-permute-start(f32[4,128,128]{2,1,0:T(8,128)S(1)} %get-tuple-element.210), channel_id=1, source_target_pairs={{0,4},{4,0},{8,12},{12,8},{16,20},{20,16},{24,28},{28,24},{1,5},{5... | collective-permute-start | bytes 786440 | tf_op jit(solution)/shard_map/ppermute | solution.py:888
  201.8 46.0 %collective-permute-start.22 = (f32[512,1792]{1,0:T(8,128)}, f32[512,1792]{1,0:T(8,128)}, u32[]{:S(2)}, u32[]{:S(2)}) collective-permute-start(f32[512,1792]{1,0:T(8,128)} %get-tuple-element.228), channel_id=1, source_target_pairs={{0,4},{1,3},{2,6},{3,1},{4,0},{5,7},{6,2},{7,5},{8,12},{9,11},{10,... | collective-permute-start | bytes 11010056 | tf_op jit(solution)/shard_map/ppermute | solution.py:892
  203.3 44.5 %collective-permute-start.23 = (f32[592,512]{1,0:T(8,128)}, f32[592,512]{1,0:T(8,128)S(1)}, u32[]{:S(2)}, u32[]{:S(2)}) collective-permute-start(f32[592,512]{1,0:T(8,128)} %get-tuple-element.229), channel_id=1, source_target_pairs={{0,8},{4,12},{8,0},{12,4},{16,24},{20,28},{24,16},{28,20},{1,9},{5... | collective-permute-start | bytes 3637256 | tf_op jit(solution)/shard_map/ppermute | solution.py:888
  210.6 33.2 %copy-start.21 = (f32[144,2048]{1,0:T(8,128)S(1)}, f32[144,2048]{1,0:T(8,128)}, u32[]{:S(2)}) copy-start(f32[144,2048]{1,0:T(8,128)} %copy-done.20) | copy-start | bytes 3538948
  210.6 33.2 %copy-start.23 = (f32[144,2048]{1,0:T(8,128)S(1)}, f32[144,2048]{1,0:T(8,128)}, u32[]{:S(2)}) copy-start(f32[144,2048]{1,0:T(8,128)} %copy-done.22) | copy-start | bytes 3538948
  248.4 7.7 %collective-permute-start.24 = (f32[3,8,1024]{2,1,0:T(8,128)S(1)}, f32[3,8,1024]{2,1,0:T(8,128)S(1)}, u32[]{:S(2)}, u32[]{:S(2)}) collective-permute-start(f32[3,8,1024]{2,1,0:T(8,128)S(1)} %copy-done.35), channel_id=1, source_target_pairs={{4,0},{8,4},{12,8},{16,12},{20,16},{24,20},{28,24},{5,1},{9,5},{13... | collective-permute-start | bytes 294920 | tf_op jit(solution)/shard_map/ppermute | solution.py:875
  256.5 15.4 %copy-start.2 = (bf16[3,384,1024]{2,1,0:T(8,128)(2,1)}, bf16[3,384,1024]{2,1,0:T(8,128)(2,1)S(1)}, u32[]{:S(2)}) copy-start(bf16[3,384,1024]{2,1,0:T(8,128)(2,1)S(1)} %convert_element_type.27.grads) | copy-start | bytes 7077892
  256.5 46.1 %collective-permute-start.27 = (f32[2,2,64,3840]{3,2,1,0:T(8,128)}, f32[2,2,64,3840]{3,2,1,0:T(8,128)}, u32[]{:S(2)}, u32[]{:S(2)}) collective-permute-start(f32[2,2,64,3840]{3,2,1,0:T(8,128)} %pad_maximum_fusion.1), channel_id=1, source_target_pairs={{0,2},{1,5},{2,0},{3,7},{4,6},{5,1},{6,4},{7,3},{8,10},{9,13},{10,... | collective-permute-start | bytes 11796488 | tf_op jit(solution)/shard_map/ppermute | solution.py:892
  257.8 36.1 %collective-permute-start.28 = (f32[816,512]{1,0:T(8,128)}, f32[816,512]{1,0:T(8,128)}, u32[]{:S(2)}, u32[]{:S(2)}) collective-permute-start(f32[816,512]{1,0:T(8,128)} %get-tuple-element.237), channel_id=1, source_target_pairs={{0,8},{4,12},{8,0},{12,4},{16,24},{20,28},{24,16},{28,20},{1,9},{5... | collective-permute-start | bytes 5013512 | tf_op jit(solution)/shard_map/ppermute | solution.py:888
  265.8 7.1 %collective-permute-start.25 = (f32[384,1024]{1,0:T(8,128)}, f32[384,1024]{1,0:T(8,128)}, u32[]{:S(2)}, u32[]{:S(2)}) collective-permute-start(f32[384,1024]{1,0:T(8,128)} %fusion), channel_id=1, source_target_pairs={{0,1},{1,0},{2,3},{3,2},{4,5},{5,4},{6,7},{7,6},{8,9},{9,8},{10,11... | collective-permute-start | bytes 4718600 | tf_op jit(solution)/shard_map/ppermute | solution.py:888
  267.3 5.6 %collective-permute-start.26 = (f32[384,512]{1,0:T(8,128)S(1)}, f32[384,512]{1,0:T(8,128)S(1)}, u32[]{:S(2)}, u32[]{:S(2)}) collective-permute-start(f32[384,512]{1,0:T(8,128)S(1)} %fusion.2), channel_id=1, source_target_pairs={{0,1},{1,0},{2,3},{3,2},{4,5},{5,4},{6,7},{7,6},{8,9},{9,8},{10,11... | collective-permute-start | bytes 2359304 | tf_op jit(solution)/shard_map/ppermute | solution.py:888
  272.9 29.7 %copy-start.19 = (f32[592,512]{1,0:T(8,128)S(1)}, f32[592,512]{1,0:T(8,128)}, u32[]{:S(2)}) copy-start(f32[592,512]{1,0:T(8,128)} %copy-done.18) | copy-start | bytes 3637252
  308.4 12.8 %copy-start.31 = (f32[3,4,1024]{2,1,0:T(4,128)S(1)}, f32[3,4,1024]{2,1,0:T(4,128)}, u32[]{:S(2)}) copy-start(f32[3,4,1024]{2,1,0:T(4,128)} %get-tuple-element.251) | copy-start | bytes 147460
  308.4 12.8 %copy-start.3 = (f32[1024,384]{1,0:T(8,128)S(1)}, f32[1024,384]{1,0:T(8,128)}, u32[]{:S(2)}) copy-start(f32[1024,384]{1,0:T(8,128)} %get-tuple-element.197.refs_5_.refs_1_.refs_3_) | copy-start | bytes 4718596
  308.4 12.8 %copy-start.24 = (f32[384,8]{1,0:T(8,128)S(1)}, f32[384,8]{1,0:T(8,128)}, u32[]{:S(2)}) copy-start(f32[384,8]{1,0:T(8,128)} %get-tuple-element.249.grad_beta) | copy-start | bytes 36868
  309.9 54.3 %collective-permute-start.31 = (f32[512,1536]{1,0:T(8,128)}, f32[512,1536]{1,0:T(8,128)}, u32[]{:S(2)}, u32[]{:S(2)}) collective-permute-start(f32[512,1536]{1,0:T(8,128)} %get-tuple-element.245), channel_id=1, source_target_pairs={{0,4},{1,3},{2,6},{3,1},{4,0},{5,7},{6,2},{7,5},{8,12},{9,11},{10,... | collective-permute-start | bytes 9437192 | tf_op jit(solution)/shard_map/ppermute | solution.py:892
  313.2 51.0 %collective-permute-start.29 = (f32[2,64,3840]{2,1,0:T(8,128)}, f32[2,64,3840]{2,1,0:T(8,128)}, u32[]{:S(2)}, u32[]{:S(2)}) collective-permute-start(f32[2,64,3840]{2,1,0:T(8,128)} %maximum_add_fusion), channel_id=1, source_target_pairs={{0,8},{1,17},{2,10},{3,19},{4,12},{5,21},{6,14},{7,23},{8,0},{9,25... | collective-permute-start | bytes 5898248 | tf_op jit(solution)/shard_map/ppermute | solution.py:892
  319.9 44.3 %collective-permute-start.30 = (f32[2,2,176,512]{3,2,1,0:T(8,128)}, f32[2,2,176,512]{3,2,1,0:T(8,128)}, u32[]{:S(2)}, u32[]{:S(2)}) collective-permute-start(f32[2,2,176,512]{3,2,1,0:T(8,128)} %add_bitcast_fusion.3), channel_id=1, source_target_pairs={{0,4},{1,3},{2,6},{3,1},{4,0},{5,7},{6,2},{7,5},{8,12},{9,11},{10,... | collective-permute-start | bytes 4325384 | tf_op jit(solution)/shard_map/ppermute | solution.py:892
  327.4 36.8 %copy-start.7 = (f32[1408,512]{1,0:T(8,128)S(1)}, f32[1408,512]{1,0:T(8,128)}, u32[]{:S(2)}) copy-start(f32[1408,512]{1,0:T(8,128)} %copy-done.6) | copy-start | bytes 8650756
  372.6 34.3 %collective-permute-start.32 = (f32[2,2,64,1536]{3,2,1,0:T(8,128)}, f32[2,2,64,1536]{3,2,1,0:T(8,128)}, u32[]{:S(2)}, u32[]{:S(2)}) collective-permute-start(f32[2,2,64,1536]{3,2,1,0:T(8,128)} %add_bitcast_fusion.2), channel_id=1, source_target_pairs={{0,2},{1,5},{2,0},{3,7},{4,6},{5,1},{6,4},{7,3},{8,10},{9,13},{10,... | collective-permute-start | bytes 4718600 | tf_op jit(solution)/shard_map/ppermute | solution.py:892
  373.8 33.1 %collective-permute-start.33 = (f32[64,3840]{1,0:T(8,128)}, f32[64,3840]{1,0:T(8,128)}, u32[]{:S(2)}, u32[]{:S(2)}) collective-permute-start(f32[64,3840]{1,0:T(8,128)} %maximum_add_fusion.1), channel_id=1, source_target_pairs={{0,16},{1,9},{2,18},{3,11},{4,20},{5,13},{6,22},{7,15},{8,24},{9,1... | collective-permute-start | bytes 2949128 | tf_op jit(solution)/shard_map/ppermute | solution.py:892
  384.0 17.0 %collective-permute-start.34 = (f32[2,176,512]{2,1,0:T(8,128)}, f32[2,176,512]{2,1,0:T(8,128)}, u32[]{:S(2)}, u32[]{:S(2)}) collective-permute-start(f32[2,176,512]{2,1,0:T(8,128)} %bitcast_add_fusion.3), channel_id=1, source_target_pairs={{0,2},{1,5},{2,0},{3,7},{4,6},{5,1},{6,4},{7,3},{8,10},{9,13},{10,... | collective-permute-start | bytes 2162696 | tf_op jit(solution)/shard_map/ppermute | solution.py:892
  384.8 1.3 collective-permute-start.35
  414.7 21.5 %collective-permute-start.38 = (f32[64,3840]{1,0:T(8,128)}, f32[64,3840]{1,0:T(8,128)}, u32[]{:S(2)}, u32[]{:S(2)}) collective-permute-start(f32[64,3840]{1,0:T(8,128)} %maximum_add_fusion.2), channel_id=1, source_target_pairs={{0,2},{1,3},{2,0},{3,1},{4,6},{5,7},{6,4},{7,5},{8,10},{9,11},{10,... | collective-permute-start | bytes 2949128 | tf_op jit(solution)/shard_map/ppermute | solution.py:888
  415.5 20.7 %collective-permute-start.36 = (f32[2,64,1536]{2,1,0:T(8,128)}, f32[2,64,1536]{2,1,0:T(8,128)}, u32[]{:S(2)}, u32[]{:S(2)}) collective-permute-start(f32[2,64,1536]{2,1,0:T(8,128)} %bitcast_add_fusion.2), channel_id=1, source_target_pairs={{0,8},{1,17},{2,10},{3,19},{4,12},{5,21},{6,14},{7,23},{8,0},{9,25... | collective-permute-start | bytes 2359304 | tf_op jit(solution)/shard_map/ppermute | solution.py:892
  416.8 17.1 %collective-permute-start.37 = (f32[176,512]{1,0:T(8,128)}, f32[176,512]{1,0:T(8,128)S(1)}, u32[]{:S(2)}, u32[]{:S(2)}) collective-permute-start(f32[176,512]{1,0:T(8,128)} %fusion.10), channel_id=1, source_target_pairs={{0,16},{4,20},{8,24},{12,28},{16,0},{20,4},{24,8},{28,12},{1,17},{... | collective-permute-start | bytes 1081352 | tf_op jit(solution)/shard_map/ppermute | solution.py:888
  422.3 4.3 collective-permute-start.39
  443.0 18.9 %collective-permute-start.42 = (f32[128,3840]{1,0:T(8,128)}, f32[128,3840]{1,0:T(8,128)}, u32[]{:S(2)}, u32[]{:S(2)}) collective-permute-start(f32[128,3840]{1,0:T(8,128)} %pad_maximum_fusion.3), channel_id=1, source_target_pairs={{0,1},{1,0},{2,3},{3,2},{4,5},{5,4},{6,7},{7,6},{8,9},{9,8},{10,11... | collective-permute-start | bytes 5898248 | tf_op jit(solution)/shard_map/ppermute | solution.py:888
  449.6 12.3 %collective-permute-start.40 = (f32[64,1536]{1,0:T(8,128)}, f32[64,1536]{1,0:T(8,128)S(1)}, u32[]{:S(2)}, u32[]{:S(2)}) collective-permute-start(f32[64,1536]{1,0:T(8,128)} %fusion.7), channel_id=1, source_target_pairs={{0,16},{1,9},{2,18},{3,11},{4,20},{5,13},{6,22},{7,15},{8,24},{9,1... | collective-permute-start | bytes 1179656 | tf_op jit(solution)/shard_map/ppermute | solution.py:892
  453.6 7.4 %collective-permute-start.41 = (f32[176,512]{1,0:T(8,128)S(1)}, f32[176,512]{1,0:T(8,128)S(1)}, u32[]{:S(2)}, u32[]{:S(2)}) collective-permute-start(f32[176,512]{1,0:T(8,128)S(1)} %fusion.9), channel_id=1, source_target_pairs={{0,2},{1,3},{2,0},{3,1},{4,6},{5,7},{6,4},{7,5},{8,10},{9,11},{10,... | collective-permute-start | bytes 1081352 | tf_op jit(solution)/shard_map/ppermute | solution.py:888
  454.5 5.8 %collective-permute-start.43 = (f32[2,32,128]{2,1,0:T(8,128)S(1)}, f32[2,32,128]{2,1,0:T(8,128)S(1)}, u32[]{:S(2)}, u32[]{:S(2)}) collective-permute-start(f32[2,32,128]{2,1,0:T(8,128)S(1)} %bitcast_add_fusion.8), channel_id=1, source_target_pairs={{0,8},{4,12},{8,0},{12,4},{16,24},{20,28},{24,16},{28,20},{1,9},{5... | collective-permute-start | bytes 98312 | tf_op jit(solution)/shard_map/ppermute | solution.py:888
  463.6 7.6 %collective-permute-start.46 = (f32[32,128]{1,0:T(8,128)S(1)}, f32[32,128]{1,0:T(8,128)S(1)}, u32[]{:S(2)}, u32[]{:S(2)}) collective-permute-start(f32[32,128]{1,0:T(8,128)S(1)} %bitcast_add_fusion.9), channel_id=1, source_target_pairs={{0,16},{4,20},{8,24},{12,28},{16,0},{20,4},{24,8},{28,12},{1,17},{... | collective-permute-start | bytes 49160 | tf_op jit(solution)/shard_map/ppermute | solution.py:888
  468.4 10.6 %collective-permute-start.44 = (f32[64,1536]{1,0:T(8,128)S(1)}, f32[64,1536]{1,0:T(8,128)S(1)}, u32[]{:S(2)}, u32[]{:S(2)}) collective-permute-start(f32[64,1536]{1,0:T(8,128)S(1)} %fusion.6), channel_id=1, source_target_pairs={{0,2},{1,3},{2,0},{3,1},{4,6},{5,7},{6,4},{7,5},{8,10},{9,11},{10,... | collective-permute-start | bytes 1179656 | tf_op jit(solution)/shard_map/ppermute | solution.py:888
  469.3 9.7 %collective-permute-start.45 = (f32[352,512]{1,0:T(8,128)S(1)}, f32[352,512]{1,0:T(8,128)S(1)}, u32[]{:S(2)}, u32[]{:S(2)}) collective-permute-start(f32[352,512]{1,0:T(8,128)S(1)} %pad_maximum_fusion.6), channel_id=1, source_target_pairs={{0,1},{1,0},{2,3},{3,2},{4,5},{5,4},{6,7},{7,6},{8,9},{9,8},{10,11... | collective-permute-start | bytes 2162696 | tf_op jit(solution)/shard_map/ppermute | solution.py:888
  479.2 8.0 %collective-permute-start.47 = (f32[128,1536]{1,0:T(8,128)S(1)}, f32[128,1536]{1,0:T(8,128)S(1)}, u32[]{:S(2)}, u32[]{:S(2)}) collective-permute-start(f32[128,1536]{1,0:T(8,128)S(1)} %pad_maximum_fusion.5), channel_id=1, source_target_pairs={{0,1},{1,0},{2,3},{3,2},{4,5},{5,4},{6,7},{7,6},{8,9},{9,8},{10,11... | collective-permute-start | bytes 2359304 | tf_op jit(solution)/shard_map/ppermute | solution.py:888
  483.4 3.7 collective-permute-start.48
  (24 other events, 89.4 us)
